TPU v7x, 32 devices: a whole 2x2x4 slice. The times are simulated.
32 devices in a mesh: dom: 16 (over z, y, core), band: 2 (over x).
Axes of the slice: x: 2, y: 2, z: 4, core: 2. Of those that a mesh axis runs over, the one named last changes fastest.
Arguments:
- orbitals: float32 [16, 16, 12, 16, 128], P('dom', 'band'), may hold values from -6 to 6
- potential: float32 [16, 12, 16, 128], P('dom'), may hold values from -12 to 4
- projectors: bfloat16 [4096, 4, 128], P('dom'), may hold values from -0.359375 to 0.359375
- entry_atom: int32 [4096], P('dom'), may hold values from 0 to 63, as said below
- entry_block: int32 [4096], P('dom'), may hold values from 0 to 191
- kb_energy: float32 [64, 4], replicated, may hold values from 1 to 10
- panel: bfloat16 [16, 16], replicated, may hold values from -1.5 to 1.5
Outputs:
- rotated: float32 [16, 16, 12, 16, 128], P('dom', 'band')
Inputs may be any that keep to these rules, and one draw needn't show every extreme that they name: `entry_atom`: atom a is owned by domain a // 4; every entry of domain d belongs to an atom owned by d or by a domain that shares a face with d in the 2 x 2 x 4 arrangement of domains (no wrap-around).
All inputs are finite; a program needn't handle non-finite values.
Results may differ from a plain program's by a relative error of at most 0.00115.
The roundings to bfloat16 on the way count: a program that leaves them out, or rounds other values in their place, can miss the bound.
Values may be sent and summed in bfloat16 or wider, within the bound.
No kernel may reach another device: no remote copies, remote signals or barrier semaphores. Data moves between devices by JAX's collectives and lax.ppermute only.
A program may use at most 64 MiB of HBM per device.

v0:
```python
import jax
import jax.numpy as jnp
from jax import lax
from jax.sharding import PartitionSpec as P

RADIUS = 6


COEFFS = (
    -5369.0 / 1800.0,
    12.0 / 7.0,
    -15.0 / 56.0,
    10.0 / 189.0,
    -1.0 / 112.0,
    2.0 / 1925.0,
    -1.0 / 16632.0,
)
KINETIC = -3.125
CENTER = 36.0
HALF_WIDTH = 34.0


def from_behind(block, axis, distance):
    devices = range(lax.axis_size(axis))
    route = [(i - distance, i) for i in devices if i - distance in devices]
    return lax.ppermute(block, axis, route)


def extend(values, depth_cells, position, stride, location, extent):
    length = values.shape[position]
    top_layers = lax.slice_in_dim(values, length - depth_cells, length, axis=position)
    bottom_layers = lax.slice_in_dim(values, 0, depth_cells, axis=position)
    from_lower = from_behind(top_layers, "dom", stride)
    from_upper = from_behind(bottom_layers, "dom", -stride)
    from_lower = jnp.where(location > 0, from_lower, jnp.zeros_like(from_lower))
    from_upper = jnp.where(location < extent - 1, from_upper, jnp.zeros_like(from_upper))
    return jnp.concatenate([from_lower, values, from_upper], axis=position)


def local_part(values, pot_local, geometry):
    laplace = 3.0 * COEFFS[0] * values
    for position, stride, location, extent in geometry:
        padded = extend(values, RADIUS, position, stride, location, extent)
        length = values.shape[position]
        for offset in range(1, RADIUS + 1):
            upward = lax.slice_in_dim(
                padded, RADIUS + offset, RADIUS + offset + length, axis=position
            )
            downward = lax.slice_in_dim(
                padded, RADIUS - offset, RADIUS - offset + length, axis=position
            )
            laplace = laplace + COEFFS[offset] * (upward + downward)
    return KINETIC * laplace + pot_local * values


def nonlocal_part(values, proj_values, block_index, one_hot, combine):
    orbit_count = values.shape[0]
    rows_view = values.reshape(orbit_count, -1, proj_values.shape[2])
    picked = jnp.take(rows_view, block_index, axis=1)
    intersections = jnp.einsum("epk,oek->epo", proj_values, picked, precision=lax.Precision.HIGHEST)
    atom_table = jnp.einsum("ea,epo->apo", one_hot, intersections, precision=lax.Precision.HIGHEST)
    scaled = combine(atom_table)
    per_entry = jnp.einsum("ea,apo->epo", one_hot, scaled, precision=lax.Precision.HIGHEST)
    additions = jnp.einsum("epk,epo->oek", proj_values, per_entry, precision=lax.Precision.HIGHEST)
    result = jnp.zeros_like(rows_view).at[:, block_index].add(additions)
    return result.reshape(values.shape)


def send_owner(piece, stride):
    return from_behind(piece, "dom", stride)


def send_back(piece, stride):
    return from_behind(piece, "dom", -stride)


def shards(orbitals, potential, projectors, entry_atom, entry_block, kb_energy, panel):
    start_values = orbitals[0]
    pot_local = potential[0]
    orbit_count = start_values.shape[0]
    dom_count = lax.axis_size("dom")
    dom_third = 4
    dom_second = min(8, dom_count // 8)
    plane_size = dom_second * dom_third
    dom_index = lax.axis_index("dom")
    geometry = (
        (1, plane_size, dom_index // plane_size, dom_count // plane_size),
        (2, dom_third, dom_index // dom_third % dom_second, dom_second),
        (3, 1, dom_index % dom_third, dom_third),
    )
    atom_total = kb_energy.shape[0]
    owned = atom_total // dom_count
    proj_values = projectors.astype(jnp.float32)
    strides = (0, plane_size, -plane_size, dom_third, -dom_third, 1, -1)
    owner_of = entry_atom // owned
    gap = owner_of - dom_index
    slot = jnp.zeros_like(entry_atom)
    for number in range(1, 7):
        slot = jnp.where(gap == strides[number], number, slot)
    column = slot * owned + entry_atom % owned
    one_hot = (column[:, None] == jnp.arange(7 * owned, dtype=jnp.int32)[None, :]).astype(
        jnp.float32
    )
    own_energy = lax.dynamic_slice_in_dim(kb_energy, dom_index * owned, owned, 0)

    def combine(atom_table):
        total = atom_table[0:owned]
        for number in range(1, 7):
            total = total + send_owner(
                atom_table[number * owned : (number + 1) * owned], strides[number]
            )
        scaled_own = own_energy[:, :, None] * total
        pieces = [scaled_own]
        for number in range(1, 7):
            pieces.append(send_back(scaled_own, strides[number]))
        return jnp.concatenate(pieces, axis=0)

    def apply_ham(current):
        return local_part(current, pot_local, geometry) + nonlocal_part(
            current, proj_values, entry_block, one_hot, combine
        )

    applied = apply_ham(start_values)
    first_step = (applied - CENTER * start_values) / HALF_WIDTH
    applied_again = apply_ham(first_step)
    second_step = 2.0 * (applied_again - CENTER * first_step) / HALF_WIDTH - start_values
    filtered = second_step.astype(jnp.bfloat16)
    band_index = lax.axis_index("band")
    own_rows = lax.dynamic_slice_in_dim(panel, band_index * orbit_count, orbit_count, 0)
    rotated = lax.psum_scatter(
        jnp.einsum("iabc,ij->jabc", filtered, own_rows, preferred_element_type=jnp.float32),
        "band",
        scatter_dimension=0,
        tiled=True,
    )
    return rotated[None]


def solution(mesh):
    in_specs = (
        P("dom", "band", None, None, None),
        P("dom", None, None, None),
        P("dom", None, None),
        P("dom"),
        P("dom"),
        P(),
        P(),
    )
    out_specs = P("dom", "band", None, None, None)
    return jax.shard_map(shards, mesh=mesh, in_specs=in_specs, out_specs=out_specs, check_vma=False)
```

profile of v0, /device:TPU:0, one launch (start us, length us, event | category | flops | bytes accessed | tf_op | source)
XLA Modules:
  0.0 287.8 jit_solution(11989531024906517860)
XLA Ops:
  12.8 2.9 %collective-permute-start.10 = (f32[4,4,8]{0,2,1:T(8,128)}, f32[4,4,8]{0,2,1:T(8,128)}, u32[]{:S(2)}, u32[]{:S(2)}) collective-permute-start(f32[4,4,8]{0,2,1:T(8,128)} %get-tuple-element.28), channel_id=1, source_target_pairs={{0,2},{2,4},{4,6},{6,8},{8,10},{10,12},{12,14},{14,16},{16,18},{18... | collective-permute-start | bytes 1544 | tf_op jit(solution)/shard_map/ppermute | solution.py:26
  17.0 8.8 %collective-permute-start.6 = (f32[4,4,8]{0,2,1:T(8,128)}, f32[4,4,8]{0,2,1:T(8,128)}, u32[]{:S(2)}, u32[]{:S(2)}) collective-permute-start(f32[4,4,8]{0,2,1:T(8,128)} %get-tuple-element.26), channel_id=1, source_target_pairs={{0,16},{2,18},{4,20},{6,22},{8,24},{10,26},{12,28},{14,30},{1,17},... | collective-permute-start | bytes 1544 | tf_op jit(solution)/shard_map/ppermute | solution.py:26
  27.1 4.1 %collective-permute-start.8 = (f32[4,4,8]{0,2,1:T(8,128)}, f32[4,4,8]{0,2,1:T(8,128)}, u32[]{:S(2)}, u32[]{:S(2)}) collective-permute-start(f32[4,4,8]{0,2,1:T(8,128)} %get-tuple-element.30), channel_id=1, source_target_pairs={{0,8},{2,10},{4,12},{6,14},{8,16},{10,18},{12,20},{14,22},{16,24},... | collective-permute-start | bytes 1544 | tf_op jit(solution)/shard_map/ppermute | solution.py:26
  43.7 5.4 %collective-permute-start.13 = (f32[4,4,8]{0,2,1:T(8,128)S(1)}, f32[4,4,8]{0,2,1:T(8,128)S(1)}, u32[]{:S(2)}, u32[]{:S(2)}) collective-permute-start(f32[4,4,8]{0,2,1:T(8,128)S(1)} %fusion.199), channel_id=1, source_target_pairs={{0,16},{2,18},{4,20},{6,22},{8,24},{10,26},{12,28},{14,30},{1,17},... | collective-permute-start | bytes 1544 | tf_op jit(solution)/shard_map/ppermute | solution.py:26
  50.5 4.5 %collective-permute-start.15 = (f32[4,4,8]{0,2,1:T(8,128)S(1)}, f32[4,4,8]{0,2,1:T(8,128)S(1)}, u32[]{:S(2)}, u32[]{:S(2)}) collective-permute-start(f32[4,4,8]{0,2,1:T(8,128)S(1)} %fusion.199), channel_id=1, source_target_pairs={{0,8},{2,10},{4,12},{6,14},{8,16},{10,18},{12,20},{14,22},{16,24},... | collective-permute-start | bytes 1544 | tf_op jit(solution)/shard_map/ppermute | solution.py:26
  56.3 3.0 %collective-permute-start.17 = (f32[4,4,8]{0,2,1:T(8,128)S(1)}, f32[4,4,8]{0,2,1:T(8,128)S(1)}, u32[]{:S(2)}, u32[]{:S(2)}) collective-permute-start(f32[4,4,8]{0,2,1:T(8,128)S(1)} %fusion.199), channel_id=1, source_target_pairs={{0,2},{2,4},{4,6},{6,8},{8,10},{10,12},{12,14},{14,16},{16,18},{18... | collective-permute-start | bytes 1544 | tf_op jit(solution)/shard_map/ppermute | solution.py:26
  59.4 4.7 %collective-permute-start.3 = (f32[8,12,6,128]{3,0,2,1:T(8,128)}, f32[8,12,6,128]{3,0,2,1:T(8,128)}, u32[]{:S(2)}, u32[]{:S(2)}) collective-permute-start(f32[8,12,6,128]{3,0,2,1:T(8,128)} %copy.83), channel_id=1, source_target_pairs={{0,8},{2,10},{4,12},{6,14},{8,16},{10,18},{12,20},{14,22},{16,24},... | collective-permute-start | bytes 884744 | tf_op jit(solution)/shard_map/ppermute | solution.py:26
  66.7 3.7 %collective-permute-start.5 = (f32[8,12,16,6]{2,0,3,1:T(8,128)}, f32[8,12,16,6]{2,0,3,1:T(8,128)}, u32[]{:S(2)}, u32[]{:S(2)}) collective-permute-start(f32[8,12,16,6]{2,0,3,1:T(8,128)} %copy.87), channel_id=1, source_target_pairs={{0,2},{2,4},{4,6},{6,8},{8,10},{10,12},{12,14},{14,16},{16,18},{18... | collective-permute-start | bytes 110600 | tf_op jit(solution)/shard_map/ppermute | solution.py:26
  70.4 4.4 %collective-permute-start.1 = (f32[8,6,16,128]{3,2,1,0:T(8,128)}, f32[8,6,16,128]{3,2,1,0:T(8,128)S(1)}, u32[]{:S(2)}, u32[]{:S(2)}) collective-permute-start(f32[8,6,16,128]{3,2,1,0:T(8,128)} %get-tuple-element.15), channel_id=1, source_target_pairs={{0,16},{2,18},{4,20},{6,22},{8,24},{10,26},{12,28},{14,30},{1,17},... | collective-permute-start | bytes 1179656 | tf_op jit(solution)/shard_map/ppermute | solution.py:26
  77.6 18.2 %scatter_fusion = f32[8,192,128]{2,0,1:T(8,128)S(1)} fusion(f32[8,192,128]{2,0,1:T(8,128)S(1)} %broadcast.87.clone, s32[256]{0:T(256)S(1)} %compare_select_fusion, f32[256,8,128]{2,1,0:T(8,128)} %fusion.222), kind=kCustom, calls=%fused_computation.2 | custom fusion | flops 262144 | bytes 3146752 | tf_op jit(solution)/shard_map/scatter-add | solution.py:65
  105.7 11.5 %collective-permute-done = f32[8,6,16,128]{3,2,1,0:T(8,128)} collective-permute-done((f32[8,6,16,128]{3,2,1,0:T(8,128)S(1)}, f32[8,6,16,128]{3,2,1,0:T(8,128)}, u32[]{:S(2)}, u32[]{:S(2)}) %collective-permute-start) | collective-permute-done | bytes 393248 | tf_op jit(solution)/shard_map/ppermute | solution.py:26
  119.0 11.6 %broadcast_multiply_fusion = (f32[8,12,16,128]{3,2,1,0:T(8,128)S(1)}, f32[8,12,16,128]{3,2,1,0:T(8,128)S(1)}) fusion(f32[8,12,16,128]{3,2,1,0:T(8,128)S(1)} %bitcast.53, f32[8,12,16,128]{3,0,2,1:T(8,128)S(1)} %bitcast.55, f32[12,16,128]{2,1,0:T(8,128)S(1)} %bitcast.59, f32[8,12,16,6]{3,2,1,0:T(8,128)} %copy.88, f32[8,12,16,6]{3,2,1,0:T(8,128)} %copy.86, ...), kind=kLoop, calls=%fused_computation.333 | loop fusion | flops 19267584 | bytes 4694016 | tf_op jit(solution)/shard_map/div | solution.py:124
  146.6 3.0 %collective-permute-done.27 = f32[4,4,8]{0,2,1:T(8,128)S(1)} collective-permute-done((f32[4,4,8]{0,2,1:T(8,128)S(1)}, f32[4,4,8]{0,2,1:T(8,128)S(1)}, u32[]{:S(2)}, u32[]{:S(2)}) %collective-permute-start.27) | collective-permute-done | bytes 544 | tf_op jit(solution)/shard_map/ppermute | solution.py:26
  151.8 9.6 %collective-permute-start.31 = (f32[4,4,8]{0,2,1:T(8,128)S(1)}, f32[4,4,8]{0,2,1:T(8,128)S(1)}, u32[]{:S(2)}, u32[]{:S(2)}) collective-permute-start(f32[4,4,8]{0,2,1:T(8,128)S(1)} %fusion.193), channel_id=1, source_target_pairs={{0,16},{2,18},{4,20},{6,22},{8,24},{10,26},{12,28},{14,30},{1,17},... | collective-permute-start | bytes 1544 | tf_op jit(solution)/shard_map/ppermute | solution.py:26
  163.6 4.6 %collective-permute-start.33 = (f32[4,4,8]{0,2,1:T(8,128)S(1)}, f32[4,4,8]{0,2,1:T(8,128)S(1)}, u32[]{:S(2)}, u32[]{:S(2)}) collective-permute-start(f32[4,4,8]{0,2,1:T(8,128)S(1)} %fusion.193), channel_id=1, source_target_pairs={{0,8},{2,10},{4,12},{6,14},{8,16},{10,18},{12,20},{14,22},{16,24},... | collective-permute-start | bytes 1544 | tf_op jit(solution)/shard_map/ppermute | solution.py:26
  168.2 2.5 copy.99
  172.0 3.0 %collective-permute-start.35 = (f32[4,4,8]{0,2,1:T(8,128)S(1)}, f32[4,4,8]{0,2,1:T(8,128)S(1)}, u32[]{:S(2)}, u32[]{:S(2)}) collective-permute-start(f32[4,4,8]{0,2,1:T(8,128)S(1)} %fusion.193), channel_id=1, source_target_pairs={{0,2},{2,4},{4,6},{6,8},{8,10},{10,12},{12,14},{14,16},{16,18},{18... | collective-permute-start | bytes 1544 | tf_op jit(solution)/shard_map/ppermute | solution.py:26
  176.5 5.9 %collective-permute-start.21 = (f32[8,12,6,128]{3,0,2,1:T(8,128)}, f32[8,12,6,128]{3,0,2,1:T(8,128)}, u32[]{:S(2)}, u32[]{:S(2)}) collective-permute-start(f32[8,12,6,128]{3,0,2,1:T(8,128)} %copy.95), channel_id=1, source_target_pairs={{0,8},{2,10},{4,12},{6,14},{8,16},{10,18},{12,20},{14,22},{16,24},... | collective-permute-start | bytes 884744 | tf_op jit(solution)/shard_map/ppermute | solution.py:26
  187.0 9.1 %collective-permute-start.19 = (f32[8,6,16,128]{3,2,1,0:T(8,128)}, f32[8,6,16,128]{3,2,1,0:T(8,128)}, u32[]{:S(2)}, u32[]{:S(2)}) collective-permute-start(f32[8,6,16,128]{3,2,1,0:T(8,128)} %get-tuple-element.9), channel_id=1, source_target_pairs={{0,16},{2,18},{4,20},{6,22},{8,24},{10,26},{12,28},{14,30},{1,17},... | collective-permute-start | bytes 1179656 | tf_op jit(solution)/shard_map/ppermute | solution.py:26
  198.9 18.2 %scatter_fusion.1 = f32[8,192,128]{2,0,1:T(8,128)S(1)} fusion(f32[8,192,128]{2,0,1:T(8,128)S(1)} %broadcast.87, s32[256]{0:T(256)S(1)} %compare_select_fusion, f32[256,8,128]{2,1,0:T(8,128)} %fusion.223), kind=kCustom, calls=%fused_computation.3 | custom fusion | flops 262144 | bytes 3146752 | tf_op jit(solution)/shard_map/scatter-add | solution.py:65
  230.4 6.7 %collective-permute-done.18 = f32[8,6,16,128]{3,2,1,0:T(8,128)} collective-permute-done((f32[8,6,16,128]{3,2,1,0:T(8,128)}, f32[8,6,16,128]{3,2,1,0:T(8,128)}, u32[]{:S(2)}, u32[]{:S(2)}) %collective-permute-start.18) | collective-permute-done | bytes 393248 | tf_op jit(solution)/shard_map/ppermute | solution.py:26
  238.9 12.4 %subtract_convert_fusion = bf16[8,12,16,128]{3,2,1,0:T(8,128)(2,1)} fusion(f32[8,12,16,128]{3,2,1,0:T(8,128)S(1)} %get-tuple-element.7, f32[8,12,16,128]{3,0,2,1:T(8,128)S(1)} %bitcast.54, f32[8,12,16,128]{3,2,1,0:T(8,128)S(1)} %get-tuple-element.6, f32[8,12,16,6]{3,2,1,0:T(8,128)} %copy.100, f32[8,12,16,6]{3,2,1,0:T(8,128)} %copy.98, ...), kind=kLoop, calls=%fused_computation.322 | loop fusion | flops 19660800 | bytes 5087232 | tf_op jit(solution)/shard_map/convert_element_type | solution.py:127
  251.3 2.6 fusion.184
  253.9 24.9 %reduce-scatter.2.cloned.1.call-done = f32[8,12,16,128]{3,0,2,1:T(8,128)} async-done(((f32[16,12,16,128]{3,0,2,1:T(8,128)}), f32[8,12,16,128]{3,0,2,1:T(8,128)}) %reduce-scatter.2.cloned.1.call-update) | async-done | bytes 786448 | tf_op jit(solution)/shard_map/reduce_scatter | solution.py:130
  (137 shorter events, 88.4 us)
Async XLA Ops:
  6.5 272.3 %reduce-scatter.2.cloned.1.call-start = ((), (), s32[]{:S(2)}) async-start(), calls=%async_computation.1 | async-start | bytes 2359296 | tf_op jit(solution)/shard_map/reduce_scatter | solution.py:130
  12.8 21.1 %collective-permute-start.10 = (f32[4,4,8]{0,2,1:T(8,128)}, f32[4,4,8]{0,2,1:T(8,128)}, u32[]{:S(2)}, u32[]{:S(2)}) collective-permute-start(f32[4,4,8]{0,2,1:T(8,128)} %get-tuple-element.28), channel_id=1, source_target_pairs={{0,2},{2,4},{4,6},{6,8},{8,10},{10,12},{12,14},{14,16},{16,18},{18... | collective-permute-start | bytes 1544 | tf_op jit(solution)/shard_map/ppermute | solution.py:26
  15.7 22.7 %collective-permute-start.11 = (f32[4,4,8]{0,2,1:T(8,128)}, f32[4,4,8]{0,2,1:T(8,128)}, u32[]{:S(2)}, u32[]{:S(2)}) collective-permute-start(f32[4,4,8]{0,2,1:T(8,128)} %get-tuple-element.27), channel_id=1, source_target_pairs={{2,0},{4,2},{6,4},{8,6},{10,8},{12,10},{14,12},{16,14},{18,16},{20... | collective-permute-start | bytes 1544 | tf_op jit(solution)/shard_map/ppermute | solution.py:26
  17.0 21.4 %collective-permute-start.6 = (f32[4,4,8]{0,2,1:T(8,128)}, f32[4,4,8]{0,2,1:T(8,128)}, u32[]{:S(2)}, u32[]{:S(2)}) collective-permute-start(f32[4,4,8]{0,2,1:T(8,128)} %get-tuple-element.26), channel_id=1, source_target_pairs={{0,16},{2,18},{4,20},{6,22},{8,24},{10,26},{12,28},{14,30},{1,17},... | collective-permute-start | bytes 1544 | tf_op jit(solution)/shard_map/ppermute | solution.py:26
  41.0 15.3 %collective-permute-start.12 = (f32[4,4,8]{0,2,1:T(8,128)S(1)}, f32[4,4,8]{0,2,1:T(8,128)S(1)}, u32[]{:S(2)}, u32[]{:S(2)}) collective-permute-start(f32[4,4,8]{0,2,1:T(8,128)S(1)} %fusion.199), channel_id=1, source_target_pairs={{16,0},{18,2},{20,4},{22,6},{24,8},{26,10},{28,12},{30,14},{17,1},... | collective-permute-start | bytes 1544 | tf_op jit(solution)/shard_map/ppermute | solution.py:26
  43.7 15.6 %collective-permute-start.13 = (f32[4,4,8]{0,2,1:T(8,128)S(1)}, f32[4,4,8]{0,2,1:T(8,128)S(1)}, u32[]{:S(2)}, u32[]{:S(2)}) collective-permute-start(f32[4,4,8]{0,2,1:T(8,128)S(1)} %fusion.199), channel_id=1, source_target_pairs={{0,16},{2,18},{4,20},{6,22},{8,24},{10,26},{12,28},{14,30},{1,17},... | collective-permute-start | bytes 1544 | tf_op jit(solution)/shard_map/ppermute | solution.py:26
  59.4 41.9 %collective-permute-start.3 = (f32[8,12,6,128]{3,0,2,1:T(8,128)}, f32[8,12,6,128]{3,0,2,1:T(8,128)}, u32[]{:S(2)}, u32[]{:S(2)}) collective-permute-start(f32[8,12,6,128]{3,0,2,1:T(8,128)} %copy.83), channel_id=1, source_target_pairs={{0,8},{2,10},{4,12},{6,14},{8,16},{10,18},{12,20},{14,22},{16,24},... | collective-permute-start | bytes 884744 | tf_op jit(solution)/shard_map/ppermute | solution.py:26
  64.0 39.1 %collective-permute-start.2 = (f32[8,12,6,128]{3,0,2,1:T(8,128)}, f32[8,12,6,128]{3,0,2,1:T(8,128)}, u32[]{:S(2)}, u32[]{:S(2)}) collective-permute-start(f32[8,12,6,128]{3,0,2,1:T(8,128)} %copy.81), channel_id=1, source_target_pairs={{8,0},{10,2},{12,4},{14,6},{16,8},{18,10},{20,12},{22,14},{24,16},... | collective-permute-start | bytes 884744 | tf_op jit(solution)/shard_map/ppermute | solution.py:26
  65.3 30.4 %collective-permute-start.4 = (f32[8,12,16,6]{2,0,3,1:T(8,128)}, f32[8,12,16,6]{2,0,3,1:T(8,128)}, u32[]{:S(2)}, u32[]{:S(2)}) collective-permute-start(f32[8,12,16,6]{2,0,3,1:T(8,128)} %copy.85), channel_id=1, source_target_pairs={{2,0},{4,2},{6,4},{8,6},{10,8},{12,10},{14,12},{16,14},{18,16},{20... | collective-permute-start | bytes 110600 | tf_op jit(solution)/shard_map/ppermute | solution.py:26
  66.7 31.6 %collective-permute-start.5 = (f32[8,12,16,6]{2,0,3,1:T(8,128)}, f32[8,12,16,6]{2,0,3,1:T(8,128)}, u32[]{:S(2)}, u32[]{:S(2)}) collective-permute-start(f32[8,12,16,6]{2,0,3,1:T(8,128)} %copy.87), channel_id=1, source_target_pairs={{0,2},{2,4},{4,6},{6,8},{8,10},{10,12},{12,14},{14,16},{16,18},{18... | collective-permute-start | bytes 110600 | tf_op jit(solution)/shard_map/ppermute | solution.py:26
  70.4 34.5 %collective-permute-start.1 = (f32[8,6,16,128]{3,2,1,0:T(8,128)}, f32[8,6,16,128]{3,2,1,0:T(8,128)S(1)}, u32[]{:S(2)}, u32[]{:S(2)}) collective-permute-start(f32[8,6,16,128]{3,2,1,0:T(8,128)} %get-tuple-element.15), channel_id=1, source_target_pairs={{0,16},{2,18},{4,20},{6,22},{8,24},{10,26},{12,28},{14,30},{1,17},... | collective-permute-start | bytes 1179656 | tf_op jit(solution)/shard_map/ppermute | solution.py:26
  95.8 21.5 %collective-permute-start = (f32[8,6,16,128]{3,2,1,0:T(8,128)S(1)}, f32[8,6,16,128]{3,2,1,0:T(8,128)}, u32[]{:S(2)}, u32[]{:S(2)}) collective-permute-start(f32[8,6,16,128]{3,2,1,0:T(8,128)S(1)} %copy-done.3), channel_id=1, source_target_pairs={{16,0},{18,2},{20,4},{22,6},{24,8},{26,10},{28,12},{30,14},{17,1},... | collective-permute-start | bytes 1179656 | tf_op jit(solution)/shard_map/ppermute | solution.py:26
  149.6 22.4 %collective-permute-start.30 = (f32[4,4,8]{0,2,1:T(8,128)S(1)}, f32[4,4,8]{0,2,1:T(8,128)S(1)}, u32[]{:S(2)}, u32[]{:S(2)}) collective-permute-start(f32[4,4,8]{0,2,1:T(8,128)S(1)} %fusion.193), channel_id=1, source_target_pairs={{16,0},{18,2},{20,4},{22,6},{24,8},{26,10},{28,12},{30,14},{17,1},... | collective-permute-start | bytes 1544 | tf_op jit(solution)/shard_map/ppermute | solution.py:26
  151.8 24.6 %collective-permute-start.31 = (f32[4,4,8]{0,2,1:T(8,128)S(1)}, f32[4,4,8]{0,2,1:T(8,128)S(1)}, u32[]{:S(2)}, u32[]{:S(2)}) collective-permute-start(f32[4,4,8]{0,2,1:T(8,128)S(1)} %fusion.193), channel_id=1, source_target_pairs={{0,16},{2,18},{4,20},{6,22},{8,24},{10,26},{12,28},{14,30},{1,17},... | collective-permute-start | bytes 1544 | tf_op jit(solution)/shard_map/ppermute | solution.py:26
  162.3 20.1 %collective-permute-start.32 = (f32[4,4,8]{0,2,1:T(8,128)S(1)}, f32[4,4,8]{0,2,1:T(8,128)S(1)}, u32[]{:S(2)}, u32[]{:S(2)}) collective-permute-start(f32[4,4,8]{0,2,1:T(8,128)S(1)} %fusion.193), channel_id=1, source_target_pairs={{8,0},{10,2},{12,4},{14,6},{16,8},{18,10},{20,12},{22,14},{24,16},... | collective-permute-start | bytes 1544 | tf_op jit(solution)/shard_map/ppermute | solution.py:26
  163.6 20.1 %collective-permute-start.33 = (f32[4,4,8]{0,2,1:T(8,128)S(1)}, f32[4,4,8]{0,2,1:T(8,128)S(1)}, u32[]{:S(2)}, u32[]{:S(2)}) collective-permute-start(f32[4,4,8]{0,2,1:T(8,128)S(1)} %fusion.193), channel_id=1, source_target_pairs={{0,8},{2,10},{4,12},{6,14},{8,16},{10,18},{12,20},{14,22},{16,24},... | collective-permute-start | bytes 1544 | tf_op jit(solution)/shard_map/ppermute | solution.py:26
  170.7 15.0 %collective-permute-start.34 = (f32[4,4,8]{0,2,1:T(8,128)S(1)}, f32[4,4,8]{0,2,1:T(8,128)S(1)}, u32[]{:S(2)}, u32[]{:S(2)}) collective-permute-start(f32[4,4,8]{0,2,1:T(8,128)S(1)} %fusion.193), channel_id=1, source_target_pairs={{2,0},{4,2},{6,4},{8,6},{10,8},{12,10},{14,12},{16,14},{18,16},{20... | collective-permute-start | bytes 1544 | tf_op jit(solution)/shard_map/ppermute | solution.py:26
  172.0 15.0 %collective-permute-start.35 = (f32[4,4,8]{0,2,1:T(8,128)S(1)}, f32[4,4,8]{0,2,1:T(8,128)S(1)}, u32[]{:S(2)}, u32[]{:S(2)}) collective-permute-start(f32[4,4,8]{0,2,1:T(8,128)S(1)} %fusion.193), channel_id=1, source_target_pairs={{0,2},{2,4},{4,6},{6,8},{8,10},{10,12},{12,14},{14,16},{16,18},{18... | collective-permute-start | bytes 1544 | tf_op jit(solution)/shard_map/ppermute | solution.py:26
  176.5 49.5 %collective-permute-start.21 = (f32[8,12,6,128]{3,0,2,1:T(8,128)}, f32[8,12,6,128]{3,0,2,1:T(8,128)}, u32[]{:S(2)}, u32[]{:S(2)}) collective-permute-start(f32[8,12,6,128]{3,0,2,1:T(8,128)} %copy.95), channel_id=1, source_target_pairs={{0,8},{2,10},{4,12},{6,14},{8,16},{10,18},{12,20},{14,22},{16,24},... | collective-permute-start | bytes 884744 | tf_op jit(solution)/shard_map/ppermute | solution.py:26
  182.4 45.4 %collective-permute-start.20 = (f32[8,12,6,128]{3,0,2,1:T(8,128)}, f32[8,12,6,128]{3,0,2,1:T(8,128)}, u32[]{:S(2)}, u32[]{:S(2)}) collective-permute-start(f32[8,12,6,128]{3,0,2,1:T(8,128)} %copy.93), channel_id=1, source_target_pairs={{8,0},{10,2},{12,4},{14,6},{16,8},{18,10},{20,12},{22,14},{24,16},... | collective-permute-start | bytes 884744 | tf_op jit(solution)/shard_map/ppermute | solution.py:26
  183.7 33.3 %collective-permute-start.23 = (f32[8,12,16,6]{2,0,3,1:T(8,128)}, f32[8,12,16,6]{2,0,3,1:T(8,128)}, u32[]{:S(2)}, u32[]{:S(2)}) collective-permute-start(f32[8,12,16,6]{2,0,3,1:T(8,128)} %copy.99), channel_id=1, source_target_pairs={{0,2},{2,4},{4,6},{6,8},{8,10},{10,12},{12,14},{14,16},{16,18},{18... | collective-permute-start | bytes 110600 | tf_op jit(solution)/shard_map/ppermute | solution.py:26
  185.7 33.6 %collective-permute-start.22 = (f32[8,12,16,6]{2,0,3,1:T(8,128)}, f32[8,12,16,6]{2,0,3,1:T(8,128)}, u32[]{:S(2)}, u32[]{:S(2)}) collective-permute-start(f32[8,12,16,6]{2,0,3,1:T(8,128)} %copy.97), channel_id=1, source_target_pairs={{2,0},{4,2},{6,4},{8,6},{10,8},{12,10},{14,12},{16,14},{18,16},{20... | collective-permute-start | bytes 110600 | tf_op jit(solution)/shard_map/ppermute | solution.py:26
  187.0 42.6 %collective-permute-start.19 = (f32[8,6,16,128]{3,2,1,0:T(8,128)}, f32[8,6,16,128]{3,2,1,0:T(8,128)}, u32[]{:S(2)}, u32[]{:S(2)}) collective-permute-start(f32[8,6,16,128]{3,2,1,0:T(8,128)} %get-tuple-element.9), channel_id=1, source_target_pairs={{0,16},{2,18},{4,20},{6,22},{8,24},{10,26},{12,28},{14,30},{1,17},... | collective-permute-start | bytes 1179656 | tf_op jit(solution)/shard_map/ppermute | solution.py:26
  217.1 20.0 %collective-permute-start.18 = (f32[8,6,16,128]{3,2,1,0:T(8,128)}, f32[8,6,16,128]{3,2,1,0:T(8,128)}, u32[]{:S(2)}, u32[]{:S(2)}) collective-permute-start(f32[8,6,16,128]{3,2,1,0:T(8,128)} %get-tuple-element.8), channel_id=1, source_target_pairs={{16,0},{18,2},{20,4},{22,6},{24,8},{26,10},{28,12},{30,14},{17,1},... | collective-permute-start | bytes 1179656 | tf_op jit(solution)/shard_map/ppermute | solution.py:26
  (23 other events, 225.4 us)
Sparse Core Ops, SparseCore 0:
  254.1 24.7 reduce-scatter.1
where the time goes:
time: 291 us; the launch traced here: 288 us
  starting transfers between devices  104 us (36%)
  other arithmetic  79.2 us (27%)
  waiting for transfers between devices  47.9 us (16%)
  local copies, waits for them, and re-layouts  32 us (11%)
  between operations  14 us (5%)
  matrix products  10.9 us (4%)
    ppermute x36, starting transfers between devices, from_behind(): return lax.ppermute(block, axis, route)  104 us
    scatter-add x2, other arithmetic, nonlocal_part(): result = jnp.zeros_like(rows_view).at[:, block_index].add(additions)  36.3 us
    reduce_scatter x1, waiting for transfers between devices, shards(): lax.psum_scatter(jnp.einsum('iabc,ij->jabc', filtered, own_rows, preferre...  24.9 us
    ppermute x36, waiting for transfers between devices, from_behind(): return lax.ppermute(block, axis, route)  23 us
    convert_element_type x1, other arithmetic, shards(): filtered = second_step.astype(jnp.bfloat16)  12.4 us
    div x1, other arithmetic, shards(): first_step = (applied - CENTER * start_values) / HALF_WIDTH  11.6 us
    select_n x6, other arithmetic, extend(): jnp.where(location < extent - 1, from_upper, jnp.zeros_like(from_upper))  9.93 us
    slice x10, local copies, waits for them, and re-layouts, extend(): bottom_layers = lax.slice_in_dim(values, 0, depth_cells, axis=position)  8.34 us
  transfers between devices with their start and end apart: 37, of which 5 were waited for; matrix products, arithmetic and copies ran while one was open for 26% of the time, Pallas kernels for 0%

commit v1 on v0

v1 whole, which is shorter than its diff:
```python
import functools

import jax
import jax.numpy as jnp
from jax import lax
from jax.experimental import pallas as pl
from jax.experimental.pallas import tpu as pltpu
from jax.sharding import PartitionSpec as P

RADIUS = 6
COEFFS = (
    -5369.0 / 1800.0,
    12.0 / 7.0,
    -15.0 / 56.0,
    10.0 / 189.0,
    -1.0 / 112.0,
    2.0 / 1925.0,
    -1.0 / 16632.0,
)
KINETIC = -3.125
CENTER = 36.0
HALF_WIDTH = 34.0
WEIGHT = [KINETIC * c / HALF_WIDTH for c in COEFFS]
DIAGONAL = (3.0 * KINETIC * COEFFS[0] - CENTER) / HALF_WIDTH

F32 = jnp.float32
BF16 = jnp.bfloat16
VMEM = pl.BlockSpec(memory_space=pltpu.VMEM)
SMEM = pl.BlockSpec(memory_space=pltpu.SMEM)
NT = (((1,), (1,)), ((), ()))
TN = (((0,), (0,)), ((), ()))
NN = (((1,), (0,)), ((), ()))


def split2(x):
    high = x.astype(BF16)
    low = (x - high.astype(F32)).astype(BF16)
    return high, low


def iota(shape, dim):
    return lax.broadcasted_iota(jnp.int32, shape, dim)


def weight_at(distance, scale):
    out = jnp.zeros(distance.shape, F32)
    for k in range(1, RADIUS + 1):
        out = jnp.where(distance == k, scale * WEIGHT[k], out)
    return out


class Geometry:
    def __init__(self, orbitals, entries, nproj, atoms, dom_count):
        _, self.no, self.cx, self.cy, self.cz = orbitals
        self.rows = self.cx * self.cy
        self.flat = self.rows * self.no
        self.ent = entries
        self.nproj = nproj
        self.dom_count = dom_count
        self.owned = atoms // dom_count
        self.third = 4
        self.second = min(8, dom_count // 8)
        self.plane = self.second * self.third
        self.first = dom_count // self.plane
        self.strides = (0, self.plane, -self.plane, self.third, -self.third, 1, -1)
        self.table = self.owned * nproj * self.no
        self.slab = self.cy * self.no
        assert self.no == 8

    def faces(self, dom):
        out = []
        for dim, extent, place in (
            (0, self.first, dom // self.plane),
            (1, self.second, dom // self.third % self.second),
        ):
            if extent == 2:
                out.append((dim, 1 - place))
            elif extent > 2:
                out.extend([(dim, 0), (dim, 1)])
        return out

    def face_shapes(self):
        out = []
        for dim, _ in self.faces(0):
            out.append(RADIUS * self.slab if dim == 0 else self.cx * RADIUS * self.no)
        return out


def layer(side, length, j):
    if isinstance(side, int):
        return length - 1 - j if side else j
    return side * (length - 1 - j) + (1 - side) * j


def aligned(start, unit):
    return start if isinstance(start, int) else pl.multiple_of(start, unit)


def pack_faces(g, dom, v_ref, face_refs):
    for (dim, side), out in zip(g.faces(dom), face_refs):
        if dim == 0:
            for j in range(RADIUS):
                at = aligned(layer(side, g.cx, j) * g.slab, g.slab)
                out[j * g.slab : (j + 1) * g.slab, :] = v_ref[pl.ds(at, g.slab), :].astype(BF16)
        else:
            size = RADIUS * g.no
            for x in range(g.cx):
                pieces = []
                for j in range(RADIUS):
                    at = aligned(x * g.slab + layer(side, g.cy, j) * g.no, g.no)
                    pieces.append(v_ref[pl.ds(at, g.no), :])
                out[x * size : (x + 1) * size, :] = jnp.concatenate(pieces, axis=0).astype(BF16)


def pack_ends(g, v_ref, low_ref, high_ref):
    row, col = iota((16, g.cz), 0), iota((16, g.cz), 1)
    place = jnp.where(row < 8, row, g.cz - 1 - (row - 8))
    used = (row % 8) < RADIUS
    pick = jnp.where((place == col) & used, 1.0, 0.0).astype(BF16)
    pick = jnp.concatenate([pick, pick], axis=1)
    for x in range(g.cx):
        rows = slice(x * g.slab, (x + 1) * g.slab)
        both = jnp.concatenate(split2(v_ref[rows, :]), axis=1)
        ends = lax.dot_general(pick, both, NT, preferred_element_type=F32)
        low_ref[:, rows] = ends[:8]
        high_ref[:, rows] = ends[8:]


def fill_lut(g, dom, lut):
    for number, stride in enumerate(g.strides):
        lut[g.plane + dom + stride] = number * g.owned


def column_of(g, lut, atom):
    owner = lax.div(atom, jnp.int32(g.owned))
    return lut[owner + g.plane] + (atom - owner * g.owned)


def inner_tables(g, dom, v_ref, projf, blk, atom, lut, sums, table_ref):
    size = g.nproj * g.no
    for part in sums:
        part[...] = jnp.zeros(part.shape, F32)

    def step(i, _):
        for u, part in enumerate(sums):
            e = i * len(sums) + u
            col = column_of(g, lut, atom[e])
            v = v_ref[pl.ds(pl.multiple_of(blk[e] * g.no, g.no), g.no), :]
            for p in range(g.nproj):
                at = pl.ds(pl.multiple_of(col * size + p * g.no, g.no), g.no)
                coef = jnp.broadcast_to(projf[e, p : p + 1, :], v.shape)
                part[at, :] += v * coef
        return 0

    lax.fori_loop(0, g.ent // len(sums), step, 0)
    total = sums[0][...]
    for part in sums[1:]:
        total = total + part[...]
    both = jnp.concatenate(split2(total), axis=1)
    ones = jnp.ones((8, both.shape[1]), BF16)
    summed = lax.dot_general(ones, both, NT, preferred_element_type=F32)
    table_ref[...] = jnp.zeros(table_ref.shape, F32)
    for number, stride in enumerate(g.strides):
        target = jnp.clip(dom + stride, 0, g.dom_count - 1)
        table_ref[pl.ds(target, 1), :] += summed[0:1, number * g.table : (number + 1) * g.table]


def first_kernel(g, orb, proj, blk, atom, *refs):
    nf = len(g.face_shapes())
    v_ref, projf, table, low, high = refs[:5]
    face_refs = refs[5 : 5 + nf]
    lut = refs[5 + nf]
    sums = refs[6 + nf :]
    dom = lax.axis_index("dom")
    for r in range(g.rows):
        v_ref[r * g.no : (r + 1) * g.no, :] = orb[pl.ds(r, g.no, stride=g.rows), :]
    projf[...] = proj[...].astype(F32)
    pack_faces(g, dom, v_ref, face_refs)
    pack_ends(g, v_ref, low, high)
    fill_lut(g, dom, lut)
    inner_tables(g, dom, v_ref, projf, blk, atom, lut, sums, table)


def inside_kernel(g, scale, subtract, v_ref, pot, *refs):
    prev, out = refs if subtract else (None, refs[0])
    row, col = iota((g.cz, g.cz), 0), iota((g.cz, g.cz), 1)
    high, low = split2(weight_at(jnp.abs(row - col), scale))
    band = jnp.concatenate([high, low], axis=1)
    band = jnp.concatenate([band, band], axis=0)

    def cell(x, y):
        at = (x * g.cy + y) * g.no
        return v_ref[at : at + g.no, :]

    for x in range(g.cx):
        both = jnp.concatenate(split2(v_ref[x * g.slab : (x + 1) * g.slab, :]), axis=1)
        along = lax.dot_general(both, band, NN, preferred_element_type=F32)
        for y in range(g.cy):
            at = (x * g.cy + y) * g.no
            rows = slice(y * g.no, (y + 1) * g.no)
            here = cell(x, y)
            diag = jnp.broadcast_to(pot[x * g.cy + y : x * g.cy + y + 1, :], here.shape)
            total = along[rows, : g.cz] + along[rows, g.cz :]
            total = total + (scale * DIAGONAL + (scale / HALF_WIDTH) * diag) * here
            if subtract:
                total = total - prev[at : at + g.no, :]
            for k in range(1, RADIUS + 1):
                near = []
                for a, b in ((x - k, y), (x + k, y), (x, y - k), (x, y + k)):
                    if 0 <= a < g.cx and 0 <= b < g.cy:
                        near.append(cell(a, b))
                if near:
                    total = total + (scale * WEIGHT[k]) * sum(near[1:], near[0])
            out[at : at + g.no, :] = total


def add_halos(g, dom, scale, acc, low, high, face_refs, out):
    row, col = iota((16, g.cz), 0), iota((16, g.cz), 1)
    inward = jnp.where(row < 8, col, g.cz - 1 - col)
    coef = jnp.where(row % 8 < RADIUS, weight_at(inward + row % 8 + 1, scale), 0.0)
    c_high, c_low = split2(coef)
    coefs = jnp.concatenate([c_high, c_high, c_low, c_low], axis=0)
    for x in range(g.cx):
        rows = slice(x * g.slab, (x + 1) * g.slab)
        h_high, h_low = split2(jnp.concatenate([low[:, rows], high[:, rows]], axis=0))
        halo = jnp.concatenate([h_high, h_low, h_high, h_low], axis=0)
        out[rows, :] = acc[rows, :] + lax.dot_general(halo, coefs, TN, preferred_element_type=F32)
    for (dim, side), face in zip(g.faces(dom), face_refs):
        if dim == 0:
            for y in range(0, g.cy, 2):
                unit = 2 * g.no
                starts = [j * g.slab + y * g.no for j in range(RADIUS)]
                part = [face[at : at + unit, :].astype(F32) for at in starts]
                for i in range(RADIUS):
                    at = aligned(layer(side, g.cx, i) * g.slab + y * g.no, unit)
                    total = out[pl.ds(at, unit), :]
                    for j in range(RADIUS - i):
                        total = total + (scale * WEIGHT[i + j + 1]) * part[j]
                    out[pl.ds(at, unit), :] = total
        else:
            size = RADIUS * g.no
            for x in range(g.cx):
                part = face[x * size : (x + 1) * size, :].astype(F32)
                for i in range(RADIUS):
                    at = aligned(x * g.slab + layer(side, g.cy, i) * g.no, g.no)
                    total = out[pl.ds(at, g.no), :]
                    for j in range(RADIUS - i):
                        total = total + (scale * WEIGHT[i + j + 1]) * part[j * g.no : (j + 1) * g.no]
                    out[pl.ds(at, g.no), :] = total


def add_nonlocal(g, dom, scale, table, energy, projf, blk, atom, lut, spread, out):
    size = g.nproj * g.no
    lanes = g.table
    rows = []
    for stride in g.strides:
        at = jnp.clip(dom + stride, 0, g.dom_count - 1)
        rows.append(table[pl.ds(at, 1), :] * energy[pl.ds(at, 1), :])
    rows.append(jnp.zeros((1, lanes), F32))
    scaled = (scale / HALF_WIDTH) * jnp.concatenate(rows, axis=0)
    high = scaled.astype(BF16)
    rest = scaled - high.astype(F32)
    mid = rest.astype(BF16)
    low = (rest - mid.astype(F32)).astype(BF16)
    parts = jnp.concatenate([high, mid, low], axis=0)
    wide = len(g.strides) * g.cz
    row, col = iota((24, wide), 0), iota((24, wide), 1)
    ones = jnp.where(row % 8 == col // g.cz, 1.0, 0.0).astype(BF16)
    out_all = lax.dot_general(parts, ones, TN, preferred_element_type=F32)
    for number in range(len(g.strides)):
        spread[number * lanes : (number + 1) * lanes, :] = out_all[:, number * g.cz : (number + 1) * g.cz]
    unroll = 4

    def step(i, _):
        additions = []
        for u in range(unroll):
            e = i * unroll + u
            col = column_of(g, lut, atom[e])
            total = None
            for p in range(g.nproj):
                at = pl.ds(pl.multiple_of(col * size + p * g.no, g.no), g.no)
                coef = jnp.broadcast_to(projf[e, p : p + 1, :], (g.no, g.cz))
                term = spread[at, :] * coef
                total = term if total is None else total + term
            additions.append((pl.ds(pl.multiple_of(blk[e] * g.no, g.no), g.no), total))
        for at, total in additions:
            out[at, :] += total
        return 0

    lax.fori_loop(0, g.ent // unroll, step, 0)


def middle_kernel(g, acc, low, high, total, energy, projf, blk, atom, *refs):
    nf = len(g.face_shapes())
    face_in = refs[:nf]
    u_ref, table, low_out, high_out = refs[nf : nf + 4]
    face_out = refs[nf + 4 : 2 * nf + 4]
    lut, spread = refs[2 * nf + 4 : 2 * nf + 6]
    sums = refs[2 * nf + 6 :]
    dom = lax.axis_index("dom")
    fill_lut(g, dom, lut)
    add_halos(g, dom, 1.0, acc, low, high, face_in, u_ref)
    add_nonlocal(g, dom, 1.0, total, energy, projf, blk, atom, lut, spread, u_ref)
    pack_faces(g, dom, u_ref, face_out)
    pack_ends(g, u_ref, low_out, high_out)
    inner_tables(g, dom, u_ref, projf, blk, atom, lut, sums, table)


def last_kernel(g, acc, low, high, total, energy, projf, blk, atom, *refs):
    nf = len(g.face_shapes())
    face_in = refs[:nf]
    filtered, lut, spread, work = refs[nf:]
    dom = lax.axis_index("dom")
    fill_lut(g, dom, lut)
    add_halos(g, dom, 2.0, acc, low, high, face_in, work)
    add_nonlocal(g, dom, 2.0, total, energy, projf, blk, atom, lut, spread, work)
    filtered[...] = work[...].astype(BF16)


def rotate_kernel(g, own, other, panel, out):
    band = lax.axis_index("band")
    group = 16
    span = group * g.no
    norb = panel.shape[0]
    row, col = iota((span, norb), 0), iota((span, norb), 1)
    pick_out = jnp.where(col == band * g.no + row // group, 1.0, 0.0).astype(BF16)
    picked = lax.dot_general(pick_out, panel[...], NT, preferred_element_type=F32).astype(BF16)
    row, col = iota((norb, 2 * span), 0), iota((norb, 2 * span), 1)
    source = jnp.where(col < span, band, 1 - band) * g.no + col % g.no
    pick_in = jnp.where(row == source, 1.0, 0.0).astype(BF16)
    spread = lax.dot_general(picked, pick_in, NN, preferred_element_type=F32)
    row, col = iota((span, 2 * span), 0), iota((span, 2 * span), 1)
    same = row % group == (col % span) // g.no
    weights = jnp.where(same, spread, 0.0).astype(BF16)
    for n in range(g.rows // group):
        rows = slice(n * span, (n + 1) * span)
        both = jnp.concatenate([own[rows, :], other[rows, :]], axis=0)
        result = lax.dot_general(weights, both, NN, preferred_element_type=F32)
        for j in range(g.no):
            at = j * g.rows + n * group
            out[at : at + group, :] = result[j * group : (j + 1) * group, :]


def call(kernel, name, out_shape, scratch, flops, args, specs):
    size = sum(a.size * a.dtype.itemsize for a in args)
    outs = out_shape if isinstance(out_shape, (tuple, list)) else [out_shape]
    size += sum(o.size * o.dtype.itemsize for o in outs)
    return pl.pallas_call(
        kernel,
        name=name,
        out_shape=out_shape,
        in_specs=specs,
        out_specs=jax.tree.map(lambda _: VMEM, out_shape),
        scratch_shapes=scratch,
        compiler_params=pltpu.CompilerParams(vmem_limit_bytes=48 * 1024 * 1024),
        cost_estimate=pl.CostEstimate(flops=flops, bytes_accessed=size, transcendentals=0),
    )(*args)


def exchange(g, faces, low, high):
    n = g.dom_count

    def pairs(stride, extent, step, up):
        out = []
        for i in range(n):
            place = i // stride % extent
            to = place + step
            if 0 <= to < extent:
                out.append((i, i + step * stride))
        return out

    def swap(stride):
        return [(i, i + stride if i // stride % 2 == 0 else i - stride) for i in range(n)]

    got = []
    at = 0
    for extent, stride in ((g.first, g.plane), (g.second, g.third)):
        if extent == 2:
            got.append(lax.ppermute(faces[at], "dom", swap(stride)))
            at += 1
        elif extent > 2:
            down, up = faces[at], faces[at + 1]
            got.append(lax.ppermute(up, "dom", pairs(stride, extent, 1, True)))
            got.append(lax.ppermute(down, "dom", pairs(stride, extent, -1, False)))
            at += 2
    from_low = lax.ppermute(high, "dom", pairs(1, g.third, 1, True))
    from_high = lax.ppermute(low, "dom", pairs(1, g.third, -1, False))
    return got, from_low, from_high


def shards(orbitals, potential, projectors, entry_atom, entry_block, kb_energy, panel):
    g = Geometry(
        orbitals.shape, projectors.shape[0], projectors.shape[1], kb_energy.shape[0], lax.axis_size("dom")
    )
    orb = orbitals.reshape(g.flat, g.cz)
    pot = potential.reshape(g.rows, g.cz)
    field = jax.ShapeDtypeStruct((g.flat, g.cz), F32)
    faces = [jax.ShapeDtypeStruct((n, g.cz), BF16) for n in g.face_shapes()]
    ends = jax.ShapeDtypeStruct((8, g.flat), F32)
    table = jax.ShapeDtypeStruct((g.dom_count, g.table), F32)
    projf = jax.ShapeDtypeStruct(projectors.shape, F32)
    lut = pltpu.SMEM((g.dom_count + 2 * g.plane,), jnp.int32)
    sums = [pltpu.VMEM((len(g.strides) * g.table, g.cz), F32) for _ in range(4)]
    spread = pltpu.VMEM((len(g.strides) * g.table, g.cz), F32)
    nf = len(faces)

    v, proj, part, low, high, *sent = call(
        functools.partial(first_kernel, g),
        "first_faces",
        [field, projf, table, ends, ends, *faces],
        [lut, *sums],
        10_000_000,
        [orb, projectors, entry_block, entry_atom],
        [VMEM, VMEM, SMEM, SMEM],
    )
    got, low, high = exchange(g, sent, low, high)
    total = lax.psum(part, "dom")
    energy = jnp.repeat(kb_energy.reshape(g.dom_count, g.owned * g.nproj), g.no, axis=1)
    acc = call(
        functools.partial(inside_kernel, g, 1.0, False),
        "inside_first",
        field,
        [],
        200_000_000,
        [v, pot],
        [VMEM, VMEM],
    )
    u, part, low, high, *sent = call(
        functools.partial(middle_kernel, g),
        "middle",
        [field, table, ends, ends, *faces],
        [lut, spread, *sums],
        10_000_000,
        [acc, low, high, total, energy, proj, entry_block, entry_atom, *got],
        [VMEM] * 6 + [SMEM] * 2 + [VMEM] * nf,
    )
    got, low, high = exchange(g, sent, low, high)
    total = lax.psum(part, "dom")
    acc = call(
        functools.partial(inside_kernel, g, 2.0, True),
        "inside_second",
        field,
        [],
        200_000_000,
        [u, pot, v],
        [VMEM, VMEM, VMEM],
    )
    filtered = call(
        functools.partial(last_kernel, g),
        "filtered",
        jax.ShapeDtypeStruct((g.flat, g.cz), BF16),
        [lut, spread, pltpu.VMEM((g.flat, g.cz), F32)],
        10_000_000,
        [acc, low, high, total, energy, proj, entry_block, entry_atom, *got],
        [VMEM] * 6 + [SMEM] * 2 + [VMEM] * nf,
    )
    other = lax.ppermute(filtered, "band", [(0, 1), (1, 0)])
    rotated = call(
        functools.partial(rotate_kernel, g),
        "rotate",
        field,
        [],
        200_000_000,
        [filtered, other, panel],
        [VMEM] * 3,
    )
    return rotated.reshape(orbitals.shape)


def solution(mesh):
    in_specs = (
        P("dom", "band", None, None, None),
        P("dom", None, None, None),
        P("dom", None, None),
        P("dom"),
        P("dom"),
        P(),
        P(),
    )
    out_specs = P("dom", "band", None, None, None)
    return jax.shard_map(shards, mesh=mesh, in_specs=in_specs, out_specs=out_specs, check_vma=False)
```

time: 291 us -> 106 us (0.36); the launches traced: 288 us -> 106 us
  starting transfers between devices: 104 us -> 13 us
  other arithmetic: 79.2 us -> 0 us
  blocking collectives: 0 us -> 64.9 us
  waiting for transfers between devices: 47.9 us -> 7.27 us
  local copies, waits for them, and re-layouts: 32 us -> 4.39 us
  Pallas kernels: 0 us -> 16.3 us
  between operations: 14 us -> 0.19 us
  matrix products: 10.9 us -> 0 us
    ppermute x36 -> x9, starting transfers between devices: 104 us -> 13 us  [the longest x4 5.18 us: exchange(): got.append(lax.ppermute(faces[at], 'dom', swap(stride)))]
    psum x0 -> x2, blocking collectives: none -> 64.9 us  [shards(): total = lax.psum(part, 'dom')]
    scatter-add x2 -> x0, other arithmetic: 36.3 us -> none  [nonlocal_part(): result = jnp.zeros_like(rows_view).at[:, block_index].add(additions)]
    reduce_scatter x1 -> x0, waiting for transfers between devices: 24.9 us -> none  [shards(): lax.psum_scatter(jnp.einsum('iabc,ij->jabc', filtered, own_rows, preferre...]
    select_n x13 -> x0, other arithmetic: 16.6 us -> none  [the longest x6 9.93 us: extend(): jnp.where(location < extent - 1, from_upper, jnp.zeros_like(from_upper))]
    pallas_call x0 -> x6, Pallas kernels: none -> 16.3 us  [call(): pl.pallas_call(kernel, name=name, out_shape=out_shape, in_specs=specs, ou...]
    ppermute x36 -> x9, waiting for transfers between devices: 23 us -> 7.27 us  [the longest x1 7.25 us: shards(): other = lax.ppermute(filtered, 'band', [(0, 1), (1, 0)])]
    slice x16 -> x0, local copies, waits for them, and re-layouts: 14.9 us -> none  [the longest x10 8.34 us: extend(): bottom_layers = lax.slice_in_dim(values, 0, depth_cells, axis=position)]
  transfers between devices with their start and end apart: 37 -> 9, of which waited for: 5 -> 1; matrix products, arithmetic and copies ran while one was open for 26% -> 0% of each run, Pallas kernels for 0% -> 2%
where the time goes in v1:
time: 106 us
  blocking collectives  64.9 us (61%)
  Pallas kernels  16.3 us (15%)
  starting transfers between devices  13 us (12%)
  waiting for transfers between devices  7.27 us (7%)
  local copies, waits for them, and re-layouts  4.39 us (4%)
    psum x2, blocking collectives, shards(): total = lax.psum(part, 'dom')  64.9 us
    pallas_call x6, Pallas kernels, call(): pl.pallas_call(kernel, name=name, out_shape=out_shape, in_specs=specs, ou...  16.3 us
    ppermute x1, waiting for transfers between devices, shards(): other = lax.ppermute(filtered, 'band', [(0, 1), (1, 0)])  7.25 us
    ppermute x4, starting transfers between devices, exchange(): got.append(lax.ppermute(faces[at], 'dom', swap(stride)))  5.18 us
    unnamed x17, local copies, waits for them, and re-layouts  4.18 us
    ppermute x2, starting transfers between devices, exchange(): from_low = lax.ppermute(high, 'dom', pairs(1, g.third, 1, True))  3.67 us
    ppermute x2, starting transfers between devices, exchange(): from_high = lax.ppermute(low, 'dom', pairs(1, g.third, -1, False))  2.58 us
  transfers between devices with their start and end apart: 9, of which 1 were waited for; matrix products, arithmetic and copies ran while one was open for 0% of the time, Pallas kernels for 2%

profile of v1, /device:TPU:0, one launch (start us, length us, event | category | flops | bytes accessed | tf_op | source)
XLA Modules:
  0.0 106.0 jit_solution(8045131917900276908)
XLA Ops:
  0.0 0.7 copy-done.3
  0.7 1.1 %copy-done = f32[1,8,12,16,128]{4,3,2,1,0:T(8,128)S(1)} copy-done((f32[1,8,12,16,128]{4,3,2,1,0:T(8,128)S(1)}, f32[1,8,12,16,128]{4,3,2,1,0:T(8,128)}, u32[]{:S(2)}) %copy-start) | copy-done | bytes 786456
  1.8 0.9 copy-done.2
  2.8 0.7 copy-done.4
  3.4 3.2 %first_faces.1 = (f32[1536,128]{1,0:T(8,128)S(1)}, f32[256,4,128]{2,1,0:T(4,128)S(1)}, f32[16,128]{1,0:T(8,128)S(1)}, f32[8,1536]{1,0:T(8,128)S(1)}, f32[8,1536]...) custom-call(f32[1536,128]{1,0:T(8,128)S(1)} %bitcast.5, ...), custom_call_target="tpu_custom_call" | custom-call | flops 10000000 | bytes 2811904 | tf_op jit(solution)/shard_map/first_faces/pallas_call | solution.py:348
  6.7 2.4 %collective-permute-start = (f32[8,1536]{1,0:T(8,128)S(1)}, f32[8,1536]{1,0:T(8,128)S(1)}, u32[]{:S(2)}, u32[]{:S(2)}) collective-permute-start(f32[8,1536]{1,0:T(8,128)S(1)} %get-tuple-element.19), channel_id=1, source_target_pairs={{0,2},{2,4},{4,6},{8,10},{10,12},{12,14},{16,18},{18,20},{20,22},{... | collective-permute-start | bytes 147464 | tf_op jit(solution)/shard_map/ppermute | solution.py:386
  9.1 1.3 %collective-permute-start.1 = (f32[8,1536]{1,0:T(8,128)S(1)}, f32[8,1536]{1,0:T(8,128)S(1)}, u32[]{:S(2)}, u32[]{:S(2)}) collective-permute-start(f32[8,1536]{1,0:T(8,128)S(1)} %get-tuple-element.20), channel_id=1, source_target_pairs={{2,0},{4,2},{6,4},{10,8},{12,10},{14,12},{18,16},{20,18},{22,20},{... | collective-permute-start | bytes 147464 | tf_op jit(solution)/shard_map/ppermute | solution.py:387
  10.4 2.5 %collective-permute-start.3 = (bf16[576,128]{1,0:T(8,128)(2,1)S(1)}, bf16[576,128]{1,0:T(8,128)(2,1)S(1)}, u32[]{:S(2)}, u32[]{:S(2)}) collective-permute-start(bf16[576,128]{1,0:T(8,128)(2,1)S(1)} %get-tuple-element.24), channel_id=1, source_target_pairs={{0,8},{2,10},{4,12},{6,14},{8,0},{10,2},{12,4},{14,6},{16,24},{18,... | collective-permute-start | bytes 442376 | tf_op jit(solution)/shard_map/ppermute | solution.py:379
  12.9 2.6 %collective-permute-start.2 = (bf16[768,128]{1,0:T(8,128)(2,1)S(1)}, bf16[768,128]{1,0:T(8,128)(2,1)S(1)}, u32[]{:S(2)}, u32[]{:S(2)}) collective-permute-start(bf16[768,128]{1,0:T(8,128)(2,1)S(1)} %get-tuple-element.23), channel_id=1, source_target_pairs={{0,16},{2,18},{4,20},{6,22},{8,24},{10,26},{12,28},{14,30},{16,0},... | collective-permute-start | bytes 589832 | tf_op jit(solution)/shard_map/ppermute | solution.py:379
  15.4 0.1 copy.8
  15.5 0.1 reshape.17
  15.6 0.1 copy.9
  15.8 32.8 %psum.14.total = f32[16,128]{1,0:T(8,128)S(1)} all-reduce(f32[16,128]{1,0:T(8,128)S(1)} %get-tuple-element.21), channel_id=1, replica_groups=mesh['dom'=16,'band'=2] {'dom'}, use_global_device_ids=true, to_apply=%region_0.0 | all-reduce | flops 2048 | bytes 16384 | tf_op jit(solution)/shard_map/psum | solution.py:417
  48.5 0.9 inside_first.1.acc
  49.6 0.6 copy-done.5
  50.2 6.1 %middle.1 = (f32[1536,128]{1,0:T(8,128)S(1)}, f32[16,128]{1,0:T(8,128)S(1)}, f32[8,1536]{1,0:T(8,128)S(1)}, f32[8,1536]{1,0:T(8,128)S(1)}, bf16[768,128]{1,0:T(8,128)(2,1)S(1)}, /*index=5*/bf16[576,128]{1,0:T(8,128)(2,1)S(1)}) custom-call(f32[1536,128]{1,0:T(8,128)S(1)} %inside_first.1.acc, f32[8,1536]{1,0:T(8,128)S(1)} %collective-permute-done.low, ...), custom_call_target="tpu_custom_call" | custom-call | flops 10000000 | bytes 3008512 | tf_op jit(solution)/shard_map/middle/pallas_call | solution.py:348
  56.4 1.3 %collective-permute-start.4 = (f32[8,1536]{1,0:T(8,128)S(1)}, f32[8,1536]{1,0:T(8,128)S(1)}, u32[]{:S(2)}, u32[]{:S(2)}) collective-permute-start(f32[8,1536]{1,0:T(8,128)S(1)} %get-tuple-element.26), channel_id=1, source_target_pairs={{0,2},{2,4},{4,6},{8,10},{10,12},{12,14},{16,18},{18,20},{20,22},{... | collective-permute-start | bytes 147464 | tf_op jit(solution)/shard_map/ppermute | solution.py:386
  57.7 1.3 %collective-permute-start.5 = (f32[8,1536]{1,0:T(8,128)S(1)}, f32[8,1536]{1,0:T(8,128)S(1)}, u32[]{:S(2)}, u32[]{:S(2)}) collective-permute-start(f32[8,1536]{1,0:T(8,128)S(1)} %get-tuple-element.27), channel_id=1, source_target_pairs={{2,0},{4,2},{6,4},{10,8},{12,10},{14,12},{18,16},{20,18},{22,20},{... | collective-permute-start | bytes 147464 | tf_op jit(solution)/shard_map/ppermute | solution.py:387
  59.0 32.1 %psum.15.total = f32[16,128]{1,0:T(8,128)S(1)} all-reduce(f32[16,128]{1,0:T(8,128)S(1)} %get-tuple-element.28), channel_id=1, replica_groups=mesh['dom'=16,'band'=2] {'dom'}, use_global_device_ids=true, to_apply=%region_1.0 | all-reduce | flops 2048 | bytes 16384 | tf_op jit(solution)/shard_map/psum | solution.py:438
  91.1 1.0 inside_second.1.acc
  92.1 3.6 %filtered.1.own = bf16[1536,128]{1,0:T(8,128)(2,1)S(1)} custom-call(f32[1536,128]{1,0:T(8,128)S(1)} %inside_second.1.acc, f32[8,1536]{1,0:T(8,128)S(1)} %collective-permute-done.4.low, f32[8,1536]{1,0:T(8,128)S(1)} %collective-permute-done.5.high, f32[16,128]{1,0:T(8,128)S(1)} %psum.15.total, f32[16,128]{1,0:T(8,128)S(1)} %copy.10.energy, ...), custom_call_target="tpu_custom_call" | custom-call | flops 10000000 | bytes 2164736 | tf_op jit(solution)/shard_map/filtered/pallas_call | solution.py:348
  95.7 1.6 %collective-permute-start.8 = (bf16[1536,128]{1,0:T(8,128)(2,1)S(1)}, bf16[1536,128]{1,0:T(8,128)(2,1)S(1)}, u32[]{:S(2)}, u32[]{:S(2)}) collective-permute-start(bf16[1536,128]{1,0:T(8,128)(2,1)S(1)} %filtered.1.own), channel_id=1, source_target_pairs={{0,1},{1,0},{2,3},{3,2},{4,5},{5,4},{6,7},{7,6},{8,9},{9,8},{10,11... | collective-permute-start | bytes 1179656 | tf_op jit(solution)/shard_map/ppermute | solution.py:457
  97.3 7.2 %collective-permute-done.8.other = bf16[1536,128]{1,0:T(8,128)(2,1)S(1)} collective-permute-done((bf16[1536,128]{1,0:T(8,128)(2,1)S(1)}, bf16[1536,128]{1,0:T(8,128)(2,1)S(1)}, u32[]{:S(2)}, u32[]{:S(2)}) %collective-permute-start.8) | collective-permute-done | bytes 393248 | tf_op jit(solution)/shard_map/ppermute | solution.py:457
  104.5 1.5 %rotate.1 = f32[1536,128]{1,0:T(8,128)} custom-call(bf16[1536,128]{1,0:T(8,128)(2,1)S(1)} %filtered.1.own, bf16[1536,128]{1,0:T(8,128)(2,1)S(1)} %collective-permute-done.8.other, bf16[16,16]{1,0:T(8,128)(2,1)S(1)} %copy-done.6), custom_call_target="tpu_custom_call" | custom-call | flops 200000000 | bytes 1573376 | tf_op jit(solution)/shard_map/rotate/pallas_call | solution.py:348
  (23 shorter events, 0.2 us)
Async XLA Ops:
  0.0 0.7 copy-start.3
  0.7 1.1 %copy-start = (f32[1,8,12,16,128]{4,3,2,1,0:T(8,128)S(1)}, f32[1,8,12,16,128]{4,3,2,1,0:T(8,128)}, u32[]{:S(2)}) copy-start(f32[1,8,12,16,128]{4,3,2,1,0:T(8,128)} %param.7) | copy-start | bytes 2359300
  1.8 0.9 copy-start.2
  2.8 0.7 copy-start.4
  6.7 42.8 %collective-permute-start = (f32[8,1536]{1,0:T(8,128)S(1)}, f32[8,1536]{1,0:T(8,128)S(1)}, u32[]{:S(2)}, u32[]{:S(2)}) collective-permute-start(f32[8,1536]{1,0:T(8,128)S(1)} %get-tuple-element.19), channel_id=1, source_target_pairs={{0,2},{2,4},{4,6},{8,10},{10,12},{12,14},{16,18},{18,20},{20,22},{... | collective-permute-start | bytes 147464 | tf_op jit(solution)/shard_map/ppermute | solution.py:386
  9.1 6.4 %copy-start.7 = (f32[64,4]{0,1:T(4,128)S(1)}, f32[64,4]{0,1:T(4,128)}, u32[]{:S(2)}) copy-start(f32[64,4]{0,1:T(4,128)} %param.12) | copy-start | bytes 3076
  9.1 40.4 %collective-permute-start.1 = (f32[8,1536]{1,0:T(8,128)S(1)}, f32[8,1536]{1,0:T(8,128)S(1)}, u32[]{:S(2)}, u32[]{:S(2)}) collective-permute-start(f32[8,1536]{1,0:T(8,128)S(1)} %get-tuple-element.20), channel_id=1, source_target_pairs={{2,0},{4,2},{6,4},{10,8},{12,10},{14,12},{18,16},{20,18},{22,20},{... | collective-permute-start | bytes 147464 | tf_op jit(solution)/shard_map/ppermute | solution.py:387
  10.4 39.1 %collective-permute-start.3 = (bf16[576,128]{1,0:T(8,128)(2,1)S(1)}, bf16[576,128]{1,0:T(8,128)(2,1)S(1)}, u32[]{:S(2)}, u32[]{:S(2)}) collective-permute-start(bf16[576,128]{1,0:T(8,128)(2,1)S(1)} %get-tuple-element.24), channel_id=1, source_target_pairs={{0,8},{2,10},{4,12},{6,14},{8,0},{10,2},{12,4},{14,6},{16,24},{18,... | collective-permute-start | bytes 442376 | tf_op jit(solution)/shard_map/ppermute | solution.py:379
  12.9 36.7 %collective-permute-start.2 = (bf16[768,128]{1,0:T(8,128)(2,1)S(1)}, bf16[768,128]{1,0:T(8,128)(2,1)S(1)}, u32[]{:S(2)}, u32[]{:S(2)}) collective-permute-start(bf16[768,128]{1,0:T(8,128)(2,1)S(1)} %get-tuple-element.23), channel_id=1, source_target_pairs={{0,16},{2,18},{4,20},{6,22},{8,24},{10,26},{12,28},{14,30},{16,0},... | collective-permute-start | bytes 589832 | tf_op jit(solution)/shard_map/ppermute | solution.py:379
  15.6 32.9 %copy-start.1 = (f32[1,12,16,128]{3,2,1,0:T(8,128)S(1)}, f32[1,12,16,128]{3,2,1,0:T(8,128)}, u32[]{:S(2)}) copy-start(f32[1,12,16,128]{3,2,1,0:T(8,128)} %param.8) | copy-start | bytes 294916
  49.5 0.7 copy-start.5
  56.3 35.9 %collective-permute-start.6 = (bf16[768,128]{1,0:T(8,128)(2,1)S(1)}, bf16[768,128]{1,0:T(8,128)(2,1)S(1)}, u32[]{:S(2)}, u32[]{:S(2)}) collective-permute-start(bf16[768,128]{1,0:T(8,128)(2,1)S(1)} %get-tuple-element.29), channel_id=1, source_target_pairs={{0,16},{2,18},{4,20},{6,22},{8,24},{10,26},{12,28},{14,30},{16,0},... | collective-permute-start | bytes 589832 | tf_op jit(solution)/shard_map/ppermute | solution.py:379
  56.3 35.8 %collective-permute-start.7 = (bf16[576,128]{1,0:T(8,128)(2,1)S(1)}, bf16[576,128]{1,0:T(8,128)(2,1)S(1)}, u32[]{:S(2)}, u32[]{:S(2)}) collective-permute-start(bf16[576,128]{1,0:T(8,128)(2,1)S(1)} %get-tuple-element.30), channel_id=1, source_target_pairs={{0,8},{2,10},{4,12},{6,14},{8,0},{10,2},{12,4},{14,6},{16,24},{18,... | collective-permute-start | bytes 442376 | tf_op jit(solution)/shard_map/ppermute | solution.py:379
  56.4 35.7 %collective-permute-start.4 = (f32[8,1536]{1,0:T(8,128)S(1)}, f32[8,1536]{1,0:T(8,128)S(1)}, u32[]{:S(2)}, u32[]{:S(2)}) collective-permute-start(f32[8,1536]{1,0:T(8,128)S(1)} %get-tuple-element.26), channel_id=1, source_target_pairs={{0,2},{2,4},{4,6},{8,10},{10,12},{12,14},{16,18},{18,20},{20,22},{... | collective-permute-start | bytes 147464 | tf_op jit(solution)/shard_map/ppermute | solution.py:386
  57.7 34.4 %collective-permute-start.5 = (f32[8,1536]{1,0:T(8,128)S(1)}, f32[8,1536]{1,0:T(8,128)S(1)}, u32[]{:S(2)}, u32[]{:S(2)}) collective-permute-start(f32[8,1536]{1,0:T(8,128)S(1)} %get-tuple-element.27), channel_id=1, source_target_pairs={{2,0},{4,2},{6,4},{10,8},{12,10},{14,12},{18,16},{20,18},{22,20},{... | collective-permute-start | bytes 147464 | tf_op jit(solution)/shard_map/ppermute | solution.py:387
  92.1 12.5 %copy-start.6 = (bf16[16,16]{1,0:T(8,128)(2,1)S(1)}, bf16[16,16]{1,0:T(8,128)(2,1)}, u32[]{:S(2)}) copy-start(bf16[16,16]{1,0:T(8,128)(2,1)} %panel.1) | copy-start | bytes 1540
  95.7 8.8 %collective-permute-start.8 = (bf16[1536,128]{1,0:T(8,128)(2,1)S(1)}, bf16[1536,128]{1,0:T(8,128)(2,1)S(1)}, u32[]{:S(2)}, u32[]{:S(2)}) collective-permute-start(bf16[1536,128]{1,0:T(8,128)(2,1)S(1)} %filtered.1.own), channel_id=1, source_target_pairs={{0,1},{1,0},{2,3},{3,2},{4,5},{5,4},{6,7},{7,6},{8,9},{9,8},{10,11... | collective-permute-start | bytes 1179656 | tf_op jit(solution)/shard_map/ppermute | solution.py:457

commit v2 on v1

--- a/solution.py
+++ b/solution.py
@@ -26,7 +26,7 @@
 F32 = jnp.float32
 BF16 = jnp.bfloat16
 VMEM = pl.BlockSpec(memory_space=pltpu.VMEM)
-SMEM = pl.BlockSpec(memory_space=pltpu.SMEM)
+HBM = pl.BlockSpec(memory_space=pltpu.HBM)
 NT = (((1,), (1,)), ((), ()))
 TN = (((0,), (0,)), ((), ()))
 NN = (((1,), (0,)), ((), ()))
@@ -67,23 +67,20 @@
         self.slab = self.cy * self.no
         assert self.no == 8
 
-    def faces(self, dom):
-        out = []
-        for dim, extent, place in (
-            (0, self.first, dom // self.plane),
-            (1, self.second, dom // self.third % self.second),
-        ):
-            if extent == 2:
-                out.append((dim, 1 - place))
-            elif extent > 2:
-                out.extend([(dim, 0), (dim, 1)])
-        return out
-
-    def face_shapes(self):
-        out = []
-        for dim, _ in self.faces(0):
-            out.append(RADIUS * self.slab if dim == 0 else self.cx * RADIUS * self.no)
-        return out
+    def faces(self, dom, dim):
+        if dim == 0:
+            extent, place = self.first, dom // self.plane
+        else:
+            extent, place = self.second, dom // self.third % self.second
+        if extent == 2:
+            return [(1 - place, None)]
+        if extent > 2:
+            return [(0, place > 0), (1, place < extent - 1)]
+        return []
+
+    def face_rows(self, dim):
+        rows = RADIUS * self.slab if dim == 0 else self.cx * RADIUS * self.no
+        return [rows] * len(self.faces(0, dim))
 
 
 def layer(side, length, j):
@@ -96,20 +93,19 @@
     return start if isinstance(start, int) else pl.multiple_of(start, unit)
 
 
-def pack_faces(g, dom, v_ref, face_refs):
-    for (dim, side), out in zip(g.faces(dom), face_refs):
-        if dim == 0:
+def pack_faces(g, dom, v_ref, x_refs, y_refs):
+    for (side, _), out in zip(g.faces(dom, 0), x_refs):
+        for j in range(RADIUS):
+            at = aligned(layer(side, g.cx, j) * g.slab, g.slab)
+            out[j * g.slab : (j + 1) * g.slab, :] = v_ref[pl.ds(at, g.slab), :].astype(BF16)
+    size = RADIUS * g.no
+    for (side, _), out in zip(g.faces(dom, 1), y_refs):
+        for x in range(g.cx):
+            pieces = []
             for j in range(RADIUS):
-                at = aligned(layer(side, g.cx, j) * g.slab, g.slab)
-                out[j * g.slab : (j + 1) * g.slab, :] = v_ref[pl.ds(at, g.slab), :].astype(BF16)
-        else:
-            size = RADIUS * g.no
-            for x in range(g.cx):
-                pieces = []
-                for j in range(RADIUS):
-                    at = aligned(x * g.slab + layer(side, g.cy, j) * g.no, g.no)
-                    pieces.append(v_ref[pl.ds(at, g.no), :])
-                out[x * size : (x + 1) * size, :] = jnp.concatenate(pieces, axis=0).astype(BF16)
+                at = aligned(x * g.slab + layer(side, g.cy, j) * g.no, g.no)
+                pieces.append(v_ref[pl.ds(at, g.no), :])
+            out[x * size : (x + 1) * size, :] = jnp.concatenate(pieces, axis=0).astype(BF16)
 
 
 def pack_ends(g, v_ref, low_ref, high_ref):
@@ -136,10 +132,8 @@
     return lut[owner + g.plane] + (atom - owner * g.owned)
 
 
-def inner_tables(g, dom, v_ref, projf, blk, atom, lut, sums, table_ref):
+def inner_tables(g, v_ref, projf, blk, atom, lut, sums, table_ref):
     size = g.nproj * g.no
-    for part in sums:
-        part[...] = jnp.zeros(part.shape, F32)
 
     def step(i, _):
         for u, part in enumerate(sums):
@@ -160,25 +154,41 @@
     ones = jnp.ones((8, both.shape[1]), BF16)
     summed = lax.dot_general(ones, both, NT, preferred_element_type=F32)
     table_ref[...] = jnp.zeros(table_ref.shape, F32)
-    for number, stride in enumerate(g.strides):
-        target = jnp.clip(dom + stride, 0, g.dom_count - 1)
-        table_ref[pl.ds(target, 1), :] += summed[0:1, number * g.table : (number + 1) * g.table]
-
-
-def first_kernel(g, orb, proj, blk, atom, *refs):
-    nf = len(g.face_shapes())
+    for number in range(len(g.strides)):
+        table_ref[number : number + 1, :] = summed[0:1, number * g.table : (number + 1) * g.table]
+
+
+def clear(sums):
+    for part in sums:
+        part[...] = jnp.zeros(part.shape, F32)
+
+
+def first_kernel(g, orb_hbm, proj_hbm, blk_hbm, atom_hbm, *refs):
+    nx, ny = len(g.face_rows(0)), len(g.face_rows(1))
     v_ref, projf, table, low, high = refs[:5]
-    face_refs = refs[5 : 5 + nf]
-    lut = refs[5 + nf]
-    sums = refs[6 + nf :]
+    x_refs = refs[5 : 5 + nx]
+    y_refs = refs[5 + nx : 5 + nx + ny]
+    orb, proj, blk, atom, lut, sem = refs[5 + nx + ny : 11 + nx + ny]
+    sums = refs[11 + nx + ny :]
+    copies = []
+    for number, (src, dst) in enumerate(
+        ((orb_hbm, orb), (proj_hbm, proj), (blk_hbm, blk), (atom_hbm, atom))
+    ):
+        copies.append(pltpu.make_async_copy(src, dst, sem.at[number]))
+        copies[-1].start()
     dom = lax.axis_index("dom")
+    fill_lut(g, dom, lut)
+    clear(sums)
+    copies[0].wait()
     for r in range(g.rows):
         v_ref[r * g.no : (r + 1) * g.no, :] = orb[pl.ds(r, g.no, stride=g.rows), :]
+    pack_faces(g, dom, v_ref, x_refs, y_refs)
+    pack_ends(g, v_ref, low, high)
+    copies[1].wait()
     projf[...] = proj[...].astype(F32)
-    pack_faces(g, dom, v_ref, face_refs)
-    pack_ends(g, v_ref, low, high)
-    fill_lut(g, dom, lut)
-    inner_tables(g, dom, v_ref, projf, blk, atom, lut, sums, table)
+    copies[2].wait()
+    copies[3].wait()
+    inner_tables(g, v_ref, projf, blk, atom, lut, sums, table)
 
 
 def inside_kernel(g, scale, subtract, v_ref, pot, *refs):
@@ -214,10 +224,16 @@
             out[at : at + g.no, :] = total
 
 
-def add_halos(g, dom, scale, acc, low, high, face_refs, out):
+def flag(present):
+    return 1.0 if present is None else jnp.where(present, 1.0, 0.0)
+
+
+def add_ends(g, dom, scale, acc, low, high, out):
+    place = dom % g.third
     row, col = iota((16, g.cz), 0), iota((16, g.cz), 1)
     inward = jnp.where(row < 8, col, g.cz - 1 - col)
-    coef = jnp.where(row % 8 < RADIUS, weight_at(inward + row % 8 + 1, scale), 0.0)
+    present = jnp.where(row < 8, place, g.third - 1 - place) > 0
+    coef = jnp.where((row % 8 < RADIUS) & present, weight_at(inward + row % 8 + 1, scale), 0.0)
     c_high, c_low = split2(coef)
     coefs = jnp.concatenate([c_high, c_high, c_low, c_low], axis=0)
     for x in range(g.cx):
@@ -225,37 +241,52 @@
         h_high, h_low = split2(jnp.concatenate([low[:, rows], high[:, rows]], axis=0))
         halo = jnp.concatenate([h_high, h_low, h_high, h_low], axis=0)
         out[rows, :] = acc[rows, :] + lax.dot_general(halo, coefs, TN, preferred_element_type=F32)
-    for (dim, side), face in zip(g.faces(dom), face_refs):
-        if dim == 0:
-            for y in range(0, g.cy, 2):
-                unit = 2 * g.no
-                starts = [j * g.slab + y * g.no for j in range(RADIUS)]
-                part = [face[at : at + unit, :].astype(F32) for at in starts]
-                for i in range(RADIUS):
-                    at = aligned(layer(side, g.cx, i) * g.slab + y * g.no, unit)
-                    total = out[pl.ds(at, unit), :]
-                    for j in range(RADIUS - i):
-                        total = total + (scale * WEIGHT[i + j + 1]) * part[j]
-                    out[pl.ds(at, unit), :] = total
-        else:
-            size = RADIUS * g.no
-            for x in range(g.cx):
-                part = face[x * size : (x + 1) * size, :].astype(F32)
-                for i in range(RADIUS):
-                    at = aligned(x * g.slab + layer(side, g.cy, i) * g.no, g.no)
-                    total = out[pl.ds(at, g.no), :]
-                    for j in range(RADIUS - i):
-                        total = total + (scale * WEIGHT[i + j + 1]) * part[j * g.no : (j + 1) * g.no]
-                    out[pl.ds(at, g.no), :] = total
-
-
-def add_nonlocal(g, dom, scale, table, energy, projf, blk, atom, lut, spread, out):
+
+
+def add_x_faces(g, dom, scale, face_refs, out):
+    unit = 2 * g.no
+    for (side, present), face in zip(g.faces(dom, 0), face_refs):
+        for y in range(0, g.cy, 2):
+            starts = [j * g.slab + y * g.no for j in range(RADIUS)]
+            part = [flag(present) * face[at : at + unit, :].astype(F32) for at in starts]
+            for i in range(RADIUS):
+                at = aligned(layer(side, g.cx, i) * g.slab + y * g.no, unit)
+                total = out[pl.ds(at, unit), :]
+                for j in range(RADIUS - i):
+                    total = total + (scale * WEIGHT[i + j + 1]) * part[j]
+                out[pl.ds(at, unit), :] = total
+
+
+def add_y_faces(g, dom, scale, face_refs, out):
+    size = RADIUS * g.no
+    for (side, present), face in zip(g.faces(dom, 1), face_refs):
+        for x in range(g.cx):
+            part = flag(present) * face[x * size : (x + 1) * size, :].astype(F32)
+            for i in range(RADIUS):
+                at = aligned(x * g.slab + layer(side, g.cy, i) * g.no, g.no)
+                total = out[pl.ds(at, g.no), :]
+                for j in range(RADIUS - i):
+                    total = total + (scale * WEIGHT[i + j + 1]) * part[j * g.no : (j + 1) * g.no]
+                out[pl.ds(at, g.no), :] = total
+
+
+def scaled_rows(g, dom, tables, energy):
+    rows = []
+    for stride in g.strides:
+        owner = jnp.clip(dom + stride, 0, g.dom_count - 1)
+        total = None
+        for number, back in enumerate(g.strides):
+            source = owner - back
+            inside = (source >= 0) & (source < g.dom_count)
+            row = tables[pl.ds(jnp.where(inside, source * 8 + number, 7), 1), :]
+            total = row if total is None else total + row
+        rows.append(total * energy[pl.ds(owner, 1), :])
+    return rows
+
+
+def add_nonlocal(g, scale, rows, projf, blk, atom, lut, spread, out):
     size = g.nproj * g.no
     lanes = g.table
-    rows = []
-    for stride in g.strides:
-        at = jnp.clip(dom + stride, 0, g.dom_count - 1)
-        rows.append(table[pl.ds(at, 1), :] * energy[pl.ds(at, 1), :])
     rows.append(jnp.zeros((1, lanes), F32))
     scaled = (scale / HALF_WIDTH) * jnp.concatenate(rows, axis=0)
     high = scaled.astype(BF16)
@@ -290,30 +321,58 @@
     lax.fori_loop(0, g.ent // unroll, step, 0)
 
 
-def middle_kernel(g, acc, low, high, total, energy, projf, blk, atom, *refs):
-    nf = len(g.face_shapes())
-    face_in = refs[:nf]
-    u_ref, table, low_out, high_out = refs[nf : nf + 4]
-    face_out = refs[nf + 4 : 2 * nf + 4]
-    lut, spread = refs[2 * nf + 4 : 2 * nf + 6]
-    sums = refs[2 * nf + 6 :]
+def sides_kernel(g, scale, acc, low, high, tables, energy, projf, blk_hbm, atom_hbm, *refs):
+    ny = len(g.face_rows(1))
+    y_refs = refs[:ny]
+    out, blk, atom, lut, spread, sem = refs[ny:]
+    copies = [
+        pltpu.make_async_copy(blk_hbm, blk, sem.at[0]),
+        pltpu.make_async_copy(atom_hbm, atom, sem.at[1]),
+    ]
+    for copy in copies:
+        copy.start()
     dom = lax.axis_index("dom")
     fill_lut(g, dom, lut)
-    add_halos(g, dom, 1.0, acc, low, high, face_in, u_ref)
-    add_nonlocal(g, dom, 1.0, total, energy, projf, blk, atom, lut, spread, u_ref)
-    pack_faces(g, dom, u_ref, face_out)
-    pack_ends(g, u_ref, low_out, high_out)
-    inner_tables(g, dom, u_ref, projf, blk, atom, lut, sums, table)
-
-
-def last_kernel(g, acc, low, high, total, energy, projf, blk, atom, *refs):
-    nf = len(g.face_shapes())
-    face_in = refs[:nf]
-    filtered, lut, spread, work = refs[nf:]
+    add_ends(g, dom, scale, acc, low, high, out)
+    add_y_faces(g, dom, scale, y_refs, out)
+    rows = scaled_rows(g, dom, tables, energy)
+    for copy in copies:
+        copy.wait()
+    add_nonlocal(g, scale, rows, projf, blk, atom, lut, spread, out)
+
+
+def middle_kernel(g, acc, projf, blk_hbm, atom_hbm, *refs):
+    nx, ny = len(g.face_rows(0)), len(g.face_rows(1))
+    x_in = refs[:nx]
+    u_ref, table, low_out, high_out = refs[nx : nx + 4]
+    x_out = refs[nx + 4 : 2 * nx + 4]
+    y_out = refs[2 * nx + 4 : 2 * nx + 4 + ny]
+    blk, atom, lut, sem = refs[2 * nx + 4 + ny : 2 * nx + 8 + ny]
+    sums = refs[2 * nx + 8 + ny :]
+    copies = [
+        pltpu.make_async_copy(blk_hbm, blk, sem.at[0]),
+        pltpu.make_async_copy(atom_hbm, atom, sem.at[1]),
+    ]
+    for copy in copies:
+        copy.start()
     dom = lax.axis_index("dom")
     fill_lut(g, dom, lut)
-    add_halos(g, dom, 2.0, acc, low, high, face_in, work)
-    add_nonlocal(g, dom, 2.0, total, energy, projf, blk, atom, lut, spread, work)
+    clear(sums)
+    u_ref[...] = acc[...]
+    add_x_faces(g, dom, 1.0, x_in, u_ref)
+    pack_faces(g, dom, u_ref, x_out, y_out)
+    pack_ends(g, u_ref, low_out, high_out)
+    for copy in copies:
+        copy.wait()
+    inner_tables(g, u_ref, projf, blk, atom, lut, sums, table)
+
+
+def last_kernel(g, acc, *refs):
+    x_in = refs[: len(g.face_rows(0))]
+    filtered, work = refs[len(g.face_rows(0)) :]
+    dom = lax.axis_index("dom")
+    work[...] = acc[...]
+    add_x_faces(g, dom, 2.0, x_in, work)
     filtered[...] = work[...].astype(BF16)
 
 
@@ -357,35 +416,20 @@
     )(*args)
 
 
-def exchange(g, faces, low, high):
-    n = g.dom_count
-
-    def pairs(stride, extent, step, up):
-        out = []
-        for i in range(n):
-            place = i // stride % extent
-            to = place + step
-            if 0 <= to < extent:
-                out.append((i, i + step * stride))
-        return out
-
-    def swap(stride):
-        return [(i, i + stride if i // stride % 2 == 0 else i - stride) for i in range(n)]
-
-    got = []
-    at = 0
-    for extent, stride in ((g.first, g.plane), (g.second, g.third)):
-        if extent == 2:
-            got.append(lax.ppermute(faces[at], "dom", swap(stride)))
-            at += 1
-        elif extent > 2:
-            down, up = faces[at], faces[at + 1]
-            got.append(lax.ppermute(up, "dom", pairs(stride, extent, 1, True)))
-            got.append(lax.ppermute(down, "dom", pairs(stride, extent, -1, False)))
-            at += 2
-    from_low = lax.ppermute(high, "dom", pairs(1, g.third, 1, True))
-    from_high = lax.ppermute(low, "dom", pairs(1, g.third, -1, False))
-    return got, from_low, from_high
+def shift(g, array, stride, extent, step):
+    pairs = []
+    for i in range(g.dom_count):
+        place = i // stride % extent
+        pairs.append((i, i + ((place + step) % extent - place) * stride))
+    return lax.ppermute(array, "dom", pairs)
+
+
+def swap_faces(g, faces, stride, extent):
+    if extent == 2:
+        return [shift(g, faces[0], stride, extent, 1)]
+    if extent > 2:
+        return [shift(g, faces[1], stride, extent, 1), shift(g, faces[0], stride, extent, -1)]
+    return []
 
 
 def shards(orbitals, potential, projectors, entry_atom, entry_block, kb_energy, panel):
@@ -395,26 +439,52 @@
     orb = orbitals.reshape(g.flat, g.cz)
     pot = potential.reshape(g.rows, g.cz)
     field = jax.ShapeDtypeStruct((g.flat, g.cz), F32)
-    faces = [jax.ShapeDtypeStruct((n, g.cz), BF16) for n in g.face_shapes()]
+    x_faces = [jax.ShapeDtypeStruct((n, g.cz), BF16) for n in g.face_rows(0)]
+    y_faces = [jax.ShapeDtypeStruct((n, g.cz), BF16) for n in g.face_rows(1)]
+    nx, ny = len(x_faces), len(y_faces)
     ends = jax.ShapeDtypeStruct((8, g.flat), F32)
-    table = jax.ShapeDtypeStruct((g.dom_count, g.table), F32)
+    table = jax.ShapeDtypeStruct((8, g.table), F32)
     projf = jax.ShapeDtypeStruct(projectors.shape, F32)
     lut = pltpu.SMEM((g.dom_count + 2 * g.plane,), jnp.int32)
+    entries = [pltpu.SMEM((g.ent,), jnp.int32)] * 2
     sums = [pltpu.VMEM((len(g.strides) * g.table, g.cz), F32) for _ in range(4)]
     spread = pltpu.VMEM((len(g.strides) * g.table, g.cz), F32)
-    nf = len(faces)
+
+    def exchange(sent, low, high, part):
+        tables = lax.all_gather(part, "dom", tiled=True)
+        low, high = shift(g, high, 1, g.third, 1), shift(g, low, 1, g.third, -1)
+        from_y = swap_faces(g, sent[nx:], g.third, g.second)
+        from_x = swap_faces(g, sent[:nx], g.plane, g.first)
+        return tables, low, high, from_x, from_y
+
+    def sides(scale, name, acc, low, high, tables, from_y):
+        return call(
+            functools.partial(sides_kernel, g, scale),
+            name,
+            field,
+            [*entries, lut, spread, pltpu.SemaphoreType.DMA((2,))],
+            10_000_000,
+            [acc, low, high, tables, energy, proj, entry_block, entry_atom, *from_y],
+            [VMEM] * 6 + [HBM] * 2 + [VMEM] * ny,
+        )
 
     v, proj, part, low, high, *sent = call(
         functools.partial(first_kernel, g),
         "first_faces",
-        [field, projf, table, ends, ends, *faces],
-        [lut, *sums],
+        [field, projf, table, ends, ends, *x_faces, *y_faces],
+        [
+            pltpu.VMEM(orb.shape, F32),
+            pltpu.VMEM(projectors.shape, BF16),
+            *entries,
+            lut,
+            pltpu.SemaphoreType.DMA((4,)),
+            *sums,
+        ],
         10_000_000,
         [orb, projectors, entry_block, entry_atom],
-        [VMEM, VMEM, SMEM, SMEM],
-    )
-    got, low, high = exchange(g, sent, low, high)
-    total = lax.psum(part, "dom")
+        [HBM] * 4,
+    )
+    tables, low, high, from_x, from_y = exchange(sent, low, high, part)
     energy = jnp.repeat(kb_energy.reshape(g.dom_count, g.owned * g.nproj), g.no, axis=1)
     acc = call(
         functools.partial(inside_kernel, g, 1.0, False),
@@ -425,17 +495,17 @@
         [v, pot],
         [VMEM, VMEM],
     )
+    acc = sides(1.0, "sides_first", acc, low, high, tables, from_y)
     u, part, low, high, *sent = call(
         functools.partial(middle_kernel, g),
         "middle",
-        [field, table, ends, ends, *faces],
-        [lut, spread, *sums],
+        [field, table, ends, ends, *x_faces, *y_faces],
+        [*entries, lut, pltpu.SemaphoreType.DMA((2,)), *sums],
         10_000_000,
-        [acc, low, high, total, energy, proj, entry_block, entry_atom, *got],
-        [VMEM] * 6 + [SMEM] * 2 + [VMEM] * nf,
-    )
-    got, low, high = exchange(g, sent, low, high)
-    total = lax.psum(part, "dom")
+        [acc, proj, entry_block, entry_atom, *from_x],
+        [VMEM] * 2 + [HBM] * 2 + [VMEM] * nx,
+    )
+    tables, low, high, from_x, from_y = exchange(sent, low, high, part)
     acc = call(
         functools.partial(inside_kernel, g, 2.0, True),
         "inside_second",
@@ -445,14 +515,15 @@
         [u, pot, v],
         [VMEM, VMEM, VMEM],
     )
+    acc = sides(2.0, "sides_second", acc, low, high, tables, from_y)
     filtered = call(
         functools.partial(last_kernel, g),
         "filtered",
         jax.ShapeDtypeStruct((g.flat, g.cz), BF16),
-        [lut, spread, pltpu.VMEM((g.flat, g.cz), F32)],
+        [pltpu.VMEM((g.flat, g.cz), F32)],
         10_000_000,
-        [acc, low, high, total, energy, proj, entry_block, entry_atom, *got],
-        [VMEM] * 6 + [SMEM] * 2 + [VMEM] * nf,
+        [acc, *from_x],
+        [VMEM] * (1 + nx),
     )
     other = lax.ppermute(filtered, "band", [(0, 1), (1, 0)])
     rotated = call(

time: 106 us -> 82.6 us (0.78)
  blocking collectives: 64.9 us -> 40.1 us
  waiting for transfers between devices: 7.27 us -> 9.9 us
  starting transfers between devices: 13 us -> 11.1 us
    psum x2 -> x0, blocking collectives: 64.9 us -> none  [shards(): total = lax.psum(part, 'dom')]
    all_gather x0 -> x2, blocking collectives: none -> 40.1 us  [exchange(): tables = lax.all_gather(part, 'dom', tiled=True)]
    ppermute x1, waiting for transfers between devices: 7.25 us -> 9.88 us  [shards(): other = lax.ppermute(filtered, 'band', [(0, 1), (1, 0)])]
    ppermute x8, starting transfers between devices: 11.4 us -> 9.55 us  [shift(): return lax.ppermute(array, 'dom', pairs)]
    pallas_call x6 -> x8, Pallas kernels: 16.3 us -> 15.9 us  [call(): pl.pallas_call(kernel, name=name, out_shape=out_shape, in_specs=specs, ou...]
  transfers between devices with their start and end apart: 9 -> 9, of which waited for: 1 -> 1; matrix products, arithmetic and copies ran while one was open for 0% -> 0% of each run, Pallas kernels for 2% -> 10%
where the time goes in v2:
time: 82.6 us; the launch traced here: 82.3 us
  blocking collectives  40.1 us (49%)
  Pallas kernels  15.9 us (19%)
  starting transfers between devices  11.1 us (13%)
  waiting for transfers between devices  9.9 us (12%)
  local copies, waits for them, and re-layouts  5.1 us (6%)
    all_gather x2, blocking collectives, exchange(): tables = lax.all_gather(part, 'dom', tiled=True)  40.1 us
    pallas_call x8, Pallas kernels, call(): pl.pallas_call(kernel, name=name, out_shape=out_shape, in_specs=specs, ou...  15.9 us
    ppermute x1, waiting for transfers between devices, shards(): other = lax.ppermute(filtered, 'band', [(0, 1), (1, 0)])  9.88 us
    ppermute x8, starting transfers between devices, shift(): return lax.ppermute(array, 'dom', pairs)  9.55 us
    unnamed x17, local copies, waits for them, and re-layouts  4.9 us
  transfers between devices with their start and end apart: 9, of which 1 were waited for; matrix products, arithmetic and copies ran while one was open for 0% of the time, Pallas kernels for 10%

profile of v2, /device:TPU:0, one launch (start us, length us, event | category | flops | bytes accessed | tf_op | source)
XLA Modules:
  0.0 82.3 jit_solution(12360066750160129309)
XLA Ops:
  0.0 0.7 copy-done.3
  0.7 1.1 %copy-done = f32[1,8,12,16,128]{4,3,2,1,0:T(8,128)S(1)} copy-done((f32[1,8,12,16,128]{4,3,2,1,0:T(8,128)S(1)}, f32[1,8,12,16,128]{4,3,2,1,0:T(8,128)}, u32[]{:S(2)}) %copy-start) | copy-done | bytes 786456
  1.8 0.9 %copy-done.2 = bf16[256,4,128]{2,1,0:T(4,128)(2,1)S(1)} copy-done((bf16[256,4,128]{2,1,0:T(4,128)(2,1)S(1)}, bf16[256,4,128]{2,1,0:T(4,128)(2,1)}, u32[]{:S(2)}) %copy-start.2) | copy-done | bytes 262168
  2.8 0.7 copy-done.4
  3.4 3.0 %first_faces.1 = (f32[1536,128]{1,0:T(8,128)S(1)}, f32[256,4,128]{2,1,0:T(4,128)S(1)}, f32[8,128]{1,0:T(8,128)S(1)}, f32[8,1536]{1,0:T(8,128)S(1)}, f32[8,1536]{...) custom-call(f32[1536,128]{1,0:T(8,128)S(1)} %bitcast.5, bf16[256,4,128]{2,1,0:T(4,128)(2,1)S(1)} %copy-done.2, ...), custom_call_target="tpu_custom_call" | custom-call | flops 10000000 | bytes 2807808 | tf_op jit(solution)/shard_map/first_faces/pallas_call | solution.py:407
  6.5 0.5 collective-permute-start
  7.0 2.0 %collective-permute-start.1 = (f32[8,1536]{1,0:T(8,128)S(1)}, f32[8,1536]{1,0:T(8,128)S(1)}, u32[]{:S(2)}, u32[]{:S(2)}) collective-permute-start(f32[8,1536]{1,0:T(8,128)S(1)} %get-tuple-element.20), channel_id=1, source_target_pairs={{0,6},{2,0},{4,2},{6,4},{8,14},{10,8},{12,10},{14,12},{16,22},{18,... | collective-permute-start | bytes 147464 | tf_op jit(solution)/shard_map/ppermute | solution.py:424
  9.0 2.3 %collective-permute-start.2 = (bf16[576,128]{1,0:T(8,128)(2,1)S(1)}, bf16[576,128]{1,0:T(8,128)(2,1)S(1)}, u32[]{:S(2)}, u32[]{:S(2)}) collective-permute-start(bf16[576,128]{1,0:T(8,128)(2,1)S(1)} %get-tuple-element.23), channel_id=1, source_target_pairs={{0,8},{2,10},{4,12},{6,14},{8,0},{10,2},{12,4},{14,6},{16,24},{18,... | collective-permute-start | bytes 442376 | tf_op jit(solution)/shard_map/ppermute | solution.py:424
  11.3 2.6 %collective-permute-start.3 = (bf16[768,128]{1,0:T(8,128)(2,1)S(1)}, bf16[768,128]{1,0:T(8,128)(2,1)S(1)}, u32[]{:S(2)}, u32[]{:S(2)}) collective-permute-start(bf16[768,128]{1,0:T(8,128)(2,1)S(1)} %get-tuple-element.24), channel_id=1, source_target_pairs={{0,16},{2,18},{4,20},{6,22},{8,24},{10,26},{12,28},{14,30},{16,0},... | collective-permute-start | bytes 589832 | tf_op jit(solution)/shard_map/ppermute | solution.py:424
  14.2 0.7 copy-done.1
  14.9 0.9 %inside_first.1.acc = f32[1536,128]{1,0:T(8,128)S(1)} custom-call(f32[1536,128]{1,0:T(8,128)S(1)} %get-tuple-element.18.v_ref.refs_0_, f32[192,128]{1,0:T(8,128)S(1)} %bitcast.6), custom_call_target="tpu_custom_call" | custom-call | flops 200000000 | bytes 1671168 | tf_op jit(solution)/shard_map/inside_first/pallas_call | solution.py:407
  15.8 18.8 %all_gather.6.tables = f32[128,128]{1,0:T(8,128)S(1)} all-gather(f32[8,128]{1,0:T(8,128)S(1)} %get-tuple-element.21), channel_id=1, replica_groups=mesh['dom'=16,'band'=2] {'dom'}, dimensions={0}, use_global_device_ids=true | all-gather | bytes 69632 | tf_op jit(solution)/shard_map/all_gather | solution.py:454
  34.6 0.7 copy-done.5
  35.3 3.1 %sides_first.1.acc = f32[1536,128]{1,0:T(8,128)S(1)} custom-call(f32[1536,128]{1,0:T(8,128)S(1)} %inside_first.1.acc, f32[8,1536]{1,0:T(8,128)S(1)} %collective-permute-done.low, f32[8,1536]{1,0:T(8,128)S(1)} %collective-permute-done.1.high, f32[128,128]{1,0:T(8,128)S(1)} %all_gather.6.tables, f32[16,128]{1,0:T(8,128)S(1)} %copy.10.energy, ...), custom_call_target="tpu_custom_call" | custom-call | flops 10000000 | bytes 2418688 | tf_op jit(solution)/shard_map/sides_first/pallas_call | solution.py:407
  38.4 3.0 %middle.1 = (f32[1536,128]{1,0:T(8,128)S(1)}, f32[8,128]{1,0:T(8,128)S(1)}, f32[8,1536]{1,0:T(8,128)S(1)}, f32[8,1536]{1,0:T(8,128)S(1)}, bf16[768,128]{1,0:T(8,128)(2,1)S(1)}, /*index=5*/bf16[576,128]{1,0:T(8,128)(2,1)S(1)}) custom-call(f32[1536,128]{1,0:T(8,128)S(1)} %sides_first.1.acc, f32[256,4,128]{2,1,0:T(4,128)S(1)} %get-tuple-element.22.projf, ...), custom_call_target="tpu_custom_call" | custom-call | flops 10000000 | bytes 2742272 | tf_op jit(solution)/shard_map/middle/pallas_call | solution.py:407
  41.4 0.3 collective-permute-start.6
  41.9 1.6 %collective-permute-start.5 = (f32[8,1536]{1,0:T(8,128)S(1)}, f32[8,1536]{1,0:T(8,128)S(1)}, u32[]{:S(2)}, u32[]{:S(2)}) collective-permute-start(f32[8,1536]{1,0:T(8,128)S(1)} %get-tuple-element.27), channel_id=1, source_target_pairs={{0,6},{2,0},{4,2},{6,4},{8,14},{10,8},{12,10},{14,12},{16,22},{18,... | collective-permute-start | bytes 147464 | tf_op jit(solution)/shard_map/ppermute | solution.py:424
  43.5 1.0 %inside_second.1.acc = f32[1536,128]{1,0:T(8,128)S(1)} custom-call(f32[1536,128]{1,0:T(8,128)S(1)} %get-tuple-element.25.v_ref, f32[192,128]{1,0:T(8,128)S(1)} %bitcast.7, f32[1536,128]{1,0:T(8,128)S(1)} %get-tuple-element.18.v_ref.refs_0_), custom_call_target="tpu_custom_call" | custom-call | flops 200000000 | bytes 2457600 | tf_op jit(solution)/shard_map/inside_second/pallas_call | solution.py:407
  44.5 21.3 %all_gather.7.tables = f32[128,128]{1,0:T(8,128)S(1)} all-gather(f32[8,128]{1,0:T(8,128)S(1)} %get-tuple-element.28), channel_id=1, replica_groups=mesh['dom'=16,'band'=2] {'dom'}, dimensions={0}, use_global_device_ids=true | all-gather | bytes 69632 | tf_op jit(solution)/shard_map/all_gather | solution.py:454
  65.9 3.1 %sides_second.1.acc = f32[1536,128]{1,0:T(8,128)S(1)} custom-call(f32[1536,128]{1,0:T(8,128)S(1)} %inside_second.1.acc, f32[8,1536]{1,0:T(8,128)S(1)} %collective-permute-done.4.low, f32[8,1536]{1,0:T(8,128)S(1)} %collective-permute-done.5.high, f32[128,128]{1,0:T(8,128)S(1)} %all_gather.7.tables, f32[16,128]{1,0:T(8,128)S(1)} %copy.10.energy, ...), custom_call_target="tpu_custom_call" | custom-call | flops 10000000 | bytes 2418688 | tf_op jit(solution)/shard_map/sides_second/pallas_call | solution.py:407
  69.0 0.3 filtered.1.own
  69.4 1.6 %collective-permute-start.8 = (bf16[1536,128]{1,0:T(8,128)(2,1)S(1)}, bf16[1536,128]{1,0:T(8,128)(2,1)S(1)}, u32[]{:S(2)}, u32[]{:S(2)}) collective-permute-start(bf16[1536,128]{1,0:T(8,128)(2,1)S(1)} %filtered.1.own), channel_id=1, source_target_pairs={{0,1},{1,0},{2,3},{3,2},{4,5},{5,4},{6,7},{7,6},{8,9},{9,8},{10,11... | collective-permute-start | bytes 1179656 | tf_op jit(solution)/shard_map/ppermute | solution.py:528
  70.9 9.9 %collective-permute-done.8.other = bf16[1536,128]{1,0:T(8,128)(2,1)S(1)} collective-permute-done((bf16[1536,128]{1,0:T(8,128)(2,1)S(1)}, bf16[1536,128]{1,0:T(8,128)(2,1)S(1)}, u32[]{:S(2)}, u32[]{:S(2)}) %collective-permute-start.8) | collective-permute-done | bytes 393248 | tf_op jit(solution)/shard_map/ppermute | solution.py:528
  80.8 1.5 %rotate.1 = f32[1536,128]{1,0:T(8,128)} custom-call(bf16[1536,128]{1,0:T(8,128)(2,1)S(1)} %filtered.1.own, bf16[1536,128]{1,0:T(8,128)(2,1)S(1)} %collective-permute-done.8.other, bf16[16,16]{1,0:T(8,128)(2,1)S(1)} %copy-done.6), custom_call_target="tpu_custom_call" | custom-call | flops 200000000 | bytes 1573376 | tf_op jit(solution)/shard_map/rotate/pallas_call | solution.py:407
  (25 shorter events, 0.6 us)
Async XLA Ops:
  0.0 0.7 copy-start.3
  0.7 1.1 %copy-start = (f32[1,8,12,16,128]{4,3,2,1,0:T(8,128)S(1)}, f32[1,8,12,16,128]{4,3,2,1,0:T(8,128)}, u32[]{:S(2)}) copy-start(f32[1,8,12,16,128]{4,3,2,1,0:T(8,128)} %param.7) | copy-start | bytes 2359300
  1.8 0.9 %copy-start.2 = (bf16[256,4,128]{2,1,0:T(4,128)(2,1)S(1)}, bf16[256,4,128]{2,1,0:T(4,128)(2,1)}, u32[]{:S(2)}) copy-start(bf16[256,4,128]{2,1,0:T(4,128)(2,1)} %proj_hbm.1) | copy-start | bytes 786436
  2.8 0.7 copy-start.4
  6.5 28.1 %collective-permute-start = (f32[8,1536]{1,0:T(8,128)S(1)}, f32[8,1536]{1,0:T(8,128)S(1)}, u32[]{:S(2)}, u32[]{:S(2)}) collective-permute-start(f32[8,1536]{1,0:T(8,128)S(1)} %get-tuple-element.19), channel_id=1, source_target_pairs={{0,2},{2,4},{4,6},{6,0},{8,10},{10,12},{12,14},{14,8},{16,18},{18,... | collective-permute-start | bytes 147464 | tf_op jit(solution)/shard_map/ppermute | solution.py:424
  7.0 6.9 %copy-start.7 = (f32[64,4]{0,1:T(4,128)S(1)}, f32[64,4]{0,1:T(4,128)}, u32[]{:S(2)}) copy-start(f32[64,4]{0,1:T(4,128)} %param.12) | copy-start | bytes 3076
  7.0 27.6 %collective-permute-start.1 = (f32[8,1536]{1,0:T(8,128)S(1)}, f32[8,1536]{1,0:T(8,128)S(1)}, u32[]{:S(2)}, u32[]{:S(2)}) collective-permute-start(f32[8,1536]{1,0:T(8,128)S(1)} %get-tuple-element.20), channel_id=1, source_target_pairs={{0,6},{2,0},{4,2},{6,4},{8,14},{10,8},{12,10},{14,12},{16,22},{18,... | collective-permute-start | bytes 147464 | tf_op jit(solution)/shard_map/ppermute | solution.py:424
  9.0 25.6 %collective-permute-start.2 = (bf16[576,128]{1,0:T(8,128)(2,1)S(1)}, bf16[576,128]{1,0:T(8,128)(2,1)S(1)}, u32[]{:S(2)}, u32[]{:S(2)}) collective-permute-start(bf16[576,128]{1,0:T(8,128)(2,1)S(1)} %get-tuple-element.23), channel_id=1, source_target_pairs={{0,8},{2,10},{4,12},{6,14},{8,0},{10,2},{12,4},{14,6},{16,24},{18,... | collective-permute-start | bytes 442376 | tf_op jit(solution)/shard_map/ppermute | solution.py:424
  11.3 27.1 %collective-permute-start.3 = (bf16[768,128]{1,0:T(8,128)(2,1)S(1)}, bf16[768,128]{1,0:T(8,128)(2,1)S(1)}, u32[]{:S(2)}, u32[]{:S(2)}) collective-permute-start(bf16[768,128]{1,0:T(8,128)(2,1)S(1)} %get-tuple-element.24), channel_id=1, source_target_pairs={{0,16},{2,18},{4,20},{6,22},{8,24},{10,26},{12,28},{14,30},{16,0},... | collective-permute-start | bytes 589832 | tf_op jit(solution)/shard_map/ppermute | solution.py:424
  14.0 0.9 %copy-start.1 = (f32[1,12,16,128]{3,2,1,0:T(8,128)S(1)}, f32[1,12,16,128]{3,2,1,0:T(8,128)}, u32[]{:S(2)}) copy-start(f32[1,12,16,128]{3,2,1,0:T(8,128)} %param.8) | copy-start | bytes 294916
  34.6 0.7 copy-start.5
  41.4 27.7 %collective-permute-start.7 = (bf16[768,128]{1,0:T(8,128)(2,1)S(1)}, bf16[768,128]{1,0:T(8,128)(2,1)S(1)}, u32[]{:S(2)}, u32[]{:S(2)}) collective-permute-start(bf16[768,128]{1,0:T(8,128)(2,1)S(1)} %get-tuple-element.30), channel_id=1, source_target_pairs={{0,16},{2,18},{4,20},{6,22},{8,24},{10,26},{12,28},{14,30},{16,0},... | collective-permute-start | bytes 589832 | tf_op jit(solution)/shard_map/ppermute | solution.py:424
  41.4 24.5 %collective-permute-start.6 = (bf16[576,128]{1,0:T(8,128)(2,1)S(1)}, bf16[576,128]{1,0:T(8,128)(2,1)S(1)}, u32[]{:S(2)}, u32[]{:S(2)}) collective-permute-start(bf16[576,128]{1,0:T(8,128)(2,1)S(1)} %get-tuple-element.29), channel_id=1, source_target_pairs={{0,8},{2,10},{4,12},{6,14},{8,0},{10,2},{12,4},{14,6},{16,24},{18,... | collective-permute-start | bytes 442376 | tf_op jit(solution)/shard_map/ppermute | solution.py:424
  41.8 24.1 %collective-permute-start.4 = (f32[8,1536]{1,0:T(8,128)S(1)}, f32[8,1536]{1,0:T(8,128)S(1)}, u32[]{:S(2)}, u32[]{:S(2)}) collective-permute-start(f32[8,1536]{1,0:T(8,128)S(1)} %get-tuple-element.26), channel_id=1, source_target_pairs={{0,2},{2,4},{4,6},{6,0},{8,10},{10,12},{12,14},{14,8},{16,18},{18,... | collective-permute-start | bytes 147464 | tf_op jit(solution)/shard_map/ppermute | solution.py:424
  41.9 24.0 %collective-permute-start.5 = (f32[8,1536]{1,0:T(8,128)S(1)}, f32[8,1536]{1,0:T(8,128)S(1)}, u32[]{:S(2)}, u32[]{:S(2)}) collective-permute-start(f32[8,1536]{1,0:T(8,128)S(1)} %get-tuple-element.27), channel_id=1, source_target_pairs={{0,6},{2,0},{4,2},{6,4},{8,14},{10,8},{12,10},{14,12},{16,22},{18,... | collective-permute-start | bytes 147464 | tf_op jit(solution)/shard_map/ppermute | solution.py:424
  69.0 11.8 %copy-start.6 = (bf16[16,16]{1,0:T(8,128)(2,1)S(1)}, bf16[16,16]{1,0:T(8,128)(2,1)}, u32[]{:S(2)}) copy-start(bf16[16,16]{1,0:T(8,128)(2,1)} %panel.1) | copy-start | bytes 1540
  69.4 11.4 %collective-permute-start.8 = (bf16[1536,128]{1,0:T(8,128)(2,1)S(1)}, bf16[1536,128]{1,0:T(8,128)(2,1)S(1)}, u32[]{:S(2)}, u32[]{:S(2)}) collective-permute-start(bf16[1536,128]{1,0:T(8,128)(2,1)S(1)} %filtered.1.own), channel_id=1, source_target_pairs={{0,1},{1,0},{2,3},{3,2},{4,5},{5,4},{6,7},{7,6},{8,9},{9,8},{10,11... | collective-permute-start | bytes 1179656 | tf_op jit(solution)/shard_map/ppermute | solution.py:528

commit v3 on v2

--- a/solution.py
+++ b/solution.py
@@ -8,6 +8,7 @@
 from jax.sharding import PartitionSpec as P
 
 RADIUS = 6
+EARLY = 3
 COEFFS = (
     -5369.0 / 1800.0,
     12.0 / 7.0,
@@ -62,7 +63,6 @@
         self.second = min(8, dom_count // 8)
         self.plane = self.second * self.third
         self.first = dom_count // self.plane
-        self.strides = (0, self.plane, -self.plane, self.third, -self.third, 1, -1)
         self.table = self.owned * nproj * self.no
         self.slab = self.cy * self.no
         assert self.no == 8
@@ -78,9 +78,18 @@
             return [(0, place > 0), (1, place < extent - 1)]
         return []
 
-    def face_rows(self, dim):
-        rows = RADIUS * self.slab if dim == 0 else self.cx * RADIUS * self.no
+    def face_rows(self, dim, layers=RADIUS):
+        rows = layers * self.slab if dim == 0 else self.cx * layers * self.no
         return [rows] * len(self.faces(0, dim))
+
+    def links(self):
+        out = []
+        for extent, stride in ((self.first, self.plane), (self.second, self.third), (self.third, 1)):
+            if extent == 2:
+                out.append((stride, 2, 0))
+            elif extent > 2:
+                out.extend([(stride, extent, 1), (stride, extent, -1)])
+        return out
 
 
 def layer(side, length, j):
@@ -93,13 +102,17 @@
     return start if isinstance(start, int) else pl.multiple_of(start, unit)
 
 
-def pack_faces(g, dom, v_ref, x_refs, y_refs):
-    for (side, _), out in zip(g.faces(dom, 0), x_refs):
-        for j in range(RADIUS):
+def pack_x(g, dom, v_ref, first, last, refs):
+    for (side, _), out in zip(g.faces(dom, 0), refs):
+        for j in range(first, last):
             at = aligned(layer(side, g.cx, j) * g.slab, g.slab)
-            out[j * g.slab : (j + 1) * g.slab, :] = v_ref[pl.ds(at, g.slab), :].astype(BF16)
+            to = (j - first) * g.slab
+            out[to : to + g.slab, :] = v_ref[pl.ds(at, g.slab), :].astype(BF16)
+
+
+def pack_y(g, dom, v_ref, refs):
     size = RADIUS * g.no
-    for (side, _), out in zip(g.faces(dom, 1), y_refs):
+    for (side, _), out in zip(g.faces(dom, 1), refs):
         for x in range(g.cx):
             pieces = []
             for j in range(RADIUS):
@@ -123,8 +136,11 @@
 
 
 def fill_lut(g, dom, lut):
-    for number, stride in enumerate(g.strides):
-        lut[g.plane + dom + stride] = number * g.owned
+    lut[g.plane + dom] = 0
+    for number, (stride, _, step) in enumerate(g.links()):
+        if step == 0:
+            step = 1 - 2 * (dom // stride % 2)
+        lut[g.plane + dom + step * stride] = (number + 1) * g.owned
 
 
 def column_of(g, lut, atom):
@@ -132,7 +148,7 @@
     return lut[owner + g.plane] + (atom - owner * g.owned)
 
 
-def inner_tables(g, v_ref, projf, blk, atom, lut, sums, table_ref):
+def inner_tables(g, v_ref, projf, blk, atom, lut, sums):
     size = g.nproj * g.no
 
     def step(i, _):
@@ -153,9 +169,7 @@
     both = jnp.concatenate(split2(total), axis=1)
     ones = jnp.ones((8, both.shape[1]), BF16)
     summed = lax.dot_general(ones, both, NT, preferred_element_type=F32)
-    table_ref[...] = jnp.zeros(table_ref.shape, F32)
-    for number in range(len(g.strides)):
-        table_ref[number : number + 1, :] = summed[0:1, number * g.table : (number + 1) * g.table]
+    return [summed[0:1, n * g.table : (n + 1) * g.table] for n in range(len(g.links()) + 1)]
 
 
 def clear(sums):
@@ -163,32 +177,68 @@
         part[...] = jnp.zeros(part.shape, F32)
 
 
-def first_kernel(g, orb_hbm, proj_hbm, blk_hbm, atom_hbm, *refs):
-    nx, ny = len(g.face_rows(0)), len(g.face_rows(1))
-    v_ref, projf, table, low, high = refs[:5]
-    x_refs = refs[5 : 5 + nx]
-    y_refs = refs[5 + nx : 5 + nx + ny]
-    orb, proj, blk, atom, lut, sem = refs[5 + nx + ny : 11 + nx + ny]
-    sums = refs[11 + nx + ny :]
-    copies = []
-    for number, (src, dst) in enumerate(
-        ((orb_hbm, orb), (proj_hbm, proj), (blk_hbm, blk), (atom_hbm, atom))
-    ):
-        copies.append(pltpu.make_async_copy(src, dst, sem.at[number]))
-        copies[-1].start()
+def first_kernel(g, orb_hbm, proj_hbm, pot_hbm, v_ref, projf, pot, *refs):
+    nx = len(g.face_rows(0))
+    orb, proj, sem = refs[nx:]
+    copies = [
+        pltpu.make_async_copy(orb_hbm, orb, sem.at[0]),
+        pltpu.make_async_copy(proj_hbm, proj, sem.at[1]),
+        pltpu.make_async_copy(pot_hbm, pot, sem.at[2]),
+    ]
+    for copy in copies:
+        copy.start()
+    dom = lax.axis_index("dom")
+    copies[0].wait()
+    for r in range(g.rows):
+        v_ref[r * g.no : (r + 1) * g.no, :] = orb[pl.ds(r, g.no, stride=g.rows), :]
+    pack_x(g, dom, v_ref, 0, EARLY, refs[:nx])
+    copies[1].wait()
+    projf[...] = proj[...].astype(F32)
+    copies[2].wait()
+
+
+def entry_copies(blk_hbm, atom_hbm, blk, atom, sem):
+    return [
+        pltpu.make_async_copy(blk_hbm, blk, sem.at[0]),
+        pltpu.make_async_copy(atom_hbm, atom, sem.at[1]),
+    ]
+
+
+def tables_kernel(g, v_ref, projf, blk_hbm, atom_hbm, *refs):
+    nlinks = len(g.links())
+    rows_out = refs[: nlinks - 1]
+    low, high = refs[nlinks - 1 : nlinks + 1]
+    blk, atom, lut, sem = refs[nlinks + 1 : nlinks + 5]
+    sums = refs[nlinks + 5 :]
+    copies = entry_copies(blk_hbm, atom_hbm, blk, atom, sem)
+    for copy in copies:
+        copy.start()
     dom = lax.axis_index("dom")
     fill_lut(g, dom, lut)
     clear(sums)
-    copies[0].wait()
-    for r in range(g.rows):
-        v_ref[r * g.no : (r + 1) * g.no, :] = orb[pl.ds(r, g.no, stride=g.rows), :]
-    pack_faces(g, dom, v_ref, x_refs, y_refs)
     pack_ends(g, v_ref, low, high)
-    copies[1].wait()
-    projf[...] = proj[...].astype(F32)
-    copies[2].wait()
-    copies[3].wait()
-    inner_tables(g, v_ref, projf, blk, atom, lut, sums, table)
+    for copy in copies:
+        copy.wait()
+    rows = inner_tables(g, v_ref, projf, blk, atom, lut, sums)
+    for out, row in zip(rows_out, rows):
+        out[...] = row
+    high[RADIUS : RADIUS + 1, : g.table] = rows[-2]
+    low[RADIUS : RADIUS + 1, : g.table] = rows[-1]
+
+
+def rest_kernel(g, v_ref, after, *refs):
+    nx = len(g.face_rows(0))
+    dom = lax.axis_index("dom")
+    pack_x(g, dom, v_ref, EARLY, RADIUS, refs[:nx])
+    pack_y(g, dom, v_ref, refs[nx:])
+
+
+def scale_kernel(g, energy, low, high, *refs):
+    rows, out = refs[:-1], refs[-1]
+    total = low[RADIUS : RADIUS + 1, : g.table] + high[RADIUS : RADIUS + 1, : g.table]
+    for row in rows:
+        total = total + row[...]
+    out[...] = total * energy[pl.ds(lax.axis_index("dom"), 1), :]
 
 
 def inside_kernel(g, scale, subtract, v_ref, pot, *refs):
@@ -243,12 +293,15 @@
         out[rows, :] = acc[rows, :] + lax.dot_general(halo, coefs, TN, preferred_element_type=F32)
 
 
-def add_x_faces(g, dom, scale, face_refs, out):
+def add_x_faces(g, dom, scale, early_refs, late_refs, out):
     unit = 2 * g.no
-    for (side, present), face in zip(g.faces(dom, 0), face_refs):
+    for (side, present), early, late in zip(g.faces(dom, 0), early_refs, late_refs):
         for y in range(0, g.cy, 2):
-            starts = [j * g.slab + y * g.no for j in range(RADIUS)]
-            part = [flag(present) * face[at : at + unit, :].astype(F32) for at in starts]
+            part = []
+            for j in range(RADIUS):
+                face, at = (early, j) if j < EARLY else (late, j - EARLY)
+                at = at * g.slab + y * g.no
+                part.append(flag(present) * face[at : at + unit, :].astype(F32))
             for i in range(RADIUS):
                 at = aligned(layer(side, g.cx, i) * g.slab + y * g.no, unit)
                 total = out[pl.ds(at, unit), :]
@@ -270,35 +323,22 @@
                 out[pl.ds(at, g.no), :] = total
 
 
-def scaled_rows(g, dom, tables, energy):
-    rows = []
-    for stride in g.strides:
-        owner = jnp.clip(dom + stride, 0, g.dom_count - 1)
-        total = None
-        for number, back in enumerate(g.strides):
-            source = owner - back
-            inside = (source >= 0) & (source < g.dom_count)
-            row = tables[pl.ds(jnp.where(inside, source * 8 + number, 7), 1), :]
-            total = row if total is None else total + row
-        rows.append(total * energy[pl.ds(owner, 1), :])
-    return rows
-
-
 def add_nonlocal(g, scale, rows, projf, blk, atom, lut, spread, out):
     size = g.nproj * g.no
     lanes = g.table
-    rows.append(jnp.zeros((1, lanes), F32))
+    count = len(rows)
+    rows = rows + [jnp.zeros((8 - count, lanes), F32)]
     scaled = (scale / HALF_WIDTH) * jnp.concatenate(rows, axis=0)
     high = scaled.astype(BF16)
     rest = scaled - high.astype(F32)
     mid = rest.astype(BF16)
     low = (rest - mid.astype(F32)).astype(BF16)
     parts = jnp.concatenate([high, mid, low], axis=0)
-    wide = len(g.strides) * g.cz
+    wide = count * g.cz
     row, col = iota((24, wide), 0), iota((24, wide), 1)
     ones = jnp.where(row % 8 == col // g.cz, 1.0, 0.0).astype(BF16)
     out_all = lax.dot_general(parts, ones, TN, preferred_element_type=F32)
-    for number in range(len(g.strides)):
+    for number in range(count):
         spread[number * lanes : (number + 1) * lanes, :] = out_all[:, number * g.cz : (number + 1) * g.cz]
     unroll = 4
 
@@ -321,58 +361,43 @@
     lax.fori_loop(0, g.ent // unroll, step, 0)
 
 
-def sides_kernel(g, scale, acc, low, high, tables, energy, projf, blk_hbm, atom_hbm, *refs):
-    ny = len(g.face_rows(1))
-    y_refs = refs[:ny]
-    out, blk, atom, lut, spread, sem = refs[ny:]
-    copies = [
-        pltpu.make_async_copy(blk_hbm, blk, sem.at[0]),
-        pltpu.make_async_copy(atom_hbm, atom, sem.at[1]),
-    ]
+def sides_kernel(g, scale, acc, low, high, *refs):
+    y_refs, out = refs[:-1], refs[-1]
+    dom = lax.axis_index("dom")
+    add_ends(g, dom, scale, acc, low, high, out)
+    add_y_faces(g, dom, scale, y_refs, out)
+
+
+def finish(g, scale, acc, projf, blk_hbm, atom_hbm, inputs, out, scratch):
+    nx = len(g.face_rows(0))
+    early, late, rows = inputs[:nx], inputs[nx : 2 * nx], inputs[2 * nx :]
+    blk, atom, lut, sem, spread = scratch
+    copies = entry_copies(blk_hbm, atom_hbm, blk, atom, sem)
     for copy in copies:
         copy.start()
     dom = lax.axis_index("dom")
     fill_lut(g, dom, lut)
-    add_ends(g, dom, scale, acc, low, high, out)
-    add_y_faces(g, dom, scale, y_refs, out)
-    rows = scaled_rows(g, dom, tables, energy)
+    out[...] = acc[...]
+    add_x_faces(g, dom, scale, early, late, out)
     for copy in copies:
         copy.wait()
-    add_nonlocal(g, scale, rows, projf, blk, atom, lut, spread, out)
+    add_nonlocal(g, scale, [row[...] for row in rows], projf, blk, atom, lut, spread, out)
+    return dom
 
 
 def middle_kernel(g, acc, projf, blk_hbm, atom_hbm, *refs):
-    nx, ny = len(g.face_rows(0)), len(g.face_rows(1))
-    x_in = refs[:nx]
-    u_ref, table, low_out, high_out = refs[nx : nx + 4]
-    x_out = refs[nx + 4 : 2 * nx + 4]
-    y_out = refs[2 * nx + 4 : 2 * nx + 4 + ny]
-    blk, atom, lut, sem = refs[2 * nx + 4 + ny : 2 * nx + 8 + ny]
-    sums = refs[2 * nx + 8 + ny :]
-    copies = [
-        pltpu.make_async_copy(blk_hbm, blk, sem.at[0]),
-        pltpu.make_async_copy(atom_hbm, atom, sem.at[1]),
-    ]
-    for copy in copies:
-        copy.start()
-    dom = lax.axis_index("dom")
-    fill_lut(g, dom, lut)
-    clear(sums)
-    u_ref[...] = acc[...]
-    add_x_faces(g, dom, 1.0, x_in, u_ref)
-    pack_faces(g, dom, u_ref, x_out, y_out)
-    pack_ends(g, u_ref, low_out, high_out)
-    for copy in copies:
-        copy.wait()
-    inner_tables(g, u_ref, projf, blk, atom, lut, sums, table)
-
-
-def last_kernel(g, acc, *refs):
-    x_in = refs[: len(g.face_rows(0))]
-    filtered, work = refs[len(g.face_rows(0)) :]
-    dom = lax.axis_index("dom")
-    work[...] = acc[...]
-    add_x_faces(g, dom, 2.0, x_in, work)
+    nx = len(g.face_rows(0))
+    nin = 2 * nx + len(g.links()) + 1
+    u_ref = refs[nin]
+    x_out = refs[nin + 1 : nin + 1 + nx]
+    dom = finish(g, 1.0, acc, projf, blk_hbm, atom_hbm, refs[:nin], u_ref, refs[nin + 1 + nx :])
+    pack_x(g, dom, u_ref, 0, EARLY, x_out)
+
+
+def last_kernel(g, acc, projf, blk_hbm, atom_hbm, *refs):
+    nin = 2 * len(g.face_rows(0)) + len(g.links()) + 1
+    filtered, work = refs[nin : nin + 2]
+    finish(g, 2.0, acc, projf, blk_hbm, atom_hbm, refs[:nin], work, refs[nin + 2 :])
     filtered[...] = work[...].astype(BF16)
 
 
@@ -436,56 +461,96 @@
     g = Geometry(
         orbitals.shape, projectors.shape[0], projectors.shape[1], kb_energy.shape[0], lax.axis_size("dom")
     )
-    orb = orbitals.reshape(g.flat, g.cz)
-    pot = potential.reshape(g.rows, g.cz)
+
+    def in_hbm(array):
+        return pltpu.with_memory_space_constraint(array, pltpu.HBM)
+
+    orb = in_hbm(orbitals.reshape(g.flat, g.cz))
+    pot = in_hbm(potential.reshape(g.rows, g.cz))
+    proj = in_hbm(projectors)
+    blk, atom = in_hbm(entry_block), in_hbm(entry_atom)
     field = jax.ShapeDtypeStruct((g.flat, g.cz), F32)
-    x_faces = [jax.ShapeDtypeStruct((n, g.cz), BF16) for n in g.face_rows(0)]
+    x_early = [jax.ShapeDtypeStruct((n, g.cz), BF16) for n in g.face_rows(0, EARLY)]
+    x_late = [jax.ShapeDtypeStruct((n, g.cz), BF16) for n in g.face_rows(0, RADIUS - EARLY)]
     y_faces = [jax.ShapeDtypeStruct((n, g.cz), BF16) for n in g.face_rows(1)]
-    nx, ny = len(x_faces), len(y_faces)
+    nx, ny = len(x_early), len(y_faces)
+    links = g.links()
     ends = jax.ShapeDtypeStruct((8, g.flat), F32)
-    table = jax.ShapeDtypeStruct((8, g.table), F32)
-    projf = jax.ShapeDtypeStruct(projectors.shape, F32)
-    lut = pltpu.SMEM((g.dom_count + 2 * g.plane,), jnp.int32)
-    entries = [pltpu.SMEM((g.ent,), jnp.int32)] * 2
-    sums = [pltpu.VMEM((len(g.strides) * g.table, g.cz), F32) for _ in range(4)]
-    spread = pltpu.VMEM((len(g.strides) * g.table, g.cz), F32)
-
-    def exchange(sent, low, high, part):
-        tables = lax.all_gather(part, "dom", tiled=True)
+    row = jax.ShapeDtypeStruct((1, g.table), F32)
+    slots = (len(links) + 1) * g.table
+    entries = [
+        pltpu.SMEM((g.ent,), jnp.int32),
+        pltpu.SMEM((g.ent,), jnp.int32),
+        pltpu.SMEM((g.dom_count + 2 * g.plane,), jnp.int32),
+        pltpu.SemaphoreType.DMA((2,)),
+    ]
+    sums = [pltpu.VMEM((slots, g.cz), F32) for _ in range(4)]
+    spread = pltpu.VMEM((slots, g.cz), F32)
+    energy = jnp.repeat(kb_energy.reshape(g.dom_count, g.owned * g.nproj), g.no, axis=1)
+
+    def swap_x(faces):
+        return swap_faces(g, faces, g.plane, g.first)
+
+    def neighbours(which, values, early):
+        x1 = swap_x(early)
+        *rows, low, high = call(
+            functools.partial(tables_kernel, g),
+            "tables_" + which,
+            [row] * (len(links) - 1) + [ends, ends],
+            [*entries, *sums],
+            10_000_000,
+            [values, projf, blk, atom],
+            [VMEM] * 2 + [HBM] * 2,
+        )
         low, high = shift(g, high, 1, g.third, 1), shift(g, low, 1, g.third, -1)
-        from_y = swap_faces(g, sent[nx:], g.third, g.second)
-        from_x = swap_faces(g, sent[:nx], g.plane, g.first)
-        return tables, low, high, from_x, from_y
-
-    def sides(scale, name, acc, low, high, tables, from_y):
+        for n, (stride, extent, step) in enumerate(links[:-2]):
+            rows[n + 1] = shift(g, rows[n + 1], stride, extent, step or 1)
+        later = call(
+            functools.partial(rest_kernel, g),
+            "rest_" + which,
+            [*x_late, *y_faces],
+            [],
+            1_000_000,
+            [values, low],
+            [VMEM] * 2,
+        )
+        x2 = swap_x(later[:nx])
+        from_y = swap_faces(g, later[nx:], g.third, g.second)
+        scaled = call(
+            functools.partial(scale_kernel, g),
+            "scale_" + which,
+            row,
+            [],
+            1_000_000,
+            [energy, low, high, *rows],
+            [VMEM] * (3 + len(rows)),
+        )
+        rows = [scaled]
+        for stride, extent, step in links:
+            rows.append(shift(g, scaled, stride, extent, -step or 1))
+        return low, high, from_y, [*x1, *x2, *rows]
+
+    def sides(scale, which, acc, low, high, from_y):
         return call(
             functools.partial(sides_kernel, g, scale),
-            name,
+            "sides_" + which,
             field,
-            [*entries, lut, spread, pltpu.SemaphoreType.DMA((2,))],
+            [],
             10_000_000,
-            [acc, low, high, tables, energy, proj, entry_block, entry_atom, *from_y],
-            [VMEM] * 6 + [HBM] * 2 + [VMEM] * ny,
+            [acc, low, high, *from_y],
+            [VMEM] * (3 + ny),
         )
 
-    v, proj, part, low, high, *sent = call(
+    v, projf, pot, *early = call(
         functools.partial(first_kernel, g),
-        "first_faces",
-        [field, projf, table, ends, ends, *x_faces, *y_faces],
-        [
-            pltpu.VMEM(orb.shape, F32),
-            pltpu.VMEM(projectors.shape, BF16),
-            *entries,
-            lut,
-            pltpu.SemaphoreType.DMA((4,)),
-            *sums,
-        ],
+        "early_first",
+        [field, jax.ShapeDtypeStruct(proj.shape, F32), jax.ShapeDtypeStruct(pot.shape, F32), *x_early],
+        [pltpu.VMEM(orb.shape, F32), pltpu.VMEM(proj.shape, BF16), pltpu.SemaphoreType.DMA((3,))],
         10_000_000,
-        [orb, projectors, entry_block, entry_atom],
-        [HBM] * 4,
-    )
-    tables, low, high, from_x, from_y = exchange(sent, low, high, part)
-    energy = jnp.repeat(kb_energy.reshape(g.dom_count, g.owned * g.nproj), g.no, axis=1)
+        [orb, proj, pot],
+        [HBM] * 3,
+    )
+    low, high, from_y, others = neighbours("first", v, early)
     acc = call(
         functools.partial(inside_kernel, g, 1.0, False),
         "inside_first",
@@ -495,17 +560,17 @@
         [v, pot],
         [VMEM, VMEM],
     )
-    acc = sides(1.0, "sides_first", acc, low, high, tables, from_y)
-    u, part, low, high, *sent = call(
+    acc = sides(1.0, "first", acc, low, high, from_y)
+    u, *early = call(
         functools.partial(middle_kernel, g),
         "middle",
-        [field, table, ends, ends, *x_faces, *y_faces],
-        [*entries, lut, pltpu.SemaphoreType.DMA((2,)), *sums],
+        [field, *x_early],
+        [*entries, spread],
         10_000_000,
-        [acc, proj, entry_block, entry_atom, *from_x],
-        [VMEM] * 2 + [HBM] * 2 + [VMEM] * nx,
-    )
-    tables, low, high, from_x, from_y = exchange(sent, low, high, part)
+        [acc, projf, blk, atom, *others],
+        [VMEM] * 2 + [HBM] * 2 + [VMEM] * len(others),
+    )
+    low, high, from_y, others = neighbours("second", u, early)
     acc = call(
         functools.partial(inside_kernel, g, 2.0, True),
         "inside_second",
@@ -515,15 +580,15 @@
         [u, pot, v],
         [VMEM, VMEM, VMEM],
     )
-    acc = sides(2.0, "sides_second", acc, low, high, tables, from_y)
+    acc = sides(2.0, "second", acc, low, high, from_y)
     filtered = call(
         functools.partial(last_kernel, g),
         "filtered",
         jax.ShapeDtypeStruct((g.flat, g.cz), BF16),
-        [pltpu.VMEM((g.flat, g.cz), F32)],
+        [pltpu.VMEM((g.flat, g.cz), F32), *entries, spread],
         10_000_000,
-        [acc, *from_x],
-        [VMEM] * (1 + nx),
+        [acc, projf, blk, atom, *others],
+        [VMEM] * 2 + [HBM] * 2 + [VMEM] * len(others),
     )
     other = lax.ppermute(filtered, "band", [(0, 1), (1, 0)])
     rotated = call(

time: 82.6 us -> 73 us (0.88)
  blocking collectives: 40.1 us -> 0 us
  waiting for transfers between devices: 9.9 us -> 32 us
  starting transfers between devices: 11.1 us -> 22.6 us
  local copies, waits for them, and re-layouts: 5.1 us -> 0.31 us
  Pallas kernels: 15.9 us -> 17.7 us
    all_gather x2 -> x0, blocking collectives: 40.1 us -> none  [exchange(): tables = lax.all_gather(part, 'dom', tiled=True)]
    ppermute x8 -> x22, waiting for transfers between devices: 0.02 us -> 22.5 us  [shift(): return lax.ppermute(array, 'dom', pairs)]
    ppermute x8 -> x22, starting transfers between devices: 9.55 us -> 21.1 us  [shift(): return lax.ppermute(array, 'dom', pairs)]
    unnamed x17 -> x5, local copies, waits for them, and re-layouts: 4.9 us -> 0.11 us
    pallas_call x8 -> x14, Pallas kernels: 15.9 us -> 17.7 us  [call(): pl.pallas_call(kernel, name=name, out_shape=out_shape, in_specs=specs, ou...]
  transfers between devices with their start and end apart: 9 -> 23, of which waited for: 1 -> 11; matrix products, arithmetic and copies ran while one was open for 0% -> 0% of each run, Pallas kernels for 10% -> 5%
where the time goes in v3:
time: 73 us; the launch traced here: 72.8 us
  waiting for transfers between devices  32 us (44%)
  starting transfers between devices  22.6 us (31%)
  Pallas kernels  17.7 us (24%)
    ppermute x22, waiting for transfers between devices, shift(): return lax.ppermute(array, 'dom', pairs)  22.5 us
    ppermute x22, starting transfers between devices, shift(): return lax.ppermute(array, 'dom', pairs)  21.1 us
    pallas_call x14, Pallas kernels, call(): pl.pallas_call(kernel, name=name, out_shape=out_shape, in_specs=specs, ou...  17.7 us
    ppermute x1, waiting for transfers between devices, shards(): other = lax.ppermute(filtered, 'band', [(0, 1), (1, 0)])  9.49 us
    ppermute x1, starting transfers between devices, shards(): other = lax.ppermute(filtered, 'band', [(0, 1), (1, 0)])  1.55 us
  transfers between devices with their start and end apart: 23, of which 11 were waited for; matrix products, arithmetic and copies ran while one was open for 0% of the time, Pallas kernels for 5%

profile of v3, /device:TPU:0, one launch (start us, length us, event | category | flops | bytes accessed | tf_op | source)
XLA Modules:
  0.0 72.8 jit_solution(1689733238538409558)
XLA Ops:
  0.0 1.7 %early_first.1 = (f32[1536,128]{1,0:T(8,128)S(1)}, f32[256,4,128]{2,1,0:T(4,128)S(1)}, f32[192,128]{1,0:T(8,128)S(1)}, bf16[384,128]{1,0:T(8,128)(2,1)S(1)}) custom-call(f32[1536,128]{1,0:T(8,128)} %bitcast.5, bf16[256,4,128]{2,1,0:T(4,128)(2,1)} %proj_hbm.1, f32[192,128]{1,0:T(8,128)} %bitcast.6), custom_call_target="tpu_custom_call" | custom-call | flops 10000000 | bytes 2654208 | tf_op jit(solution)/shard_map/early_first/pallas_call | solution.py:432
  1.7 2.6 %tables_first.1 = (f32[1,128]{1,0:T(1,128)S(1)}, f32[1,128]{1,0:T(1,128)S(1)}, f32[1,128]{1,0:T(1,128)S(1)}, f32[8,1536]{1,0:T(8,128)S(1)}, f32[8,1536]{1,0:T(8,128)S(1)}) custom-call(f32[1536,128]{1,0:T(8,128)S(1)} %get-tuple-element.25.v_ref.refs_0_, f32[256,4,128]{2,1,0:T(4,128)S(1)} %get-tuple-element.27.projf, s32[256]{0:T(256)} %blk_hbm.7, s32[256]{0:T(256)} %atom_hbm.7), custom_call_target="tpu_custom_call" | custom-call | flops 10000000 | bytes 1412608 | tf_op jit(solution)/shard_map/tables_first/pallas_call | solution.py:432
  4.8 2.0 %collective-permute-start.1 = (f32[8,1536]{1,0:T(8,128)S(1)}, f32[8,1536]{1,0:T(8,128)S(1)}, u32[]{:S(2)}, u32[]{:S(2)}) collective-permute-start(f32[8,1536]{1,0:T(8,128)S(1)} %get-tuple-element.29), channel_id=1, source_target_pairs={{0,6},{2,0},{4,2},{6,4},{8,14},{10,8},{12,10},{14,12},{16,22},{18,... | collective-permute-start | bytes 147464 | tf_op jit(solution)/shard_map/ppermute | solution.py:449
  6.9 3.3 %collective-permute-start.3 = (bf16[384,128]{1,0:T(8,128)(2,1)S(1)}, bf16[384,128]{1,0:T(8,128)(2,1)S(1)}, u32[]{:S(2)}, u32[]{:S(2)}) collective-permute-start(bf16[384,128]{1,0:T(8,128)(2,1)S(1)} %get-tuple-element.31), channel_id=1, source_target_pairs={{0,16},{2,18},{4,20},{6,22},{8,24},{10,26},{12,28},{14,30},{16,0},... | collective-permute-start | bytes 294920 | tf_op jit(solution)/shard_map/ppermute | solution.py:449
  10.2 1.9 %collective-permute-start.6 = (f32[1,128]{1,0:T(1,128)S(1)}, f32[1,128]{1,0:T(1,128)S(1)}, u32[]{:S(2)}, u32[]{:S(2)}) collective-permute-start(f32[1,128]{1,0:T(1,128)S(1)} %get-tuple-element.35), channel_id=1, source_target_pairs={{0,8},{2,10},{4,12},{6,14},{8,0},{10,2},{12,4},{14,6},{16,24},{18,... | collective-permute-start | bytes 1544 | tf_op jit(solution)/shard_map/ppermute | solution.py:449
  12.6 2.8 %collective-permute-done.5.refs_1_ = f32[1,128]{1,0:T(1,128)S(1)} collective-permute-done((f32[1,128]{1,0:T(1,128)S(1)}, f32[1,128]{1,0:T(1,128)S(1)}, u32[]{:S(2)}, u32[]{:S(2)}) %collective-permute-start.5) | collective-permute-done | bytes 544 | tf_op jit(solution)/shard_map/ppermute | solution.py:449
  16.1 2.3 %collective-permute-start.7 = (f32[1,128]{1,0:T(1,128)S(1)}, f32[1,128]{1,0:T(1,128)S(1)}, u32[]{:S(2)}, u32[]{:S(2)}) collective-permute-start(f32[1,128]{1,0:T(1,128)S(1)} %scale_first.1.refs_2_), channel_id=1, source_target_pairs={{0,16},{2,18},{4,20},{6,22},{8,24},{10,26},{12,28},{14,30},{16,0},... | collective-permute-start | bytes 1544 | tf_op jit(solution)/shard_map/ppermute | solution.py:449
  19.4 1.2 %collective-permute-start.8 = (f32[1,128]{1,0:T(1,128)S(1)}, f32[1,128]{1,0:T(1,128)S(1)}, u32[]{:S(2)}, u32[]{:S(2)}) collective-permute-start(f32[1,128]{1,0:T(1,128)S(1)} %scale_first.1.refs_2_), channel_id=1, source_target_pairs={{0,8},{2,10},{4,12},{6,14},{8,0},{10,2},{12,4},{14,6},{16,24},{18,... | collective-permute-start | bytes 1544 | tf_op jit(solution)/shard_map/ppermute | solution.py:449
  20.6 2.2 %collective-permute-done.7.refs_3_ = f32[1,128]{1,0:T(1,128)S(1)} collective-permute-done((f32[1,128]{1,0:T(1,128)S(1)}, f32[1,128]{1,0:T(1,128)S(1)}, u32[]{:S(2)}, u32[]{:S(2)}) %collective-permute-start.7) | collective-permute-done | bytes 544 | tf_op jit(solution)/shard_map/ppermute | solution.py:449
  24.2 1.7 %collective-permute-done.10.refs_6_ = f32[1,128]{1,0:T(1,128)S(1)} collective-permute-done((f32[1,128]{1,0:T(1,128)S(1)}, f32[1,128]{1,0:T(1,128)S(1)}, u32[]{:S(2)}, u32[]{:S(2)}) %collective-permute-start.10) | collective-permute-done | bytes 544 | tf_op jit(solution)/shard_map/ppermute | solution.py:449
  25.8 3.0 %middle.1 = (f32[1536,128]{1,0:T(8,128)S(1)}, bf16[384,128]{1,0:T(8,128)(2,1)S(1)}) custom-call(f32[1536,128]{1,0:T(8,128)S(1)} %sides_first.1.acc, f32[256,4,128]{2,1,0:T(4,128)S(1)} %get-tuple-element.27.projf, s32[256]{0:T(256)} %blk_hbm.7, s32[256]{0:T(256)} %atom_hbm.7, bf16[384,128]{1,0:T(8,128)(2,1)S(1)} %collective-permute-done.3.refs_0_, ...), custom_call_target="tpu_custom_call" | custom-call | flops 10000000 | bytes 2396672 | tf_op jit(solution)/shard_map/middle/pallas_call | solution.py:432
  28.8 2.6 %tables_second.1 = (f32[1,128]{1,0:T(1,128)S(1)}, f32[1,128]{1,0:T(1,128)S(1)}, f32[1,128]{1,0:T(1,128)S(1)}, f32[8,1536]{1,0:T(8,128)S(1)}, f32[8,1536]{1,0:T(8,128)S(1)}) custom-call(f32[1536,128]{1,0:T(8,128)S(1)} %get-tuple-element.36.v_ref, f32[256,4,128]{2,1,0:T(4,128)S(1)} %get-tuple-element.27.projf, s32[256]{0:T(256)} %blk_hbm.7, s32[256]{0:T(256)} %atom_hbm.7), custom_call_target="tpu_custom_call" | custom-call | flops 10000000 | bytes 1412608 | tf_op jit(solution)/shard_map/tables_second/pallas_call | solution.py:432
  31.5 3.5 %collective-permute-done.11.after.low = f32[8,1536]{1,0:T(8,128)S(1)} collective-permute-done((f32[8,1536]{1,0:T(8,128)S(1)}, f32[8,1536]{1,0:T(8,128)S(1)}, u32[]{:S(2)}, u32[]{:S(2)}) %collective-permute-start.11) | collective-permute-done | bytes 49184 | tf_op jit(solution)/shard_map/ppermute | solution.py:449
  35.0 1.2 %collective-permute-start.13 = (bf16[576,128]{1,0:T(8,128)(2,1)S(1)}, bf16[576,128]{1,0:T(8,128)(2,1)S(1)}, u32[]{:S(2)}, u32[]{:S(2)}) collective-permute-start(bf16[576,128]{1,0:T(8,128)(2,1)S(1)} %get-tuple-element.39), channel_id=1, source_target_pairs={{0,8},{2,10},{4,12},{6,14},{8,0},{10,2},{12,4},{14,6},{16,24},{18,... | collective-permute-start | bytes 442376 | tf_op jit(solution)/shard_map/ppermute | solution.py:449
  36.3 1.2 %collective-permute-start.14 = (bf16[384,128]{1,0:T(8,128)(2,1)S(1)}, bf16[384,128]{1,0:T(8,128)(2,1)S(1)}, u32[]{:S(2)}, u32[]{:S(2)}) collective-permute-start(bf16[384,128]{1,0:T(8,128)(2,1)S(1)} %get-tuple-element.40), channel_id=1, source_target_pairs={{0,16},{2,18},{4,20},{6,22},{8,24},{10,26},{12,28},{14,30},{16,0},... | collective-permute-start | bytes 294920 | tf_op jit(solution)/shard_map/ppermute | solution.py:449
  37.4 1.8 %collective-permute-start.15 = (bf16[384,128]{1,0:T(8,128)(2,1)S(1)}, bf16[384,128]{1,0:T(8,128)(2,1)S(1)}, u32[]{:S(2)}, u32[]{:S(2)}) collective-permute-start(bf16[384,128]{1,0:T(8,128)(2,1)S(1)} %get-tuple-element.41), channel_id=1, source_target_pairs={{0,16},{2,18},{4,20},{6,22},{8,24},{10,26},{12,28},{14,30},{16,0},... | collective-permute-start | bytes 294920 | tf_op jit(solution)/shard_map/ppermute | solution.py:449
  40.4 5.8 %collective-permute-done.16.refs_1_ = f32[1,128]{1,0:T(1,128)S(1)} collective-permute-done((f32[1,128]{1,0:T(1,128)S(1)}, f32[1,128]{1,0:T(1,128)S(1)}, u32[]{:S(2)}, u32[]{:S(2)}) %collective-permute-start.16) | collective-permute-done | bytes 544 | tf_op jit(solution)/shard_map/ppermute | solution.py:449
  46.2 3.5 %collective-permute-done.17.refs_2_ = f32[1,128]{1,0:T(1,128)S(1)} collective-permute-done((f32[1,128]{1,0:T(1,128)S(1)}, f32[1,128]{1,0:T(1,128)S(1)}, u32[]{:S(2)}, u32[]{:S(2)}) %collective-permute-start.17) | collective-permute-done | bytes 544 | tf_op jit(solution)/shard_map/ppermute | solution.py:449
  51.2 2.1 %collective-permute-start.19 = (f32[1,128]{1,0:T(1,128)S(1)}, f32[1,128]{1,0:T(1,128)S(1)}, u32[]{:S(2)}, u32[]{:S(2)}) collective-permute-start(f32[1,128]{1,0:T(1,128)S(1)} %scale_second.1.refs_2_), channel_id=1, source_target_pairs={{0,8},{2,10},{4,12},{6,14},{8,0},{10,2},{12,4},{14,6},{16,24},{18,... | collective-permute-start | bytes 1544 | tf_op jit(solution)/shard_map/ppermute | solution.py:449
  55.6 1.7 %collective-permute-done.21.refs_6_ = f32[1,128]{1,0:T(1,128)S(1)} collective-permute-done((f32[1,128]{1,0:T(1,128)S(1)}, f32[1,128]{1,0:T(1,128)S(1)}, u32[]{:S(2)}, u32[]{:S(2)}) %collective-permute-start.21) | collective-permute-done | bytes 544 | tf_op jit(solution)/shard_map/ppermute | solution.py:449
  57.3 3.0 %filtered.1.own = bf16[1536,128]{1,0:T(8,128)(2,1)S(1)} custom-call(f32[1536,128]{1,0:T(8,128)S(1)} %sides_second.1.acc, f32[256,4,128]{2,1,0:T(4,128)S(1)} %get-tuple-element.27.projf, s32[256]{0:T(256)} %blk_hbm.7, s32[256]{0:T(256)} %atom_hbm.7, bf16[384,128]{1,0:T(8,128)(2,1)S(1)} %collective-permute-done.14.refs_0_, ...), custom_call_target="tpu_custom_call" | custom-call | flops 10000000 | bytes 1905152 | tf_op jit(solution)/shard_map/filtered/pallas_call | solution.py:432
  60.2 1.6 %collective-permute-start.22 = (bf16[1536,128]{1,0:T(8,128)(2,1)S(1)}, bf16[1536,128]{1,0:T(8,128)(2,1)S(1)}, u32[]{:S(2)}, u32[]{:S(2)}) collective-permute-start(bf16[1536,128]{1,0:T(8,128)(2,1)S(1)} %filtered.1.own), channel_id=1, source_target_pairs={{0,1},{1,0},{2,3},{3,2},{4,5},{5,4},{6,7},{7,6},{8,9},{9,8},{10,11... | collective-permute-start | bytes 1179656 | tf_op jit(solution)/shard_map/ppermute | solution.py:593
  61.8 9.5 %collective-permute-done.22.other = bf16[1536,128]{1,0:T(8,128)(2,1)S(1)} collective-permute-done((bf16[1536,128]{1,0:T(8,128)(2,1)S(1)}, bf16[1536,128]{1,0:T(8,128)(2,1)S(1)}, u32[]{:S(2)}, u32[]{:S(2)}) %collective-permute-start.22) | collective-permute-done | bytes 393248 | tf_op jit(solution)/shard_map/ppermute | solution.py:593
  71.3 1.5 %rotate.1 = f32[1536,128]{1,0:T(8,128)} custom-call(bf16[1536,128]{1,0:T(8,128)(2,1)S(1)} %filtered.1.own, bf16[1536,128]{1,0:T(8,128)(2,1)S(1)} %collective-permute-done.22.other, bf16[16,16]{1,0:T(8,128)(2,1)S(1)} %copy-done), custom_call_target="tpu_custom_call" | custom-call | flops 200000000 | bytes 1573376 | tf_op jit(solution)/shard_map/rotate/pallas_call | solution.py:432
  (45 shorter events, 9.0 us)
Async XLA Ops:
  4.3 8.0 %collective-permute-start = (f32[8,1536]{1,0:T(8,128)S(1)}, f32[8,1536]{1,0:T(8,128)S(1)}, u32[]{:S(2)}, u32[]{:S(2)}) collective-permute-start(f32[8,1536]{1,0:T(8,128)S(1)} %get-tuple-element.28), channel_id=1, source_target_pairs={{0,2},{2,4},{4,6},{6,0},{8,10},{10,12},{12,14},{14,8},{16,18},{18,... | collective-permute-start | bytes 147464 | tf_op jit(solution)/shard_map/ppermute | solution.py:449
  4.8 11.2 %collective-permute-start.1 = (f32[8,1536]{1,0:T(8,128)S(1)}, f32[8,1536]{1,0:T(8,128)S(1)}, u32[]{:S(2)}, u32[]{:S(2)}) collective-permute-start(f32[8,1536]{1,0:T(8,128)S(1)} %get-tuple-element.29), channel_id=1, source_target_pairs={{0,6},{2,0},{4,2},{6,4},{8,14},{10,8},{12,10},{14,12},{16,22},{18,... | collective-permute-start | bytes 147464 | tf_op jit(solution)/shard_map/ppermute | solution.py:449
  6.9 19.0 %collective-permute-start.3 = (bf16[384,128]{1,0:T(8,128)(2,1)S(1)}, bf16[384,128]{1,0:T(8,128)(2,1)S(1)}, u32[]{:S(2)}, u32[]{:S(2)}) collective-permute-start(bf16[384,128]{1,0:T(8,128)(2,1)S(1)} %get-tuple-element.31), channel_id=1, source_target_pairs={{0,16},{2,18},{4,20},{6,22},{8,24},{10,26},{12,28},{14,30},{16,0},... | collective-permute-start | bytes 294920 | tf_op jit(solution)/shard_map/ppermute | solution.py:449
  10.2 5.2 %collective-permute-start.5 = (f32[1,128]{1,0:T(1,128)S(1)}, f32[1,128]{1,0:T(1,128)S(1)}, u32[]{:S(2)}, u32[]{:S(2)}) collective-permute-start(f32[1,128]{1,0:T(1,128)S(1)} %get-tuple-element.34), channel_id=1, source_target_pairs={{0,16},{2,18},{4,20},{6,22},{8,24},{10,26},{12,28},{14,30},{16,0},... | collective-permute-start | bytes 1544 | tf_op jit(solution)/shard_map/ppermute | solution.py:449
  10.2 5.9 %collective-permute-start.6 = (f32[1,128]{1,0:T(1,128)S(1)}, f32[1,128]{1,0:T(1,128)S(1)}, u32[]{:S(2)}, u32[]{:S(2)}) collective-permute-start(f32[1,128]{1,0:T(1,128)S(1)} %get-tuple-element.35), channel_id=1, source_target_pairs={{0,8},{2,10},{4,12},{6,14},{8,0},{10,2},{12,4},{14,6},{16,24},{18,... | collective-permute-start | bytes 1544 | tf_op jit(solution)/shard_map/ppermute | solution.py:449
  12.4 10.5 %collective-permute-start.2 = (bf16[576,128]{1,0:T(8,128)(2,1)S(1)}, bf16[576,128]{1,0:T(8,128)(2,1)S(1)}, u32[]{:S(2)}, u32[]{:S(2)}) collective-permute-start(bf16[576,128]{1,0:T(8,128)(2,1)S(1)} %get-tuple-element.30), channel_id=1, source_target_pairs={{0,8},{2,10},{4,12},{6,14},{8,0},{10,2},{12,4},{14,6},{16,24},{18,... | collective-permute-start | bytes 442376 | tf_op jit(solution)/shard_map/ppermute | solution.py:449
  15.4 10.5 %collective-permute-start.4 = (bf16[384,128]{1,0:T(8,128)(2,1)S(1)}, bf16[384,128]{1,0:T(8,128)(2,1)S(1)}, u32[]{:S(2)}, u32[]{:S(2)}) collective-permute-start(bf16[384,128]{1,0:T(8,128)(2,1)S(1)} %get-tuple-element.32), channel_id=1, source_target_pairs={{0,16},{2,18},{4,20},{6,22},{8,24},{10,26},{12,28},{14,30},{16,0},... | collective-permute-start | bytes 294920 | tf_op jit(solution)/shard_map/ppermute | solution.py:449
  16.1 6.7 %collective-permute-start.7 = (f32[1,128]{1,0:T(1,128)S(1)}, f32[1,128]{1,0:T(1,128)S(1)}, u32[]{:S(2)}, u32[]{:S(2)}) collective-permute-start(f32[1,128]{1,0:T(1,128)S(1)} %scale_first.1.refs_2_), channel_id=1, source_target_pairs={{0,16},{2,18},{4,20},{6,22},{8,24},{10,26},{12,28},{14,30},{16,0},... | collective-permute-start | bytes 1544 | tf_op jit(solution)/shard_map/ppermute | solution.py:449
  19.4 4.6 %collective-permute-start.8 = (f32[1,128]{1,0:T(1,128)S(1)}, f32[1,128]{1,0:T(1,128)S(1)}, u32[]{:S(2)}, u32[]{:S(2)}) collective-permute-start(f32[1,128]{1,0:T(1,128)S(1)} %scale_first.1.refs_2_), channel_id=1, source_target_pairs={{0,8},{2,10},{4,12},{6,14},{8,0},{10,2},{12,4},{14,6},{16,24},{18,... | collective-permute-start | bytes 1544 | tf_op jit(solution)/shard_map/ppermute | solution.py:449
  22.9 1.3 %collective-permute-start.9 = (f32[1,128]{1,0:T(1,128)S(1)}, f32[1,128]{1,0:T(1,128)S(1)}, u32[]{:S(2)}, u32[]{:S(2)}) collective-permute-start(f32[1,128]{1,0:T(1,128)S(1)} %scale_first.1.refs_2_), channel_id=1, source_target_pairs={{0,6},{2,0},{4,2},{6,4},{8,14},{10,8},{12,10},{14,12},{16,22},{18,... | collective-permute-start | bytes 1544 | tf_op jit(solution)/shard_map/ppermute | solution.py:449
  22.9 3.0 %collective-permute-start.10 = (f32[1,128]{1,0:T(1,128)S(1)}, f32[1,128]{1,0:T(1,128)S(1)}, u32[]{:S(2)}, u32[]{:S(2)}) collective-permute-start(f32[1,128]{1,0:T(1,128)S(1)} %scale_first.1.refs_2_), channel_id=1, source_target_pairs={{0,2},{2,4},{4,6},{6,0},{8,10},{10,12},{12,14},{14,8},{16,18},{18,... | collective-permute-start | bytes 1544 | tf_op jit(solution)/shard_map/ppermute | solution.py:449
  31.4 3.6 %collective-permute-start.11 = (f32[8,1536]{1,0:T(8,128)S(1)}, f32[8,1536]{1,0:T(8,128)S(1)}, u32[]{:S(2)}, u32[]{:S(2)}) collective-permute-start(f32[8,1536]{1,0:T(8,128)S(1)} %get-tuple-element.37), channel_id=1, source_target_pairs={{0,2},{2,4},{4,6},{6,0},{8,10},{10,12},{12,14},{14,8},{16,18},{18,... | collective-permute-start | bytes 147464 | tf_op jit(solution)/shard_map/ppermute | solution.py:449
  35.0 19.2 %collective-permute-start.13 = (bf16[576,128]{1,0:T(8,128)(2,1)S(1)}, bf16[576,128]{1,0:T(8,128)(2,1)S(1)}, u32[]{:S(2)}, u32[]{:S(2)}) collective-permute-start(bf16[576,128]{1,0:T(8,128)(2,1)S(1)} %get-tuple-element.39), channel_id=1, source_target_pairs={{0,8},{2,10},{4,12},{6,14},{8,0},{10,2},{12,4},{14,6},{16,24},{18,... | collective-permute-start | bytes 442376 | tf_op jit(solution)/shard_map/ppermute | solution.py:449
  36.3 21.0 %collective-permute-start.14 = (bf16[384,128]{1,0:T(8,128)(2,1)S(1)}, bf16[384,128]{1,0:T(8,128)(2,1)S(1)}, u32[]{:S(2)}, u32[]{:S(2)}) collective-permute-start(bf16[384,128]{1,0:T(8,128)(2,1)S(1)} %get-tuple-element.40), channel_id=1, source_target_pairs={{0,16},{2,18},{4,20},{6,22},{8,24},{10,26},{12,28},{14,30},{16,0},... | collective-permute-start | bytes 294920 | tf_op jit(solution)/shard_map/ppermute | solution.py:449
  37.4 19.8 %collective-permute-start.15 = (bf16[384,128]{1,0:T(8,128)(2,1)S(1)}, bf16[384,128]{1,0:T(8,128)(2,1)S(1)}, u32[]{:S(2)}, u32[]{:S(2)}) collective-permute-start(bf16[384,128]{1,0:T(8,128)(2,1)S(1)} %get-tuple-element.41), channel_id=1, source_target_pairs={{0,16},{2,18},{4,20},{6,22},{8,24},{10,26},{12,28},{14,30},{16,0},... | collective-permute-start | bytes 294920 | tf_op jit(solution)/shard_map/ppermute | solution.py:449
  39.2 10.6 %collective-permute-start.12 = (f32[8,1536]{1,0:T(8,128)S(1)}, f32[8,1536]{1,0:T(8,128)S(1)}, u32[]{:S(2)}, u32[]{:S(2)}) collective-permute-start(f32[8,1536]{1,0:T(8,128)S(1)} %get-tuple-element.38), channel_id=1, source_target_pairs={{0,6},{2,0},{4,2},{6,4},{8,14},{10,8},{12,10},{14,12},{16,22},{18,... | collective-permute-start | bytes 147464 | tf_op jit(solution)/shard_map/ppermute | solution.py:449
  39.2 7.0 %collective-permute-start.16 = (f32[1,128]{1,0:T(1,128)S(1)}, f32[1,128]{1,0:T(1,128)S(1)}, u32[]{:S(2)}, u32[]{:S(2)}) collective-permute-start(f32[1,128]{1,0:T(1,128)S(1)} %get-tuple-element.43), channel_id=1, source_target_pairs={{0,16},{2,18},{4,20},{6,22},{8,24},{10,26},{12,28},{14,30},{16,0},... | collective-permute-start | bytes 1544 | tf_op jit(solution)/shard_map/ppermute | solution.py:449
  46.2 3.5 %collective-permute-start.17 = (f32[1,128]{1,0:T(1,128)S(1)}, f32[1,128]{1,0:T(1,128)S(1)}, u32[]{:S(2)}, u32[]{:S(2)}) collective-permute-start(f32[1,128]{1,0:T(1,128)S(1)} %get-tuple-element.44), channel_id=1, source_target_pairs={{0,8},{2,10},{4,12},{6,14},{8,0},{10,2},{12,4},{14,6},{16,24},{18,... | collective-permute-start | bytes 1544 | tf_op jit(solution)/shard_map/ppermute | solution.py:449
  49.8 4.5 %collective-permute-start.18 = (f32[1,128]{1,0:T(1,128)S(1)}, f32[1,128]{1,0:T(1,128)S(1)}, u32[]{:S(2)}, u32[]{:S(2)}) collective-permute-start(f32[1,128]{1,0:T(1,128)S(1)} %scale_second.1.refs_2_), channel_id=1, source_target_pairs={{0,16},{2,18},{4,20},{6,22},{8,24},{10,26},{12,28},{14,30},{16,0},... | collective-permute-start | bytes 1544 | tf_op jit(solution)/shard_map/ppermute | solution.py:449
  51.2 4.3 %collective-permute-start.19 = (f32[1,128]{1,0:T(1,128)S(1)}, f32[1,128]{1,0:T(1,128)S(1)}, u32[]{:S(2)}, u32[]{:S(2)}) collective-permute-start(f32[1,128]{1,0:T(1,128)S(1)} %scale_second.1.refs_2_), channel_id=1, source_target_pairs={{0,8},{2,10},{4,12},{6,14},{8,0},{10,2},{12,4},{14,6},{16,24},{18,... | collective-permute-start | bytes 1544 | tf_op jit(solution)/shard_map/ppermute | solution.py:449
  54.3 1.3 %collective-permute-start.20 = (f32[1,128]{1,0:T(1,128)S(1)}, f32[1,128]{1,0:T(1,128)S(1)}, u32[]{:S(2)}, u32[]{:S(2)}) collective-permute-start(f32[1,128]{1,0:T(1,128)S(1)} %scale_second.1.refs_2_), channel_id=1, source_target_pairs={{0,6},{2,0},{4,2},{6,4},{8,14},{10,8},{12,10},{14,12},{16,22},{18,... | collective-permute-start | bytes 1544 | tf_op jit(solution)/shard_map/ppermute | solution.py:449
  54.3 3.0 %collective-permute-start.21 = (f32[1,128]{1,0:T(1,128)S(1)}, f32[1,128]{1,0:T(1,128)S(1)}, u32[]{:S(2)}, u32[]{:S(2)}) collective-permute-start(f32[1,128]{1,0:T(1,128)S(1)} %scale_second.1.refs_2_), channel_id=1, source_target_pairs={{0,2},{2,4},{4,6},{6,0},{8,10},{10,12},{12,14},{14,8},{16,18},{18,... | collective-permute-start | bytes 1544 | tf_op jit(solution)/shard_map/ppermute | solution.py:449
  55.4 15.9 %copy-start = (bf16[16,16]{1,0:T(8,128)(2,1)S(1)}, bf16[16,16]{1,0:T(8,128)(2,1)}, u32[]{:S(2)}) copy-start(bf16[16,16]{1,0:T(8,128)(2,1)} %panel.1) | copy-start | bytes 1540
  60.2 11.0 %collective-permute-start.22 = (bf16[1536,128]{1,0:T(8,128)(2,1)S(1)}, bf16[1536,128]{1,0:T(8,128)(2,1)S(1)}, u32[]{:S(2)}, u32[]{:S(2)}) collective-permute-start(bf16[1536,128]{1,0:T(8,128)(2,1)S(1)} %filtered.1.own), channel_id=1, source_target_pairs={{0,1},{1,0},{2,3},{3,2},{4,5},{5,4},{6,7},{7,6},{8,9},{9,8},{10,11... | collective-permute-start | bytes 1179656 | tf_op jit(solution)/shard_map/ppermute | solution.py:593
  (1 other events, 5.2 us)

commit v4 on v3

--- a/solution.py
+++ b/solution.py
@@ -8,7 +8,6 @@
 from jax.sharding import PartitionSpec as P
 
 RADIUS = 6
-EARLY = 3
 COEFFS = (
     -5369.0 / 1800.0,
     12.0 / 7.0,
@@ -65,6 +64,8 @@
         self.first = dom_count // self.plane
         self.table = self.owned * nproj * self.no
         self.slab = self.cy * self.no
+        self.fold = self.flat // self.table
+        self.butterfly = self.first == 2 and self.second == 2 and dom_count <= 2 * self.fold
         assert self.no == 8
 
     def faces(self, dom, dim):
@@ -78,18 +79,21 @@
             return [(0, place > 0), (1, place < extent - 1)]
         return []
 
-    def face_rows(self, dim, layers=RADIUS):
-        rows = layers * self.slab if dim == 0 else self.cx * layers * self.no
+    def face_rows(self, dim):
+        rows = RADIUS * self.slab if dim == 0 else self.cx * RADIUS * self.no
         return [rows] * len(self.faces(0, dim))
 
-    def links(self):
-        out = []
+    def steps(self, dom):
+        out = [0]
         for extent, stride in ((self.first, self.plane), (self.second, self.third), (self.third, 1)):
             if extent == 2:
-                out.append((stride, 2, 0))
+                out.append((1 - 2 * (dom // stride % 2)) * stride)
             elif extent > 2:
-                out.extend([(stride, extent, 1), (stride, extent, -1)])
+                out.extend([stride, -stride])
         return out
+
+    def slots(self):
+        return len(self.steps(0))
 
 
 def layer(side, length, j):
@@ -102,17 +106,13 @@
     return start if isinstance(start, int) else pl.multiple_of(start, unit)
 
 
-def pack_x(g, dom, v_ref, first, last, refs):
-    for (side, _), out in zip(g.faces(dom, 0), refs):
-        for j in range(first, last):
+def pack_faces(g, dom, v_ref, x_refs, y_refs):
+    for (side, _), out in zip(g.faces(dom, 0), x_refs):
+        for j in range(RADIUS):
             at = aligned(layer(side, g.cx, j) * g.slab, g.slab)
-            to = (j - first) * g.slab
-            out[to : to + g.slab, :] = v_ref[pl.ds(at, g.slab), :].astype(BF16)
-
-
-def pack_y(g, dom, v_ref, refs):
+            out[j * g.slab : (j + 1) * g.slab, :] = v_ref[pl.ds(at, g.slab), :].astype(BF16)
     size = RADIUS * g.no
-    for (side, _), out in zip(g.faces(dom, 1), refs):
+    for (side, _), out in zip(g.faces(dom, 1), y_refs):
         for x in range(g.cx):
             pieces = []
             for j in range(RADIUS):
@@ -121,26 +121,44 @@
             out[x * size : (x + 1) * size, :] = jnp.concatenate(pieces, axis=0).astype(BF16)
 
 
-def pack_ends(g, v_ref, low_ref, high_ref):
+def end_columns(g, dom):
     row, col = iota((16, g.cz), 0), iota((16, g.cz), 1)
-    place = jnp.where(row < 8, row, g.cz - 1 - (row - 8))
-    used = (row % 8) < RADIUS
-    pick = jnp.where((place == col) & used, 1.0, 0.0).astype(BF16)
+    odd = dom % 2
+    side = jnp.where(row < 8, 1 - odd, odd)
+    return jnp.where(side == 1, g.cz - 1 - col, col), row
+
+
+def pack_ends(g, dom, v_ref, first_ref, second_ref):
+    inward, row = end_columns(g, dom)
+    pick = jnp.where((inward == row % 8) & (row % 8 < RADIUS), 1.0, 0.0).astype(BF16)
     pick = jnp.concatenate([pick, pick], axis=1)
     for x in range(g.cx):
         rows = slice(x * g.slab, (x + 1) * g.slab)
         both = jnp.concatenate(split2(v_ref[rows, :]), axis=1)
         ends = lax.dot_general(pick, both, NT, preferred_element_type=F32)
-        low_ref[:, rows] = ends[:8]
-        high_ref[:, rows] = ends[8:]
+        first_ref[:, rows] = ends[:8]
+        second_ref[:, rows] = ends[8:]
+
+
+def put_table(g, message, table):
+    for n in range(g.dom_count):
+        at = RADIUS + n // g.fold
+        lanes = n % g.fold * g.table
+        message[at : at + 1, lanes : lanes + g.table] = table[n : n + 1, :]
+
+
+def get_table(g, message):
+    rows = []
+    for n in range(g.dom_count):
+        at = RADIUS + n // g.fold
+        lanes = n % g.fold * g.table
+        rows.append(message[at : at + 1, lanes : lanes + g.table])
+    return jnp.concatenate(rows, axis=0)
 
 
 def fill_lut(g, dom, lut):
-    lut[g.plane + dom] = 0
-    for number, (stride, _, step) in enumerate(g.links()):
-        if step == 0:
-            step = 1 - 2 * (dom // stride % 2)
-        lut[g.plane + dom + step * stride] = (number + 1) * g.owned
+    for number, step in enumerate(g.steps(dom)):
+        lut[g.plane + dom + step] = number * g.owned
 
 
 def column_of(g, lut, atom):
@@ -148,7 +166,7 @@
     return lut[owner + g.plane] + (atom - owner * g.owned)
 
 
-def inner_tables(g, v_ref, projf, blk, atom, lut, sums):
+def inner_tables(g, dom, v_ref, projf, blk, atom, lut, sums, table):
     size = g.nproj * g.no
 
     def step(i, _):
@@ -169,7 +187,10 @@
     both = jnp.concatenate(split2(total), axis=1)
     ones = jnp.ones((8, both.shape[1]), BF16)
     summed = lax.dot_general(ones, both, NT, preferred_element_type=F32)
-    return [summed[0:1, n * g.table : (n + 1) * g.table] for n in range(len(g.links()) + 1)]
+    table[...] = jnp.zeros(table.shape, F32)
+    for number, step in enumerate(g.steps(dom)):
+        owner = jnp.clip(dom + step, 0, g.dom_count - 1)
+        table[pl.ds(owner, 1), :] += summed[0:1, number * g.table : (number + 1) * g.table]
 
 
 def clear(sums):
@@ -178,8 +199,8 @@
 
 
 def first_kernel(g, orb_hbm, proj_hbm, pot_hbm, v_ref, projf, pot, *refs):
-    nx = len(g.face_rows(0))
-    orb, proj, sem = refs[nx:]
+    nx, ny = len(g.face_rows(0)), len(g.face_rows(1))
+    orb, proj, sem = refs[nx + ny :]
     copies = [
         pltpu.make_async_copy(orb_hbm, orb, sem.at[0]),
         pltpu.make_async_copy(proj_hbm, proj, sem.at[1]),
@@ -191,7 +212,7 @@
     copies[0].wait()
     for r in range(g.rows):
         v_ref[r * g.no : (r + 1) * g.no, :] = orb[pl.ds(r, g.no, stride=g.rows), :]
-    pack_x(g, dom, v_ref, 0, EARLY, refs[:nx])
+    pack_faces(g, dom, v_ref, refs[:nx], refs[nx : nx + ny])
     copies[1].wait()
     projf[...] = proj[...].astype(F32)
     copies[2].wait()
@@ -204,41 +225,30 @@
     ]
 
 
-def tables_kernel(g, v_ref, projf, blk_hbm, atom_hbm, *refs):
-    nlinks = len(g.links())
-    rows_out = refs[: nlinks - 1]
-    low, high = refs[nlinks - 1 : nlinks + 1]
-    blk, atom, lut, sem = refs[nlinks + 1 : nlinks + 5]
-    sums = refs[nlinks + 5 :]
+def tables_kernel(g, v_ref, projf, blk_hbm, atom_hbm, table, first, second, blk, atom, lut, sem, *sums):
     copies = entry_copies(blk_hbm, atom_hbm, blk, atom, sem)
     for copy in copies:
         copy.start()
     dom = lax.axis_index("dom")
     fill_lut(g, dom, lut)
     clear(sums)
-    pack_ends(g, v_ref, low, high)
+    pack_ends(g, dom, v_ref, first, second)
     for copy in copies:
         copy.wait()
-    rows = inner_tables(g, v_ref, projf, blk, atom, lut, sums)
-    for out, row in zip(rows_out, rows):
-        out[...] = row
-    high[RADIUS : RADIUS + 1, : g.table] = rows[-2]
-    low[RADIUS : RADIUS + 1, : g.table] = rows[-1]
-
-
-def rest_kernel(g, v_ref, after, *refs):
-    nx = len(g.face_rows(0))
-    dom = lax.axis_index("dom")
-    pack_x(g, dom, v_ref, EARLY, RADIUS, refs[:nx])
-    pack_y(g, dom, v_ref, refs[nx:])
-
-
-def scale_kernel(g, energy, low, high, *refs):
-    rows, out = refs[:-1], refs[-1]
-    total = low[RADIUS : RADIUS + 1, : g.table] + high[RADIUS : RADIUS + 1, : g.table]
-    for row in rows:
-        total = total + row[...]
-    out[...] = total * energy[pl.ds(lax.axis_index("dom"), 1), :]
+    inner_tables(g, dom, v_ref, projf, blk, atom, lut, sums, table)
+    if g.butterfly:
+        put_table(g, first, table)
+
+
+def join_kernel(g, table, first_in, second, table_out, second_out):
+    table_out[...] = table[...] + get_table(g, first_in)
+    second_out[...] = second[...]
+    put_table(g, second_out, table_out)
+
+
+def unpack_kernel(g, table, second_in, *refs):
+    table_out = refs[-1]
+    table_out[...] = table[...] + get_table(g, second_in)
 
 
 def inside_kernel(g, scale, subtract, v_ref, pot, *refs):
@@ -279,11 +289,10 @@
 
 
 def add_ends(g, dom, scale, acc, low, high, out):
-    place = dom % g.third
-    row, col = iota((16, g.cz), 0), iota((16, g.cz), 1)
-    inward = jnp.where(row < 8, col, g.cz - 1 - col)
-    present = jnp.where(row < 8, place, g.third - 1 - place) > 0
-    coef = jnp.where((row % 8 < RADIUS) & present, weight_at(inward + row % 8 + 1, scale), 0.0)
+    inward, row = end_columns(g, dom)
+    middle = (dom % g.third > 0) & (dom % g.third < g.third - 1)
+    present = (row % 8 < RADIUS) & ((row < 8) | middle)
+    coef = jnp.where(present, weight_at(inward + row % 8 + 1, scale), 0.0)
     c_high, c_low = split2(coef)
     coefs = jnp.concatenate([c_high, c_high, c_low, c_low], axis=0)
     for x in range(g.cx):
@@ -293,15 +302,12 @@
         out[rows, :] = acc[rows, :] + lax.dot_general(halo, coefs, TN, preferred_element_type=F32)
 
 
-def add_x_faces(g, dom, scale, early_refs, late_refs, out):
+def add_x_faces(g, dom, scale, face_refs, out):
     unit = 2 * g.no
-    for (side, present), early, late in zip(g.faces(dom, 0), early_refs, late_refs):
+    for (side, present), face in zip(g.faces(dom, 0), face_refs):
         for y in range(0, g.cy, 2):
-            part = []
-            for j in range(RADIUS):
-                face, at = (early, j) if j < EARLY else (late, j - EARLY)
-                at = at * g.slab + y * g.no
-                part.append(flag(present) * face[at : at + unit, :].astype(F32))
+            starts = [j * g.slab + y * g.no for j in range(RADIUS)]
+            part = [flag(present) * face[at : at + unit, :].astype(F32) for at in starts]
             for i in range(RADIUS):
                 at = aligned(layer(side, g.cx, i) * g.slab + y * g.no, unit)
                 total = out[pl.ds(at, unit), :]
@@ -323,11 +329,18 @@
                 out[pl.ds(at, g.no), :] = total
 
 
-def add_nonlocal(g, scale, rows, projf, blk, atom, lut, spread, out):
+def add_nonlocal(g, dom, scale, tables, energy, projf, blk, atom, lut, spread, out):
     size = g.nproj * g.no
     lanes = g.table
-    count = len(rows)
-    rows = rows + [jnp.zeros((8 - count, lanes), F32)]
+    count = g.slots()
+    rows = []
+    for step in g.steps(dom):
+        owner = pl.ds(jnp.clip(dom + step, 0, g.dom_count - 1), 1)
+        total = tables[0][owner, :]
+        for table in tables[1:]:
+            total = total + table[owner, :]
+        rows.append(total * energy[owner, :])
+    rows.append(jnp.zeros((8 - count, lanes), F32))
     scaled = (scale / HALF_WIDTH) * jnp.concatenate(rows, axis=0)
     high = scaled.astype(BF16)
     rest = scaled - high.astype(F32)
@@ -362,15 +375,15 @@
 
 
 def sides_kernel(g, scale, acc, low, high, *refs):
-    y_refs, out = refs[:-1], refs[-1]
+    nx = len(g.face_rows(0))
+    out = refs[-1]
     dom = lax.axis_index("dom")
     add_ends(g, dom, scale, acc, low, high, out)
-    add_y_faces(g, dom, scale, y_refs, out)
-
-
-def finish(g, scale, acc, projf, blk_hbm, atom_hbm, inputs, out, scratch):
-    nx = len(g.face_rows(0))
-    early, late, rows = inputs[:nx], inputs[nx : 2 * nx], inputs[2 * nx :]
+    add_x_faces(g, dom, scale, refs[:nx], out)
+    add_y_faces(g, dom, scale, refs[nx:-1], out)
+
+
+def finish(g, scale, acc, projf, energy, blk_hbm, atom_hbm, tables, out, scratch):
     blk, atom, lut, sem, spread = scratch
     copies = entry_copies(blk_hbm, atom_hbm, blk, atom, sem)
     for copy in copies:
@@ -378,26 +391,24 @@
     dom = lax.axis_index("dom")
     fill_lut(g, dom, lut)
     out[...] = acc[...]
-    add_x_faces(g, dom, scale, early, late, out)
     for copy in copies:
         copy.wait()
-    add_nonlocal(g, scale, [row[...] for row in rows], projf, blk, atom, lut, spread, out)
+    add_nonlocal(g, dom, scale, tables, energy, projf, blk, atom, lut, spread, out)
     return dom
 
 
-def middle_kernel(g, acc, projf, blk_hbm, atom_hbm, *refs):
-    nx = len(g.face_rows(0))
-    nin = 2 * nx + len(g.links()) + 1
-    u_ref = refs[nin]
-    x_out = refs[nin + 1 : nin + 1 + nx]
-    dom = finish(g, 1.0, acc, projf, blk_hbm, atom_hbm, refs[:nin], u_ref, refs[nin + 1 + nx :])
-    pack_x(g, dom, u_ref, 0, EARLY, x_out)
-
-
-def last_kernel(g, acc, projf, blk_hbm, atom_hbm, *refs):
-    nin = 2 * len(g.face_rows(0)) + len(g.links()) + 1
-    filtered, work = refs[nin : nin + 2]
-    finish(g, 2.0, acc, projf, blk_hbm, atom_hbm, refs[:nin], work, refs[nin + 2 :])
+def middle_kernel(g, nt, acc, projf, energy, blk_hbm, atom_hbm, *refs):
+    nx, ny = len(g.face_rows(0)), len(g.face_rows(1))
+    tables, u_ref = refs[:nt], refs[nt]
+    faces = refs[nt + 1 : nt + 1 + nx + ny]
+    scratch = refs[nt + 1 + nx + ny :]
+    dom = finish(g, 1.0, acc, projf, energy, blk_hbm, atom_hbm, tables, u_ref, scratch)
+    pack_faces(g, dom, u_ref, faces[:nx], faces[nx:])
+
+
+def last_kernel(g, nt, acc, projf, energy, blk_hbm, atom_hbm, *refs):
+    tables, filtered, work = refs[:nt], refs[nt], refs[nt + 1]
+    finish(g, 2.0, acc, projf, energy, blk_hbm, atom_hbm, tables, work, refs[nt + 2 :])
     filtered[...] = work[...].astype(BF16)
 
 
@@ -425,10 +436,7 @@
             out[at : at + group, :] = result[j * group : (j + 1) * group, :]
 
 
-def call(kernel, name, out_shape, scratch, flops, args, specs):
-    size = sum(a.size * a.dtype.itemsize for a in args)
-    outs = out_shape if isinstance(out_shape, (tuple, list)) else [out_shape]
-    size += sum(o.size * o.dtype.itemsize for o in outs)
+def call(kernel, name, out_shape, scratch, args, specs):
     return pl.pallas_call(
         kernel,
         name=name,
@@ -437,7 +445,7 @@
         out_specs=jax.tree.map(lambda _: VMEM, out_shape),
         scratch_shapes=scratch,
         compiler_params=pltpu.CompilerParams(vmem_limit_bytes=48 * 1024 * 1024),
-        cost_estimate=pl.CostEstimate(flops=flops, bytes_accessed=size, transcendentals=0),
+        cost_estimate=pl.CostEstimate(flops=1000, bytes_accessed=1000, transcendentals=0),
     )(*args)
 
 
@@ -470,135 +478,109 @@
     proj = in_hbm(projectors)
     blk, atom = in_hbm(entry_block), in_hbm(entry_atom)
     field = jax.ShapeDtypeStruct((g.flat, g.cz), F32)
-    x_early = [jax.ShapeDtypeStruct((n, g.cz), BF16) for n in g.face_rows(0, EARLY)]
-    x_late = [jax.ShapeDtypeStruct((n, g.cz), BF16) for n in g.face_rows(0, RADIUS - EARLY)]
-    y_faces = [jax.ShapeDtypeStruct((n, g.cz), BF16) for n in g.face_rows(1)]
-    nx, ny = len(x_early), len(y_faces)
-    links = g.links()
+    faces = [jax.ShapeDtypeStruct((n, g.cz), BF16) for n in g.face_rows(0) + g.face_rows(1)]
+    nx = len(g.face_rows(0))
     ends = jax.ShapeDtypeStruct((8, g.flat), F32)
-    row = jax.ShapeDtypeStruct((1, g.table), F32)
-    slots = (len(links) + 1) * g.table
+    table = jax.ShapeDtypeStruct((g.dom_count, g.table), F32)
     entries = [
         pltpu.SMEM((g.ent,), jnp.int32),
         pltpu.SMEM((g.ent,), jnp.int32),
         pltpu.SMEM((g.dom_count + 2 * g.plane,), jnp.int32),
         pltpu.SemaphoreType.DMA((2,)),
     ]
+    slots = g.slots() * g.table
     sums = [pltpu.VMEM((slots, g.cz), F32) for _ in range(4)]
     spread = pltpu.VMEM((slots, g.cz), F32)
     energy = jnp.repeat(kb_energy.reshape(g.dom_count, g.owned * g.nproj), g.no, axis=1)
-
-    def swap_x(faces):
-        return swap_faces(g, faces, g.plane, g.first)
-
-    def neighbours(which, values, early):
-        x1 = swap_x(early)
-        *rows, low, high = call(
+    indices = range(g.dom_count)
+    first_pairs = [(i, i ^ 1) for i in indices]
+    second_pairs = [(i, i - i % g.third + g.third - 1 - i % g.third) for i in indices]
+
+    def neighbours(which, values, sent):
+        from_x = swap_faces(g, sent[:nx], g.plane, g.first)
+        from_y = swap_faces(g, sent[nx:], g.third, g.second)
+        part, first, second = call(
             functools.partial(tables_kernel, g),
             "tables_" + which,
-            [row] * (len(links) - 1) + [ends, ends],
+            [table, ends, ends],
             [*entries, *sums],
-            10_000_000,
             [values, projf, blk, atom],
             [VMEM] * 2 + [HBM] * 2,
         )
-        low, high = shift(g, high, 1, g.third, 1), shift(g, low, 1, g.third, -1)
-        for n, (stride, extent, step) in enumerate(links[:-2]):
-            rows[n + 1] = shift(g, rows[n + 1], stride, extent, step or 1)
-        later = call(
-            functools.partial(rest_kernel, g),
-            "rest_" + which,
-            [*x_late, *y_faces],
-            [],
-            1_000_000,
-            [values, low],
-            [VMEM] * 2,
-        )
-        x2 = swap_x(later[:nx])
-        from_y = swap_faces(g, later[nx:], g.third, g.second)
-        scaled = call(
-            functools.partial(scale_kernel, g),
-            "scale_" + which,
-            row,
-            [],
-            1_000_000,
-            [energy, low, high, *rows],
-            [VMEM] * (3 + len(rows)),
-        )
-        rows = [scaled]
-        for stride, extent, step in links:
-            rows.append(shift(g, scaled, stride, extent, -step or 1))
-        return low, high, from_y, [*x1, *x2, *rows]
-
-    def sides(scale, which, acc, low, high, from_y):
+        first = lax.ppermute(first, "dom", first_pairs)
+        if g.butterfly:
+            part, second = call(
+                functools.partial(join_kernel, g),
+                "join_" + which,
+                [table, ends],
+                [],
+                [part, first, second],
+                [VMEM] * 3,
+            )
+        second = lax.ppermute(second, "dom", second_pairs)
+        if g.butterfly:
+            part = call(
+                functools.partial(unpack_kernel, g),
+                "unpack_" + which,
+                table,
+                [],
+                [part, second, *from_x, *from_y],
+                [VMEM] * (2 + len(sent)),
+            )
+            part = part + shift(g, part, g.third, 2, 1)
+            tables = [part, shift(g, part, g.plane, 2, 1)]
+        else:
+            tables = [lax.psum(part, "dom")]
+        return tables, [first, second, *from_x, *from_y]
+
+    def sides(scale, which, acc, received):
         return call(
             functools.partial(sides_kernel, g, scale),
             "sides_" + which,
             field,
             [],
-            10_000_000,
-            [acc, low, high, *from_y],
-            [VMEM] * (3 + ny),
+            [acc, *received],
+            [VMEM] * (1 + len(received)),
         )
 
-    v, projf, pot, *early = call(
+    v, projf, pot, *sent = call(
         functools.partial(first_kernel, g),
-        "early_first",
-        [field, jax.ShapeDtypeStruct(proj.shape, F32), jax.ShapeDtypeStruct(pot.shape, F32), *x_early],
+        "faces_first",
+        [field, jax.ShapeDtypeStruct(proj.shape, F32), jax.ShapeDtypeStruct(pot.shape, F32), *faces],
         [pltpu.VMEM(orb.shape, F32), pltpu.VMEM(proj.shape, BF16), pltpu.SemaphoreType.DMA((3,))],
-        10_000_000,
         [orb, proj, pot],
         [HBM] * 3,
     )
-    low, high, from_y, others = neighbours("first", v, early)
+    tables, received = neighbours("first", v, sent)
     acc = call(
-        functools.partial(inside_kernel, g, 1.0, False),
-        "inside_first",
-        field,
-        [],
-        200_000_000,
-        [v, pot],
-        [VMEM, VMEM],
-    )
-    acc = sides(1.0, "first", acc, low, high, from_y)
-    u, *early = call(
-        functools.partial(middle_kernel, g),
+        functools.partial(inside_kernel, g, 1.0, False), "inside_first", field, [], [v, pot], [VMEM] * 2
+    )
+    acc = sides(1.0, "first", acc, received)
+    nt = len(tables)
+    u, *sent = call(
+        functools.partial(middle_kernel, g, nt),
         "middle",
-        [field, *x_early],
+        [field, *faces],
         [*entries, spread],
-        10_000_000,
-        [acc, projf, blk, atom, *others],
-        [VMEM] * 2 + [HBM] * 2 + [VMEM] * len(others),
-    )
-    low, high, from_y, others = neighbours("second", u, early)
+        [acc, projf, energy, blk, atom, *tables],
+        [VMEM] * 3 + [HBM] * 2 + [VMEM] * nt,
+    )
+    tables, received = neighbours("second", u, sent)
     acc = call(
-        functools.partial(inside_kernel, g, 2.0, True),
-        "inside_second",
-        field,
-        [],
-        200_000_000,
-        [u, pot, v],
-        [VMEM, VMEM, VMEM],
-    )
-    acc = sides(2.0, "second", acc, low, high, from_y)
+        functools.partial(inside_kernel, g, 2.0, True), "inside_second", field, [], [u, pot, v], [VMEM] * 3
+    )
+    acc = sides(2.0, "second", acc, received)
     filtered = call(
-        functools.partial(last_kernel, g),
+        functools.partial(last_kernel, g, nt),
         "filtered",
         jax.ShapeDtypeStruct((g.flat, g.cz), BF16),
         [pltpu.VMEM((g.flat, g.cz), F32), *entries, spread],
-        10_000_000,
-        [acc, projf, blk, atom, *others],
-        [VMEM] * 2 + [HBM] * 2 + [VMEM] * len(others),
+        [acc, projf, energy, blk, atom, *tables],
+        [VMEM] * 3 + [HBM] * 2 + [VMEM] * nt,
     )
     other = lax.ppermute(filtered, "band", [(0, 1), (1, 0)])
     rotated = call(
-        functools.partial(rotate_kernel, g),
-        "rotate",
-        field,
-        [],
-        200_000_000,
-        [filtered, other, panel],
-        [VMEM] * 3,
+        functools.partial(rotate_kernel, g), "rotate", field, [], [filtered, other, panel], [VMEM] * 3
     )
     return rotated.reshape(orbitals.shape)
 

time: 73 us -> 60.3 us (0.83)
  waiting for transfers between devices: 32 us -> 24.2 us
  starting transfers between devices: 22.6 us -> 16.8 us
  Pallas kernels: 17.7 us -> 18.5 us
    ppermute x22 -> x8, waiting for transfers between devices: 22.5 us -> 9.57 us  [shift(): return lax.ppermute(array, 'dom', pairs)]
    ppermute x22 -> x8, starting transfers between devices: 21.1 us -> 12.4 us  [shift(): return lax.ppermute(array, 'dom', pairs)]
    ppermute x0 -> x4, waiting for transfers between devices: none -> 7.27 us  [the longest x2 4.84 us: neighbours(): second = lax.ppermute(second, 'dom', second_pairs)]
    ppermute x0 -> x4, starting transfers between devices: none -> 2.84 us  [the longest x2 2.69 us: neighbours(): second = lax.ppermute(second, 'dom', second_pairs)]
    ppermute x1, waiting for transfers between devices: 9.49 us -> 7.39 us  [shards(): other = lax.ppermute(filtered, 'band', [(0, 1), (1, 0)])]
    pallas_call x14, Pallas kernels: 17.7 us -> 18.5 us  [call(): pl.pallas_call(kernel, name=name, out_shape=out_shape, in_specs=specs, ou...]
  transfers between devices with their start and end apart: 23 -> 13, of which waited for: 11 -> 9; matrix products, arithmetic and copies ran while one was open for 0% -> 0% of each run, Pallas kernels for 5% -> 15%
where the time goes in v4:
time: 60.3 us; the launch traced here: 60 us
  waiting for transfers between devices  24.2 us (40%)
  Pallas kernels  18.5 us (31%)
  starting transfers between devices  16.8 us (28%)
    pallas_call x14, Pallas kernels, call(): pl.pallas_call(kernel, name=name, out_shape=out_shape, in_specs=specs, ou...  18.5 us
    ppermute x8, starting transfers between devices, shift(): return lax.ppermute(array, 'dom', pairs)  12.4 us
    ppermute x8, waiting for transfers between devices, shift(): return lax.ppermute(array, 'dom', pairs)  9.57 us
    ppermute x1, waiting for transfers between devices, shards(): other = lax.ppermute(filtered, 'band', [(0, 1), (1, 0)])  7.39 us
    ppermute x2, waiting for transfers between devices, neighbours(): second = lax.ppermute(second, 'dom', second_pairs)  4.84 us
    ppermute x2, starting transfers between devices, neighbours(): second = lax.ppermute(second, 'dom', second_pairs)  2.69 us
    ppermute x2, waiting for transfers between devices, neighbours(): first = lax.ppermute(first, 'dom', first_pairs)  2.43 us
    ppermute x1, starting transfers between devices, shards(): other = lax.ppermute(filtered, 'band', [(0, 1), (1, 0)])  1.55 us
  transfers between devices with their start and end apart: 13, of which 9 were waited for; matrix products, arithmetic and copies ran while one was open for 0% of the time, Pallas kernels for 15%

profile of v4, /device:TPU:0, one launch (start us, length us, event | category | flops | bytes accessed | tf_op | source)
XLA Modules:
  0.0 60.0 jit_solution(9214657406101748660)
XLA Ops:
  0.0 1.7 %faces_first.1 = (f32[1536,128]{1,0:T(8,128)S(1)}, f32[256,4,128]{2,1,0:T(4,128)S(1)}, f32[192,128]{1,0:T(8,128)S(1)}, bf16[768,128]{1,0:T(8,128)(2,1)S(1)}, bf16[576,128]{1,0:T(8,128)(2,1)S(1)}) custom-call(f32[1536,128]{1,0:T(8,128)} %bitcast.5, bf16[256,4,128]{2,1,0:T(4,128)(2,1)} %proj_hbm.1, f32[192,128]{1,0:T(8,128)} %bitcast.6), custom_call_target="tpu_custom_call" | custom-call | flops 1000 | bytes 1000 | tf_op jit(solution)/shard_map/faces_first/pallas_call | solution.py:440
  1.7 4.1 %collective-permute-start.2 = (bf16[768,128]{1,0:T(8,128)(2,1)S(1)}, bf16[768,128]{1,0:T(8,128)(2,1)S(1)}, u32[]{:S(2)}, u32[]{:S(2)}) collective-permute-start(bf16[768,128]{1,0:T(8,128)(2,1)S(1)} %get-tuple-element.30), channel_id=1, source_target_pairs={{0,16},{2,18},{4,20},{6,22},{8,24},{10,26},{12,28},{14,30},{16,0},... | collective-permute-start | bytes 589832 | tf_op jit(solution)/shard_map/ppermute | solution.py:457
  5.8 1.6 %collective-permute-start.3 = (bf16[576,128]{1,0:T(8,128)(2,1)S(1)}, bf16[576,128]{1,0:T(8,128)(2,1)S(1)}, u32[]{:S(2)}, u32[]{:S(2)}) collective-permute-start(bf16[576,128]{1,0:T(8,128)(2,1)S(1)} %get-tuple-element.31), channel_id=1, source_target_pairs={{0,8},{2,10},{4,12},{6,14},{8,0},{10,2},{12,4},{14,6},{16,24},{18,... | collective-permute-start | bytes 442376 | tf_op jit(solution)/shard_map/ppermute | solution.py:457
  7.4 2.7 %tables_first.1 = (f32[16,128]{1,0:T(8,128)S(1)}, f32[8,1536]{1,0:T(8,128)S(1)}, f32[8,1536]{1,0:T(8,128)S(1)}) custom-call(f32[1536,128]{1,0:T(8,128)S(1)} %get-tuple-element.23.v_ref.refs_0_, f32[256,4,128]{2,1,0:T(4,128)S(1)} %get-tuple-element.25.projf, s32[256]{0:T(256)} %blk_hbm.7, s32[256]{0:T(256)} %atom_hbm.7), custom_call_target="tpu_custom_call" | custom-call | flops 1000 | bytes 1000 | tf_op jit(solution)/shard_map/tables_first/pallas_call | solution.py:440
  10.2 1.2 %collective-permute-done.first_in.low = f32[8,1536]{1,0:T(8,128)S(1)} collective-permute-done((f32[8,1536]{1,0:T(8,128)S(1)}, f32[8,1536]{1,0:T(8,128)S(1)}, u32[]{:S(2)}, u32[]{:S(2)}) %collective-permute-start) | collective-permute-done | bytes 49184 | tf_op jit(solution)/shard_map/ppermute | solution.py:510
  11.4 1.3 %collective-permute-start.1 = (f32[8,1536]{1,0:T(8,128)S(1)}, f32[8,1536]{1,0:T(8,128)S(1)}, u32[]{:S(2)}, u32[]{:S(2)}) collective-permute-start(f32[8,1536]{1,0:T(8,128)S(1)} %get-tuple-element.29), channel_id=1, source_target_pairs={{0,6},{2,4},{4,2},{6,0},{8,14},{10,12},{12,10},{14,8},{16,22},{18,... | collective-permute-start | bytes 147464 | tf_op jit(solution)/shard_map/ppermute | solution.py:520
  12.8 2.4 %collective-permute-done.1.high.second_in = f32[8,1536]{1,0:T(8,128)S(1)} collective-permute-done((f32[8,1536]{1,0:T(8,128)S(1)}, f32[8,1536]{1,0:T(8,128)S(1)}, u32[]{:S(2)}, u32[]{:S(2)}) %collective-permute-start.1) | collective-permute-done | bytes 49184 | tf_op jit(solution)/shard_map/ppermute | solution.py:520
  16.1 2.8 %collective-permute-done.4 = f32[16,128]{1,0:T(8,128)S(1)} collective-permute-done((f32[16,128]{1,0:T(8,128)S(1)}, f32[16,128]{1,0:T(8,128)S(1)}, u32[]{:S(2)}, u32[]{:S(2)}) %collective-permute-start.4) | collective-permute-done | bytes 8224 | tf_op jit(solution)/shard_map/ppermute | solution.py:457
  18.9 1.8 %collective-permute-start.5 = (f32[16,128]{1,0:T(8,128)S(1)}, f32[16,128]{1,0:T(8,128)S(1)}, u32[]{:S(2)}, u32[]{:S(2)}) collective-permute-start(f32[16,128]{1,0:T(8,128)S(1)} %add.6.refs_0_), channel_id=1, source_target_pairs={{0,16},{2,18},{4,20},{6,22},{8,24},{10,26},{12,28},{14,30},{16,0},... | collective-permute-start | bytes 24584 | tf_op jit(solution)/shard_map/ppermute | solution.py:457
  20.8 0.9 %inside_first.1.acc = f32[1536,128]{1,0:T(8,128)S(1)} custom-call(f32[1536,128]{1,0:T(8,128)S(1)} %get-tuple-element.23.v_ref.refs_0_, f32[192,128]{1,0:T(8,128)S(1)} %get-tuple-element.24.pot), custom_call_target="tpu_custom_call" | custom-call | flops 1000 | bytes 1000 | tf_op jit(solution)/shard_map/inside_first/pallas_call | solution.py:440
  23.5 3.1 %middle.1 = (f32[1536,128]{1,0:T(8,128)S(1)}, bf16[768,128]{1,0:T(8,128)(2,1)S(1)}, bf16[576,128]{1,0:T(8,128)(2,1)S(1)}) custom-call(f32[1536,128]{1,0:T(8,128)S(1)} %sides_first.1.acc, f32[256,4,128]{2,1,0:T(4,128)S(1)} %get-tuple-element.25.projf, f32[16,128]{1,0:T(8,128)S(1)} %copy.10.energy, s32[256]{0:T(256)} %blk_hbm.7, s32[256]{0:T(256)} %atom_hbm.7, ...), custom_call_target="tpu_custom_call" | custom-call | flops 1000 | bytes 1000 | tf_op jit(solution)/shard_map/middle/pallas_call | solution.py:440
  26.6 1.9 %collective-permute-start.8 = (bf16[768,128]{1,0:T(8,128)(2,1)S(1)}, bf16[768,128]{1,0:T(8,128)(2,1)S(1)}, u32[]{:S(2)}, u32[]{:S(2)}) collective-permute-start(bf16[768,128]{1,0:T(8,128)(2,1)S(1)} %get-tuple-element.38), channel_id=1, source_target_pairs={{0,16},{2,18},{4,20},{6,22},{8,24},{10,26},{12,28},{14,30},{16,0},... | collective-permute-start | bytes 589832 | tf_op jit(solution)/shard_map/ppermute | solution.py:457
  28.5 2.0 %collective-permute-start.9 = (bf16[576,128]{1,0:T(8,128)(2,1)S(1)}, bf16[576,128]{1,0:T(8,128)(2,1)S(1)}, u32[]{:S(2)}, u32[]{:S(2)}) collective-permute-start(bf16[576,128]{1,0:T(8,128)(2,1)S(1)} %get-tuple-element.39), channel_id=1, source_target_pairs={{0,8},{2,10},{4,12},{6,14},{8,0},{10,2},{12,4},{14,6},{16,24},{18,... | collective-permute-start | bytes 442376 | tf_op jit(solution)/shard_map/ppermute | solution.py:457
  30.6 2.7 %tables_second.1 = (f32[16,128]{1,0:T(8,128)S(1)}, f32[8,1536]{1,0:T(8,128)S(1)}, f32[8,1536]{1,0:T(8,128)S(1)}) custom-call(f32[1536,128]{1,0:T(8,128)S(1)} %get-tuple-element.33.v_ref, f32[256,4,128]{2,1,0:T(4,128)S(1)} %get-tuple-element.25.projf, s32[256]{0:T(256)} %blk_hbm.7, s32[256]{0:T(256)} %atom_hbm.7), custom_call_target="tpu_custom_call" | custom-call | flops 1000 | bytes 1000 | tf_op jit(solution)/shard_map/tables_second/pallas_call | solution.py:440
  33.3 1.2 %collective-permute-done.6.first_in.low = f32[8,1536]{1,0:T(8,128)S(1)} collective-permute-done((f32[8,1536]{1,0:T(8,128)S(1)}, f32[8,1536]{1,0:T(8,128)S(1)}, u32[]{:S(2)}, u32[]{:S(2)}) %collective-permute-start.6) | collective-permute-done | bytes 49184 | tf_op jit(solution)/shard_map/ppermute | solution.py:510
  34.6 1.3 %collective-permute-start.7 = (f32[8,1536]{1,0:T(8,128)S(1)}, f32[8,1536]{1,0:T(8,128)S(1)}, u32[]{:S(2)}, u32[]{:S(2)}) collective-permute-start(f32[8,1536]{1,0:T(8,128)S(1)} %get-tuple-element.37), channel_id=1, source_target_pairs={{0,6},{2,4},{4,2},{6,0},{8,14},{10,12},{12,10},{14,8},{16,22},{18,... | collective-permute-start | bytes 147464 | tf_op jit(solution)/shard_map/ppermute | solution.py:520
  35.9 2.4 %collective-permute-done.7.high.second_in = f32[8,1536]{1,0:T(8,128)S(1)} collective-permute-done((f32[8,1536]{1,0:T(8,128)S(1)}, f32[8,1536]{1,0:T(8,128)S(1)}, u32[]{:S(2)}, u32[]{:S(2)}) %collective-permute-start.7) | collective-permute-done | bytes 49184 | tf_op jit(solution)/shard_map/ppermute | solution.py:520
  38.4 3.6 %collective-permute-done.10 = f32[16,128]{1,0:T(8,128)S(1)} collective-permute-done((f32[16,128]{1,0:T(8,128)S(1)}, f32[16,128]{1,0:T(8,128)S(1)}, u32[]{:S(2)}, u32[]{:S(2)}) %collective-permute-start.10) | collective-permute-done | bytes 8224 | tf_op jit(solution)/shard_map/ppermute | solution.py:457
  42.4 1.0 %inside_second.1.acc = f32[1536,128]{1,0:T(8,128)S(1)} custom-call(f32[1536,128]{1,0:T(8,128)S(1)} %get-tuple-element.33.v_ref, f32[192,128]{1,0:T(8,128)S(1)} %get-tuple-element.24.pot, f32[1536,128]{1,0:T(8,128)S(1)} %get-tuple-element.23.v_ref.refs_0_), custom_call_target="tpu_custom_call" | custom-call | flops 1000 | bytes 1000 | tf_op jit(solution)/shard_map/inside_second/pallas_call | solution.py:440
  44.3 2.3 %collective-permute-done.11.refs_1_ = f32[16,128]{1,0:T(8,128)S(1)} collective-permute-done((f32[16,128]{1,0:T(8,128)S(1)}, f32[16,128]{1,0:T(8,128)S(1)}, u32[]{:S(2)}, u32[]{:S(2)}) %collective-permute-start.11) | collective-permute-done | bytes 8224 | tf_op jit(solution)/shard_map/ppermute | solution.py:457
  46.6 3.0 %filtered.1.own = bf16[1536,128]{1,0:T(8,128)(2,1)S(1)} custom-call(f32[1536,128]{1,0:T(8,128)S(1)} %sides_second.1.acc, f32[256,4,128]{2,1,0:T(4,128)S(1)} %get-tuple-element.25.projf, f32[16,128]{1,0:T(8,128)S(1)} %copy.10.energy, s32[256]{0:T(256)} %blk_hbm.7, s32[256]{0:T(256)} %atom_hbm.7, f32[16,128]{1,0:T(8,128)S(1)} %add.7.refs_0_, ...), custom_call_target="tpu_custom_call" | custom-call | flops 1000 | bytes 1000 | tf_op jit(solution)/shard_map/filtered/pallas_call | solution.py:440
  49.6 1.6 %collective-permute-start.12 = (bf16[1536,128]{1,0:T(8,128)(2,1)S(1)}, bf16[1536,128]{1,0:T(8,128)(2,1)S(1)}, u32[]{:S(2)}, u32[]{:S(2)}) collective-permute-start(bf16[1536,128]{1,0:T(8,128)(2,1)S(1)} %filtered.1.own), channel_id=1, source_target_pairs={{0,1},{1,0},{2,3},{3,2},{4,5},{5,4},{6,7},{7,6},{8,9},{9,8},{10,11... | collective-permute-start | bytes 1179656 | tf_op jit(solution)/shard_map/ppermute | solution.py:581
  51.2 7.4 %collective-permute-done.12.other = bf16[1536,128]{1,0:T(8,128)(2,1)S(1)} collective-permute-done((bf16[1536,128]{1,0:T(8,128)(2,1)S(1)}, bf16[1536,128]{1,0:T(8,128)(2,1)S(1)}, u32[]{:S(2)}, u32[]{:S(2)}) %collective-permute-start.12) | collective-permute-done | bytes 393248 | tf_op jit(solution)/shard_map/ppermute | solution.py:581
  58.6 1.5 %rotate.1 = f32[1536,128]{1,0:T(8,128)} custom-call(bf16[1536,128]{1,0:T(8,128)(2,1)S(1)} %filtered.1.own, bf16[1536,128]{1,0:T(8,128)(2,1)S(1)} %collective-permute-done.12.other, bf16[16,16]{1,0:T(8,128)(2,1)S(1)} %copy-done), custom_call_target="tpu_custom_call" | custom-call | flops 1000 | bytes 1000 | tf_op jit(solution)/shard_map/rotate/pallas_call | solution.py:440
  (27 shorter events, 4.1 us)
Async XLA Ops:
  1.7 13.4 %collective-permute-start.2 = (bf16[768,128]{1,0:T(8,128)(2,1)S(1)}, bf16[768,128]{1,0:T(8,128)(2,1)S(1)}, u32[]{:S(2)}, u32[]{:S(2)}) collective-permute-start(bf16[768,128]{1,0:T(8,128)(2,1)S(1)} %get-tuple-element.30), channel_id=1, source_target_pairs={{0,16},{2,18},{4,20},{6,22},{8,24},{10,26},{12,28},{14,30},{16,0},... | collective-permute-start | bytes 589832 | tf_op jit(solution)/shard_map/ppermute | solution.py:457
  5.8 9.3 %collective-permute-start.3 = (bf16[576,128]{1,0:T(8,128)(2,1)S(1)}, bf16[576,128]{1,0:T(8,128)(2,1)S(1)}, u32[]{:S(2)}, u32[]{:S(2)}) collective-permute-start(bf16[576,128]{1,0:T(8,128)(2,1)S(1)} %get-tuple-element.31), channel_id=1, source_target_pairs={{0,8},{2,10},{4,12},{6,14},{8,0},{10,2},{12,4},{14,6},{16,24},{18,... | collective-permute-start | bytes 442376 | tf_op jit(solution)/shard_map/ppermute | solution.py:457
  10.1 1.3 %collective-permute-start = (f32[8,1536]{1,0:T(8,128)S(1)}, f32[8,1536]{1,0:T(8,128)S(1)}, u32[]{:S(2)}, u32[]{:S(2)}) collective-permute-start(f32[8,1536]{1,0:T(8,128)S(1)} %get-tuple-element.26), channel_id=1, source_target_pairs={{0,2},{2,0},{4,6},{6,4},{8,10},{10,8},{12,14},{14,12},{16,18},{18,... | collective-permute-start | bytes 147464 | tf_op jit(solution)/shard_map/ppermute | solution.py:510
  11.4 3.8 %collective-permute-start.1 = (f32[8,1536]{1,0:T(8,128)S(1)}, f32[8,1536]{1,0:T(8,128)S(1)}, u32[]{:S(2)}, u32[]{:S(2)}) collective-permute-start(f32[8,1536]{1,0:T(8,128)S(1)} %get-tuple-element.29), channel_id=1, source_target_pairs={{0,6},{2,4},{4,2},{6,0},{8,14},{10,12},{12,10},{14,8},{16,22},{18,... | collective-permute-start | bytes 147464 | tf_op jit(solution)/shard_map/ppermute | solution.py:520
  15.2 0.7 %copy-start.1 = (f32[64,4]{0,1:T(4,128)S(1)}, f32[64,4]{0,1:T(4,128)}, u32[]{:S(2)}) copy-start(f32[64,4]{0,1:T(4,128)} %param.12) | copy-start | bytes 3076
  15.2 3.7 %collective-permute-start.4 = (f32[16,128]{1,0:T(8,128)S(1)}, f32[16,128]{1,0:T(8,128)S(1)}, u32[]{:S(2)}, u32[]{:S(2)}) collective-permute-start(f32[16,128]{1,0:T(8,128)S(1)} %unpack_first.1), channel_id=1, source_target_pairs={{0,8},{2,10},{4,12},{6,14},{8,0},{10,2},{12,4},{14,6},{16,24},{18,... | collective-permute-start | bytes 24584 | tf_op jit(solution)/shard_map/ppermute | solution.py:457
  18.9 4.5 %collective-permute-start.5 = (f32[16,128]{1,0:T(8,128)S(1)}, f32[16,128]{1,0:T(8,128)S(1)}, u32[]{:S(2)}, u32[]{:S(2)}) collective-permute-start(f32[16,128]{1,0:T(8,128)S(1)} %add.6.refs_0_), channel_id=1, source_target_pairs={{0,16},{2,18},{4,20},{6,22},{8,24},{10,26},{12,28},{14,30},{16,0},... | collective-permute-start | bytes 24584 | tf_op jit(solution)/shard_map/ppermute | solution.py:457
  26.6 11.7 %collective-permute-start.8 = (bf16[768,128]{1,0:T(8,128)(2,1)S(1)}, bf16[768,128]{1,0:T(8,128)(2,1)S(1)}, u32[]{:S(2)}, u32[]{:S(2)}) collective-permute-start(bf16[768,128]{1,0:T(8,128)(2,1)S(1)} %get-tuple-element.38), channel_id=1, source_target_pairs={{0,16},{2,18},{4,20},{6,22},{8,24},{10,26},{12,28},{14,30},{16,0},... | collective-permute-start | bytes 589832 | tf_op jit(solution)/shard_map/ppermute | solution.py:457
  28.5 9.8 %collective-permute-start.9 = (bf16[576,128]{1,0:T(8,128)(2,1)S(1)}, bf16[576,128]{1,0:T(8,128)(2,1)S(1)}, u32[]{:S(2)}, u32[]{:S(2)}) collective-permute-start(bf16[576,128]{1,0:T(8,128)(2,1)S(1)} %get-tuple-element.39), channel_id=1, source_target_pairs={{0,8},{2,10},{4,12},{6,14},{8,0},{10,2},{12,4},{14,6},{16,24},{18,... | collective-permute-start | bytes 442376 | tf_op jit(solution)/shard_map/ppermute | solution.py:457
  33.2 1.3 %collective-permute-start.6 = (f32[8,1536]{1,0:T(8,128)S(1)}, f32[8,1536]{1,0:T(8,128)S(1)}, u32[]{:S(2)}, u32[]{:S(2)}) collective-permute-start(f32[8,1536]{1,0:T(8,128)S(1)} %get-tuple-element.34), channel_id=1, source_target_pairs={{0,2},{2,0},{4,6},{6,4},{8,10},{10,8},{12,14},{14,12},{16,18},{18,... | collective-permute-start | bytes 147464 | tf_op jit(solution)/shard_map/ppermute | solution.py:510
  34.6 3.8 %collective-permute-start.7 = (f32[8,1536]{1,0:T(8,128)S(1)}, f32[8,1536]{1,0:T(8,128)S(1)}, u32[]{:S(2)}, u32[]{:S(2)}) collective-permute-start(f32[8,1536]{1,0:T(8,128)S(1)} %get-tuple-element.37), channel_id=1, source_target_pairs={{0,6},{2,4},{4,2},{6,0},{8,14},{10,12},{12,10},{14,8},{16,22},{18,... | collective-permute-start | bytes 147464 | tf_op jit(solution)/shard_map/ppermute | solution.py:520
  38.3 3.7 %collective-permute-start.10 = (f32[16,128]{1,0:T(8,128)S(1)}, f32[16,128]{1,0:T(8,128)S(1)}, u32[]{:S(2)}, u32[]{:S(2)}) collective-permute-start(f32[16,128]{1,0:T(8,128)S(1)} %unpack_second.1), channel_id=1, source_target_pairs={{0,8},{2,10},{4,12},{6,14},{8,0},{10,2},{12,4},{14,6},{16,24},{18,... | collective-permute-start | bytes 24584 | tf_op jit(solution)/shard_map/ppermute | solution.py:457
  42.1 4.5 %collective-permute-start.11 = (f32[16,128]{1,0:T(8,128)S(1)}, f32[16,128]{1,0:T(8,128)S(1)}, u32[]{:S(2)}, u32[]{:S(2)}) collective-permute-start(f32[16,128]{1,0:T(8,128)S(1)} %add.7.refs_0_), channel_id=1, source_target_pairs={{0,16},{2,18},{4,20},{6,22},{8,24},{10,26},{12,28},{14,30},{16,0},... | collective-permute-start | bytes 24584 | tf_op jit(solution)/shard_map/ppermute | solution.py:457
  44.3 14.3 %copy-start = (bf16[16,16]{1,0:T(8,128)(2,1)S(1)}, bf16[16,16]{1,0:T(8,128)(2,1)}, u32[]{:S(2)}) copy-start(bf16[16,16]{1,0:T(8,128)(2,1)} %panel.1) | copy-start | bytes 1540
  49.6 8.9 %collective-permute-start.12 = (bf16[1536,128]{1,0:T(8,128)(2,1)S(1)}, bf16[1536,128]{1,0:T(8,128)(2,1)S(1)}, u32[]{:S(2)}, u32[]{:S(2)}) collective-permute-start(bf16[1536,128]{1,0:T(8,128)(2,1)S(1)} %filtered.1.own), channel_id=1, source_target_pairs={{0,1},{1,0},{2,3},{3,2},{4,5},{5,4},{6,7},{7,6},{8,9},{9,8},{10,11... | collective-permute-start | bytes 1179656 | tf_op jit(solution)/shard_map/ppermute | solution.py:581

commit v5 on v4

--- a/solution.py
+++ b/solution.py
@@ -162,8 +162,11 @@
 
 
 def column_of(g, lut, atom):
-    owner = lax.div(atom, jnp.int32(g.owned))
-    return lut[owner + g.plane] + (atom - owner * g.owned)
+    if g.owned & (g.owned - 1):
+        owner = lax.div(atom, jnp.int32(g.owned))
+        return lut[owner + g.plane] + (atom - owner * g.owned)
+    owner = lax.shift_right_logical(atom, jnp.int32(g.owned.bit_length() - 1))
+    return lut[owner + g.plane] + (atom & (g.owned - 1))
 
 
 def inner_tables(g, dom, v_ref, projf, blk, atom, lut, sums, table):
@@ -198,9 +201,19 @@
         part[...] = jnp.zeros(part.shape, F32)
 
 
-def first_kernel(g, orb_hbm, proj_hbm, pot_hbm, v_ref, projf, pot, *refs):
-    nx, ny = len(g.face_rows(0)), len(g.face_rows(1))
-    orb, proj, sem = refs[nx + ny :]
+def entry_copies(blk_hbm, atom_hbm, blk, atom, sem):
+    copies = [
+        pltpu.make_async_copy(blk_hbm, blk, sem.at[0]),
+        pltpu.make_async_copy(atom_hbm, atom, sem.at[1]),
+    ]
+    for copy in copies:
+        copy.start()
+    return copies
+
+
+def first_kernel(g, orb_hbm, proj_hbm, pot_hbm, blk_hbm, atom_hbm, v_ref, projf, pot, table, *scratch):
+    orb, proj, sem, blk, atom, lut, entry_sem = scratch[:7]
+    sums = scratch[7:]
     copies = [
         pltpu.make_async_copy(orb_hbm, orb, sem.at[0]),
         pltpu.make_async_copy(proj_hbm, proj, sem.at[1]),
@@ -208,47 +221,34 @@
     ]
     for copy in copies:
         copy.start()
+    copies += entry_copies(blk_hbm, atom_hbm, blk, atom, entry_sem)
     dom = lax.axis_index("dom")
+    fill_lut(g, dom, lut)
+    clear(sums)
+    copies[1].wait()
+    projf[...] = proj[...].astype(F32)
     copies[0].wait()
     for r in range(g.rows):
         v_ref[r * g.no : (r + 1) * g.no, :] = orb[pl.ds(r, g.no, stride=g.rows), :]
-    pack_faces(g, dom, v_ref, refs[:nx], refs[nx : nx + ny])
-    copies[1].wait()
-    projf[...] = proj[...].astype(F32)
-    copies[2].wait()
-
-
-def entry_copies(blk_hbm, atom_hbm, blk, atom, sem):
-    return [
-        pltpu.make_async_copy(blk_hbm, blk, sem.at[0]),
-        pltpu.make_async_copy(atom_hbm, atom, sem.at[1]),
-    ]
-
-
-def tables_kernel(g, v_ref, projf, blk_hbm, atom_hbm, table, first, second, blk, atom, lut, sem, *sums):
-    copies = entry_copies(blk_hbm, atom_hbm, blk, atom, sem)
-    for copy in copies:
-        copy.start()
-    dom = lax.axis_index("dom")
-    fill_lut(g, dom, lut)
-    clear(sums)
-    pack_ends(g, dom, v_ref, first, second)
-    for copy in copies:
+    for copy in copies[2:]:
         copy.wait()
     inner_tables(g, dom, v_ref, projf, blk, atom, lut, sums, table)
+
+
+def pack_kernel(g, v_ref, *refs):
+    nx, ny = len(g.face_rows(0)), len(g.face_rows(1))
+    dom = lax.axis_index("dom")
     if g.butterfly:
-        put_table(g, first, table)
-
-
-def join_kernel(g, table, first_in, second, table_out, second_out):
-    table_out[...] = table[...] + get_table(g, first_in)
-    second_out[...] = second[...]
-    put_table(g, second_out, table_out)
-
-
-def unpack_kernel(g, table, second_in, *refs):
-    table_out = refs[-1]
-    table_out[...] = table[...] + get_table(g, second_in)
+        part, from_x, from_y, from_xy = refs[:4]
+        group = refs[-1]
+        group[...] = (part[...] + from_x[...]) + (from_y[...] + from_xy[...])
+        refs = refs[4:-1]
+    first, second = refs[:2]
+    pack_faces(g, dom, v_ref, refs[2 : 2 + nx], refs[2 + nx :])
+    pack_ends(g, dom, v_ref, first, second)
+    if g.butterfly:
+        put_table(g, first, group)
+        put_table(g, second, group)
 
 
 def inside_kernel(g, scale, subtract, v_ref, pot, *refs):
@@ -329,17 +329,14 @@
                 out[pl.ds(at, g.no), :] = total
 
 
-def add_nonlocal(g, dom, scale, tables, energy, projf, blk, atom, lut, spread, out):
+def add_nonlocal(g, dom, scale, table, energy, projf, blk, atom, lut, spread, out):
     size = g.nproj * g.no
     lanes = g.table
     count = g.slots()
     rows = []
     for step in g.steps(dom):
         owner = pl.ds(jnp.clip(dom + step, 0, g.dom_count - 1), 1)
-        total = tables[0][owner, :]
-        for table in tables[1:]:
-            total = total + table[owner, :]
-        rows.append(total * energy[owner, :])
+        rows.append(table[owner, :] * energy[owner, :])
     rows.append(jnp.zeros((8 - count, lanes), F32))
     scaled = (scale / HALF_WIDTH) * jnp.concatenate(rows, axis=0)
     high = scaled.astype(BF16)
@@ -374,41 +371,46 @@
     lax.fori_loop(0, g.ent // unroll, step, 0)
 
 
-def sides_kernel(g, scale, acc, low, high, *refs):
-    nx = len(g.face_rows(0))
-    out = refs[-1]
-    dom = lax.axis_index("dom")
-    add_ends(g, dom, scale, acc, low, high, out)
-    add_x_faces(g, dom, scale, refs[:nx], out)
-    add_y_faces(g, dom, scale, refs[nx:-1], out)
-
-
-def finish(g, scale, acc, projf, energy, blk_hbm, atom_hbm, tables, out, scratch):
-    blk, atom, lut, sem, spread = scratch
+def nonlocal_kernel(g, scale, acc, projf, energy, blk_hbm, atom_hbm, first, second, *refs):
+    out, table, blk, atom, lut, sem, spread = refs[-7:]
     copies = entry_copies(blk_hbm, atom_hbm, blk, atom, sem)
-    for copy in copies:
-        copy.start()
     dom = lax.axis_index("dom")
     fill_lut(g, dom, lut)
-    out[...] = acc[...]
+    if g.butterfly:
+        group, opposite = refs[:2]
+        table[...] = (group[...] + get_table(g, first)) + (get_table(g, second) + opposite[...])
+    else:
+        table[...] = refs[0][...]
+    add_ends(g, dom, scale, acc, first, second, out)
     for copy in copies:
         copy.wait()
-    add_nonlocal(g, dom, scale, tables, energy, projf, blk, atom, lut, spread, out)
-    return dom
-
-
-def middle_kernel(g, nt, acc, projf, energy, blk_hbm, atom_hbm, *refs):
+    add_nonlocal(g, dom, scale, table, energy, projf, blk, atom, lut, spread, out)
+
+
+def middle_kernel(g, acc, projf, blk_hbm, atom_hbm, *refs):
     nx, ny = len(g.face_rows(0)), len(g.face_rows(1))
-    tables, u_ref = refs[:nt], refs[nt]
-    faces = refs[nt + 1 : nt + 1 + nx + ny]
-    scratch = refs[nt + 1 + nx + ny :]
-    dom = finish(g, 1.0, acc, projf, energy, blk_hbm, atom_hbm, tables, u_ref, scratch)
-    pack_faces(g, dom, u_ref, faces[:nx], faces[nx:])
-
-
-def last_kernel(g, nt, acc, projf, energy, blk_hbm, atom_hbm, *refs):
-    tables, filtered, work = refs[:nt], refs[nt], refs[nt + 1]
-    finish(g, 2.0, acc, projf, energy, blk_hbm, atom_hbm, tables, work, refs[nt + 2 :])
+    faces = refs[: nx + ny]
+    u_ref, table, blk, atom, lut, sem = refs[nx + ny : nx + ny + 6]
+    sums = refs[nx + ny + 6 :]
+    copies = entry_copies(blk_hbm, atom_hbm, blk, atom, sem)
+    dom = lax.axis_index("dom")
+    fill_lut(g, dom, lut)
+    clear(sums)
+    u_ref[...] = acc[...]
+    add_x_faces(g, dom, 1.0, faces[:nx], u_ref)
+    add_y_faces(g, dom, 1.0, faces[nx:], u_ref)
+    for copy in copies:
+        copy.wait()
+    inner_tables(g, dom, u_ref, projf, blk, atom, lut, sums, table)
+
+
+def last_kernel(g, acc, *refs):
+    nx = len(g.face_rows(0))
+    filtered, work = refs[-2:]
+    dom = lax.axis_index("dom")
+    work[...] = acc[...]
+    add_x_faces(g, dom, 2.0, refs[:nx], work)
+    add_y_faces(g, dom, 2.0, refs[nx:-2], work)
     filtered[...] = work[...].astype(BF16)
 
 
@@ -493,90 +495,77 @@
     spread = pltpu.VMEM((slots, g.cz), F32)
     energy = jnp.repeat(kb_energy.reshape(g.dom_count, g.owned * g.nproj), g.no, axis=1)
     indices = range(g.dom_count)
-    first_pairs = [(i, i ^ 1) for i in indices]
-    second_pairs = [(i, i - i % g.third + g.third - 1 - i % g.third) for i in indices]
-
-    def neighbours(which, values, sent):
-        from_x = swap_faces(g, sent[:nx], g.plane, g.first)
-        from_y = swap_faces(g, sent[nx:], g.third, g.second)
-        part, first, second = call(
-            functools.partial(tables_kernel, g),
-            "tables_" + which,
-            [table, ends, ends],
-            [*entries, *sums],
-            [values, projf, blk, atom],
-            [VMEM] * 2 + [HBM] * 2,
-        )
-        first = lax.ppermute(first, "dom", first_pairs)
+
+    def swap(array, *strides):
+        pairs = [(i, i + sum(s * (1 - 2 * (i // s % 2)) for s in strides)) for i in indices]
+        return lax.ppermute(array, "dom", pairs)
+
+    def reverse(array):
+        pairs = [(i, i - i % g.third + g.third - 1 - i % g.third) for i in indices]
+        return lax.ppermute(array, "dom", pairs)
+
+    def local_and_ends(scale, which, values, prev, part):
+        inputs = [values]
+        outputs = [ends, ends, *faces]
         if g.butterfly:
-            part, second = call(
-                functools.partial(join_kernel, g),
-                "join_" + which,
-                [table, ends],
-                [],
-                [part, first, second],
-                [VMEM] * 3,
-            )
-        second = lax.ppermute(second, "dom", second_pairs)
-        if g.butterfly:
-            part = call(
-                functools.partial(unpack_kernel, g),
-                "unpack_" + which,
-                table,
-                [],
-                [part, second, *from_x, *from_y],
-                [VMEM] * (2 + len(sent)),
-            )
-            part = part + shift(g, part, g.third, 2, 1)
-            tables = [part, shift(g, part, g.plane, 2, 1)]
-        else:
-            tables = [lax.psum(part, "dom")]
-        return tables, [first, second, *from_x, *from_y]
-
-    def sides(scale, which, acc, received):
-        return call(
-            functools.partial(sides_kernel, g, scale),
-            "sides_" + which,
+            inputs += [part, swap(part, g.plane), swap(part, g.third), swap(part, g.plane, g.third)]
+            outputs.append(table)
+        acc = call(
+            functools.partial(inside_kernel, g, scale, len(prev) > 0),
+            "inside_" + which,
             field,
             [],
-            [acc, *received],
-            [VMEM] * (1 + len(received)),
+            [values, pot, *prev],
+            [VMEM] * (2 + len(prev)),
         )
-
-    v, projf, pot, *sent = call(
+        first, second, *sent = call(
+            functools.partial(pack_kernel, g), "pack_" + which, outputs, [], inputs, [VMEM] * len(inputs)
+        )
+        from_x = swap_faces(g, sent[:nx], g.plane, g.first)
+        from_y = swap_faces(g, sent[nx : len(faces)], g.third, g.second)
+        first, second = swap(first, 1), reverse(second)
+        tables = [sent[-1], swap(sent[-1], 2)] if g.butterfly else [lax.psum(part, "dom")]
+        acc = call(
+            functools.partial(nonlocal_kernel, g, scale),
+            "nonlocal_" + which,
+            field,
+            [pltpu.VMEM(table.shape, F32), *entries, spread],
+            [acc, projf, energy, blk, atom, first, second, *tables],
+            [VMEM] * 3 + [HBM] * 2 + [VMEM] * (2 + len(tables)),
+        )
+        return acc, from_x + from_y
+
+    v, projf, pot, part = call(
         functools.partial(first_kernel, g),
-        "faces_first",
-        [field, jax.ShapeDtypeStruct(proj.shape, F32), jax.ShapeDtypeStruct(pot.shape, F32), *faces],
-        [pltpu.VMEM(orb.shape, F32), pltpu.VMEM(proj.shape, BF16), pltpu.SemaphoreType.DMA((3,))],
-        [orb, proj, pot],
-        [HBM] * 3,
+        "tables_first",
+        [field, jax.ShapeDtypeStruct(proj.shape, F32), jax.ShapeDtypeStruct(pot.shape, F32), table],
+        [
+            pltpu.VMEM(orb.shape, F32),
+            pltpu.VMEM(proj.shape, BF16),
+            pltpu.SemaphoreType.DMA((3,)),
+            *entries,
+            *sums,
+        ],
+        [orb, proj, pot, blk, atom],
+        [HBM] * 5,
     )
-    tables, received = neighbours("first", v, sent)
-    acc = call(
-        functools.partial(inside_kernel, g, 1.0, False), "inside_first", field, [], [v, pot], [VMEM] * 2
+    acc, received = local_and_ends(1.0, "first", v, [], part)
+    u, part = call(
+        functools.partial(middle_kernel, g),
+        "tables_second",
+        [field, table],
+        [*entries, *sums],
+        [acc, projf, blk, atom, *received],
+        [VMEM] * 2 + [HBM] * 2 + [VMEM] * len(received),
     )
-    acc = sides(1.0, "first", acc, received)
-    nt = len(tables)
-    u, *sent = call(
-        functools.partial(middle_kernel, g, nt),
-        "middle",
-        [field, *faces],
-        [*entries, spread],
-        [acc, projf, energy, blk, atom, *tables],
-        [VMEM] * 3 + [HBM] * 2 + [VMEM] * nt,
-    )
-    tables, received = neighbours("second", u, sent)
-    acc = call(
-        functools.partial(inside_kernel, g, 2.0, True), "inside_second", field, [], [u, pot, v], [VMEM] * 3
-    )
-    acc = sides(2.0, "second", acc, received)
+    acc, received = local_and_ends(2.0, "second", u, [v], part)
     filtered = call(
-        functools.partial(last_kernel, g, nt),
+        functools.partial(last_kernel, g),
         "filtered",
         jax.ShapeDtypeStruct((g.flat, g.cz), BF16),
-        [pltpu.VMEM((g.flat, g.cz), F32), *entries, spread],
-        [acc, projf, energy, blk, atom, *tables],
-        [VMEM] * 3 + [HBM] * 2 + [VMEM] * nt,
+        [pltpu.VMEM((g.flat, g.cz), F32)],
+        [acc, *received],
+        [VMEM] * (1 + len(received)),
     )
     other = lax.ppermute(filtered, "band", [(0, 1), (1, 0)])
     rotated = call(

time: 60.3 us -> 61 us (1.012)
  starting transfers between devices: 16.8 us -> 21 us
  Pallas kernels: 18.5 us -> 15.2 us
    ppermute x4 -> x12, starting transfers between devices: 2.84 us -> 14.5 us  [the longest x10 12.2 us: swap(): return lax.ppermute(array, 'dom', pairs)]
    ppermute x8 -> x4, starting transfers between devices: 12.4 us -> 4.96 us  [shift(): return lax.ppermute(array, 'dom', pairs)]
    pallas_call x14 -> x10, Pallas kernels: 18.5 us -> 15.2 us  [call(): pl.pallas_call(kernel, name=name, out_shape=out_shape, in_specs=specs, ou...]
    ppermute x8 -> x4, waiting for transfers between devices: 9.57 us -> 7.95 us  [shift(): return lax.ppermute(array, 'dom', pairs)]
    ppermute x1, waiting for transfers between devices: 7.39 us -> 8.68 us  [shards(): other = lax.ppermute(filtered, 'band', [(0, 1), (1, 0)])]
    ppermute x4 -> x12, waiting for transfers between devices: 7.27 us -> 7.5 us  [the longest x10 7.48 us: swap(): return lax.ppermute(array, 'dom', pairs)]
  transfers between devices with their start and end apart: 13 -> 17, of which waited for: 9 -> 9; matrix products, arithmetic and copies ran while one was open for 0% -> 0% of each run, Pallas kernels for 15% -> 11%
where the time goes in v5:
time: 61 us; the launch traced here: 60.8 us
  waiting for transfers between devices  24.1 us (40%)
  starting transfers between devices  21 us (34%)
  Pallas kernels  15.2 us (25%)
    pallas_call x10, Pallas kernels, call(): pl.pallas_call(kernel, name=name, out_shape=out_shape, in_specs=specs, ou...  15.2 us
    ppermute x10, starting transfers between devices, swap(): return lax.ppermute(array, 'dom', pairs)  12.2 us
    ppermute x1, waiting for transfers between devices, shards(): other = lax.ppermute(filtered, 'band', [(0, 1), (1, 0)])  8.68 us
    ppermute x4, waiting for transfers between devices, shift(): return lax.ppermute(array, 'dom', pairs)  7.95 us
    ppermute x10, waiting for transfers between devices, swap(): return lax.ppermute(array, 'dom', pairs)  7.48 us
    ppermute x4, starting transfers between devices, shift(): return lax.ppermute(array, 'dom', pairs)  4.96 us
    ppermute x2, starting transfers between devices, reverse(): return lax.ppermute(array, 'dom', pairs)  2.26 us
    ppermute x1, starting transfers between devices, shards(): other = lax.ppermute(filtered, 'band', [(0, 1), (1, 0)])  1.56 us
  transfers between devices with their start and end apart: 17, of which 9 were waited for; matrix products, arithmetic and copies ran while one was open for 0% of the time, Pallas kernels for 11%

profile of v5, /device:TPU:0, one launch (start us, length us, event | category | flops | bytes accessed | tf_op | source)
XLA Modules:
  0.0 60.8 jit_solution(3538150389571254550)
XLA Ops:
  0.0 3.2 %tables_first.1 = (f32[1536,128]{1,0:T(8,128)S(1)}, f32[256,4,128]{2,1,0:T(4,128)S(1)}, f32[192,128]{1,0:T(8,128)S(1)}, f32[16,128]{1,0:T(8,128)S(1)}) custom-call(f32[1536,128]{1,0:T(8,128)} %bitcast.5, bf16[256,4,128]{2,1,0:T(4,128)(2,1)} %proj_hbm.1, f32[192,128]{1,0:T(8,128)} %bitcast.6, s32[256]{0:T(256)} %blk_hbm.7, s32[256]{0:T(256)} %atom_hbm.7), custom_call_target="tpu_custom_call" | custom-call | flops 1000 | bytes 1000 | tf_op jit(solution)/shard_map/tables_first/pallas_call | solution.py:442
  3.2 5.1 %collective-permute-start.2 = (f32[16,128]{1,0:T(8,128)S(1)}, f32[16,128]{1,0:T(8,128)S(1)}, u32[]{:S(2)}, u32[]{:S(2)}) collective-permute-start(f32[16,128]{1,0:T(8,128)S(1)} %get-tuple-element.24.refs_0_), channel_id=1, source_target_pairs={{0,24},{2,26},{4,28},{6,30},{8,16},{10,18},{12,20},{14,22},{16,8},... | collective-permute-start | bytes 24584 | tf_op jit(solution)/shard_map/ppermute | solution.py:501
  8.3 0.6 %collective-permute-start = (f32[16,128]{1,0:T(8,128)S(1)}, f32[16,128]{1,0:T(8,128)S(1)}, u32[]{:S(2)}, u32[]{:S(2)}) collective-permute-start(f32[16,128]{1,0:T(8,128)S(1)} %get-tuple-element.24.refs_0_), channel_id=1, source_target_pairs={{0,16},{2,18},{4,20},{6,22},{8,24},{10,26},{12,28},{14,30},{16,0},... | collective-permute-start | bytes 24584 | tf_op jit(solution)/shard_map/ppermute | solution.py:501
  9.2 0.7 %collective-permute-done.2.refs_3_ = f32[16,128]{1,0:T(8,128)S(1)} collective-permute-done((f32[16,128]{1,0:T(8,128)S(1)}, f32[16,128]{1,0:T(8,128)S(1)}, u32[]{:S(2)}, u32[]{:S(2)}) %collective-permute-start.2) | collective-permute-done | bytes 8224 | tf_op jit(solution)/shard_map/ppermute | solution.py:501
  10.0 2.0 %collective-permute-done.1.refs_2_ = f32[16,128]{1,0:T(8,128)S(1)} collective-permute-done((f32[16,128]{1,0:T(8,128)S(1)}, f32[16,128]{1,0:T(8,128)S(1)}, u32[]{:S(2)}, u32[]{:S(2)}) %collective-permute-start.1) | collective-permute-done | bytes 8224 | tf_op jit(solution)/shard_map/ppermute | solution.py:501
  12.0 0.9 %collective-permute-done.refs_1_ = f32[16,128]{1,0:T(8,128)S(1)} collective-permute-done((f32[16,128]{1,0:T(8,128)S(1)}, f32[16,128]{1,0:T(8,128)S(1)}, u32[]{:S(2)}, u32[]{:S(2)}) %collective-permute-start) | collective-permute-done | bytes 8224 | tf_op jit(solution)/shard_map/ppermute | solution.py:501
  13.2 1.5 %collective-permute-start.5 = (f32[16,128]{1,0:T(8,128)S(1)}, f32[16,128]{1,0:T(8,128)S(1)}, u32[]{:S(2)}, u32[]{:S(2)}) collective-permute-start(f32[16,128]{1,0:T(8,128)S(1)} %get-tuple-element.27.refs_0_), channel_id=1, source_target_pairs={{0,4},{2,6},{4,0},{6,2},{8,12},{10,14},{12,8},{14,10},{16,20},{18,... | collective-permute-start | bytes 24584 | tf_op jit(solution)/shard_map/ppermute | solution.py:501
  15.4 2.0 %collective-permute-start.7 = (bf16[576,128]{1,0:T(8,128)(2,1)S(1)}, bf16[576,128]{1,0:T(8,128)(2,1)S(1)}, u32[]{:S(2)}, u32[]{:S(2)}) collective-permute-start(bf16[576,128]{1,0:T(8,128)(2,1)S(1)} %get-tuple-element.29), channel_id=1, source_target_pairs={{0,8},{2,10},{4,12},{6,14},{8,0},{10,2},{12,4},{14,6},{16,24},{18,... | collective-permute-start | bytes 442376 | tf_op jit(solution)/shard_map/ppermute | solution.py:459
  17.4 0.9 %inside_first.1.acc = f32[1536,128]{1,0:T(8,128)S(1)} custom-call(f32[1536,128]{1,0:T(8,128)S(1)} %get-tuple-element.21.v_ref.refs_0_, f32[192,128]{1,0:T(8,128)S(1)} %get-tuple-element.22.pot), custom_call_target="tpu_custom_call" | custom-call | flops 1000 | bytes 1000 | tf_op jit(solution)/shard_map/inside_first/pallas_call | solution.py:442
  18.5 2.5 %nonlocal_first.1.acc = f32[1536,128]{1,0:T(8,128)S(1)} custom-call(f32[1536,128]{1,0:T(8,128)S(1)} %inside_first.1.acc, f32[256,4,128]{2,1,0:T(4,128)S(1)} %get-tuple-element.23.projf, f32[16,128]{1,0:T(8,128)S(1)} %copy.10.energy, s32[256]{0:T(256)} %blk_hbm.7, s32[256]{0:T(256)} %atom_hbm.7, f32[8,1536]{1,0:T(8,128)S(1)} %collective-permute-done.3.first, ...), custom_call_target="tpu_custom_call" | custom-call | flops 1000 | bytes 1000 | tf_op jit(solution)/shard_map/nonlocal_first/pallas_call | solution.py:442
  21.0 1.2 %collective-permute-done.7.refs_1_ = bf16[576,128]{1,0:T(8,128)(2,1)S(1)} collective-permute-done((bf16[576,128]{1,0:T(8,128)(2,1)S(1)}, bf16[576,128]{1,0:T(8,128)(2,1)S(1)}, u32[]{:S(2)}, u32[]{:S(2)}) %collective-permute-start.7) | collective-permute-done | bytes 147488 | tf_op jit(solution)/shard_map/ppermute | solution.py:459
  22.2 6.7 %collective-permute-done.6.refs_0_ = bf16[768,128]{1,0:T(8,128)(2,1)S(1)} collective-permute-done((bf16[768,128]{1,0:T(8,128)(2,1)S(1)}, bf16[768,128]{1,0:T(8,128)(2,1)S(1)}, u32[]{:S(2)}, u32[]{:S(2)}) %collective-permute-start.6) | collective-permute-done | bytes 196640 | tf_op jit(solution)/shard_map/ppermute | solution.py:459
  28.9 2.2 %tables_second.1 = (f32[1536,128]{1,0:T(8,128)S(1)}, f32[16,128]{1,0:T(8,128)S(1)}) custom-call(f32[1536,128]{1,0:T(8,128)S(1)} %nonlocal_first.1.acc, f32[256,4,128]{2,1,0:T(4,128)S(1)} %get-tuple-element.23.projf, s32[256]{0:T(256)} %blk_hbm.7, s32[256]{0:T(256)} %atom_hbm.7, bf16[768,128]{1,0:T(8,128)(2,1)S(1)} %collective-permute-done.6.refs_0_, ...), custom_call_target="tpu_custom_call" | custom-call | flops 1000 | bytes 1000 | tf_op jit(solution)/shard_map/tables_second/pallas_call | solution.py:442
  31.3 4.3 %collective-permute-start.8 = (f32[16,128]{1,0:T(8,128)S(1)}, f32[16,128]{1,0:T(8,128)S(1)}, u32[]{:S(2)}, u32[]{:S(2)}) collective-permute-start(f32[16,128]{1,0:T(8,128)S(1)} %get-tuple-element.31.refs_0_), channel_id=1, source_target_pairs={{0,16},{2,18},{4,20},{6,22},{8,24},{10,26},{12,28},{14,30},{16,0},... | collective-permute-start | bytes 24584 | tf_op jit(solution)/shard_map/ppermute | solution.py:501
  35.6 1.1 %collective-permute-done.10.refs_3_ = f32[16,128]{1,0:T(8,128)S(1)} collective-permute-done((f32[16,128]{1,0:T(8,128)S(1)}, f32[16,128]{1,0:T(8,128)S(1)}, u32[]{:S(2)}, u32[]{:S(2)}) %collective-permute-start.10) | collective-permute-done | bytes 8224 | tf_op jit(solution)/shard_map/ppermute | solution.py:501
  37.6 2.9 %collective-permute-start.14 = (bf16[768,128]{1,0:T(8,128)(2,1)S(1)}, bf16[768,128]{1,0:T(8,128)(2,1)S(1)}, u32[]{:S(2)}, u32[]{:S(2)}) collective-permute-start(bf16[768,128]{1,0:T(8,128)(2,1)S(1)} %get-tuple-element.35), channel_id=1, source_target_pairs={{0,16},{2,18},{4,20},{6,22},{8,24},{10,26},{12,28},{14,30},{16,0},... | collective-permute-start | bytes 589832 | tf_op jit(solution)/shard_map/ppermute | solution.py:459
  40.5 1.6 %collective-permute-start.12 = (f32[8,1536]{1,0:T(8,128)S(1)}, f32[8,1536]{1,0:T(8,128)S(1)}, u32[]{:S(2)}, u32[]{:S(2)}) collective-permute-start(f32[8,1536]{1,0:T(8,128)S(1)} %get-tuple-element.33), channel_id=1, source_target_pairs={{0,6},{2,4},{4,2},{6,0},{8,14},{10,12},{12,10},{14,8},{16,22},{18,... | collective-permute-start | bytes 147464 | tf_op jit(solution)/shard_map/ppermute | solution.py:505
  42.7 1.0 %inside_second.1.acc = f32[1536,128]{1,0:T(8,128)S(1)} custom-call(f32[1536,128]{1,0:T(8,128)S(1)} %get-tuple-element.30.v_ref, f32[192,128]{1,0:T(8,128)S(1)} %get-tuple-element.22.pot, f32[1536,128]{1,0:T(8,128)S(1)} %get-tuple-element.21.v_ref.refs_0_), custom_call_target="tpu_custom_call" | custom-call | flops 1000 | bytes 1000 | tf_op jit(solution)/shard_map/inside_second/pallas_call | solution.py:442
  43.6 2.2 %collective-permute-done.13.refs_1_ = f32[16,128]{1,0:T(8,128)S(1)} collective-permute-done((f32[16,128]{1,0:T(8,128)S(1)}, f32[16,128]{1,0:T(8,128)S(1)}, u32[]{:S(2)}, u32[]{:S(2)}) %collective-permute-start.13) | collective-permute-done | bytes 8224 | tf_op jit(solution)/shard_map/ppermute | solution.py:501
  45.8 2.5 %nonlocal_second.1.acc = f32[1536,128]{1,0:T(8,128)S(1)} custom-call(f32[1536,128]{1,0:T(8,128)S(1)} %inside_second.1.acc, f32[256,4,128]{2,1,0:T(4,128)S(1)} %get-tuple-element.23.projf, f32[16,128]{1,0:T(8,128)S(1)} %copy.10.energy, s32[256]{0:T(256)} %blk_hbm.7, s32[256]{0:T(256)} %atom_hbm.7, f32[8,1536]{1,0:T(8,128)S(1)} %collective-permute-done.11.first, ...), custom_call_target="tpu_custom_call" | custom-call | flops 1000 | bytes 1000 | tf_op jit(solution)/shard_map/nonlocal_second/pallas_call | solution.py:442
  48.4 0.7 %filtered.1.own = bf16[1536,128]{1,0:T(8,128)(2,1)S(1)} custom-call(f32[1536,128]{1,0:T(8,128)S(1)} %nonlocal_second.1.acc, bf16[768,128]{1,0:T(8,128)(2,1)S(1)} %collective-permute-done.14.refs_0_, bf16[576,128]{1,0:T(8,128)(2,1)S(1)} %collective-permute-done.15.refs_1_), custom_call_target="tpu_custom_call" | custom-call | flops 1000 | bytes 1000 | tf_op jit(solution)/shard_map/filtered/pallas_call | solution.py:442
  49.1 1.6 %collective-permute-start.16 = (bf16[1536,128]{1,0:T(8,128)(2,1)S(1)}, bf16[1536,128]{1,0:T(8,128)(2,1)S(1)}, u32[]{:S(2)}, u32[]{:S(2)}) collective-permute-start(bf16[1536,128]{1,0:T(8,128)(2,1)S(1)} %filtered.1.own), channel_id=1, source_target_pairs={{0,1},{1,0},{2,3},{3,2},{4,5},{5,4},{6,7},{7,6},{8,9},{9,8},{10,11... | collective-permute-start | bytes 1179656 | tf_op jit(solution)/shard_map/ppermute | solution.py:570
  50.6 8.7 %collective-permute-done.16.other = bf16[1536,128]{1,0:T(8,128)(2,1)S(1)} collective-permute-done((bf16[1536,128]{1,0:T(8,128)(2,1)S(1)}, bf16[1536,128]{1,0:T(8,128)(2,1)S(1)}, u32[]{:S(2)}, u32[]{:S(2)}) %collective-permute-start.16) | collective-permute-done | bytes 393248 | tf_op jit(solution)/shard_map/ppermute | solution.py:570
  59.3 1.5 %rotate.1 = f32[1536,128]{1,0:T(8,128)} custom-call(bf16[1536,128]{1,0:T(8,128)(2,1)S(1)} %filtered.1.own, bf16[1536,128]{1,0:T(8,128)(2,1)S(1)} %collective-permute-done.16.other, bf16[16,16]{1,0:T(8,128)(2,1)S(1)} %copy-done), custom_call_target="tpu_custom_call" | custom-call | flops 1000 | bytes 1000 | tf_op jit(solution)/shard_map/rotate/pallas_call | solution.py:442
  (29 shorter events, 2.9 us)
Async XLA Ops:
  0.0 9.0 %copy-start.1 = (f32[64,4]{0,1:T(4,128)S(1)}, f32[64,4]{0,1:T(4,128)}, u32[]{:S(2)}) copy-start(f32[64,4]{0,1:T(4,128)} %param.12) | copy-start | bytes 3076
  3.2 6.7 %collective-permute-start.2 = (f32[16,128]{1,0:T(8,128)S(1)}, f32[16,128]{1,0:T(8,128)S(1)}, u32[]{:S(2)}, u32[]{:S(2)}) collective-permute-start(f32[16,128]{1,0:T(8,128)S(1)} %get-tuple-element.24.refs_0_), channel_id=1, source_target_pairs={{0,24},{2,26},{4,28},{6,30},{8,16},{10,18},{12,20},{14,22},{16,8},... | collective-permute-start | bytes 24584 | tf_op jit(solution)/shard_map/ppermute | solution.py:501
  8.3 3.7 %collective-permute-start.1 = (f32[16,128]{1,0:T(8,128)S(1)}, f32[16,128]{1,0:T(8,128)S(1)}, u32[]{:S(2)}, u32[]{:S(2)}) collective-permute-start(f32[16,128]{1,0:T(8,128)S(1)} %get-tuple-element.24.refs_0_), channel_id=1, source_target_pairs={{0,8},{2,10},{4,12},{6,14},{8,0},{10,2},{12,4},{14,6},{16,24},{18,... | collective-permute-start | bytes 24584 | tf_op jit(solution)/shard_map/ppermute | solution.py:501
  8.3 4.5 %collective-permute-start = (f32[16,128]{1,0:T(8,128)S(1)}, f32[16,128]{1,0:T(8,128)S(1)}, u32[]{:S(2)}, u32[]{:S(2)}) collective-permute-start(f32[16,128]{1,0:T(8,128)S(1)} %get-tuple-element.24.refs_0_), channel_id=1, source_target_pairs={{0,16},{2,18},{4,20},{6,22},{8,24},{10,26},{12,28},{14,30},{16,0},... | collective-permute-start | bytes 24584 | tf_op jit(solution)/shard_map/ppermute | solution.py:501
  13.2 5.2 %collective-permute-start.5 = (f32[16,128]{1,0:T(8,128)S(1)}, f32[16,128]{1,0:T(8,128)S(1)}, u32[]{:S(2)}, u32[]{:S(2)}) collective-permute-start(f32[16,128]{1,0:T(8,128)S(1)} %get-tuple-element.27.refs_0_), channel_id=1, source_target_pairs={{0,4},{2,6},{4,0},{6,2},{8,12},{10,14},{12,8},{14,10},{16,20},{18,... | collective-permute-start | bytes 24584 | tf_op jit(solution)/shard_map/ppermute | solution.py:501
  14.8 3.7 %collective-permute-start.3 = (f32[8,1536]{1,0:T(8,128)S(1)}, f32[8,1536]{1,0:T(8,128)S(1)}, u32[]{:S(2)}, u32[]{:S(2)}) collective-permute-start(f32[8,1536]{1,0:T(8,128)S(1)} %get-tuple-element.25), channel_id=1, source_target_pairs={{0,2},{2,0},{4,6},{6,4},{8,10},{10,8},{12,14},{14,12},{16,18},{18,... | collective-permute-start | bytes 147464 | tf_op jit(solution)/shard_map/ppermute | solution.py:501
  14.8 3.7 %collective-permute-start.4 = (f32[8,1536]{1,0:T(8,128)S(1)}, f32[8,1536]{1,0:T(8,128)S(1)}, u32[]{:S(2)}, u32[]{:S(2)}) collective-permute-start(f32[8,1536]{1,0:T(8,128)S(1)} %get-tuple-element.26), channel_id=1, source_target_pairs={{0,6},{2,4},{4,2},{6,0},{8,14},{10,12},{12,10},{14,8},{16,22},{18,... | collective-permute-start | bytes 147464 | tf_op jit(solution)/shard_map/ppermute | solution.py:505
  15.4 6.8 %collective-permute-start.7 = (bf16[576,128]{1,0:T(8,128)(2,1)S(1)}, bf16[576,128]{1,0:T(8,128)(2,1)S(1)}, u32[]{:S(2)}, u32[]{:S(2)}) collective-permute-start(bf16[576,128]{1,0:T(8,128)(2,1)S(1)} %get-tuple-element.29), channel_id=1, source_target_pairs={{0,8},{2,10},{4,12},{6,14},{8,0},{10,2},{12,4},{14,6},{16,24},{18,... | collective-permute-start | bytes 442376 | tf_op jit(solution)/shard_map/ppermute | solution.py:459
  17.4 11.5 %collective-permute-start.6 = (bf16[768,128]{1,0:T(8,128)(2,1)S(1)}, bf16[768,128]{1,0:T(8,128)(2,1)S(1)}, u32[]{:S(2)}, u32[]{:S(2)}) collective-permute-start(bf16[768,128]{1,0:T(8,128)(2,1)S(1)} %get-tuple-element.28), channel_id=1, source_target_pairs={{0,16},{2,18},{4,20},{6,22},{8,24},{10,26},{12,28},{14,30},{16,0},... | collective-permute-start | bytes 589832 | tf_op jit(solution)/shard_map/ppermute | solution.py:459
  31.2 5.5 %collective-permute-start.10 = (f32[16,128]{1,0:T(8,128)S(1)}, f32[16,128]{1,0:T(8,128)S(1)}, u32[]{:S(2)}, u32[]{:S(2)}) collective-permute-start(f32[16,128]{1,0:T(8,128)S(1)} %get-tuple-element.31.refs_0_), channel_id=1, source_target_pairs={{0,24},{2,26},{4,28},{6,30},{8,16},{10,18},{12,20},{14,22},{16,8},... | collective-permute-start | bytes 24584 | tf_op jit(solution)/shard_map/ppermute | solution.py:501
  31.2 5.4 %collective-permute-start.9 = (f32[16,128]{1,0:T(8,128)S(1)}, f32[16,128]{1,0:T(8,128)S(1)}, u32[]{:S(2)}, u32[]{:S(2)}) collective-permute-start(f32[16,128]{1,0:T(8,128)S(1)} %get-tuple-element.31.refs_0_), channel_id=1, source_target_pairs={{0,8},{2,10},{4,12},{6,14},{8,0},{10,2},{12,4},{14,6},{16,24},{18,... | collective-permute-start | bytes 24584 | tf_op jit(solution)/shard_map/ppermute | solution.py:501
  31.3 5.9 %collective-permute-start.8 = (f32[16,128]{1,0:T(8,128)S(1)}, f32[16,128]{1,0:T(8,128)S(1)}, u32[]{:S(2)}, u32[]{:S(2)}) collective-permute-start(f32[16,128]{1,0:T(8,128)S(1)} %get-tuple-element.31.refs_0_), channel_id=1, source_target_pairs={{0,16},{2,18},{4,20},{6,22},{8,24},{10,26},{12,28},{14,30},{16,0},... | collective-permute-start | bytes 24584 | tf_op jit(solution)/shard_map/ppermute | solution.py:501
  37.6 10.8 %collective-permute-start.14 = (bf16[768,128]{1,0:T(8,128)(2,1)S(1)}, bf16[768,128]{1,0:T(8,128)(2,1)S(1)}, u32[]{:S(2)}, u32[]{:S(2)}) collective-permute-start(bf16[768,128]{1,0:T(8,128)(2,1)S(1)} %get-tuple-element.35), channel_id=1, source_target_pairs={{0,16},{2,18},{4,20},{6,22},{8,24},{10,26},{12,28},{14,30},{16,0},... | collective-permute-start | bytes 589832 | tf_op jit(solution)/shard_map/ppermute | solution.py:459
  40.5 7.8 %collective-permute-start.15 = (bf16[576,128]{1,0:T(8,128)(2,1)S(1)}, bf16[576,128]{1,0:T(8,128)(2,1)S(1)}, u32[]{:S(2)}, u32[]{:S(2)}) collective-permute-start(bf16[576,128]{1,0:T(8,128)(2,1)S(1)} %get-tuple-element.36), channel_id=1, source_target_pairs={{0,8},{2,10},{4,12},{6,14},{8,0},{10,2},{12,4},{14,6},{16,24},{18,... | collective-permute-start | bytes 442376 | tf_op jit(solution)/shard_map/ppermute | solution.py:459
  40.5 5.3 %collective-permute-start.11 = (f32[8,1536]{1,0:T(8,128)S(1)}, f32[8,1536]{1,0:T(8,128)S(1)}, u32[]{:S(2)}, u32[]{:S(2)}) collective-permute-start(f32[8,1536]{1,0:T(8,128)S(1)} %get-tuple-element.32), channel_id=1, source_target_pairs={{0,2},{2,0},{4,6},{6,4},{8,10},{10,8},{12,14},{14,12},{16,18},{18,... | collective-permute-start | bytes 147464 | tf_op jit(solution)/shard_map/ppermute | solution.py:501
  40.5 5.3 %collective-permute-start.12 = (f32[8,1536]{1,0:T(8,128)S(1)}, f32[8,1536]{1,0:T(8,128)S(1)}, u32[]{:S(2)}, u32[]{:S(2)}) collective-permute-start(f32[8,1536]{1,0:T(8,128)S(1)} %get-tuple-element.33), channel_id=1, source_target_pairs={{0,6},{2,4},{4,2},{6,0},{8,14},{10,12},{12,10},{14,8},{16,22},{18,... | collective-permute-start | bytes 147464 | tf_op jit(solution)/shard_map/ppermute | solution.py:505
  42.2 3.7 %collective-permute-start.13 = (f32[16,128]{1,0:T(8,128)S(1)}, f32[16,128]{1,0:T(8,128)S(1)}, u32[]{:S(2)}, u32[]{:S(2)}) collective-permute-start(f32[16,128]{1,0:T(8,128)S(1)} %get-tuple-element.34.refs_0_), channel_id=1, source_target_pairs={{0,4},{2,6},{4,0},{6,2},{8,12},{10,14},{12,8},{14,10},{16,20},{18,... | collective-permute-start | bytes 24584 | tf_op jit(solution)/shard_map/ppermute | solution.py:501
  48.3 11.0 %copy-start = (bf16[16,16]{1,0:T(8,128)(2,1)S(1)}, bf16[16,16]{1,0:T(8,128)(2,1)}, u32[]{:S(2)}) copy-start(bf16[16,16]{1,0:T(8,128)(2,1)} %panel.1) | copy-start | bytes 1540
  49.1 10.2 %collective-permute-start.16 = (bf16[1536,128]{1,0:T(8,128)(2,1)S(1)}, bf16[1536,128]{1,0:T(8,128)(2,1)S(1)}, u32[]{:S(2)}, u32[]{:S(2)}) collective-permute-start(bf16[1536,128]{1,0:T(8,128)(2,1)S(1)} %filtered.1.own), channel_id=1, source_target_pairs={{0,1},{1,0},{2,3},{3,2},{4,5},{5,4},{6,7},{7,6},{8,9},{9,8},{10,11... | collective-permute-start | bytes 1179656 | tf_op jit(solution)/shard_map/ppermute | solution.py:570

commit v6 on v5

--- a/solution.py
+++ b/solution.py
@@ -172,9 +172,12 @@
 def inner_tables(g, dom, v_ref, projf, blk, atom, lut, sums, table):
     size = g.nproj * g.no
 
+    unroll = 16
+
     def step(i, _):
-        for u, part in enumerate(sums):
-            e = i * len(sums) + u
+        for u in range(unroll):
+            part = sums[u % len(sums)]
+            e = i * unroll + u
             col = column_of(g, lut, atom[e])
             v = v_ref[pl.ds(pl.multiple_of(blk[e] * g.no, g.no), g.no), :]
             for p in range(g.nproj):
@@ -183,7 +186,7 @@
                 part[at, :] += v * coef
         return 0
 
-    lax.fori_loop(0, g.ent // len(sums), step, 0)
+    lax.fori_loop(0, g.ent // unroll, step, 0)
     total = sums[0][...]
     for part in sums[1:]:
         total = total + part[...]
@@ -235,14 +238,13 @@
     inner_tables(g, dom, v_ref, projf, blk, atom, lut, sums, table)
 
 
-def pack_kernel(g, v_ref, *refs):
+def pack_kernel(g, v_ref, after, *refs):
     nx, ny = len(g.face_rows(0)), len(g.face_rows(1))
     dom = lax.axis_index("dom")
     if g.butterfly:
-        part, from_x, from_y, from_xy = refs[:4]
-        group = refs[-1]
-        group[...] = (part[...] + from_x[...]) + (from_y[...] + from_xy[...])
-        refs = refs[4:-1]
+        tables, group = refs[0], refs[-1]
+        group[...] = (tables[0] + tables[1]) + (tables[2] + tables[3])
+        refs = refs[1:-1]
     first, second = refs[:2]
     pack_faces(g, dom, v_ref, refs[2 : 2 + nx], refs[2 + nx :])
     pack_ends(g, dom, v_ref, first, second)
@@ -350,7 +352,7 @@
     out_all = lax.dot_general(parts, ones, TN, preferred_element_type=F32)
     for number in range(count):
         spread[number * lanes : (number + 1) * lanes, :] = out_all[:, number * g.cz : (number + 1) * g.cz]
-    unroll = 4
+    unroll = 16
 
     def step(i, _):
         additions = []
@@ -404,17 +406,32 @@
     inner_tables(g, dom, u_ref, projf, blk, atom, lut, sums, table)
 
 
-def last_kernel(g, acc, *refs):
+def halves(g, dom):
+    if g.first != 2 or g.cx != 2 * RADIUS:
+        return [(0, g.cx)]
+    side = 1 - dom // g.plane
+    return [((1 - side) * RADIUS, RADIUS), (side * RADIUS, RADIUS)]
+
+
+def last_kernel(g, number, acc, *refs):
     nx = len(g.face_rows(0))
     filtered, work = refs[-2:]
+    refs = refs[:-2]
     dom = lax.axis_index("dom")
+    parts = halves(g, dom)
+    start, count = parts[number]
     work[...] = acc[...]
-    add_x_faces(g, dom, 2.0, refs[:nx], work)
-    add_y_faces(g, dom, 2.0, refs[nx:-2], work)
-    filtered[...] = work[...].astype(BF16)
-
-
-def rotate_kernel(g, own, other, panel, out):
+    if number == len(parts) - 1:
+        add_x_faces(g, dom, 2.0, refs[:nx], work)
+        refs = refs[nx:]
+    add_y_faces(g, dom, 2.0, refs, work)
+    at = aligned(start * g.slab, g.slab)
+    filtered[...] = work[pl.ds(at, count * g.slab), :].astype(BF16)
+
+
+def rotate_kernel(g, number, own, other, panel, *refs):
+    out_hbm, out, sem = refs[-3:]
+    start, count = halves(g, lax.axis_index("dom"))[number]
     band = lax.axis_index("band")
     group = 16
     span = group * g.no
@@ -429,25 +446,33 @@
     row, col = iota((span, 2 * span), 0), iota((span, 2 * span), 1)
     same = row % group == (col % span) // g.no
     weights = jnp.where(same, spread, 0.0).astype(BF16)
-    for n in range(g.rows // group):
+    size = count * g.cy
+    for n in range(size // group):
         rows = slice(n * span, (n + 1) * span)
         both = jnp.concatenate([own[rows, :], other[rows, :]], axis=0)
         result = lax.dot_general(weights, both, NN, preferred_element_type=F32)
         for j in range(g.no):
-            at = j * g.rows + n * group
-            out[at : at + group, :] = result[j * group : (j + 1) * group, :]
-
-
-def call(kernel, name, out_shape, scratch, args, specs):
+            out[j, n * group : (n + 1) * group, :] = result[j * group : (j + 1) * group, :]
+    copies = []
+    for j in range(g.no):
+        at = aligned(j * g.rows + start * g.cy, group)
+        copies.append(pltpu.make_async_copy(out.at[j], out_hbm.at[pl.ds(at, size), :], sem.at[j]))
+        copies[-1].start()
+    for copy in copies:
+        copy.wait()
+
+
+def call(kernel, name, out_shape, scratch, args, specs, **options):
     return pl.pallas_call(
         kernel,
         name=name,
         out_shape=out_shape,
         in_specs=specs,
-        out_specs=jax.tree.map(lambda _: VMEM, out_shape),
+        out_specs=options.pop("out_specs", jax.tree.map(lambda _: VMEM, out_shape)),
         scratch_shapes=scratch,
         compiler_params=pltpu.CompilerParams(vmem_limit_bytes=48 * 1024 * 1024),
         cost_estimate=pl.CostEstimate(flops=1000, bytes_accessed=1000, transcendentals=0),
+        **options,
     )(*args)
 
 
@@ -505,10 +530,11 @@
         return lax.ppermute(array, "dom", pairs)
 
     def local_and_ends(scale, which, values, prev, part):
-        inputs = [values]
+        inputs = [values, energy]
         outputs = [ends, ends, *faces]
         if g.butterfly:
-            inputs += [part, swap(part, g.plane), swap(part, g.third), swap(part, g.plane, g.third)]
+            groups = [[i + j * g.third for j in range(4)] for i in range(g.third)]
+            inputs.append(lax.all_gather(part, "dom", axis_index_groups=groups))
             outputs.append(table)
         acc = call(
             functools.partial(inside_kernel, g, scale, len(prev) > 0),
@@ -559,18 +585,32 @@
         [VMEM] * 2 + [HBM] * 2 + [VMEM] * len(received),
     )
     acc, received = local_and_ends(2.0, "second", u, [v], part)
-    filtered = call(
-        functools.partial(last_kernel, g),
-        "filtered",
-        jax.ShapeDtypeStruct((g.flat, g.cz), BF16),
-        [pltpu.VMEM((g.flat, g.cz), F32)],
-        [acc, *received],
-        [VMEM] * (1 + len(received)),
-    )
-    other = lax.ppermute(filtered, "band", [(0, 1), (1, 0)])
-    rotated = call(
-        functools.partial(rotate_kernel, g), "rotate", field, [], [filtered, other, panel], [VMEM] * 3
-    )
+    rotated = None
+    pieces = []
+    parts = halves(g, 0)
+    for number, (_, count) in enumerate(parts):
+        inputs = [acc, *received[nx:]] if number < len(parts) - 1 else [acc, *received]
+        filtered = call(
+            functools.partial(last_kernel, g, number),
+            "filtered_%d" % number,
+            jax.ShapeDtypeStruct((count * g.slab, g.cz), BF16),
+            [pltpu.VMEM((g.flat, g.cz), F32)],
+            inputs,
+            [VMEM] * len(inputs),
+        )
+        pieces.append((filtered, lax.ppermute(filtered, "band", [(0, 1), (1, 0)]), count))
+    for number, (filtered, other, count) in enumerate(pieces):
+        inputs = [filtered, other, panel] + ([] if rotated is None else [rotated])
+        rotated = call(
+            functools.partial(rotate_kernel, g, number),
+            "rotate_%d" % number,
+            field,
+            [pltpu.VMEM((g.no, count * g.cy, g.cz), F32), pltpu.SemaphoreType.DMA((g.no,))],
+            inputs,
+            [VMEM] * 3 + [HBM] * (len(inputs) - 3),
+            out_specs=HBM,
+            input_output_aliases={} if rotated is None else {3: 0},
+        )
     return rotated.reshape(orbitals.shape)
 
 

time: 61 us -> 66.7 us (1.093)
  blocking collectives: 0 us -> 27.9 us
  waiting for transfers between devices: 24.1 us -> 10.4 us
  starting transfers between devices: 21 us -> 11.4 us
  local copies, waits for them, and re-layouts: 0.31 us -> 0.98 us
    all_gather x0 -> x2, blocking collectives: none -> 27.9 us  [local_and_ends(): inputs.append(lax.all_gather(part, 'dom', axis_index_groups=groups))]
    ppermute x10 -> x4, starting transfers between devices: 12.2 us -> 1.82 us  [swap(): return lax.ppermute(array, 'dom', pairs)]
    ppermute x4, waiting for transfers between devices: 7.95 us -> 0.07 us  [shift(): return lax.ppermute(array, 'dom', pairs)]
    ppermute x10 -> x4, waiting for transfers between devices: 7.48 us -> 3.56 us  [swap(): return lax.ppermute(array, 'dom', pairs)]
    ppermute x1 -> x2, waiting for transfers between devices: 8.68 us -> 6.73 us  [shards(): lax.ppermute(filtered, 'band', [(0, 1), (1, 0)])]
    unnamed x5 -> x3, local copies, waits for them, and re-layouts: 0.11 us -> 0.78 us
    ppermute x1 -> x2, starting transfers between devices: 1.56 us -> 2.16 us  [shards(): lax.ppermute(filtered, 'band', [(0, 1), (1, 0)])]
    pallas_call x10 -> x12, Pallas kernels: 15.2 us -> 15.6 us  [call(): pl.pallas_call(kernel, name=name, out_shape=out_shape, in_specs=specs, ou...]
  transfers between devices with their start and end apart: 17 -> 12, of which waited for: 9 -> 5; matrix products, arithmetic and copies ran while one was open for 0% -> 0% of each run, Pallas kernels for 11% -> 13%
where the time goes in v6:
time: 66.7 us; the launch traced here: 66.4 us
  blocking collectives  27.9 us (42%)
  Pallas kernels  15.6 us (23%)
  starting transfers between devices  11.4 us (17%)
  waiting for transfers between devices  10.4 us (16%)
  local copies, waits for them, and re-layouts  0.98 us (1%)
    all_gather x2, blocking collectives, local_and_ends(): inputs.append(lax.all_gather(part, 'dom', axis_index_groups=groups))  27.9 us
    pallas_call x12, Pallas kernels, call(): pl.pallas_call(kernel, name=name, out_shape=out_shape, in_specs=specs, ou...  15.6 us
    ppermute x2, waiting for transfers between devices, shards(): lax.ppermute(filtered, 'band', [(0, 1), (1, 0)])  6.73 us
    ppermute x4, starting transfers between devices, shift(): return lax.ppermute(array, 'dom', pairs)  4.97 us
    ppermute x4, waiting for transfers between devices, swap(): return lax.ppermute(array, 'dom', pairs)  3.56 us
    ppermute x2, starting transfers between devices, reverse(): return lax.ppermute(array, 'dom', pairs)  2.46 us
    ppermute x2, starting transfers between devices, shards(): lax.ppermute(filtered, 'band', [(0, 1), (1, 0)])  2.16 us
    ppermute x4, starting transfers between devices, swap(): return lax.ppermute(array, 'dom', pairs)  1.82 us
  transfers between devices with their start and end apart: 12, of which 5 were waited for; matrix products, arithmetic and copies ran while one was open for 0% of the time, Pallas kernels for 13%

profile of v6, /device:TPU:0, one launch (start us, length us, event | category | flops | bytes accessed | tf_op | source)
XLA Modules:
  0.0 66.4 jit_solution(13545070764263541368)
XLA Ops:
  0.0 0.8 %copy.9 = f32[64,4]{1,0:T(8,128)S(1)} copy(f32[64,4]{0,1:T(4,128)} %param.12) | data formatting | bytes 2048 | tf_op args[5]
  1.0 2.9 %tables_first.1 = (f32[1536,128]{1,0:T(8,128)S(1)}, f32[256,4,128]{2,1,0:T(4,128)S(1)}, f32[192,128]{1,0:T(8,128)S(1)}, f32[16,128]{1,0:T(8,128)S(1)}) custom-call(f32[1536,128]{1,0:T(8,128)} %bitcast.9, bf16[256,4,128]{2,1,0:T(4,128)(2,1)} %proj_hbm.1, f32[192,128]{1,0:T(8,128)} %bitcast.10, s32[256]{0:T(256)} %blk_hbm.7, s32[256]{0:T(256)} %atom_hbm.7), custom_call_target="tpu_custom_call" | custom-call | flops 1000 | bytes 1000 | tf_op jit(solution)/shard_map/tables_first/pallas_call | solution.py:466
  3.9 14.8 %all-gather = f32[64,128]{1,0:T(8,128)S(1)} all-gather(f32[16,128]{1,0:T(8,128)S(1)} %get-tuple-element.24), channel_id=2, replica_groups={{0,8,16,24},{2,10,18,26},{4,12,20,28},{6,14,22,30},{1,9,17,25},{3,11,19..., dimensions={0}, use_global_device_ids=true | all-gather | bytes 40960 | tf_op jit(solution)/shard_map/all_gather | solution.py:537
  19.1 0.6 collective-permute-start.3
  19.6 3.4 %collective-permute-start.4 = (bf16[576,128]{1,0:T(8,128)(2,1)S(1)}, bf16[576,128]{1,0:T(8,128)(2,1)S(1)}, u32[]{:S(2)}, u32[]{:S(2)}) collective-permute-start(bf16[576,128]{1,0:T(8,128)(2,1)S(1)} %get-tuple-element.29), channel_id=1, source_target_pairs={{0,8},{2,10},{4,12},{6,14},{8,0},{10,2},{12,4},{14,6},{16,24},{18,... | collective-permute-start | bytes 442376 | tf_op jit(solution)/shard_map/ppermute | solution.py:484
  23.0 1.6 %collective-permute-start.1 = (f32[8,1536]{1,0:T(8,128)S(1)}, f32[8,1536]{1,0:T(8,128)S(1)}, u32[]{:S(2)}, u32[]{:S(2)}) collective-permute-start(f32[8,1536]{1,0:T(8,128)S(1)} %get-tuple-element.26), channel_id=1, source_target_pairs={{0,6},{2,4},{4,2},{6,0},{8,14},{10,12},{12,10},{14,8},{16,22},{18,... | collective-permute-start | bytes 147464 | tf_op jit(solution)/shard_map/ppermute | solution.py:530
  25.2 0.9 %inside_first.1.acc = f32[1536,128]{1,0:T(8,128)S(1)} custom-call(f32[1536,128]{1,0:T(8,128)S(1)} %get-tuple-element.21.v_ref.refs_0_, f32[192,128]{1,0:T(8,128)S(1)} %get-tuple-element.22.pot), custom_call_target="tpu_custom_call" | custom-call | flops 1000 | bytes 1000 | tf_op jit(solution)/shard_map/inside_first/pallas_call | solution.py:466
  26.1 2.2 %collective-permute-done.2.refs_1_ = f32[16,128]{1,0:T(8,128)S(1)} collective-permute-done((f32[16,128]{1,0:T(8,128)S(1)}, f32[16,128]{1,0:T(8,128)S(1)}, u32[]{:S(2)}, u32[]{:S(2)}) %collective-permute-start.2) | collective-permute-done | bytes 8224 | tf_op jit(solution)/shard_map/ppermute | solution.py:526
  28.3 2.3 %nonlocal_first.1.acc = f32[1536,128]{1,0:T(8,128)S(1)} custom-call(f32[1536,128]{1,0:T(8,128)S(1)} %inside_first.1.acc, f32[256,4,128]{2,1,0:T(4,128)S(1)} %get-tuple-element.23.projf, f32[16,128]{1,0:T(8,128)S(1)} %copy.12.after.energy, s32[256]{0:T(256)} %blk_hbm.7, s32[256]{0:T(256)} %atom_hbm.7, f32[8,1536]{1,0:T(8,128)S(1)} %collective-permute-done.first, ...), custom_call_target="tpu_custom_call" | custom-call | flops 1000 | bytes 1000 | tf_op jit(solution)/shard_map/nonlocal_first/pallas_call | solution.py:466
  30.6 1.9 %tables_second.1 = (f32[1536,128]{1,0:T(8,128)S(1)}, f32[16,128]{1,0:T(8,128)S(1)}) custom-call(f32[1536,128]{1,0:T(8,128)S(1)} %nonlocal_first.1.acc, f32[256,4,128]{2,1,0:T(4,128)S(1)} %get-tuple-element.23.projf, s32[256]{0:T(256)} %blk_hbm.7, s32[256]{0:T(256)} %atom_hbm.7, bf16[768,128]{1,0:T(8,128)(2,1)S(1)} %collective-permute-done.3.refs_0_, ...), custom_call_target="tpu_custom_call" | custom-call | flops 1000 | bytes 1000 | tf_op jit(solution)/shard_map/tables_second/pallas_call | solution.py:466
  32.5 13.1 %all-gather.1 = f32[64,128]{1,0:T(8,128)S(1)} all-gather(f32[16,128]{1,0:T(8,128)S(1)} %get-tuple-element.31), channel_id=3, replica_groups={{0,8,16,24},{2,10,18,26},{4,12,20,28},{6,14,22,30},{1,9,17,25},{3,11,19..., dimensions={0}, use_global_device_ids=true | all-gather | bytes 40960 | tf_op jit(solution)/shard_map/all_gather | solution.py:537
  46.0 0.6 collective-permute-start.8
  47.0 0.8 %collective-permute-start.6 = (f32[8,1536]{1,0:T(8,128)S(1)}, f32[8,1536]{1,0:T(8,128)S(1)}, u32[]{:S(2)}, u32[]{:S(2)}) collective-permute-start(f32[8,1536]{1,0:T(8,128)S(1)} %get-tuple-element.33), channel_id=1, source_target_pairs={{0,6},{2,4},{4,2},{6,0},{8,14},{10,12},{12,10},{14,8},{16,22},{18,... | collective-permute-start | bytes 147464 | tf_op jit(solution)/shard_map/ppermute | solution.py:530
  47.9 1.3 %collective-permute-start.7 = (f32[16,128]{1,0:T(8,128)S(1)}, f32[16,128]{1,0:T(8,128)S(1)}, u32[]{:S(2)}, u32[]{:S(2)}) collective-permute-start(f32[16,128]{1,0:T(8,128)S(1)} %get-tuple-element.34.refs_0_), channel_id=1, source_target_pairs={{0,4},{2,6},{4,0},{6,2},{8,12},{10,14},{12,8},{14,10},{16,20},{18,... | collective-permute-start | bytes 24584 | tf_op jit(solution)/shard_map/ppermute | solution.py:526
  49.2 1.0 %inside_second.1.acc = f32[1536,128]{1,0:T(8,128)S(1)} custom-call(f32[1536,128]{1,0:T(8,128)S(1)} %get-tuple-element.30.v_ref, f32[192,128]{1,0:T(8,128)S(1)} %get-tuple-element.22.pot, f32[1536,128]{1,0:T(8,128)S(1)} %get-tuple-element.21.v_ref.refs_0_), custom_call_target="tpu_custom_call" | custom-call | flops 1000 | bytes 1000 | tf_op jit(solution)/shard_map/inside_second/pallas_call | solution.py:466
  50.1 1.4 %collective-permute-done.7.refs_1_ = f32[16,128]{1,0:T(8,128)S(1)} collective-permute-done((f32[16,128]{1,0:T(8,128)S(1)}, f32[16,128]{1,0:T(8,128)S(1)}, u32[]{:S(2)}, u32[]{:S(2)}) %collective-permute-start.7) | collective-permute-done | bytes 8224 | tf_op jit(solution)/shard_map/ppermute | solution.py:526
  51.5 2.3 %nonlocal_second.1.acc = f32[1536,128]{1,0:T(8,128)S(1)} custom-call(f32[1536,128]{1,0:T(8,128)S(1)} %inside_second.1.acc, f32[256,4,128]{2,1,0:T(4,128)S(1)} %get-tuple-element.23.projf, f32[16,128]{1,0:T(8,128)S(1)} %copy.12.after.energy, s32[256]{0:T(256)} %blk_hbm.7, s32[256]{0:T(256)} %atom_hbm.7, f32[8,1536]{1,0:T(8,128)S(1)} %collective-permute-done.5.first, ...), custom_call_target="tpu_custom_call" | custom-call | flops 1000 | bytes 1000 | tf_op jit(solution)/shard_map/nonlocal_second/pallas_call | solution.py:466
  54.3 1.6 %collective-permute-start.11 = (bf16[768,128]{1,0:T(8,128)(2,1)S(1)}, bf16[768,128]{1,0:T(8,128)(2,1)S(1)}, u32[]{:S(2)}, u32[]{:S(2)}) collective-permute-start(bf16[768,128]{1,0:T(8,128)(2,1)S(1)} %filtered_0.1.own), channel_id=1, source_target_pairs={{0,1},{1,0},{2,3},{3,2},{4,5},{5,4},{6,7},{7,6},{8,9},{9,8},{10,11... | collective-permute-start | bytes 589832 | tf_op jit(solution)/shard_map/ppermute | solution.py:601
  55.9 0.7 filtered_1.1.own
  56.5 0.6 collective-permute-start.10
  57.1 5.0 %collective-permute-done.11.other = bf16[768,128]{1,0:T(8,128)(2,1)S(1)} collective-permute-done((bf16[768,128]{1,0:T(8,128)(2,1)S(1)}, bf16[768,128]{1,0:T(8,128)(2,1)S(1)}, u32[]{:S(2)}, u32[]{:S(2)}) %collective-permute-start.11) | collective-permute-done | bytes 196640 | tf_op jit(solution)/shard_map/ppermute | solution.py:601
  62.2 1.3 %rotate_0.1.refs_0_ = f32[1536,128]{1,0:T(8,128)} custom-call(bf16[768,128]{1,0:T(8,128)(2,1)S(1)} %filtered_0.1.own, bf16[768,128]{1,0:T(8,128)(2,1)S(1)} %collective-permute-done.11.other, bf16[16,16]{1,0:T(8,128)(2,1)S(1)} %copy-done), custom_call_target="tpu_custom_call" | custom-call | flops 1000 | bytes 1000 | tf_op jit(solution)/shard_map/rotate_0/pallas_call | solution.py:466
  63.5 1.7 %collective-permute-done.10.other = bf16[768,128]{1,0:T(8,128)(2,1)S(1)} collective-permute-done((bf16[768,128]{1,0:T(8,128)(2,1)S(1)}, bf16[768,128]{1,0:T(8,128)(2,1)S(1)}, u32[]{:S(2)}, u32[]{:S(2)}) %collective-permute-start.10) | collective-permute-done | bytes 196640 | tf_op jit(solution)/shard_map/ppermute | solution.py:601
  65.2 1.3 %rotate_1.1 = f32[1536,128]{1,0:T(8,128)} custom-call(bf16[768,128]{1,0:T(8,128)(2,1)S(1)} %filtered_1.1.own, bf16[768,128]{1,0:T(8,128)(2,1)S(1)} %collective-permute-done.10.other, bf16[16,16]{1,0:T(8,128)(2,1)S(1)} %copy-done, f32[1536,128]{1,0:T(8,128)} %rotate_0.1.refs_0_), custom_call_target="tpu_custom_call", output_to_operand_aliasing={{}: (3, {})} | custom-call | flops 1000 | bytes 1000 | tf_op jit(solution)/shard_map/rotate_1/pallas_call | solution.py:466
  (21 shorter events, 2.3 us)
Async XLA Ops:
  19.1 11.6 %collective-permute-start.3 = (bf16[768,128]{1,0:T(8,128)(2,1)S(1)}, bf16[768,128]{1,0:T(8,128)(2,1)S(1)}, u32[]{:S(2)}, u32[]{:S(2)}) collective-permute-start(bf16[768,128]{1,0:T(8,128)(2,1)S(1)} %get-tuple-element.28), channel_id=1, source_target_pairs={{0,16},{2,18},{4,20},{6,22},{8,24},{10,26},{12,28},{14,30},{16,0},... | collective-permute-start | bytes 589832 | tf_op jit(solution)/shard_map/ppermute | solution.py:484
  19.6 11.0 %collective-permute-start.4 = (bf16[576,128]{1,0:T(8,128)(2,1)S(1)}, bf16[576,128]{1,0:T(8,128)(2,1)S(1)}, u32[]{:S(2)}, u32[]{:S(2)}) collective-permute-start(bf16[576,128]{1,0:T(8,128)(2,1)S(1)} %get-tuple-element.29), channel_id=1, source_target_pairs={{0,8},{2,10},{4,12},{6,14},{8,0},{10,2},{12,4},{14,6},{16,24},{18,... | collective-permute-start | bytes 442376 | tf_op jit(solution)/shard_map/ppermute | solution.py:484
  23.0 5.3 %collective-permute-start = (f32[8,1536]{1,0:T(8,128)S(1)}, f32[8,1536]{1,0:T(8,128)S(1)}, u32[]{:S(2)}, u32[]{:S(2)}) collective-permute-start(f32[8,1536]{1,0:T(8,128)S(1)} %get-tuple-element.25), channel_id=1, source_target_pairs={{0,2},{2,0},{4,6},{6,4},{8,10},{10,8},{12,14},{14,12},{16,18},{18,... | collective-permute-start | bytes 147464 | tf_op jit(solution)/shard_map/ppermute | solution.py:526
  23.0 5.3 %collective-permute-start.1 = (f32[8,1536]{1,0:T(8,128)S(1)}, f32[8,1536]{1,0:T(8,128)S(1)}, u32[]{:S(2)}, u32[]{:S(2)}) collective-permute-start(f32[8,1536]{1,0:T(8,128)S(1)} %get-tuple-element.26), channel_id=1, source_target_pairs={{0,6},{2,4},{4,2},{6,0},{8,14},{10,12},{12,10},{14,8},{16,22},{18,... | collective-permute-start | bytes 147464 | tf_op jit(solution)/shard_map/ppermute | solution.py:530
  24.7 3.7 %collective-permute-start.2 = (f32[16,128]{1,0:T(8,128)S(1)}, f32[16,128]{1,0:T(8,128)S(1)}, u32[]{:S(2)}, u32[]{:S(2)}) collective-permute-start(f32[16,128]{1,0:T(8,128)S(1)} %get-tuple-element.27.refs_0_), channel_id=1, source_target_pairs={{0,4},{2,6},{4,0},{6,2},{8,12},{10,14},{12,8},{14,10},{16,20},{18,... | collective-permute-start | bytes 24584 | tf_op jit(solution)/shard_map/ppermute | solution.py:526
  46.0 9.9 %collective-permute-start.8 = (bf16[768,128]{1,0:T(8,128)(2,1)S(1)}, bf16[768,128]{1,0:T(8,128)(2,1)S(1)}, u32[]{:S(2)}, u32[]{:S(2)}) collective-permute-start(bf16[768,128]{1,0:T(8,128)(2,1)S(1)} %get-tuple-element.35), channel_id=1, source_target_pairs={{0,16},{2,18},{4,20},{6,22},{8,24},{10,26},{12,28},{14,30},{16,0},... | collective-permute-start | bytes 589832 | tf_op jit(solution)/shard_map/ppermute | solution.py:484
  46.6 7.2 %collective-permute-start.9 = (bf16[576,128]{1,0:T(8,128)(2,1)S(1)}, bf16[576,128]{1,0:T(8,128)(2,1)S(1)}, u32[]{:S(2)}, u32[]{:S(2)}) collective-permute-start(bf16[576,128]{1,0:T(8,128)(2,1)S(1)} %get-tuple-element.36), channel_id=1, source_target_pairs={{0,8},{2,10},{4,12},{6,14},{8,0},{10,2},{12,4},{14,6},{16,24},{18,... | collective-permute-start | bytes 442376 | tf_op jit(solution)/shard_map/ppermute | solution.py:484
  47.0 4.5 %collective-permute-start.5 = (f32[8,1536]{1,0:T(8,128)S(1)}, f32[8,1536]{1,0:T(8,128)S(1)}, u32[]{:S(2)}, u32[]{:S(2)}) collective-permute-start(f32[8,1536]{1,0:T(8,128)S(1)} %get-tuple-element.32), channel_id=1, source_target_pairs={{0,2},{2,0},{4,6},{6,4},{8,10},{10,8},{12,14},{14,12},{16,18},{18,... | collective-permute-start | bytes 147464 | tf_op jit(solution)/shard_map/ppermute | solution.py:526
  47.0 4.5 %collective-permute-start.6 = (f32[8,1536]{1,0:T(8,128)S(1)}, f32[8,1536]{1,0:T(8,128)S(1)}, u32[]{:S(2)}, u32[]{:S(2)}) collective-permute-start(f32[8,1536]{1,0:T(8,128)S(1)} %get-tuple-element.33), channel_id=1, source_target_pairs={{0,6},{2,4},{4,2},{6,0},{8,14},{10,12},{12,10},{14,8},{16,22},{18,... | collective-permute-start | bytes 147464 | tf_op jit(solution)/shard_map/ppermute | solution.py:530
  47.9 3.7 %collective-permute-start.7 = (f32[16,128]{1,0:T(8,128)S(1)}, f32[16,128]{1,0:T(8,128)S(1)}, u32[]{:S(2)}, u32[]{:S(2)}) collective-permute-start(f32[16,128]{1,0:T(8,128)S(1)} %get-tuple-element.34.refs_0_), channel_id=1, source_target_pairs={{0,4},{2,6},{4,0},{6,2},{8,12},{10,14},{12,8},{14,10},{16,20},{18,... | collective-permute-start | bytes 24584 | tf_op jit(solution)/shard_map/ppermute | solution.py:526
  54.3 7.9 %copy-start = (bf16[16,16]{1,0:T(8,128)(2,1)S(1)}, bf16[16,16]{1,0:T(8,128)(2,1)}, u32[]{:S(2)}) copy-start(bf16[16,16]{1,0:T(8,128)(2,1)} %panel.3) | copy-start | bytes 1540
  54.3 7.9 %collective-permute-start.11 = (bf16[768,128]{1,0:T(8,128)(2,1)S(1)}, bf16[768,128]{1,0:T(8,128)(2,1)S(1)}, u32[]{:S(2)}, u32[]{:S(2)}) collective-permute-start(bf16[768,128]{1,0:T(8,128)(2,1)S(1)} %filtered_0.1.own), channel_id=1, source_target_pairs={{0,1},{1,0},{2,3},{3,2},{4,5},{5,4},{6,7},{7,6},{8,9},{9,8},{10,11... | collective-permute-start | bytes 589832 | tf_op jit(solution)/shard_map/ppermute | solution.py:601
  56.5 8.6 %collective-permute-start.10 = (bf16[768,128]{1,0:T(8,128)(2,1)S(1)}, bf16[768,128]{1,0:T(8,128)(2,1)S(1)}, u32[]{:S(2)}, u32[]{:S(2)}) collective-permute-start(bf16[768,128]{1,0:T(8,128)(2,1)S(1)} %filtered_1.1.own), channel_id=1, source_target_pairs={{0,1},{1,0},{2,3},{3,2},{4,5},{5,4},{6,7},{7,6},{8,9},{9,8},{10,11... | collective-permute-start | bytes 589832 | tf_op jit(solution)/shard_map/ppermute | solution.py:601

commit v7 on v6

--- a/solution.py
+++ b/solution.py
@@ -106,13 +106,16 @@
     return start if isinstance(start, int) else pl.multiple_of(start, unit)
 
 
-def pack_faces(g, dom, v_ref, x_refs, y_refs):
-    for (side, _), out in zip(g.faces(dom, 0), x_refs):
+def pack_x(g, dom, v_ref, refs):
+    for (side, _), out in zip(g.faces(dom, 0), refs):
         for j in range(RADIUS):
             at = aligned(layer(side, g.cx, j) * g.slab, g.slab)
             out[j * g.slab : (j + 1) * g.slab, :] = v_ref[pl.ds(at, g.slab), :].astype(BF16)
+
+
+def pack_y(g, dom, v_ref, refs):
     size = RADIUS * g.no
-    for (side, _), out in zip(g.faces(dom, 1), y_refs):
+    for (side, _), out in zip(g.faces(dom, 1), refs):
         for x in range(g.cx):
             pieces = []
             for j in range(RADIUS):
@@ -238,15 +241,17 @@
     inner_tables(g, dom, v_ref, projf, blk, atom, lut, sums, table)
 
 
-def pack_kernel(g, v_ref, after, *refs):
-    nx, ny = len(g.face_rows(0)), len(g.face_rows(1))
+def pack_kernel(g, v_ref, energy, inside, *refs):
+    nx = len(g.face_rows(0))
     dom = lax.axis_index("dom")
     if g.butterfly:
-        tables, group = refs[0], refs[-1]
-        group[...] = (tables[0] + tables[1]) + (tables[2] + tables[3])
-        refs = refs[1:-1]
+        part, from_x, from_y, from_xy = refs[:4]
+        group = refs[-1]
+        group[...] = (part[...] + from_x[...]) + (from_y[...] + from_xy[...])
+        refs = refs[4:-1]
     first, second = refs[:2]
-    pack_faces(g, dom, v_ref, refs[2 : 2 + nx], refs[2 + nx :])
+    pack_x(g, dom, v_ref, refs[2 : 2 + nx])
+    pack_y(g, dom, v_ref, refs[2 + nx :])
     pack_ends(g, dom, v_ref, first, second)
     if g.butterfly:
         put_table(g, first, group)
@@ -429,9 +434,7 @@
     filtered[...] = work[pl.ds(at, count * g.slab), :].astype(BF16)
 
 
-def rotate_kernel(g, number, own, other, panel, *refs):
-    out_hbm, out, sem = refs[-3:]
-    start, count = halves(g, lax.axis_index("dom"))[number]
+def panel_kernel(g, panel, weights):
     band = lax.axis_index("band")
     group = 16
     span = group * g.no
@@ -445,18 +448,25 @@
     spread = lax.dot_general(picked, pick_in, NN, preferred_element_type=F32)
     row, col = iota((span, 2 * span), 0), iota((span, 2 * span), 1)
     same = row % group == (col % span) // g.no
-    weights = jnp.where(same, spread, 0.0).astype(BF16)
+    weights[...] = jnp.where(same, spread, 0.0).astype(BF16)
+
+
+def rotate_kernel(g, number, own, other, weights, *refs):
+    out_hbm, out, sem = refs[-3:]
+    start, count = halves(g, lax.axis_index("dom"))[number]
+    group = 16
+    span = group * g.no
+    copies = []
     size = count * g.cy
     for n in range(size // group):
         rows = slice(n * span, (n + 1) * span)
         both = jnp.concatenate([own[rows, :], other[rows, :]], axis=0)
-        result = lax.dot_general(weights, both, NN, preferred_element_type=F32)
+        result = lax.dot_general(weights[...], both, NN, preferred_element_type=F32)
         for j in range(g.no):
             out[j, n * group : (n + 1) * group, :] = result[j * group : (j + 1) * group, :]
-    copies = []
-    for j in range(g.no):
-        at = aligned(j * g.rows + start * g.cy, group)
-        copies.append(pltpu.make_async_copy(out.at[j], out_hbm.at[pl.ds(at, size), :], sem.at[j]))
+        to = pl.ds(aligned(start * g.cy + n * group, group), group)
+        source = out.at[:, pl.ds(n * group, group), :]
+        copies.append(pltpu.make_async_copy(source, out_hbm.at[:, to, :], sem.at[n]))
         copies[-1].start()
     for copy in copies:
         copy.wait()
@@ -505,8 +515,9 @@
     proj = in_hbm(projectors)
     blk, atom = in_hbm(entry_block), in_hbm(entry_atom)
     field = jax.ShapeDtypeStruct((g.flat, g.cz), F32)
-    faces = [jax.ShapeDtypeStruct((n, g.cz), BF16) for n in g.face_rows(0) + g.face_rows(1)]
-    nx = len(g.face_rows(0))
+    x_faces = [jax.ShapeDtypeStruct((n, g.cz), BF16) for n in g.face_rows(0)]
+    y_faces = [jax.ShapeDtypeStruct((n, g.cz), BF16) for n in g.face_rows(1)]
+    nx = len(x_faces)
     ends = jax.ShapeDtypeStruct((8, g.flat), F32)
     table = jax.ShapeDtypeStruct((g.dom_count, g.table), F32)
     entries = [
@@ -530,12 +541,6 @@
         return lax.ppermute(array, "dom", pairs)
 
     def local_and_ends(scale, which, values, prev, part):
-        inputs = [values, energy]
-        outputs = [ends, ends, *faces]
-        if g.butterfly:
-            groups = [[i + j * g.third for j in range(4)] for i in range(g.third)]
-            inputs.append(lax.all_gather(part, "dom", axis_index_groups=groups))
-            outputs.append(table)
         acc = call(
             functools.partial(inside_kernel, g, scale, len(prev) > 0),
             "inside_" + which,
@@ -544,11 +549,16 @@
             [values, pot, *prev],
             [VMEM] * (2 + len(prev)),
         )
+        inputs = [values, energy, acc]
+        outputs = [ends, ends, *x_faces, *y_faces]
+        if g.butterfly:
+            inputs += [part, swap(part, g.plane), swap(part, g.third), swap(part, g.plane, g.third)]
+            outputs.append(table)
         first, second, *sent = call(
             functools.partial(pack_kernel, g), "pack_" + which, outputs, [], inputs, [VMEM] * len(inputs)
         )
         from_x = swap_faces(g, sent[:nx], g.plane, g.first)
-        from_y = swap_faces(g, sent[nx : len(faces)], g.third, g.second)
+        from_y = swap_faces(g, sent[nx : nx + len(y_faces)], g.third, g.second)
         first, second = swap(first, 1), reverse(second)
         tables = [sent[-1], swap(sent[-1], 2)] if g.butterfly else [lax.psum(part, "dom")]
         acc = call(
@@ -585,6 +595,14 @@
         [VMEM] * 2 + [HBM] * 2 + [VMEM] * len(received),
     )
     acc, received = local_and_ends(2.0, "second", u, [v], part)
+    weights = call(
+        functools.partial(panel_kernel, g),
+        "panel",
+        jax.ShapeDtypeStruct((16 * g.no, 32 * g.no), BF16),
+        [],
+        [panel],
+        [VMEM],
+    )
     rotated = None
     pieces = []
     parts = halves(g, 0)
@@ -600,12 +618,12 @@
         )
         pieces.append((filtered, lax.ppermute(filtered, "band", [(0, 1), (1, 0)]), count))
     for number, (filtered, other, count) in enumerate(pieces):
-        inputs = [filtered, other, panel] + ([] if rotated is None else [rotated])
+        inputs = [filtered, other, weights] + ([] if rotated is None else [rotated])
         rotated = call(
             functools.partial(rotate_kernel, g, number),
             "rotate_%d" % number,
-            field,
-            [pltpu.VMEM((g.no, count * g.cy, g.cz), F32), pltpu.SemaphoreType.DMA((g.no,))],
+            jax.ShapeDtypeStruct((g.no, g.rows, g.cz), F32),
+            [pltpu.VMEM((g.no, count * g.cy, g.cz), F32), pltpu.SemaphoreType.DMA((count * g.cy // 16,))],
             inputs,
             [VMEM] * 3 + [HBM] * (len(inputs) - 3),
             out_specs=HBM,

time: 66.7 us -> 54.7 us (0.82)
  blocking collectives: 27.9 us -> 0 us
  waiting for transfers between devices: 10.4 us -> 19.4 us
  starting transfers between devices: 11.4 us -> 19.3 us
  local copies, waits for them, and re-layouts: 0.98 us -> 0.31 us
    all_gather x2 -> x0, blocking collectives: 27.9 us -> none  [local_and_ends(): inputs.append(lax.all_gather(part, 'dom', axis_index_groups=groups))]
    ppermute x4 -> x10, starting transfers between devices: 1.82 us -> 12 us  [swap(): return lax.ppermute(array, 'dom', pairs)]
    ppermute x4 -> x10, waiting for transfers between devices: 3.56 us -> 12.3 us  [swap(): return lax.ppermute(array, 'dom', pairs)]
    ppermute x4, starting transfers between devices: 4.97 us -> 2.73 us  [shift(): return lax.ppermute(array, 'dom', pairs)]
    ppermute x4, waiting for transfers between devices: 0.07 us -> 1.13 us  [shift(): return lax.ppermute(array, 'dom', pairs)]
    ppermute x2, waiting for transfers between devices: 6.73 us -> 5.9 us  [shards(): lax.ppermute(filtered, 'band', [(0, 1), (1, 0)])]
    unnamed x3 -> x5, local copies, waits for them, and re-layouts: 0.78 us -> 0.11 us
    pallas_call x12 -> x13, Pallas kernels: 15.6 us -> 15.3 us  [call(): pl.pallas_call(kernel, name=name, out_shape=out_shape, in_specs=specs, ou...]
  transfers between devices with their start and end apart: 12 -> 18, of which waited for: 5 -> 8; matrix products, arithmetic and copies ran while one was open for 0% -> 1% of each run, Pallas kernels for 13% -> 16%
where the time goes in v7:
time: 54.7 us; the launch traced here: 54.4 us
  waiting for transfers between devices  19.4 us (35%)
  starting transfers between devices  19.3 us (35%)
  Pallas kernels  15.3 us (28%)
    pallas_call x13, Pallas kernels, call(): pl.pallas_call(kernel, name=name, out_shape=out_shape, in_specs=specs, ou...  15.3 us
    ppermute x10, waiting for transfers between devices, swap(): return lax.ppermute(array, 'dom', pairs)  12.3 us
    ppermute x10, starting transfers between devices, swap(): return lax.ppermute(array, 'dom', pairs)  12 us
    ppermute x2, waiting for transfers between devices, shards(): lax.ppermute(filtered, 'band', [(0, 1), (1, 0)])  5.9 us
    ppermute x4, starting transfers between devices, shift(): return lax.ppermute(array, 'dom', pairs)  2.73 us
    ppermute x2, starting transfers between devices, reverse(): return lax.ppermute(array, 'dom', pairs)  2.37 us
    ppermute x2, starting transfers between devices, shards(): lax.ppermute(filtered, 'band', [(0, 1), (1, 0)])  2.16 us
    ppermute x4, waiting for transfers between devices, shift(): return lax.ppermute(array, 'dom', pairs)  1.13 us
  transfers between devices with their start and end apart: 18, of which 8 were waited for; matrix products, arithmetic and copies ran while one was open for 1% of the time, Pallas kernels for 16%

profile of v7, /device:TPU:0, one launch (start us, length us, event | category | flops | bytes accessed | tf_op | source)
XLA Modules:
  0.0 54.4 jit_solution(13892015087557128465)
XLA Ops:
  0.0 2.9 %tables_first.1 = (f32[1536,128]{1,0:T(8,128)S(1)}, f32[256,4,128]{2,1,0:T(4,128)S(1)}, f32[192,128]{1,0:T(8,128)S(1)}, f32[16,128]{1,0:T(8,128)S(1)}) custom-call(f32[1536,128]{1,0:T(8,128)} %bitcast.5, bf16[256,4,128]{2,1,0:T(4,128)(2,1)} %proj_hbm.1, f32[192,128]{1,0:T(8,128)} %bitcast.6, s32[256]{0:T(256)} %blk_hbm.7, s32[256]{0:T(256)} %atom_hbm.7), custom_call_target="tpu_custom_call" | custom-call | flops 1000 | bytes 1000 | tf_op jit(solution)/shard_map/tables_first/pallas_call | solution.py:476
  2.9 4.1 %collective-permute-start = (f32[16,128]{1,0:T(8,128)S(1)}, f32[16,128]{1,0:T(8,128)S(1)}, u32[]{:S(2)}, u32[]{:S(2)}) collective-permute-start(f32[16,128]{1,0:T(8,128)S(1)} %get-tuple-element.24.refs_0_), channel_id=1, source_target_pairs={{0,16},{2,18},{4,20},{6,22},{8,24},{10,26},{12,28},{14,30},{16,0},... | collective-permute-start | bytes 24584 | tf_op jit(solution)/shard_map/ppermute | solution.py:537
  7.0 1.6 %collective-permute-start.1 = (f32[16,128]{1,0:T(8,128)S(1)}, f32[16,128]{1,0:T(8,128)S(1)}, u32[]{:S(2)}, u32[]{:S(2)}) collective-permute-start(f32[16,128]{1,0:T(8,128)S(1)} %get-tuple-element.24.refs_0_), channel_id=1, source_target_pairs={{0,8},{2,10},{4,12},{6,14},{8,0},{10,2},{12,4},{14,6},{16,24},{18,... | collective-permute-start | bytes 24584 | tf_op jit(solution)/shard_map/ppermute | solution.py:537
  8.9 0.9 %inside_first.1.inside.acc = f32[1536,128]{1,0:T(8,128)S(1)} custom-call(f32[1536,128]{1,0:T(8,128)S(1)} %get-tuple-element.21.v_ref.refs_0_, f32[192,128]{1,0:T(8,128)S(1)} %get-tuple-element.22.pot), custom_call_target="tpu_custom_call" | custom-call | flops 1000 | bytes 1000 | tf_op jit(solution)/shard_map/inside_first/pallas_call | solution.py:476
  9.9 0.8 %collective-permute-done.1.refs_2_ = f32[16,128]{1,0:T(8,128)S(1)} collective-permute-done((f32[16,128]{1,0:T(8,128)S(1)}, f32[16,128]{1,0:T(8,128)S(1)}, u32[]{:S(2)}, u32[]{:S(2)}) %collective-permute-start.1) | collective-permute-done | bytes 8224 | tf_op jit(solution)/shard_map/ppermute | solution.py:537
  10.7 3.4 %collective-permute-done.2.refs_3_ = f32[16,128]{1,0:T(8,128)S(1)} collective-permute-done((f32[16,128]{1,0:T(8,128)S(1)}, f32[16,128]{1,0:T(8,128)S(1)}, u32[]{:S(2)}, u32[]{:S(2)}) %collective-permute-start.2) | collective-permute-done | bytes 8224 | tf_op jit(solution)/shard_map/ppermute | solution.py:537
  15.1 1.8 %collective-permute-start.4 = (f32[8,1536]{1,0:T(8,128)S(1)}, f32[8,1536]{1,0:T(8,128)S(1)}, u32[]{:S(2)}, u32[]{:S(2)}) collective-permute-start(f32[8,1536]{1,0:T(8,128)S(1)} %get-tuple-element.26), channel_id=1, source_target_pairs={{0,6},{2,4},{4,2},{6,0},{8,14},{10,12},{12,10},{14,8},{16,22},{18,... | collective-permute-start | bytes 147464 | tf_op jit(solution)/shard_map/ppermute | solution.py:541
  17.2 3.3 %collective-permute-done.5.refs_1_ = f32[16,128]{1,0:T(8,128)S(1)} collective-permute-done((f32[16,128]{1,0:T(8,128)S(1)}, f32[16,128]{1,0:T(8,128)S(1)}, u32[]{:S(2)}, u32[]{:S(2)}) %collective-permute-start.5) | collective-permute-done | bytes 8224 | tf_op jit(solution)/shard_map/ppermute | solution.py:537
  20.5 2.3 %nonlocal_first.1.acc = f32[1536,128]{1,0:T(8,128)S(1)} custom-call(f32[1536,128]{1,0:T(8,128)S(1)} %inside_first.1.inside.acc, f32[256,4,128]{2,1,0:T(4,128)S(1)} %get-tuple-element.23.projf, f32[16,128]{1,0:T(8,128)S(1)} %copy.12.energy, s32[256]{0:T(256)} %blk_hbm.7, s32[256]{0:T(256)} %atom_hbm.7, f32[8,1536]{1,0:T(8,128)S(1)} %collective-permute-done.3.first, ...), custom_call_target="tpu_custom_call" | custom-call | flops 1000 | bytes 1000 | tf_op jit(solution)/shard_map/nonlocal_first/pallas_call | solution.py:476
  22.8 1.9 %tables_second.1 = (f32[1536,128]{1,0:T(8,128)S(1)}, f32[16,128]{1,0:T(8,128)S(1)}) custom-call(f32[1536,128]{1,0:T(8,128)S(1)} %nonlocal_first.1.acc, f32[256,4,128]{2,1,0:T(4,128)S(1)} %get-tuple-element.23.projf, s32[256]{0:T(256)} %blk_hbm.7, s32[256]{0:T(256)} %atom_hbm.7, bf16[768,128]{1,0:T(8,128)(2,1)S(1)} %collective-permute-done.6.refs_0_, ...), custom_call_target="tpu_custom_call" | custom-call | flops 1000 | bytes 1000 | tf_op jit(solution)/shard_map/tables_second/pallas_call | solution.py:476
  24.7 3.7 %collective-permute-start.10 = (f32[16,128]{1,0:T(8,128)S(1)}, f32[16,128]{1,0:T(8,128)S(1)}, u32[]{:S(2)}, u32[]{:S(2)}) collective-permute-start(f32[16,128]{1,0:T(8,128)S(1)} %get-tuple-element.31.refs_0_), channel_id=1, source_target_pairs={{0,24},{2,26},{4,28},{6,30},{8,16},{10,18},{12,20},{14,22},{16,8},... | collective-permute-start | bytes 24584 | tf_op jit(solution)/shard_map/ppermute | solution.py:537
  28.4 0.8 %collective-permute-start.9 = (f32[16,128]{1,0:T(8,128)S(1)}, f32[16,128]{1,0:T(8,128)S(1)}, u32[]{:S(2)}, u32[]{:S(2)}) collective-permute-start(f32[16,128]{1,0:T(8,128)S(1)} %get-tuple-element.31.refs_0_), channel_id=1, source_target_pairs={{0,8},{2,10},{4,12},{6,14},{8,0},{10,2},{12,4},{14,6},{16,24},{18,... | collective-permute-start | bytes 24584 | tf_op jit(solution)/shard_map/ppermute | solution.py:537
  29.1 1.0 %inside_second.1.inside.acc = f32[1536,128]{1,0:T(8,128)S(1)} custom-call(f32[1536,128]{1,0:T(8,128)S(1)} %get-tuple-element.30.v_ref, f32[192,128]{1,0:T(8,128)S(1)} %get-tuple-element.22.pot, f32[1536,128]{1,0:T(8,128)S(1)} %get-tuple-element.21.v_ref.refs_0_), custom_call_target="tpu_custom_call" | custom-call | flops 1000 | bytes 1000 | tf_op jit(solution)/shard_map/inside_second/pallas_call | solution.py:476
  30.2 2.7 %collective-permute-done.8.refs_1_ = f32[16,128]{1,0:T(8,128)S(1)} collective-permute-done((f32[16,128]{1,0:T(8,128)S(1)}, f32[16,128]{1,0:T(8,128)S(1)}, u32[]{:S(2)}, u32[]{:S(2)}) %collective-permute-start.8) | collective-permute-done | bytes 8224 | tf_op jit(solution)/shard_map/ppermute | solution.py:537
  33.3 2.1 %collective-permute-start.14 = (bf16[768,128]{1,0:T(8,128)(2,1)S(1)}, bf16[768,128]{1,0:T(8,128)(2,1)S(1)}, u32[]{:S(2)}, u32[]{:S(2)}) collective-permute-start(bf16[768,128]{1,0:T(8,128)(2,1)S(1)} %get-tuple-element.35), channel_id=1, source_target_pairs={{0,16},{2,18},{4,20},{6,22},{8,24},{10,26},{12,28},{14,30},{16,0},... | collective-permute-start | bytes 589832 | tf_op jit(solution)/shard_map/ppermute | solution.py:494
  35.9 1.5 %collective-permute-start.13 = (f32[16,128]{1,0:T(8,128)S(1)}, f32[16,128]{1,0:T(8,128)S(1)}, u32[]{:S(2)}, u32[]{:S(2)}) collective-permute-start(f32[16,128]{1,0:T(8,128)S(1)} %get-tuple-element.34.refs_0_), channel_id=1, source_target_pairs={{0,4},{2,6},{4,0},{6,2},{8,12},{10,14},{12,8},{14,10},{16,20},{18,... | collective-permute-start | bytes 24584 | tf_op jit(solution)/shard_map/ppermute | solution.py:537
  37.5 2.2 %collective-permute-done.13.refs_1_ = f32[16,128]{1,0:T(8,128)S(1)} collective-permute-done((f32[16,128]{1,0:T(8,128)S(1)}, f32[16,128]{1,0:T(8,128)S(1)}, u32[]{:S(2)}, u32[]{:S(2)}) %collective-permute-start.13) | collective-permute-done | bytes 8224 | tf_op jit(solution)/shard_map/ppermute | solution.py:537
  39.6 2.3 %nonlocal_second.1.acc = f32[1536,128]{1,0:T(8,128)S(1)} custom-call(f32[1536,128]{1,0:T(8,128)S(1)} %inside_second.1.inside.acc, f32[256,4,128]{2,1,0:T(4,128)S(1)} %get-tuple-element.23.projf, f32[16,128]{1,0:T(8,128)S(1)} %copy.12.energy, s32[256]{0:T(256)} %blk_hbm.7, s32[256]{0:T(256)} %atom_hbm.7, f32[8,1536]{1,0:T(8,128)S(1)} %collective-permute-done.11.first, ...), custom_call_target="tpu_custom_call" | custom-call | flops 1000 | bytes 1000 | tf_op jit(solution)/shard_map/nonlocal_second/pallas_call | solution.py:476
  41.9 1.1 %collective-permute-done.15.refs_1_.refs_0_ = bf16[576,128]{1,0:T(8,128)(2,1)S(1)} collective-permute-done((bf16[576,128]{1,0:T(8,128)(2,1)S(1)}, bf16[576,128]{1,0:T(8,128)(2,1)S(1)}, u32[]{:S(2)}, u32[]{:S(2)}) %collective-permute-start.15) | collective-permute-done | bytes 147488 | tf_op jit(solution)/shard_map/ppermute | solution.py:494
  43.5 1.6 %collective-permute-start.17 = (bf16[768,128]{1,0:T(8,128)(2,1)S(1)}, bf16[768,128]{1,0:T(8,128)(2,1)S(1)}, u32[]{:S(2)}, u32[]{:S(2)}) collective-permute-start(bf16[768,128]{1,0:T(8,128)(2,1)S(1)} %filtered_0.1.own), channel_id=1, source_target_pairs={{0,1},{1,0},{2,3},{3,2},{4,5},{5,4},{6,7},{7,6},{8,9},{9,8},{10,11... | collective-permute-start | bytes 589832 | tf_op jit(solution)/shard_map/ppermute | solution.py:619
  46.6 4.8 %collective-permute-done.17.other = bf16[768,128]{1,0:T(8,128)(2,1)S(1)} collective-permute-done((bf16[768,128]{1,0:T(8,128)(2,1)S(1)}, bf16[768,128]{1,0:T(8,128)(2,1)S(1)}, u32[]{:S(2)}, u32[]{:S(2)}) %collective-permute-start.17) | collective-permute-done | bytes 196640 | tf_op jit(solution)/shard_map/ppermute | solution.py:619
  51.4 1.0 %rotate_0.1.refs_0_ = f32[8,192,128]{2,1,0:T(8,128)} custom-call(bf16[768,128]{1,0:T(8,128)(2,1)S(1)} %filtered_0.1.own, bf16[768,128]{1,0:T(8,128)(2,1)S(1)} %collective-permute-done.17.other, bf16[128,256]{1,0:T(8,128)(2,1)S(1)} %panel.2.weights), custom_call_target="tpu_custom_call" | custom-call | flops 1000 | bytes 1000 | tf_op jit(solution)/shard_map/rotate_0/pallas_call | solution.py:476
  52.4 1.1 %collective-permute-done.16.other = bf16[768,128]{1,0:T(8,128)(2,1)S(1)} collective-permute-done((bf16[768,128]{1,0:T(8,128)(2,1)S(1)}, bf16[768,128]{1,0:T(8,128)(2,1)S(1)}, u32[]{:S(2)}, u32[]{:S(2)}) %collective-permute-start.16) | collective-permute-done | bytes 196640 | tf_op jit(solution)/shard_map/ppermute | solution.py:619
  53.5 1.0 %rotate_1.1 = f32[8,192,128]{2,1,0:T(8,128)} custom-call(bf16[768,128]{1,0:T(8,128)(2,1)S(1)} %filtered_1.1.own, bf16[768,128]{1,0:T(8,128)(2,1)S(1)} %collective-permute-done.16.other, bf16[128,256]{1,0:T(8,128)(2,1)S(1)} %panel.2.weights, f32[8,192,128]{2,1,0:T(8,128)} %rotate_0.1.refs_0_), custom_call_target="tpu_custom_call", output_to_operand_aliasing={{}: (3, {})} | custom-call | flops 1000 | bytes 1000 | tf_op jit(solution)/shard_map/rotate_1/pallas_call | solution.py:476
  (34 shorter events, 4.6 us)
Async XLA Ops:
  0.0 8.6 %copy-start.1 = (f32[64,4]{0,1:T(4,128)S(1)}, f32[64,4]{0,1:T(4,128)}, u32[]{:S(2)}) copy-start(f32[64,4]{0,1:T(4,128)} %param.12) | copy-start | bytes 3076
  2.9 6.9 %collective-permute-start = (f32[16,128]{1,0:T(8,128)S(1)}, f32[16,128]{1,0:T(8,128)S(1)}, u32[]{:S(2)}, u32[]{:S(2)}) collective-permute-start(f32[16,128]{1,0:T(8,128)S(1)} %get-tuple-element.24.refs_0_), channel_id=1, source_target_pairs={{0,16},{2,18},{4,20},{6,22},{8,24},{10,26},{12,28},{14,30},{16,0},... | collective-permute-start | bytes 24584 | tf_op jit(solution)/shard_map/ppermute | solution.py:537
  7.0 3.7 %collective-permute-start.1 = (f32[16,128]{1,0:T(8,128)S(1)}, f32[16,128]{1,0:T(8,128)S(1)}, u32[]{:S(2)}, u32[]{:S(2)}) collective-permute-start(f32[16,128]{1,0:T(8,128)S(1)} %get-tuple-element.24.refs_0_), channel_id=1, source_target_pairs={{0,8},{2,10},{4,12},{6,14},{8,0},{10,2},{12,4},{14,6},{16,24},{18,... | collective-permute-start | bytes 24584 | tf_op jit(solution)/shard_map/ppermute | solution.py:537
  8.6 5.4 %collective-permute-start.2 = (f32[16,128]{1,0:T(8,128)S(1)}, f32[16,128]{1,0:T(8,128)S(1)}, u32[]{:S(2)}, u32[]{:S(2)}) collective-permute-start(f32[16,128]{1,0:T(8,128)S(1)} %get-tuple-element.24.refs_0_), channel_id=1, source_target_pairs={{0,24},{2,26},{4,28},{6,30},{8,16},{10,18},{12,20},{14,22},{16,8},... | collective-permute-start | bytes 24584 | tf_op jit(solution)/shard_map/ppermute | solution.py:537
  14.4 8.4 %collective-permute-start.6 = (bf16[768,128]{1,0:T(8,128)(2,1)S(1)}, bf16[768,128]{1,0:T(8,128)(2,1)S(1)}, u32[]{:S(2)}, u32[]{:S(2)}) collective-permute-start(bf16[768,128]{1,0:T(8,128)(2,1)S(1)} %get-tuple-element.28), channel_id=1, source_target_pairs={{0,16},{2,18},{4,20},{6,22},{8,24},{10,26},{12,28},{14,30},{16,0},... | collective-permute-start | bytes 589832 | tf_op jit(solution)/shard_map/ppermute | solution.py:494
  14.4 8.4 %collective-permute-start.7 = (bf16[576,128]{1,0:T(8,128)(2,1)S(1)}, bf16[576,128]{1,0:T(8,128)(2,1)S(1)}, u32[]{:S(2)}, u32[]{:S(2)}) collective-permute-start(bf16[576,128]{1,0:T(8,128)(2,1)S(1)} %get-tuple-element.29), channel_id=1, source_target_pairs={{0,8},{2,10},{4,12},{6,14},{8,0},{10,2},{12,4},{14,6},{16,24},{18,... | collective-permute-start | bytes 442376 | tf_op jit(solution)/shard_map/ppermute | solution.py:494
  15.1 5.4 %collective-permute-start.3 = (f32[8,1536]{1,0:T(8,128)S(1)}, f32[8,1536]{1,0:T(8,128)S(1)}, u32[]{:S(2)}, u32[]{:S(2)}) collective-permute-start(f32[8,1536]{1,0:T(8,128)S(1)} %get-tuple-element.25), channel_id=1, source_target_pairs={{0,2},{2,0},{4,6},{6,4},{8,10},{10,8},{12,14},{14,12},{16,18},{18,... | collective-permute-start | bytes 147464 | tf_op jit(solution)/shard_map/ppermute | solution.py:537
  15.1 5.4 %collective-permute-start.4 = (f32[8,1536]{1,0:T(8,128)S(1)}, f32[8,1536]{1,0:T(8,128)S(1)}, u32[]{:S(2)}, u32[]{:S(2)}) collective-permute-start(f32[8,1536]{1,0:T(8,128)S(1)} %get-tuple-element.26), channel_id=1, source_target_pairs={{0,6},{2,4},{4,2},{6,0},{8,14},{10,12},{12,10},{14,8},{16,22},{18,... | collective-permute-start | bytes 147464 | tf_op jit(solution)/shard_map/ppermute | solution.py:541
  16.8 3.7 %collective-permute-start.5 = (f32[16,128]{1,0:T(8,128)S(1)}, f32[16,128]{1,0:T(8,128)S(1)}, u32[]{:S(2)}, u32[]{:S(2)}) collective-permute-start(f32[16,128]{1,0:T(8,128)S(1)} %get-tuple-element.27.refs_0_), channel_id=1, source_target_pairs={{0,4},{2,6},{4,0},{6,2},{8,12},{10,14},{12,8},{14,10},{16,20},{18,... | collective-permute-start | bytes 24584 | tf_op jit(solution)/shard_map/ppermute | solution.py:537
  24.7 5.5 %collective-permute-start.10 = (f32[16,128]{1,0:T(8,128)S(1)}, f32[16,128]{1,0:T(8,128)S(1)}, u32[]{:S(2)}, u32[]{:S(2)}) collective-permute-start(f32[16,128]{1,0:T(8,128)S(1)} %get-tuple-element.31.refs_0_), channel_id=1, source_target_pairs={{0,24},{2,26},{4,28},{6,30},{8,16},{10,18},{12,20},{14,22},{16,8},... | collective-permute-start | bytes 24584 | tf_op jit(solution)/shard_map/ppermute | solution.py:537
  28.4 4.5 %collective-permute-start.8 = (f32[16,128]{1,0:T(8,128)S(1)}, f32[16,128]{1,0:T(8,128)S(1)}, u32[]{:S(2)}, u32[]{:S(2)}) collective-permute-start(f32[16,128]{1,0:T(8,128)S(1)} %get-tuple-element.31.refs_0_), channel_id=1, source_target_pairs={{0,16},{2,18},{4,20},{6,22},{8,24},{10,26},{12,28},{14,30},{16,0},... | collective-permute-start | bytes 24584 | tf_op jit(solution)/shard_map/ppermute | solution.py:537
  28.4 4.5 %collective-permute-start.9 = (f32[16,128]{1,0:T(8,128)S(1)}, f32[16,128]{1,0:T(8,128)S(1)}, u32[]{:S(2)}, u32[]{:S(2)}) collective-permute-start(f32[16,128]{1,0:T(8,128)S(1)} %get-tuple-element.31.refs_0_), channel_id=1, source_target_pairs={{0,8},{2,10},{4,12},{6,14},{8,0},{10,2},{12,4},{14,6},{16,24},{18,... | collective-permute-start | bytes 24584 | tf_op jit(solution)/shard_map/ppermute | solution.py:537
  33.3 11.8 %collective-permute-start.14 = (bf16[768,128]{1,0:T(8,128)(2,1)S(1)}, bf16[768,128]{1,0:T(8,128)(2,1)S(1)}, u32[]{:S(2)}, u32[]{:S(2)}) collective-permute-start(bf16[768,128]{1,0:T(8,128)(2,1)S(1)} %get-tuple-element.35), channel_id=1, source_target_pairs={{0,16},{2,18},{4,20},{6,22},{8,24},{10,26},{12,28},{14,30},{16,0},... | collective-permute-start | bytes 589832 | tf_op jit(solution)/shard_map/ppermute | solution.py:494
  35.3 7.7 %collective-permute-start.15 = (bf16[576,128]{1,0:T(8,128)(2,1)S(1)}, bf16[576,128]{1,0:T(8,128)(2,1)S(1)}, u32[]{:S(2)}, u32[]{:S(2)}) collective-permute-start(bf16[576,128]{1,0:T(8,128)(2,1)S(1)} %get-tuple-element.36), channel_id=1, source_target_pairs={{0,8},{2,10},{4,12},{6,14},{8,0},{10,2},{12,4},{14,6},{16,24},{18,... | collective-permute-start | bytes 442376 | tf_op jit(solution)/shard_map/ppermute | solution.py:494
  35.3 4.3 %collective-permute-start.11 = (f32[8,1536]{1,0:T(8,128)S(1)}, f32[8,1536]{1,0:T(8,128)S(1)}, u32[]{:S(2)}, u32[]{:S(2)}) collective-permute-start(f32[8,1536]{1,0:T(8,128)S(1)} %get-tuple-element.32), channel_id=1, source_target_pairs={{0,2},{2,0},{4,6},{6,4},{8,10},{10,8},{12,14},{14,12},{16,18},{18,... | collective-permute-start | bytes 147464 | tf_op jit(solution)/shard_map/ppermute | solution.py:537
  35.3 4.3 %collective-permute-start.12 = (f32[8,1536]{1,0:T(8,128)S(1)}, f32[8,1536]{1,0:T(8,128)S(1)}, u32[]{:S(2)}, u32[]{:S(2)}) collective-permute-start(f32[8,1536]{1,0:T(8,128)S(1)} %get-tuple-element.33), channel_id=1, source_target_pairs={{0,6},{2,4},{4,2},{6,0},{8,14},{10,12},{12,10},{14,8},{16,22},{18,... | collective-permute-start | bytes 147464 | tf_op jit(solution)/shard_map/ppermute | solution.py:541
  35.9 3.7 %collective-permute-start.13 = (f32[16,128]{1,0:T(8,128)S(1)}, f32[16,128]{1,0:T(8,128)S(1)}, u32[]{:S(2)}, u32[]{:S(2)}) collective-permute-start(f32[16,128]{1,0:T(8,128)S(1)} %get-tuple-element.34.refs_0_), channel_id=1, source_target_pairs={{0,4},{2,6},{4,0},{6,2},{8,12},{10,14},{12,8},{14,10},{16,20},{18,... | collective-permute-start | bytes 24584 | tf_op jit(solution)/shard_map/ppermute | solution.py:537
  43.5 2.8 %copy-start = (bf16[16,16]{1,0:T(8,128)(2,1)S(1)}, bf16[16,16]{1,0:T(8,128)(2,1)}, u32[]{:S(2)}) copy-start(bf16[16,16]{1,0:T(8,128)(2,1)} %panel.3) | copy-start | bytes 1540
  43.5 7.9 %collective-permute-start.17 = (bf16[768,128]{1,0:T(8,128)(2,1)S(1)}, bf16[768,128]{1,0:T(8,128)(2,1)S(1)}, u32[]{:S(2)}, u32[]{:S(2)}) collective-permute-start(bf16[768,128]{1,0:T(8,128)(2,1)S(1)} %filtered_0.1.own), channel_id=1, source_target_pairs={{0,1},{1,0},{2,3},{3,2},{4,5},{5,4},{6,7},{7,6},{8,9},{9,8},{10,11... | collective-permute-start | bytes 589832 | tf_op jit(solution)/shard_map/ppermute | solution.py:619
  45.7 7.8 %collective-permute-start.16 = (bf16[768,128]{1,0:T(8,128)(2,1)S(1)}, bf16[768,128]{1,0:T(8,128)(2,1)S(1)}, u32[]{:S(2)}, u32[]{:S(2)}) collective-permute-start(bf16[768,128]{1,0:T(8,128)(2,1)S(1)} %filtered_1.1.own), channel_id=1, source_target_pairs={{0,1},{1,0},{2,3},{3,2},{4,5},{5,4},{6,7},{7,6},{8,9},{9,8},{10,11... | collective-permute-start | bytes 589832 | tf_op jit(solution)/shard_map/ppermute | solution.py:619

commit v8 on v7

--- a/solution.py
+++ b/solution.py
@@ -241,8 +241,7 @@
     inner_tables(g, dom, v_ref, projf, blk, atom, lut, sums, table)
 
 
-def pack_kernel(g, v_ref, energy, inside, *refs):
-    nx = len(g.face_rows(0))
+def pack_kernel(g, v_ref, energy, *refs):
     dom = lax.axis_index("dom")
     if g.butterfly:
         part, from_x, from_y, from_xy = refs[:4]
@@ -250,12 +249,15 @@
         group[...] = (part[...] + from_x[...]) + (from_y[...] + from_xy[...])
         refs = refs[4:-1]
     first, second = refs[:2]
-    pack_x(g, dom, v_ref, refs[2 : 2 + nx])
-    pack_y(g, dom, v_ref, refs[2 + nx :])
+    pack_y(g, dom, v_ref, refs[2:])
     pack_ends(g, dom, v_ref, first, second)
     if g.butterfly:
         put_table(g, first, group)
         put_table(g, second, group)
+
+
+def pack_x_kernel(g, nafter, v_ref, *refs):
+    pack_x(g, lax.axis_index("dom"), v_ref, refs[nafter:])
 
 
 def inside_kernel(g, scale, subtract, v_ref, pot, *refs):
@@ -336,7 +338,7 @@
                 out[pl.ds(at, g.no), :] = total
 
 
-def add_nonlocal(g, dom, scale, table, energy, projf, blk, atom, lut, spread, out):
+def add_nonlocal(g, dom, table, energy, projf, blk, atom, lut, spread, out):
     size = g.nproj * g.no
     lanes = g.table
     count = g.slots()
@@ -345,7 +347,7 @@
         owner = pl.ds(jnp.clip(dom + step, 0, g.dom_count - 1), 1)
         rows.append(table[owner, :] * energy[owner, :])
     rows.append(jnp.zeros((8 - count, lanes), F32))
-    scaled = (scale / HALF_WIDTH) * jnp.concatenate(rows, axis=0)
+    scaled = jnp.concatenate(rows, axis=0)
     high = scaled.astype(BF16)
     rest = scaled - high.astype(F32)
     mid = rest.astype(BF16)
@@ -391,7 +393,7 @@
     add_ends(g, dom, scale, acc, first, second, out)
     for copy in copies:
         copy.wait()
-    add_nonlocal(g, dom, scale, table, energy, projf, blk, atom, lut, spread, out)
+    add_nonlocal(g, dom, table, energy, projf, blk, atom, lut, spread, out)
 
 
 def middle_kernel(g, acc, projf, blk_hbm, atom_hbm, *refs):
@@ -529,7 +531,6 @@
     slots = g.slots() * g.table
     sums = [pltpu.VMEM((slots, g.cz), F32) for _ in range(4)]
     spread = pltpu.VMEM((slots, g.cz), F32)
-    energy = jnp.repeat(kb_energy.reshape(g.dom_count, g.owned * g.nproj), g.no, axis=1)
     indices = range(g.dom_count)
 
     def swap(array, *strides):
@@ -541,6 +542,8 @@
         return lax.ppermute(array, "dom", pairs)
 
     def local_and_ends(scale, which, values, prev, part):
+        energy = (scale / HALF_WIDTH) * kb_energy
+        energy = jnp.repeat(energy.reshape(g.dom_count, g.owned * g.nproj), g.no, axis=1)
         acc = call(
             functools.partial(inside_kernel, g, scale, len(prev) > 0),
             "inside_" + which,
@@ -549,16 +552,26 @@
             [values, pot, *prev],
             [VMEM] * (2 + len(prev)),
         )
-        inputs = [values, energy, acc]
-        outputs = [ends, ends, *x_faces, *y_faces]
+        inputs = [values, energy]
+        outputs = [ends, ends, *y_faces]
+        after = [acc]
         if g.butterfly:
             inputs += [part, swap(part, g.plane), swap(part, g.third), swap(part, g.plane, g.third)]
             outputs.append(table)
+            after.append(inputs[-2])
+        sent_x = call(
+            functools.partial(pack_x_kernel, g, len(after)),
+            "pack_x_" + which,
+            x_faces,
+            [],
+            [values, *after],
+            [VMEM] * (1 + len(after)),
+        )
+        from_x = swap_faces(g, sent_x, g.plane, g.first)
         first, second, *sent = call(
             functools.partial(pack_kernel, g), "pack_" + which, outputs, [], inputs, [VMEM] * len(inputs)
         )
-        from_x = swap_faces(g, sent[:nx], g.plane, g.first)
-        from_y = swap_faces(g, sent[nx : nx + len(y_faces)], g.third, g.second)
+        from_y = swap_faces(g, sent[: len(y_faces)], g.third, g.second)
         first, second = swap(first, 1), reverse(second)
         tables = [sent[-1], swap(sent[-1], 2)] if g.butterfly else [lax.psum(part, "dom")]
         acc = call(

time: 54.7 us -> 52.4 us (0.958)
  waiting for transfers between devices: 19.4 us -> 17.7 us
  starting transfers between devices: 19.3 us -> 18.4 us
    ppermute x4, waiting for transfers between devices: 1.13 us -> 0.07 us  [shift(): return lax.ppermute(array, 'dom', pairs)]
    ppermute x4, starting transfers between devices: 2.73 us -> 1.78 us  [shift(): return lax.ppermute(array, 'dom', pairs)]
    ppermute x10, waiting for transfers between devices: 12.3 us -> 11.4 us  [swap(): return lax.ppermute(array, 'dom', pairs)]
    ppermute x2, starting transfers between devices: 2.37 us -> 3.27 us  [reverse(): return lax.ppermute(array, 'dom', pairs)]
    ppermute x10, starting transfers between devices: 12 us -> 11.2 us  [swap(): return lax.ppermute(array, 'dom', pairs)]
    pallas_call x13 -> x15, Pallas kernels: 15.3 us -> 15.3 us  [call(): pl.pallas_call(kernel, name=name, out_shape=out_shape, in_specs=specs, ou...]
  transfers between devices with their start and end apart: 18 -> 18, of which waited for: 8 -> 9; matrix products, arithmetic and copies ran while one was open for 1% -> 1% of each run, Pallas kernels for 16% -> 18%
where the time goes in v8:
time: 52.4 us; the launch traced here: 52.2 us
  starting transfers between devices  18.4 us (35%)
  waiting for transfers between devices  17.7 us (34%)
  Pallas kernels  15.3 us (29%)
  local copies, waits for them, and re-layouts  0.61 us (1%)
    pallas_call x15, Pallas kernels, call(): pl.pallas_call(kernel, name=name, out_shape=out_shape, in_specs=specs, ou...  15.3 us
    ppermute x10, waiting for transfers between devices, swap(): return lax.ppermute(array, 'dom', pairs)  11.4 us
    ppermute x10, starting transfers between devices, swap(): return lax.ppermute(array, 'dom', pairs)  11.2 us
    ppermute x2, waiting for transfers between devices, shards(): lax.ppermute(filtered, 'band', [(0, 1), (1, 0)])  6.16 us
    ppermute x2, starting transfers between devices, reverse(): return lax.ppermute(array, 'dom', pairs)  3.27 us
    ppermute x2, starting transfers between devices, shards(): lax.ppermute(filtered, 'band', [(0, 1), (1, 0)])  2.16 us
    ppermute x4, starting transfers between devices, shift(): return lax.ppermute(array, 'dom', pairs)  1.78 us
  transfers between devices with their start and end apart: 18, of which 9 were waited for; matrix products, arithmetic and copies ran while one was open for 1% of the time, Pallas kernels for 18%

profile of v8, /device:TPU:0, one launch (start us, length us, event | category | flops | bytes accessed | tf_op | source)
XLA Modules:
  0.0 52.2 jit_solution(4840945280082617706)
XLA Ops:
  0.0 2.9 %tables_first.1 = (f32[1536,128]{1,0:T(8,128)S(1)}, f32[256,4,128]{2,1,0:T(4,128)S(1)}, f32[192,128]{1,0:T(8,128)S(1)}, f32[16,128]{1,0:T(8,128)S(1)}) custom-call(f32[1536,128]{1,0:T(8,128)} %bitcast.7, bf16[256,4,128]{2,1,0:T(4,128)(2,1)} %proj_hbm.1, f32[192,128]{1,0:T(8,128)} %bitcast.8, s32[256]{0:T(256)} %blk_hbm.7, s32[256]{0:T(256)} %atom_hbm.7), custom_call_target="tpu_custom_call" | custom-call | flops 1000 | bytes 1000 | tf_op jit(solution)/shard_map/tables_first/pallas_call | solution.py:478
  2.9 4.1 %collective-permute-start = (f32[16,128]{1,0:T(8,128)S(1)}, f32[16,128]{1,0:T(8,128)S(1)}, u32[]{:S(2)}, u32[]{:S(2)}) collective-permute-start(f32[16,128]{1,0:T(8,128)S(1)} %get-tuple-element.22.refs_0_), channel_id=1, source_target_pairs={{0,16},{2,18},{4,20},{6,22},{8,24},{10,26},{12,28},{14,30},{16,0},... | collective-permute-start | bytes 24584 | tf_op jit(solution)/shard_map/ppermute | solution.py:538
  7.0 1.6 %collective-permute-start.1 = (f32[16,128]{1,0:T(8,128)S(1)}, f32[16,128]{1,0:T(8,128)S(1)}, u32[]{:S(2)}, u32[]{:S(2)}) collective-permute-start(f32[16,128]{1,0:T(8,128)S(1)} %get-tuple-element.22.refs_0_), channel_id=1, source_target_pairs={{0,8},{2,10},{4,12},{6,14},{8,0},{10,2},{12,4},{14,6},{16,24},{18,... | collective-permute-start | bytes 24584 | tf_op jit(solution)/shard_map/ppermute | solution.py:538
  8.6 0.9 %inside_first.1.acc.refs_0_ = f32[1536,128]{1,0:T(8,128)S(1)} custom-call(f32[1536,128]{1,0:T(8,128)S(1)} %get-tuple-element.19.v_ref.refs_0_, f32[192,128]{1,0:T(8,128)S(1)} %get-tuple-element.20.pot), custom_call_target="tpu_custom_call" | custom-call | flops 1000 | bytes 1000 | tf_op jit(solution)/shard_map/inside_first/pallas_call | solution.py:478
  9.8 0.9 %collective-permute-done.1.refs_2_.refs_1_ = f32[16,128]{1,0:T(8,128)S(1)} collective-permute-done((f32[16,128]{1,0:T(8,128)S(1)}, f32[16,128]{1,0:T(8,128)S(1)}, u32[]{:S(2)}, u32[]{:S(2)}) %collective-permute-start.1) | collective-permute-done | bytes 8224 | tf_op jit(solution)/shard_map/ppermute | solution.py:538
  10.7 1.1 %collective-permute-start.6 = (bf16[768,128]{1,0:T(8,128)(2,1)S(1)}, bf16[768,128]{1,0:T(8,128)(2,1)S(1)}, u32[]{:S(2)}, u32[]{:S(2)}) collective-permute-start(bf16[768,128]{1,0:T(8,128)(2,1)S(1)} %pack_x_first.1), channel_id=1, source_target_pairs={{0,16},{2,18},{4,20},{6,22},{8,24},{10,26},{12,28},{14,30},{16,0},... | collective-permute-start | bytes 589832 | tf_op jit(solution)/shard_map/ppermute | solution.py:496
  11.9 2.4 %collective-permute-done.2.refs_3_ = f32[16,128]{1,0:T(8,128)S(1)} collective-permute-done((f32[16,128]{1,0:T(8,128)S(1)}, f32[16,128]{1,0:T(8,128)S(1)}, u32[]{:S(2)}, u32[]{:S(2)}) %collective-permute-start.2) | collective-permute-done | bytes 8224 | tf_op jit(solution)/shard_map/ppermute | solution.py:538
  14.7 1.6 %collective-permute-start.4 = (f32[8,1536]{1,0:T(8,128)S(1)}, f32[8,1536]{1,0:T(8,128)S(1)}, u32[]{:S(2)}, u32[]{:S(2)}) collective-permute-start(f32[8,1536]{1,0:T(8,128)S(1)} %get-tuple-element.24), channel_id=1, source_target_pairs={{0,6},{2,4},{4,2},{6,0},{8,14},{10,12},{12,10},{14,8},{16,22},{18,... | collective-permute-start | bytes 147464 | tf_op jit(solution)/shard_map/ppermute | solution.py:542
  16.9 3.1 %collective-permute-done.5.refs_1_ = f32[16,128]{1,0:T(8,128)S(1)} collective-permute-done((f32[16,128]{1,0:T(8,128)S(1)}, f32[16,128]{1,0:T(8,128)S(1)}, u32[]{:S(2)}, u32[]{:S(2)}) %collective-permute-start.5) | collective-permute-done | bytes 8224 | tf_op jit(solution)/shard_map/ppermute | solution.py:538
  20.0 2.3 %nonlocal_first.1.acc = f32[1536,128]{1,0:T(8,128)S(1)} custom-call(f32[1536,128]{1,0:T(8,128)S(1)} %inside_first.1.acc.refs_0_, f32[256,4,128]{2,1,0:T(4,128)S(1)} %get-tuple-element.21.projf, f32[16,128]{1,0:T(8,128)S(1)} %copy.12.energy, s32[256]{0:T(256)} %blk_hbm.7, s32[256]{0:T(256)} %atom_hbm.7, f32[8,1536]{1,0:T(8,128)S(1)} %collective-permute-done.3.first, ...), custom_call_target="tpu_custom_call" | custom-call | flops 1000 | bytes 1000 | tf_op jit(solution)/shard_map/nonlocal_first/pallas_call | solution.py:478
  22.3 1.9 %tables_second.1 = (f32[1536,128]{1,0:T(8,128)S(1)}, f32[16,128]{1,0:T(8,128)S(1)}) custom-call(f32[1536,128]{1,0:T(8,128)S(1)} %nonlocal_first.1.acc, f32[256,4,128]{2,1,0:T(4,128)S(1)} %get-tuple-element.21.projf, s32[256]{0:T(256)} %blk_hbm.7, s32[256]{0:T(256)} %atom_hbm.7, bf16[768,128]{1,0:T(8,128)(2,1)S(1)} %collective-permute-done.6.refs_0_, ...), custom_call_target="tpu_custom_call" | custom-call | flops 1000 | bytes 1000 | tf_op jit(solution)/shard_map/tables_second/pallas_call | solution.py:478
  24.2 2.0 %collective-permute-start.9 = (f32[16,128]{1,0:T(8,128)S(1)}, f32[16,128]{1,0:T(8,128)S(1)}, u32[]{:S(2)}, u32[]{:S(2)}) collective-permute-start(f32[16,128]{1,0:T(8,128)S(1)} %get-tuple-element.28.refs_0_), channel_id=1, source_target_pairs={{0,8},{2,10},{4,12},{6,14},{8,0},{10,2},{12,4},{14,6},{16,24},{18,... | collective-permute-start | bytes 24584 | tf_op jit(solution)/shard_map/ppermute | solution.py:538
  26.8 2.1 %collective-permute-start.10 = (f32[16,128]{1,0:T(8,128)S(1)}, f32[16,128]{1,0:T(8,128)S(1)}, u32[]{:S(2)}, u32[]{:S(2)}) collective-permute-start(f32[16,128]{1,0:T(8,128)S(1)} %get-tuple-element.28.refs_0_), channel_id=1, source_target_pairs={{0,24},{2,26},{4,28},{6,30},{8,16},{10,18},{12,20},{14,22},{16,8},... | collective-permute-start | bytes 24584 | tf_op jit(solution)/shard_map/ppermute | solution.py:538
  28.9 1.0 %inside_second.1.acc.refs_0_ = f32[1536,128]{1,0:T(8,128)S(1)} custom-call(f32[1536,128]{1,0:T(8,128)S(1)} %get-tuple-element.27.v_ref, f32[192,128]{1,0:T(8,128)S(1)} %get-tuple-element.20.pot, f32[1536,128]{1,0:T(8,128)S(1)} %get-tuple-element.19.v_ref.refs_0_), custom_call_target="tpu_custom_call" | custom-call | flops 1000 | bytes 1000 | tf_op jit(solution)/shard_map/inside_second/pallas_call | solution.py:478
  31.0 1.5 %collective-permute-done.10.refs_3_ = f32[16,128]{1,0:T(8,128)S(1)} collective-permute-done((f32[16,128]{1,0:T(8,128)S(1)}, f32[16,128]{1,0:T(8,128)S(1)}, u32[]{:S(2)}, u32[]{:S(2)}) %collective-permute-start.10) | collective-permute-done | bytes 8224 | tf_op jit(solution)/shard_map/ppermute | solution.py:538
  32.9 1.6 %collective-permute-start.12 = (f32[8,1536]{1,0:T(8,128)S(1)}, f32[8,1536]{1,0:T(8,128)S(1)}, u32[]{:S(2)}, u32[]{:S(2)}) collective-permute-start(f32[8,1536]{1,0:T(8,128)S(1)} %get-tuple-element.30), channel_id=1, source_target_pairs={{0,6},{2,4},{4,2},{6,0},{8,14},{10,12},{12,10},{14,8},{16,22},{18,... | collective-permute-start | bytes 147464 | tf_op jit(solution)/shard_map/ppermute | solution.py:542
  35.0 3.1 %collective-permute-done.13.refs_1_ = f32[16,128]{1,0:T(8,128)S(1)} collective-permute-done((f32[16,128]{1,0:T(8,128)S(1)}, f32[16,128]{1,0:T(8,128)S(1)}, u32[]{:S(2)}, u32[]{:S(2)}) %collective-permute-start.13) | collective-permute-done | bytes 8224 | tf_op jit(solution)/shard_map/ppermute | solution.py:538
  38.2 2.3 %nonlocal_second.1.acc = f32[1536,128]{1,0:T(8,128)S(1)} custom-call(f32[1536,128]{1,0:T(8,128)S(1)} %inside_second.1.acc.refs_0_, f32[256,4,128]{2,1,0:T(4,128)S(1)} %get-tuple-element.21.projf, f32[16,128]{1,0:T(8,128)S(1)} %copy.16.energy, s32[256]{0:T(256)} %blk_hbm.7, s32[256]{0:T(256)} %atom_hbm.7, f32[8,1536]{1,0:T(8,128)S(1)} %collective-permute-done.11.first, ...), custom_call_target="tpu_custom_call" | custom-call | flops 1000 | bytes 1000 | tf_op jit(solution)/shard_map/nonlocal_second/pallas_call | solution.py:478
  40.9 1.6 %collective-permute-start.17 = (bf16[768,128]{1,0:T(8,128)(2,1)S(1)}, bf16[768,128]{1,0:T(8,128)(2,1)S(1)}, u32[]{:S(2)}, u32[]{:S(2)}) collective-permute-start(bf16[768,128]{1,0:T(8,128)(2,1)S(1)} %filtered_0.1.own), channel_id=1, source_target_pairs={{0,1},{1,0},{2,3},{3,2},{4,5},{5,4},{6,7},{7,6},{8,9},{9,8},{10,11... | collective-permute-start | bytes 589832 | tf_op jit(solution)/shard_map/ppermute | solution.py:632
  42.5 0.7 %filtered_1.1.own = bf16[768,128]{1,0:T(8,128)(2,1)S(1)} custom-call(f32[1536,128]{1,0:T(8,128)S(1)} %nonlocal_second.1.acc, bf16[768,128]{1,0:T(8,128)(2,1)S(1)} %collective-permute-done.14.refs_0_, bf16[576,128]{1,0:T(8,128)(2,1)S(1)} %collective-permute-done.15.refs_1_.refs_0_), custom_call_target="tpu_custom_call" | custom-call | flops 1000 | bytes 1000 | tf_op jit(solution)/shard_map/filtered_1/pallas_call | solution.py:478
  44.1 4.8 %collective-permute-done.17.other = bf16[768,128]{1,0:T(8,128)(2,1)S(1)} collective-permute-done((bf16[768,128]{1,0:T(8,128)(2,1)S(1)}, bf16[768,128]{1,0:T(8,128)(2,1)S(1)}, u32[]{:S(2)}, u32[]{:S(2)}) %collective-permute-start.17) | collective-permute-done | bytes 196640 | tf_op jit(solution)/shard_map/ppermute | solution.py:632
  48.9 1.0 %rotate_0.1.refs_0_ = f32[8,192,128]{2,1,0:T(8,128)} custom-call(bf16[768,128]{1,0:T(8,128)(2,1)S(1)} %filtered_0.1.own, bf16[768,128]{1,0:T(8,128)(2,1)S(1)} %collective-permute-done.17.other, bf16[128,256]{1,0:T(8,128)(2,1)S(1)} %panel.2.weights), custom_call_target="tpu_custom_call" | custom-call | flops 1000 | bytes 1000 | tf_op jit(solution)/shard_map/rotate_0/pallas_call | solution.py:478
  49.8 1.4 %collective-permute-done.16.other = bf16[768,128]{1,0:T(8,128)(2,1)S(1)} collective-permute-done((bf16[768,128]{1,0:T(8,128)(2,1)S(1)}, bf16[768,128]{1,0:T(8,128)(2,1)S(1)}, u32[]{:S(2)}, u32[]{:S(2)}) %collective-permute-start.16) | collective-permute-done | bytes 196640 | tf_op jit(solution)/shard_map/ppermute | solution.py:632
  51.2 1.0 %rotate_1.1 = f32[8,192,128]{2,1,0:T(8,128)} custom-call(bf16[768,128]{1,0:T(8,128)(2,1)S(1)} %filtered_1.1.own, bf16[768,128]{1,0:T(8,128)(2,1)S(1)} %collective-permute-done.16.other, bf16[128,256]{1,0:T(8,128)(2,1)S(1)} %panel.2.weights, f32[8,192,128]{2,1,0:T(8,128)} %rotate_0.1.refs_0_), custom_call_target="tpu_custom_call", output_to_operand_aliasing={{}: (3, {})} | custom-call | flops 1000 | bytes 1000 | tf_op jit(solution)/shard_map/rotate_1/pallas_call | solution.py:478
  (42 shorter events, 5.3 us)
Async XLA Ops:
  0.0 8.6 %copy-start.1 = (f32[64,4]{0,1:T(4,128)S(1)}, f32[64,4]{0,1:T(4,128)}, u32[]{:S(2)}) copy-start(f32[64,4]{0,1:T(4,128)} %param.12) | copy-start | bytes 3076
  2.9 8.9 %collective-permute-start = (f32[16,128]{1,0:T(8,128)S(1)}, f32[16,128]{1,0:T(8,128)S(1)}, u32[]{:S(2)}, u32[]{:S(2)}) collective-permute-start(f32[16,128]{1,0:T(8,128)S(1)} %get-tuple-element.22.refs_0_), channel_id=1, source_target_pairs={{0,16},{2,18},{4,20},{6,22},{8,24},{10,26},{12,28},{14,30},{16,0},... | collective-permute-start | bytes 24584 | tf_op jit(solution)/shard_map/ppermute | solution.py:538
  7.0 3.7 %collective-permute-start.1 = (f32[16,128]{1,0:T(8,128)S(1)}, f32[16,128]{1,0:T(8,128)S(1)}, u32[]{:S(2)}, u32[]{:S(2)}) collective-permute-start(f32[16,128]{1,0:T(8,128)S(1)} %get-tuple-element.22.refs_0_), channel_id=1, source_target_pairs={{0,8},{2,10},{4,12},{6,14},{8,0},{10,2},{12,4},{14,6},{16,24},{18,... | collective-permute-start | bytes 24584 | tf_op jit(solution)/shard_map/ppermute | solution.py:538
  8.6 5.6 %collective-permute-start.2 = (f32[16,128]{1,0:T(8,128)S(1)}, f32[16,128]{1,0:T(8,128)S(1)}, u32[]{:S(2)}, u32[]{:S(2)}) collective-permute-start(f32[16,128]{1,0:T(8,128)S(1)} %get-tuple-element.22.refs_0_), channel_id=1, source_target_pairs={{0,24},{2,26},{4,28},{6,30},{8,16},{10,18},{12,20},{14,22},{16,8},... | collective-permute-start | bytes 24584 | tf_op jit(solution)/shard_map/ppermute | solution.py:538
  10.7 11.6 %collective-permute-start.6 = (bf16[768,128]{1,0:T(8,128)(2,1)S(1)}, bf16[768,128]{1,0:T(8,128)(2,1)S(1)}, u32[]{:S(2)}, u32[]{:S(2)}) collective-permute-start(bf16[768,128]{1,0:T(8,128)(2,1)S(1)} %pack_x_first.1), channel_id=1, source_target_pairs={{0,16},{2,18},{4,20},{6,22},{8,24},{10,26},{12,28},{14,30},{16,0},... | collective-permute-start | bytes 589832 | tf_op jit(solution)/shard_map/ppermute | solution.py:496
  14.6 7.7 %collective-permute-start.7 = (bf16[576,128]{1,0:T(8,128)(2,1)S(1)}, bf16[576,128]{1,0:T(8,128)(2,1)S(1)}, u32[]{:S(2)}, u32[]{:S(2)}) collective-permute-start(bf16[576,128]{1,0:T(8,128)(2,1)S(1)} %get-tuple-element.26), channel_id=1, source_target_pairs={{0,8},{2,10},{4,12},{6,14},{8,0},{10,2},{12,4},{14,6},{16,24},{18,... | collective-permute-start | bytes 442376 | tf_op jit(solution)/shard_map/ppermute | solution.py:496
  14.7 5.3 %collective-permute-start.3 = (f32[8,1536]{1,0:T(8,128)S(1)}, f32[8,1536]{1,0:T(8,128)S(1)}, u32[]{:S(2)}, u32[]{:S(2)}) collective-permute-start(f32[8,1536]{1,0:T(8,128)S(1)} %get-tuple-element.23), channel_id=1, source_target_pairs={{0,2},{2,0},{4,6},{6,4},{8,10},{10,8},{12,14},{14,12},{16,18},{18,... | collective-permute-start | bytes 147464 | tf_op jit(solution)/shard_map/ppermute | solution.py:538
  14.7 5.3 %collective-permute-start.4 = (f32[8,1536]{1,0:T(8,128)S(1)}, f32[8,1536]{1,0:T(8,128)S(1)}, u32[]{:S(2)}, u32[]{:S(2)}) collective-permute-start(f32[8,1536]{1,0:T(8,128)S(1)} %get-tuple-element.24), channel_id=1, source_target_pairs={{0,6},{2,4},{4,2},{6,0},{8,14},{10,12},{12,10},{14,8},{16,22},{18,... | collective-permute-start | bytes 147464 | tf_op jit(solution)/shard_map/ppermute | solution.py:542
  16.3 3.7 %collective-permute-start.5 = (f32[16,128]{1,0:T(8,128)S(1)}, f32[16,128]{1,0:T(8,128)S(1)}, u32[]{:S(2)}, u32[]{:S(2)}) collective-permute-start(f32[16,128]{1,0:T(8,128)S(1)} %get-tuple-element.25.refs_0_), channel_id=1, source_target_pairs={{0,4},{2,6},{4,0},{6,2},{8,12},{10,14},{12,8},{14,10},{16,20},{18,... | collective-permute-start | bytes 24584 | tf_op jit(solution)/shard_map/ppermute | solution.py:538
  24.2 5.7 %collective-permute-start.9 = (f32[16,128]{1,0:T(8,128)S(1)}, f32[16,128]{1,0:T(8,128)S(1)}, u32[]{:S(2)}, u32[]{:S(2)}) collective-permute-start(f32[16,128]{1,0:T(8,128)S(1)} %get-tuple-element.28.refs_0_), channel_id=1, source_target_pairs={{0,8},{2,10},{4,12},{6,14},{8,0},{10,2},{12,4},{14,6},{16,24},{18,... | collective-permute-start | bytes 24584 | tf_op jit(solution)/shard_map/ppermute | solution.py:538
  26.4 4.6 %collective-permute-start.8 = (f32[16,128]{1,0:T(8,128)S(1)}, f32[16,128]{1,0:T(8,128)S(1)}, u32[]{:S(2)}, u32[]{:S(2)}) collective-permute-start(f32[16,128]{1,0:T(8,128)S(1)} %get-tuple-element.28.refs_0_), channel_id=1, source_target_pairs={{0,16},{2,18},{4,20},{6,22},{8,24},{10,26},{12,28},{14,30},{16,0},... | collective-permute-start | bytes 24584 | tf_op jit(solution)/shard_map/ppermute | solution.py:538
  26.8 5.6 %collective-permute-start.10 = (f32[16,128]{1,0:T(8,128)S(1)}, f32[16,128]{1,0:T(8,128)S(1)}, u32[]{:S(2)}, u32[]{:S(2)}) collective-permute-start(f32[16,128]{1,0:T(8,128)S(1)} %get-tuple-element.28.refs_0_), channel_id=1, source_target_pairs={{0,24},{2,26},{4,28},{6,30},{8,16},{10,18},{12,20},{14,22},{16,8},... | collective-permute-start | bytes 24584 | tf_op jit(solution)/shard_map/ppermute | solution.py:538
  30.0 12.6 %collective-permute-start.14 = (bf16[768,128]{1,0:T(8,128)(2,1)S(1)}, bf16[768,128]{1,0:T(8,128)(2,1)S(1)}, u32[]{:S(2)}, u32[]{:S(2)}) collective-permute-start(bf16[768,128]{1,0:T(8,128)(2,1)S(1)} %pack_x_second.1), channel_id=1, source_target_pairs={{0,16},{2,18},{4,20},{6,22},{8,24},{10,26},{12,28},{14,30},{16,0},... | collective-permute-start | bytes 589832 | tf_op jit(solution)/shard_map/ppermute | solution.py:496
  32.8 7.8 %collective-permute-start.15 = (bf16[576,128]{1,0:T(8,128)(2,1)S(1)}, bf16[576,128]{1,0:T(8,128)(2,1)S(1)}, u32[]{:S(2)}, u32[]{:S(2)}) collective-permute-start(bf16[576,128]{1,0:T(8,128)(2,1)S(1)} %get-tuple-element.32), channel_id=1, source_target_pairs={{0,8},{2,10},{4,12},{6,14},{8,0},{10,2},{12,4},{14,6},{16,24},{18,... | collective-permute-start | bytes 442376 | tf_op jit(solution)/shard_map/ppermute | solution.py:496
  32.8 5.4 %collective-permute-start.11 = (f32[8,1536]{1,0:T(8,128)S(1)}, f32[8,1536]{1,0:T(8,128)S(1)}, u32[]{:S(2)}, u32[]{:S(2)}) collective-permute-start(f32[8,1536]{1,0:T(8,128)S(1)} %get-tuple-element.29), channel_id=1, source_target_pairs={{0,2},{2,0},{4,6},{6,4},{8,10},{10,8},{12,14},{14,12},{16,18},{18,... | collective-permute-start | bytes 147464 | tf_op jit(solution)/shard_map/ppermute | solution.py:538
  32.9 5.3 %collective-permute-start.12 = (f32[8,1536]{1,0:T(8,128)S(1)}, f32[8,1536]{1,0:T(8,128)S(1)}, u32[]{:S(2)}, u32[]{:S(2)}) collective-permute-start(f32[8,1536]{1,0:T(8,128)S(1)} %get-tuple-element.30), channel_id=1, source_target_pairs={{0,6},{2,4},{4,2},{6,0},{8,14},{10,12},{12,10},{14,8},{16,22},{18,... | collective-permute-start | bytes 147464 | tf_op jit(solution)/shard_map/ppermute | solution.py:542
  34.5 3.7 %collective-permute-start.13 = (f32[16,128]{1,0:T(8,128)S(1)}, f32[16,128]{1,0:T(8,128)S(1)}, u32[]{:S(2)}, u32[]{:S(2)}) collective-permute-start(f32[16,128]{1,0:T(8,128)S(1)} %get-tuple-element.31.refs_0_), channel_id=1, source_target_pairs={{0,4},{2,6},{4,0},{6,2},{8,12},{10,14},{12,8},{14,10},{16,20},{18,... | collective-permute-start | bytes 24584 | tf_op jit(solution)/shard_map/ppermute | solution.py:538
  40.9 2.8 %copy-start = (bf16[16,16]{1,0:T(8,128)(2,1)S(1)}, bf16[16,16]{1,0:T(8,128)(2,1)}, u32[]{:S(2)}) copy-start(bf16[16,16]{1,0:T(8,128)(2,1)} %panel.3) | copy-start | bytes 1540
  40.9 7.9 %collective-permute-start.17 = (bf16[768,128]{1,0:T(8,128)(2,1)S(1)}, bf16[768,128]{1,0:T(8,128)(2,1)S(1)}, u32[]{:S(2)}, u32[]{:S(2)}) collective-permute-start(bf16[768,128]{1,0:T(8,128)(2,1)S(1)} %filtered_0.1.own), channel_id=1, source_target_pairs={{0,1},{1,0},{2,3},{3,2},{4,5},{5,4},{6,7},{7,6},{8,9},{9,8},{10,11... | collective-permute-start | bytes 589832 | tf_op jit(solution)/shard_map/ppermute | solution.py:632
  43.2 8.0 %collective-permute-start.16 = (bf16[768,128]{1,0:T(8,128)(2,1)S(1)}, bf16[768,128]{1,0:T(8,128)(2,1)S(1)}, u32[]{:S(2)}, u32[]{:S(2)}) collective-permute-start(bf16[768,128]{1,0:T(8,128)(2,1)S(1)} %filtered_1.1.own), channel_id=1, source_target_pairs={{0,1},{1,0},{2,3},{3,2},{4,5},{5,4},{6,7},{7,6},{8,9},{9,8},{10,11... | collective-permute-start | bytes 589832 | tf_op jit(solution)/shard_map/ppermute | solution.py:632

commit v9 on v8

--- a/solution.py
+++ b/solution.py
@@ -241,15 +241,14 @@
     inner_tables(g, dom, v_ref, projf, blk, atom, lut, sums, table)
 
 
-def pack_kernel(g, v_ref, energy, *refs):
+def pack_kernel(g, v_ref, *refs):
     dom = lax.axis_index("dom")
     if g.butterfly:
         part, from_x, from_y, from_xy = refs[:4]
         group = refs[-1]
         group[...] = (part[...] + from_x[...]) + (from_y[...] + from_xy[...])
-        refs = refs[4:-1]
-    first, second = refs[:2]
-    pack_y(g, dom, v_ref, refs[2:])
+        refs = refs[:-1]
+    first, second = refs[-2:]
     pack_ends(g, dom, v_ref, first, second)
     if g.butterfly:
         put_table(g, first, group)
@@ -258,6 +257,10 @@
 
 def pack_x_kernel(g, nafter, v_ref, *refs):
     pack_x(g, lax.axis_index("dom"), v_ref, refs[nafter:])
+
+
+def pack_y_kernel(g, nafter, v_ref, *refs):
+    pack_y(g, lax.axis_index("dom"), v_ref, refs[nafter:])
 
 
 def inside_kernel(g, scale, subtract, v_ref, pot, *refs):
@@ -552,27 +555,35 @@
             [values, pot, *prev],
             [VMEM] * (2 + len(prev)),
         )
-        inputs = [values, energy]
-        outputs = [ends, ends, *y_faces]
-        after = [acc]
+
+        def layers(dim, shapes, after):
+            kernel = (pack_x_kernel, pack_y_kernel)[dim]
+            return call(
+                functools.partial(kernel, g, len(after)),
+                "pack_%s_%s" % ("xy"[dim], which),
+                shapes,
+                [],
+                [values, *after],
+                [VMEM] * (1 + len(after)),
+            )
+
+        inputs = [values]
+        outputs = [ends, ends]
         if g.butterfly:
             inputs += [part, swap(part, g.plane), swap(part, g.third), swap(part, g.plane, g.third)]
             outputs.append(table)
-            after.append(inputs[-2])
-        sent_x = call(
-            functools.partial(pack_x_kernel, g, len(after)),
-            "pack_x_" + which,
-            x_faces,
-            [],
-            [values, *after],
-            [VMEM] * (1 + len(after)),
-        )
-        from_x = swap_faces(g, sent_x, g.plane, g.first)
+        if not prev:
+            sent_x = layers(0, x_faces, inputs[-2:-1])
+            inputs += [energy]
         first, second, *sent = call(
             functools.partial(pack_kernel, g), "pack_" + which, outputs, [], inputs, [VMEM] * len(inputs)
         )
-        from_y = swap_faces(g, sent[: len(y_faces)], g.third, g.second)
+        sent_first = first
         first, second = swap(first, 1), reverse(second)
+        from_y = swap_faces(g, layers(1, y_faces, [first if prev else sent_first]), g.third, g.second)
+        if prev:
+            sent_x = layers(0, x_faces, [first])
+        from_x = swap_faces(g, sent_x, g.plane, g.first)
         tables = [sent[-1], swap(sent[-1], 2)] if g.butterfly else [lax.psum(part, "dom")]
         acc = call(
             functools.partial(nonlocal_kernel, g, scale),

time: 52.4 us -> 54.3 us (1.036)
  starting transfers between devices: 18.4 us -> 21.7 us
  waiting for transfers between devices: 17.7 us -> 16.3 us
    ppermute x4, waiting for transfers between devices: 0.07 us -> 5.08 us  [shift(): return lax.ppermute(array, 'dom', pairs)]
    ppermute x10, waiting for transfers between devices: 11.4 us -> 8.12 us  [swap(): return lax.ppermute(array, 'dom', pairs)]
    ppermute x2, waiting for transfers between devices: 6.16 us -> 3.07 us  [shards(): lax.ppermute(filtered, 'band', [(0, 1), (1, 0)])]
    ppermute x4, starting transfers between devices: 1.78 us -> 4.07 us  [shift(): return lax.ppermute(array, 'dom', pairs)]
    ppermute x10, starting transfers between devices: 11.2 us -> 12.2 us  [swap(): return lax.ppermute(array, 'dom', pairs)]
    ppermute x2, starting transfers between devices: 3.27 us -> 2.28 us  [reverse(): return lax.ppermute(array, 'dom', pairs)]
    ppermute x2, starting transfers between devices: 2.16 us -> 3.13 us  [shards(): lax.ppermute(filtered, 'band', [(0, 1), (1, 0)])]
    pallas_call x15 -> x17, Pallas kernels: 15.3 us -> 15.4 us  [call(): pl.pallas_call(kernel, name=name, out_shape=out_shape, in_specs=specs, ou...]
  transfers between devices with their start and end apart: 18 -> 18, of which waited for: 9 -> 8; matrix products, arithmetic and copies ran while one was open for 1% -> 1% of each run, Pallas kernels for 18% -> 17%
where the time goes in v9:
time: 54.3 us; the launch traced here: 54.1 us
  starting transfers between devices  21.7 us (40%)
  waiting for transfers between devices  16.3 us (30%)
  Pallas kernels  15.4 us (28%)
  local copies, waits for them, and re-layouts  0.61 us (1%)
    pallas_call x17, Pallas kernels, call(): pl.pallas_call(kernel, name=name, out_shape=out_shape, in_specs=specs, ou...  15.4 us
    ppermute x10, starting transfers between devices, swap(): return lax.ppermute(array, 'dom', pairs)  12.2 us
    ppermute x10, waiting for transfers between devices, swap(): return lax.ppermute(array, 'dom', pairs)  8.12 us
    ppermute x4, waiting for transfers between devices, shift(): return lax.ppermute(array, 'dom', pairs)  5.08 us
    ppermute x4, starting transfers between devices, shift(): return lax.ppermute(array, 'dom', pairs)  4.07 us
    ppermute x2, starting transfers between devices, shards(): lax.ppermute(filtered, 'band', [(0, 1), (1, 0)])  3.13 us
    ppermute x2, waiting for transfers between devices, shards(): lax.ppermute(filtered, 'band', [(0, 1), (1, 0)])  3.07 us
    ppermute x2, starting transfers between devices, reverse(): return lax.ppermute(array, 'dom', pairs)  2.28 us
  transfers between devices with their start and end apart: 18, of which 8 were waited for; matrix products, arithmetic and copies ran while one was open for 1% of the time, Pallas kernels for 17%

profile of v9, /device:TPU:0, one launch (start us, length us, event | category | flops | bytes accessed | tf_op | source)
XLA Modules:
  0.0 54.1 jit_solution(10705327492393161399)
XLA Ops:
  0.0 2.9 %tables_first.1 = (f32[1536,128]{1,0:T(8,128)S(1)}, f32[256,4,128]{2,1,0:T(4,128)S(1)}, f32[192,128]{1,0:T(8,128)S(1)}, f32[16,128]{1,0:T(8,128)S(1)}) custom-call(f32[1536,128]{1,0:T(8,128)} %bitcast.7, bf16[256,4,128]{2,1,0:T(4,128)(2,1)} %proj_hbm.1, f32[192,128]{1,0:T(8,128)} %bitcast.8, s32[256]{0:T(256)} %blk_hbm.7, s32[256]{0:T(256)} %atom_hbm.7), custom_call_target="tpu_custom_call" | custom-call | flops 1000 | bytes 1000 | tf_op jit(solution)/shard_map/tables_first/pallas_call | solution.py:481
  2.9 3.1 %collective-permute-start.1 = (f32[16,128]{1,0:T(8,128)S(1)}, f32[16,128]{1,0:T(8,128)S(1)}, u32[]{:S(2)}, u32[]{:S(2)}) collective-permute-start(f32[16,128]{1,0:T(8,128)S(1)} %get-tuple-element.20.refs_0_), channel_id=1, source_target_pairs={{0,8},{2,10},{4,12},{6,14},{8,0},{10,2},{12,4},{14,6},{16,24},{18,... | collective-permute-start | bytes 24584 | tf_op jit(solution)/shard_map/ppermute | solution.py:541
  6.0 2.6 %collective-permute-start = (f32[16,128]{1,0:T(8,128)S(1)}, f32[16,128]{1,0:T(8,128)S(1)}, u32[]{:S(2)}, u32[]{:S(2)}) collective-permute-start(f32[16,128]{1,0:T(8,128)S(1)} %get-tuple-element.20.refs_0_), channel_id=1, source_target_pairs={{0,16},{2,18},{4,20},{6,22},{8,24},{10,26},{12,28},{14,30},{16,0},... | collective-permute-start | bytes 24584 | tf_op jit(solution)/shard_map/ppermute | solution.py:541
  8.9 2.0 %collective-permute-start.6 = (bf16[768,128]{1,0:T(8,128)(2,1)S(1)}, bf16[768,128]{1,0:T(8,128)(2,1)S(1)}, u32[]{:S(2)}, u32[]{:S(2)}) collective-permute-start(bf16[768,128]{1,0:T(8,128)(2,1)S(1)} %pack_x_first.1), channel_id=1, source_target_pairs={{0,16},{2,18},{4,20},{6,22},{8,24},{10,26},{12,28},{14,30},{16,0},... | collective-permute-start | bytes 589832 | tf_op jit(solution)/shard_map/ppermute | solution.py:499
  10.9 3.3 %collective-permute-done.2.refs_3_ = f32[16,128]{1,0:T(8,128)S(1)} collective-permute-done((f32[16,128]{1,0:T(8,128)S(1)}, f32[16,128]{1,0:T(8,128)S(1)}, u32[]{:S(2)}, u32[]{:S(2)}) %collective-permute-start.2) | collective-permute-done | bytes 8224 | tf_op jit(solution)/shard_map/ppermute | solution.py:541
  14.7 1.6 %collective-permute-start.4 = (f32[8,1536]{1,0:T(8,128)S(1)}, f32[8,1536]{1,0:T(8,128)S(1)}, u32[]{:S(2)}, u32[]{:S(2)}) collective-permute-start(f32[8,1536]{1,0:T(8,128)S(1)} %get-tuple-element.22), channel_id=1, source_target_pairs={{0,6},{2,4},{4,2},{6,0},{8,14},{10,12},{12,10},{14,8},{16,22},{18,... | collective-permute-start | bytes 147464 | tf_op jit(solution)/shard_map/ppermute | solution.py:545
  17.8 2.2 %collective-permute-done.5.refs_1_ = f32[16,128]{1,0:T(8,128)S(1)} collective-permute-done((f32[16,128]{1,0:T(8,128)S(1)}, f32[16,128]{1,0:T(8,128)S(1)}, u32[]{:S(2)}, u32[]{:S(2)}) %collective-permute-start.5) | collective-permute-done | bytes 8224 | tf_op jit(solution)/shard_map/ppermute | solution.py:541
  20.0 2.3 %nonlocal_first.1.acc = f32[1536,128]{1,0:T(8,128)S(1)} custom-call(f32[1536,128]{1,0:T(8,128)S(1)} %inside_first.1.acc, f32[256,4,128]{2,1,0:T(4,128)S(1)} %get-tuple-element.19.projf, f32[16,128]{1,0:T(8,128)S(1)} %copy.12.refs_4_.energy, s32[256]{0:T(256)} %blk_hbm.7, s32[256]{0:T(256)} %atom_hbm.7, f32[8,1536]{1,0:T(8,128)S(1)} %collective-permute-done.3.first, ...), custom_call_target="tpu_custom_call" | custom-call | flops 1000 | bytes 1000 | tf_op jit(solution)/shard_map/nonlocal_first/pallas_call | solution.py:481
  22.3 1.9 %tables_second.1 = (f32[1536,128]{1,0:T(8,128)S(1)}, f32[16,128]{1,0:T(8,128)S(1)}) custom-call(f32[1536,128]{1,0:T(8,128)S(1)} %nonlocal_first.1.acc, f32[256,4,128]{2,1,0:T(4,128)S(1)} %get-tuple-element.19.projf, s32[256]{0:T(256)} %blk_hbm.7, s32[256]{0:T(256)} %atom_hbm.7, bf16[768,128]{1,0:T(8,128)(2,1)S(1)} %collective-permute-done.6.refs_0_, ...), custom_call_target="tpu_custom_call" | custom-call | flops 1000 | bytes 1000 | tf_op jit(solution)/shard_map/tables_second/pallas_call | solution.py:481
  24.2 1.3 %collective-permute-start.10 = (f32[16,128]{1,0:T(8,128)S(1)}, f32[16,128]{1,0:T(8,128)S(1)}, u32[]{:S(2)}, u32[]{:S(2)}) collective-permute-start(f32[16,128]{1,0:T(8,128)S(1)} %get-tuple-element.25.refs_0_), channel_id=1, source_target_pairs={{0,24},{2,26},{4,28},{6,30},{8,16},{10,18},{12,20},{14,22},{16,8},... | collective-permute-start | bytes 24584 | tf_op jit(solution)/shard_map/ppermute | solution.py:541
  25.5 2.2 %collective-permute-start.8 = (f32[16,128]{1,0:T(8,128)S(1)}, f32[16,128]{1,0:T(8,128)S(1)}, u32[]{:S(2)}, u32[]{:S(2)}) collective-permute-start(f32[16,128]{1,0:T(8,128)S(1)} %get-tuple-element.25.refs_0_), channel_id=1, source_target_pairs={{0,16},{2,18},{4,20},{6,22},{8,24},{10,26},{12,28},{14,30},{16,0},... | collective-permute-start | bytes 24584 | tf_op jit(solution)/shard_map/ppermute | solution.py:541
  27.7 1.0 %collective-permute-start.9 = (f32[16,128]{1,0:T(8,128)S(1)}, f32[16,128]{1,0:T(8,128)S(1)}, u32[]{:S(2)}, u32[]{:S(2)}) collective-permute-start(f32[16,128]{1,0:T(8,128)S(1)} %get-tuple-element.25.refs_0_), channel_id=1, source_target_pairs={{0,8},{2,10},{4,12},{6,14},{8,0},{10,2},{12,4},{14,6},{16,24},{18,... | collective-permute-start | bytes 24584 | tf_op jit(solution)/shard_map/ppermute | solution.py:541
  28.7 1.1 %collective-permute-done.10.refs_3_ = f32[16,128]{1,0:T(8,128)S(1)} collective-permute-done((f32[16,128]{1,0:T(8,128)S(1)}, f32[16,128]{1,0:T(8,128)S(1)}, u32[]{:S(2)}, u32[]{:S(2)}) %collective-permute-start.10) | collective-permute-done | bytes 8224 | tf_op jit(solution)/shard_map/ppermute | solution.py:541
  30.0 1.3 %collective-permute-done.9.refs_2_ = f32[16,128]{1,0:T(8,128)S(1)} collective-permute-done((f32[16,128]{1,0:T(8,128)S(1)}, f32[16,128]{1,0:T(8,128)S(1)}, u32[]{:S(2)}, u32[]{:S(2)}) %collective-permute-start.9) | collective-permute-done | bytes 8224 | tf_op jit(solution)/shard_map/ppermute | solution.py:541
  32.5 1.5 %collective-permute-start.13 = (f32[16,128]{1,0:T(8,128)S(1)}, f32[16,128]{1,0:T(8,128)S(1)}, u32[]{:S(2)}, u32[]{:S(2)}) collective-permute-start(f32[16,128]{1,0:T(8,128)S(1)} %get-tuple-element.28.refs_0_), channel_id=1, source_target_pairs={{0,4},{2,6},{4,0},{6,2},{8,12},{10,14},{12,8},{14,10},{16,20},{18,... | collective-permute-start | bytes 24584 | tf_op jit(solution)/shard_map/ppermute | solution.py:541
  34.1 1.1 %collective-permute-start.15 = (bf16[576,128]{1,0:T(8,128)(2,1)S(1)}, bf16[576,128]{1,0:T(8,128)(2,1)S(1)}, u32[]{:S(2)}, u32[]{:S(2)}) collective-permute-start(bf16[576,128]{1,0:T(8,128)(2,1)S(1)} %pack_y_second.1), channel_id=1, source_target_pairs={{0,8},{2,10},{4,12},{6,14},{8,0},{10,2},{12,4},{14,6},{16,24},{18,... | collective-permute-start | bytes 442376 | tf_op jit(solution)/shard_map/ppermute | solution.py:499
  36.2 1.0 %inside_second.1.acc = f32[1536,128]{1,0:T(8,128)S(1)} custom-call(f32[1536,128]{1,0:T(8,128)S(1)} %get-tuple-element.24.v_ref, f32[192,128]{1,0:T(8,128)S(1)} %get-tuple-element.18.pot, f32[1536,128]{1,0:T(8,128)S(1)} %get-tuple-element.17.v_ref.refs_0_), custom_call_target="tpu_custom_call" | custom-call | flops 1000 | bytes 1000 | tf_op jit(solution)/shard_map/inside_second/pallas_call | solution.py:481
  37.2 2.3 %nonlocal_second.1.acc = f32[1536,128]{1,0:T(8,128)S(1)} custom-call(f32[1536,128]{1,0:T(8,128)S(1)} %inside_second.1.acc, f32[256,4,128]{2,1,0:T(4,128)S(1)} %get-tuple-element.19.projf, f32[16,128]{1,0:T(8,128)S(1)} %copy.15.energy, s32[256]{0:T(256)} %blk_hbm.7, s32[256]{0:T(256)} %atom_hbm.7, f32[8,1536]{1,0:T(8,128)S(1)} %collective-permute-done.11.first.refs_0_, ...), custom_call_target="tpu_custom_call" | custom-call | flops 1000 | bytes 1000 | tf_op jit(solution)/shard_map/nonlocal_second/pallas_call | solution.py:481
  39.5 2.0 %collective-permute-done.15.refs_1_.refs_0_ = bf16[576,128]{1,0:T(8,128)(2,1)S(1)} collective-permute-done((bf16[576,128]{1,0:T(8,128)(2,1)S(1)}, bf16[576,128]{1,0:T(8,128)(2,1)S(1)}, u32[]{:S(2)}, u32[]{:S(2)}) %collective-permute-start.15) | collective-permute-done | bytes 147488 | tf_op jit(solution)/shard_map/ppermute | solution.py:499
  42.0 1.6 %collective-permute-start.17 = (bf16[768,128]{1,0:T(8,128)(2,1)S(1)}, bf16[768,128]{1,0:T(8,128)(2,1)S(1)}, u32[]{:S(2)}, u32[]{:S(2)}) collective-permute-start(bf16[768,128]{1,0:T(8,128)(2,1)S(1)} %filtered_0.1.own), channel_id=1, source_target_pairs={{0,1},{1,0},{2,3},{3,2},{4,5},{5,4},{6,7},{7,6},{8,9},{9,8},{10,11... | collective-permute-start | bytes 589832 | tf_op jit(solution)/shard_map/ppermute | solution.py:643
  43.6 3.1 %collective-permute-done.14.refs_0_ = bf16[768,128]{1,0:T(8,128)(2,1)S(1)} collective-permute-done((bf16[768,128]{1,0:T(8,128)(2,1)S(1)}, bf16[768,128]{1,0:T(8,128)(2,1)S(1)}, u32[]{:S(2)}, u32[]{:S(2)}) %collective-permute-start.14) | collective-permute-done | bytes 196640 | tf_op jit(solution)/shard_map/ppermute | solution.py:499
  47.3 1.6 %collective-permute-start.16 = (bf16[768,128]{1,0:T(8,128)(2,1)S(1)}, bf16[768,128]{1,0:T(8,128)(2,1)S(1)}, u32[]{:S(2)}, u32[]{:S(2)}) collective-permute-start(bf16[768,128]{1,0:T(8,128)(2,1)S(1)} %filtered_1.1.own), channel_id=1, source_target_pairs={{0,1},{1,0},{2,3},{3,2},{4,5},{5,4},{6,7},{7,6},{8,9},{9,8},{10,11... | collective-permute-start | bytes 589832 | tf_op jit(solution)/shard_map/ppermute | solution.py:643
  49.1 1.0 %rotate_0.1.refs_0_ = f32[8,192,128]{2,1,0:T(8,128)} custom-call(bf16[768,128]{1,0:T(8,128)(2,1)S(1)} %filtered_0.1.own, bf16[768,128]{1,0:T(8,128)(2,1)S(1)} %collective-permute-done.17.other, bf16[128,256]{1,0:T(8,128)(2,1)S(1)} %panel.2.weights), custom_call_target="tpu_custom_call" | custom-call | flops 1000 | bytes 1000 | tf_op jit(solution)/shard_map/rotate_0/pallas_call | solution.py:481
  50.1 3.1 %collective-permute-done.16.other = bf16[768,128]{1,0:T(8,128)(2,1)S(1)} collective-permute-done((bf16[768,128]{1,0:T(8,128)(2,1)S(1)}, bf16[768,128]{1,0:T(8,128)(2,1)S(1)}, u32[]{:S(2)}, u32[]{:S(2)}) %collective-permute-start.16) | collective-permute-done | bytes 196640 | tf_op jit(solution)/shard_map/ppermute | solution.py:643
  (44 shorter events, 7.2 us)
Async XLA Ops:
  0.0 8.6 %copy-start.1 = (f32[64,4]{0,1:T(4,128)S(1)}, f32[64,4]{0,1:T(4,128)}, u32[]{:S(2)}) copy-start(f32[64,4]{0,1:T(4,128)} %param.12) | copy-start | bytes 3076
  2.9 5.9 %collective-permute-start.1 = (f32[16,128]{1,0:T(8,128)S(1)}, f32[16,128]{1,0:T(8,128)S(1)}, u32[]{:S(2)}, u32[]{:S(2)}) collective-permute-start(f32[16,128]{1,0:T(8,128)S(1)} %get-tuple-element.20.refs_0_), channel_id=1, source_target_pairs={{0,8},{2,10},{4,12},{6,14},{8,0},{10,2},{12,4},{14,6},{16,24},{18,... | collective-permute-start | bytes 24584 | tf_op jit(solution)/shard_map/ppermute | solution.py:541
  6.0 4.9 %collective-permute-start = (f32[16,128]{1,0:T(8,128)S(1)}, f32[16,128]{1,0:T(8,128)S(1)}, u32[]{:S(2)}, u32[]{:S(2)}) collective-permute-start(f32[16,128]{1,0:T(8,128)S(1)} %get-tuple-element.20.refs_0_), channel_id=1, source_target_pairs={{0,16},{2,18},{4,20},{6,22},{8,24},{10,26},{12,28},{14,30},{16,0},... | collective-permute-start | bytes 24584 | tf_op jit(solution)/shard_map/ppermute | solution.py:541
  8.6 5.6 %collective-permute-start.2 = (f32[16,128]{1,0:T(8,128)S(1)}, f32[16,128]{1,0:T(8,128)S(1)}, u32[]{:S(2)}, u32[]{:S(2)}) collective-permute-start(f32[16,128]{1,0:T(8,128)S(1)} %get-tuple-element.20.refs_0_), channel_id=1, source_target_pairs={{0,24},{2,26},{4,28},{6,30},{8,16},{10,18},{12,20},{14,22},{16,8},... | collective-permute-start | bytes 24584 | tf_op jit(solution)/shard_map/ppermute | solution.py:541
  8.9 13.4 %collective-permute-start.6 = (bf16[768,128]{1,0:T(8,128)(2,1)S(1)}, bf16[768,128]{1,0:T(8,128)(2,1)S(1)}, u32[]{:S(2)}, u32[]{:S(2)}) collective-permute-start(bf16[768,128]{1,0:T(8,128)(2,1)S(1)} %pack_x_first.1), channel_id=1, source_target_pairs={{0,16},{2,18},{4,20},{6,22},{8,24},{10,26},{12,28},{14,30},{16,0},... | collective-permute-start | bytes 589832 | tf_op jit(solution)/shard_map/ppermute | solution.py:499
  14.5 7.7 %collective-permute-start.7 = (bf16[576,128]{1,0:T(8,128)(2,1)S(1)}, bf16[576,128]{1,0:T(8,128)(2,1)S(1)}, u32[]{:S(2)}, u32[]{:S(2)}) collective-permute-start(bf16[576,128]{1,0:T(8,128)(2,1)S(1)} %pack_y_first.1), channel_id=1, source_target_pairs={{0,8},{2,10},{4,12},{6,14},{8,0},{10,2},{12,4},{14,6},{16,24},{18,... | collective-permute-start | bytes 442376 | tf_op jit(solution)/shard_map/ppermute | solution.py:499
  14.6 5.4 %collective-permute-start.3 = (f32[8,1536]{1,0:T(8,128)S(1)}, f32[8,1536]{1,0:T(8,128)S(1)}, u32[]{:S(2)}, u32[]{:S(2)}) collective-permute-start(f32[8,1536]{1,0:T(8,128)S(1)} %get-tuple-element.21.refs_0_), channel_id=1, source_target_pairs={{0,2},{2,0},{4,6},{6,4},{8,10},{10,8},{12,14},{14,12},{16,18},{18,... | collective-permute-start | bytes 147464 | tf_op jit(solution)/shard_map/ppermute | solution.py:541
  14.7 5.3 %collective-permute-start.4 = (f32[8,1536]{1,0:T(8,128)S(1)}, f32[8,1536]{1,0:T(8,128)S(1)}, u32[]{:S(2)}, u32[]{:S(2)}) collective-permute-start(f32[8,1536]{1,0:T(8,128)S(1)} %get-tuple-element.22), channel_id=1, source_target_pairs={{0,6},{2,4},{4,2},{6,0},{8,14},{10,12},{12,10},{14,8},{16,22},{18,... | collective-permute-start | bytes 147464 | tf_op jit(solution)/shard_map/ppermute | solution.py:545
  16.3 3.7 %collective-permute-start.5 = (f32[16,128]{1,0:T(8,128)S(1)}, f32[16,128]{1,0:T(8,128)S(1)}, u32[]{:S(2)}, u32[]{:S(2)}) collective-permute-start(f32[16,128]{1,0:T(8,128)S(1)} %get-tuple-element.23.refs_0_), channel_id=1, source_target_pairs={{0,4},{2,6},{4,0},{6,2},{8,12},{10,14},{12,8},{14,10},{16,20},{18,... | collective-permute-start | bytes 24584 | tf_op jit(solution)/shard_map/ppermute | solution.py:541
  24.2 5.5 %collective-permute-start.10 = (f32[16,128]{1,0:T(8,128)S(1)}, f32[16,128]{1,0:T(8,128)S(1)}, u32[]{:S(2)}, u32[]{:S(2)}) collective-permute-start(f32[16,128]{1,0:T(8,128)S(1)} %get-tuple-element.25.refs_0_), channel_id=1, source_target_pairs={{0,24},{2,26},{4,28},{6,30},{8,16},{10,18},{12,20},{14,22},{16,8},... | collective-permute-start | bytes 24584 | tf_op jit(solution)/shard_map/ppermute | solution.py:541
  25.5 4.5 %collective-permute-start.8 = (f32[16,128]{1,0:T(8,128)S(1)}, f32[16,128]{1,0:T(8,128)S(1)}, u32[]{:S(2)}, u32[]{:S(2)}) collective-permute-start(f32[16,128]{1,0:T(8,128)S(1)} %get-tuple-element.25.refs_0_), channel_id=1, source_target_pairs={{0,16},{2,18},{4,20},{6,22},{8,24},{10,26},{12,28},{14,30},{16,0},... | collective-permute-start | bytes 24584 | tf_op jit(solution)/shard_map/ppermute | solution.py:541
  27.7 3.7 %collective-permute-start.9 = (f32[16,128]{1,0:T(8,128)S(1)}, f32[16,128]{1,0:T(8,128)S(1)}, u32[]{:S(2)}, u32[]{:S(2)}) collective-permute-start(f32[16,128]{1,0:T(8,128)S(1)} %get-tuple-element.25.refs_0_), channel_id=1, source_target_pairs={{0,8},{2,10},{4,12},{6,14},{8,0},{10,2},{12,4},{14,6},{16,24},{18,... | collective-permute-start | bytes 24584 | tf_op jit(solution)/shard_map/ppermute | solution.py:541
  31.6 2.4 %collective-permute-start.11 = (f32[8,1536]{1,0:T(8,128)S(1)}, f32[8,1536]{1,0:T(8,128)S(1)}, u32[]{:S(2)}, u32[]{:S(2)}) collective-permute-start(f32[8,1536]{1,0:T(8,128)S(1)} %get-tuple-element.26), channel_id=1, source_target_pairs={{0,2},{2,0},{4,6},{6,4},{8,10},{10,8},{12,14},{14,12},{16,18},{18,... | collective-permute-start | bytes 147464 | tf_op jit(solution)/shard_map/ppermute | solution.py:541
  31.9 5.3 %collective-permute-start.12 = (f32[8,1536]{1,0:T(8,128)S(1)}, f32[8,1536]{1,0:T(8,128)S(1)}, u32[]{:S(2)}, u32[]{:S(2)}) collective-permute-start(f32[8,1536]{1,0:T(8,128)S(1)} %get-tuple-element.27), channel_id=1, source_target_pairs={{0,6},{2,4},{4,2},{6,0},{8,14},{10,12},{12,10},{14,8},{16,22},{18,... | collective-permute-start | bytes 147464 | tf_op jit(solution)/shard_map/ppermute | solution.py:545
  32.5 4.7 %collective-permute-start.13 = (f32[16,128]{1,0:T(8,128)S(1)}, f32[16,128]{1,0:T(8,128)S(1)}, u32[]{:S(2)}, u32[]{:S(2)}) collective-permute-start(f32[16,128]{1,0:T(8,128)S(1)} %get-tuple-element.28.refs_0_), channel_id=1, source_target_pairs={{0,4},{2,6},{4,0},{6,2},{8,12},{10,14},{12,8},{14,10},{16,20},{18,... | collective-permute-start | bytes 24584 | tf_op jit(solution)/shard_map/ppermute | solution.py:541
  34.1 7.4 %collective-permute-start.15 = (bf16[576,128]{1,0:T(8,128)(2,1)S(1)}, bf16[576,128]{1,0:T(8,128)(2,1)S(1)}, u32[]{:S(2)}, u32[]{:S(2)}) collective-permute-start(bf16[576,128]{1,0:T(8,128)(2,1)S(1)} %pack_y_second.1), channel_id=1, source_target_pairs={{0,8},{2,10},{4,12},{6,14},{8,0},{10,2},{12,4},{14,6},{16,24},{18,... | collective-permute-start | bytes 442376 | tf_op jit(solution)/shard_map/ppermute | solution.py:499
  35.2 11.4 %collective-permute-start.14 = (bf16[768,128]{1,0:T(8,128)(2,1)S(1)}, bf16[768,128]{1,0:T(8,128)(2,1)S(1)}, u32[]{:S(2)}, u32[]{:S(2)}) collective-permute-start(bf16[768,128]{1,0:T(8,128)(2,1)S(1)} %pack_x_second.1), channel_id=1, source_target_pairs={{0,16},{2,18},{4,20},{6,22},{8,24},{10,26},{12,28},{14,30},{16,0},... | collective-permute-start | bytes 589832 | tf_op jit(solution)/shard_map/ppermute | solution.py:499
  42.0 6.9 %copy-start = (bf16[16,16]{1,0:T(8,128)(2,1)S(1)}, bf16[16,16]{1,0:T(8,128)(2,1)}, u32[]{:S(2)}) copy-start(bf16[16,16]{1,0:T(8,128)(2,1)} %panel.3) | copy-start | bytes 1540
  42.0 7.1 %collective-permute-start.17 = (bf16[768,128]{1,0:T(8,128)(2,1)S(1)}, bf16[768,128]{1,0:T(8,128)(2,1)S(1)}, u32[]{:S(2)}, u32[]{:S(2)}) collective-permute-start(bf16[768,128]{1,0:T(8,128)(2,1)S(1)} %filtered_0.1.own), channel_id=1, source_target_pairs={{0,1},{1,0},{2,3},{3,2},{4,5},{5,4},{6,7},{7,6},{8,9},{9,8},{10,11... | collective-permute-start | bytes 589832 | tf_op jit(solution)/shard_map/ppermute | solution.py:643
  47.3 5.9 %collective-permute-start.16 = (bf16[768,128]{1,0:T(8,128)(2,1)S(1)}, bf16[768,128]{1,0:T(8,128)(2,1)S(1)}, u32[]{:S(2)}, u32[]{:S(2)}) collective-permute-start(bf16[768,128]{1,0:T(8,128)(2,1)S(1)} %filtered_1.1.own), channel_id=1, source_target_pairs={{0,1},{1,0},{2,3},{3,2},{4,5},{5,4},{6,7},{7,6},{8,9},{9,8},{10,11... | collective-permute-start | bytes 589832 | tf_op jit(solution)/shard_map/ppermute | solution.py:643

commit v10 on v8

--- a/solution.py
+++ b/solution.py
@@ -241,19 +241,29 @@
     inner_tables(g, dom, v_ref, projf, blk, atom, lut, sums, table)
 
 
-def pack_kernel(g, v_ref, energy, *refs):
+def add_kernel(g, a, b, *refs):
+    refs[-1][...] = a[...] + b[...]
+
+
+def pack_kernel(g, v_ref, *refs):
     dom = lax.axis_index("dom")
+    ny = len(g.face_rows(1))
     if g.butterfly:
-        part, from_x, from_y, from_xy = refs[:4]
+        a, b = refs[:2]
         group = refs[-1]
-        group[...] = (part[...] + from_x[...]) + (from_y[...] + from_xy[...])
-        refs = refs[4:-1]
-    first, second = refs[:2]
-    pack_y(g, dom, v_ref, refs[2:])
-    pack_ends(g, dom, v_ref, first, second)
+        group[...] = a[...] + b[...]
+        refs = refs[:-1]
+    inner, outer = refs[len(refs) - ny - 2 : len(refs) - ny]
+    pack_y(g, dom, v_ref, refs[len(refs) - ny :])
+    pack_ends(g, dom, v_ref, inner, outer)
     if g.butterfly:
-        put_table(g, first, group)
-        put_table(g, second, group)
+        put_table(g, outer, group)
+
+
+def join_kernel(g, table, outer_in, inner, table_out, inner_out):
+    table_out[...] = table[...] + get_table(g, outer_in)
+    inner_out[...] = inner[...]
+    put_table(g, inner_out, table_out)
 
 
 def pack_x_kernel(g, nafter, v_ref, *refs):
@@ -385,11 +395,9 @@
     copies = entry_copies(blk_hbm, atom_hbm, blk, atom, sem)
     dom = lax.axis_index("dom")
     fill_lut(g, dom, lut)
+    table[...] = refs[0][...]
     if g.butterfly:
-        group, opposite = refs[:2]
-        table[...] = (group[...] + get_table(g, first)) + (get_table(g, second) + opposite[...])
-    else:
-        table[...] = refs[0][...]
+        table[...] += get_table(g, first)
     add_ends(g, dom, scale, acc, first, second, out)
     for copy in copies:
         copy.wait()
@@ -552,13 +560,21 @@
             [values, pot, *prev],
             [VMEM] * (2 + len(prev)),
         )
-        inputs = [values, energy]
+        inputs = [values]
         outputs = [ends, ends, *y_faces]
         after = [acc]
         if g.butterfly:
-            inputs += [part, swap(part, g.plane), swap(part, g.third), swap(part, g.plane, g.third)]
+            part = call(
+                functools.partial(add_kernel, g),
+                "pair_" + which,
+                table,
+                [],
+                [part, swap(part, g.third), acc],
+                [VMEM] * 3,
+            )
+            inputs += [part, swap(part, g.plane)]
             outputs.append(table)
-            after.append(inputs[-2])
+            after = [part]
         sent_x = call(
             functools.partial(pack_x_kernel, g, len(after)),
             "pack_x_" + which,
@@ -568,18 +584,29 @@
             [VMEM] * (1 + len(after)),
         )
         from_x = swap_faces(g, sent_x, g.plane, g.first)
-        first, second, *sent = call(
+        inputs.append(energy)
+        inner, outer, *sent = call(
             functools.partial(pack_kernel, g), "pack_" + which, outputs, [], inputs, [VMEM] * len(inputs)
         )
+        outer = reverse(outer)
         from_y = swap_faces(g, sent[: len(y_faces)], g.third, g.second)
-        first, second = swap(first, 1), reverse(second)
-        tables = [sent[-1], swap(sent[-1], 2)] if g.butterfly else [lax.psum(part, "dom")]
+        if g.butterfly:
+            part, inner = call(
+                functools.partial(join_kernel, g),
+                "join_" + which,
+                [table, ends],
+                [],
+                [sent[-1], outer, inner],
+                [VMEM] * 3,
+            )
+        inner = swap(inner, 1)
+        tables = [part] if g.butterfly else [lax.psum(part, "dom")]
         acc = call(
             functools.partial(nonlocal_kernel, g, scale),
             "nonlocal_" + which,
             field,
             [pltpu.VMEM(table.shape, F32), *entries, spread],
-            [acc, projf, energy, blk, atom, first, second, *tables],
+            [acc, projf, energy, blk, atom, inner, outer, *tables],
             [VMEM] * 3 + [HBM] * 2 + [VMEM] * (2 + len(tables)),
         )
         return acc, from_x + from_y

time: 52.4 us -> 54 us (1.031); the launches traced: 52.2 us -> 53 us
  waiting for transfers between devices: 17.7 us -> 22.9 us
  starting transfers between devices: 18.4 us -> 14 us
    ppermute x2, waiting for transfers between devices: 0.01 us -> 7.7 us  [reverse(): return lax.ppermute(array, 'dom', pairs)]
    ppermute x10 -> x6, waiting for transfers between devices: 11.4 us -> 8.03 us  [swap(): return lax.ppermute(array, 'dom', pairs)]
    ppermute x2, starting transfers between devices: 3.27 us -> 0.01 us  [reverse(): return lax.ppermute(array, 'dom', pairs)]
    ppermute x10 -> x6, starting transfers between devices: 11.2 us -> 9.31 us  [swap(): return lax.ppermute(array, 'dom', pairs)]
    ppermute x4, waiting for transfers between devices: 0.07 us -> 1.29 us  [shift(): return lax.ppermute(array, 'dom', pairs)]
    ppermute x4, starting transfers between devices: 1.78 us -> 2.57 us  [shift(): return lax.ppermute(array, 'dom', pairs)]
    pallas_call x15 -> x19, Pallas kernels: 15.3 us -> 15.3 us  [call(): pl.pallas_call(kernel, name=name, out_shape=out_shape, in_specs=specs, ou...]
  transfers between devices with their start and end apart: 18 -> 14, of which waited for: 9 -> 11; matrix products, arithmetic and copies ran while one was open for 1% -> 1% of each run, Pallas kernels for 18% -> 18%
where the time goes in v10:
time: 54 us; the launch traced here: 53 us
  waiting for transfers between devices  22.9 us (42%)
  Pallas kernels  15.3 us (28%)
  starting transfers between devices  14 us (26%)
  local copies, waits for them, and re-layouts  0.61 us (1%)
    pallas_call x19, Pallas kernels, call(): pl.pallas_call(kernel, name=name, out_shape=out_shape, in_specs=specs, ou...  15.3 us
    ppermute x6, starting transfers between devices, swap(): return lax.ppermute(array, 'dom', pairs)  9.31 us
    ppermute x6, waiting for transfers between devices, swap(): return lax.ppermute(array, 'dom', pairs)  8.03 us
    ppermute x2, waiting for transfers between devices, reverse(): return lax.ppermute(array, 'dom', pairs)  7.7 us
    ppermute x2, waiting for transfers between devices, shards(): lax.ppermute(filtered, 'band', [(0, 1), (1, 0)])  5.9 us
    ppermute x4, starting transfers between devices, shift(): return lax.ppermute(array, 'dom', pairs)  2.57 us
    ppermute x2, starting transfers between devices, shards(): lax.ppermute(filtered, 'band', [(0, 1), (1, 0)])  2.16 us
    ppermute x4, waiting for transfers between devices, shift(): return lax.ppermute(array, 'dom', pairs)  1.29 us
  transfers between devices with their start and end apart: 14, of which 11 were waited for; matrix products, arithmetic and copies ran while one was open for 1% of the time, Pallas kernels for 18%

profile of v10, /device:TPU:0, one launch (start us, length us, event | category | flops | bytes accessed | tf_op | source)
XLA Modules:
  0.0 53.0 jit_solution(8118227708272206963)
XLA Ops:
  0.0 2.9 %tables_first.1 = (f32[1536,128]{1,0:T(8,128)S(1)}, f32[256,4,128]{2,1,0:T(4,128)S(1)}, f32[192,128]{1,0:T(8,128)S(1)}, f32[16,128]{1,0:T(8,128)S(1)}) custom-call(f32[1536,128]{1,0:T(8,128)} %bitcast.7, bf16[256,4,128]{2,1,0:T(4,128)(2,1)} %proj_hbm.1, f32[192,128]{1,0:T(8,128)} %bitcast.8, s32[256]{0:T(256)} %blk_hbm.7, s32[256]{0:T(256)} %atom_hbm.7), custom_call_target="tpu_custom_call" | custom-call | flops 1000 | bytes 1000 | tf_op jit(solution)/shard_map/tables_first/pallas_call | solution.py:486
  2.9 3.1 %collective-permute-start = (f32[16,128]{1,0:T(8,128)S(1)}, f32[16,128]{1,0:T(8,128)S(1)}, u32[]{:S(2)}, u32[]{:S(2)}) collective-permute-start(f32[16,128]{1,0:T(8,128)S(1)} %get-tuple-element.26.a), channel_id=1, source_target_pairs={{0,8},{2,10},{4,12},{6,14},{8,0},{10,2},{12,4},{14,6},{16,24},{18,... | collective-permute-start | bytes 24584 | tf_op jit(solution)/shard_map/ppermute | solution.py:546
  6.0 0.9 %inside_first.1.refs_0_.acc = f32[1536,128]{1,0:T(8,128)S(1)} custom-call(f32[1536,128]{1,0:T(8,128)S(1)} %get-tuple-element.23.v_ref.refs_0_, f32[192,128]{1,0:T(8,128)S(1)} %get-tuple-element.24.pot), custom_call_target="tpu_custom_call" | custom-call | flops 1000 | bytes 1000 | tf_op jit(solution)/shard_map/inside_first/pallas_call | solution.py:486
  7.6 3.0 %collective-permute-start.1 = (f32[16,128]{1,0:T(8,128)S(1)}, f32[16,128]{1,0:T(8,128)S(1)}, u32[]{:S(2)}, u32[]{:S(2)}) collective-permute-start(f32[16,128]{1,0:T(8,128)S(1)} %pair_first.1.refs_0_), channel_id=1, source_target_pairs={{0,16},{2,18},{4,20},{6,22},{8,24},{10,26},{12,28},{14,30},{16,0},... | collective-permute-start | bytes 24584 | tf_op jit(solution)/shard_map/ppermute | solution.py:546
  10.8 1.5 %collective-permute-done.1.refs_1_ = f32[16,128]{1,0:T(8,128)S(1)} collective-permute-done((f32[16,128]{1,0:T(8,128)S(1)}, f32[16,128]{1,0:T(8,128)S(1)}, u32[]{:S(2)}, u32[]{:S(2)}) %collective-permute-start.1) | collective-permute-done | bytes 8224 | tf_op jit(solution)/shard_map/ppermute | solution.py:546
  12.6 2.0 %collective-permute-start.5 = (bf16[576,128]{1,0:T(8,128)(2,1)S(1)}, bf16[576,128]{1,0:T(8,128)(2,1)S(1)}, u32[]{:S(2)}, u32[]{:S(2)}) collective-permute-start(bf16[576,128]{1,0:T(8,128)(2,1)S(1)} %get-tuple-element.32), channel_id=1, source_target_pairs={{0,8},{2,10},{4,12},{6,14},{8,0},{10,2},{12,4},{14,6},{16,24},{18,... | collective-permute-start | bytes 442376 | tf_op jit(solution)/shard_map/ppermute | solution.py:504
  14.7 4.0 %collective-permute-done.2.outer_in.second = f32[8,1536]{1,0:T(8,128)S(1)} collective-permute-done((f32[8,1536]{1,0:T(8,128)S(1)}, f32[8,1536]{1,0:T(8,128)S(1)}, u32[]{:S(2)}, u32[]{:S(2)}) %collective-permute-start.2) | collective-permute-done | bytes 49184 | tf_op jit(solution)/shard_map/ppermute | solution.py:550
  18.9 1.0 %collective-permute-done.3.first = f32[8,1536]{1,0:T(8,128)S(1)} collective-permute-done((f32[8,1536]{1,0:T(8,128)S(1)}, f32[8,1536]{1,0:T(8,128)S(1)}, u32[]{:S(2)}, u32[]{:S(2)}) %collective-permute-start.3) | collective-permute-done | bytes 49184 | tf_op jit(solution)/shard_map/ppermute | solution.py:546
  19.9 2.3 %nonlocal_first.1.acc = f32[1536,128]{1,0:T(8,128)S(1)} custom-call(f32[1536,128]{1,0:T(8,128)S(1)} %inside_first.1.refs_0_.acc, f32[256,4,128]{2,1,0:T(4,128)S(1)} %get-tuple-element.25.projf, f32[16,128]{1,0:T(8,128)S(1)} %copy.12.refs_2_.energy, s32[256]{0:T(256)} %blk_hbm.7, s32[256]{0:T(256)} %atom_hbm.7, f32[8,1536]{1,0:T(8,128)S(1)} %collective-permute-done.3.first, ...), custom_call_target="tpu_custom_call" | custom-call | flops 1000 | bytes 1000 | tf_op jit(solution)/shard_map/nonlocal_first/pallas_call | solution.py:486
  22.2 1.9 %tables_second.1 = (f32[1536,128]{1,0:T(8,128)S(1)}, f32[16,128]{1,0:T(8,128)S(1)}) custom-call(f32[1536,128]{1,0:T(8,128)S(1)} %nonlocal_first.1.acc, f32[256,4,128]{2,1,0:T(4,128)S(1)} %get-tuple-element.25.projf, s32[256]{0:T(256)} %blk_hbm.7, s32[256]{0:T(256)} %atom_hbm.7, bf16[768,128]{1,0:T(8,128)(2,1)S(1)} %collective-permute-done.4.refs_0_, ...), custom_call_target="tpu_custom_call" | custom-call | flops 1000 | bytes 1000 | tf_op jit(solution)/shard_map/tables_second/pallas_call | solution.py:486
  24.5 1.0 %inside_second.1.refs_0_.acc = f32[1536,128]{1,0:T(8,128)S(1)} custom-call(f32[1536,128]{1,0:T(8,128)S(1)} %get-tuple-element.33.v_ref, f32[192,128]{1,0:T(8,128)S(1)} %get-tuple-element.24.pot, f32[1536,128]{1,0:T(8,128)S(1)} %get-tuple-element.23.v_ref.refs_0_), custom_call_target="tpu_custom_call" | custom-call | flops 1000 | bytes 1000 | tf_op jit(solution)/shard_map/inside_second/pallas_call | solution.py:486
  25.5 2.4 %collective-permute-done.6.b = f32[16,128]{1,0:T(8,128)S(1)} collective-permute-done((f32[16,128]{1,0:T(8,128)S(1)}, f32[16,128]{1,0:T(8,128)S(1)}, u32[]{:S(2)}, u32[]{:S(2)}) %collective-permute-start.6) | collective-permute-done | bytes 8224 | tf_op jit(solution)/shard_map/ppermute | solution.py:546
  27.9 2.8 %collective-permute-start.7 = (f32[16,128]{1,0:T(8,128)S(1)}, f32[16,128]{1,0:T(8,128)S(1)}, u32[]{:S(2)}, u32[]{:S(2)}) collective-permute-start(f32[16,128]{1,0:T(8,128)S(1)} %pair_second.1.refs_0_), channel_id=1, source_target_pairs={{0,16},{2,18},{4,20},{6,22},{8,24},{10,26},{12,28},{14,30},{16,0},... | collective-permute-start | bytes 24584 | tf_op jit(solution)/shard_map/ppermute | solution.py:546
  30.9 1.5 %collective-permute-done.7.refs_1_ = f32[16,128]{1,0:T(8,128)S(1)} collective-permute-done((f32[16,128]{1,0:T(8,128)S(1)}, f32[16,128]{1,0:T(8,128)S(1)}, u32[]{:S(2)}, u32[]{:S(2)}) %collective-permute-start.7) | collective-permute-done | bytes 8224 | tf_op jit(solution)/shard_map/ppermute | solution.py:546
  33.0 3.7 %collective-permute-done.8.outer_in.second = f32[8,1536]{1,0:T(8,128)S(1)} collective-permute-done((f32[8,1536]{1,0:T(8,128)S(1)}, f32[8,1536]{1,0:T(8,128)S(1)}, u32[]{:S(2)}, u32[]{:S(2)}) %collective-permute-start.8) | collective-permute-done | bytes 49184 | tf_op jit(solution)/shard_map/ppermute | solution.py:550
  36.9 1.2 %collective-permute-done.9.first = f32[8,1536]{1,0:T(8,128)S(1)} collective-permute-done((f32[8,1536]{1,0:T(8,128)S(1)}, f32[8,1536]{1,0:T(8,128)S(1)}, u32[]{:S(2)}, u32[]{:S(2)}) %collective-permute-start.9) | collective-permute-done | bytes 49184 | tf_op jit(solution)/shard_map/ppermute | solution.py:546
  38.1 2.3 %nonlocal_second.1.acc = f32[1536,128]{1,0:T(8,128)S(1)} custom-call(f32[1536,128]{1,0:T(8,128)S(1)} %inside_second.1.refs_0_.acc, f32[256,4,128]{2,1,0:T(4,128)S(1)} %get-tuple-element.25.projf, f32[16,128]{1,0:T(8,128)S(1)} %copy.16.refs_2_.energy, s32[256]{0:T(256)} %blk_hbm.7, s32[256]{0:T(256)} %atom_hbm.7, f32[8,1536]{1,0:T(8,128)S(1)} %collective-permute-done.9.first, ...), custom_call_target="tpu_custom_call" | custom-call | flops 1000 | bytes 1000 | tf_op jit(solution)/shard_map/nonlocal_second/pallas_call | solution.py:486
  40.4 1.3 %collective-permute-done.11.refs_1_.refs_0_ = bf16[576,128]{1,0:T(8,128)(2,1)S(1)} collective-permute-done((bf16[576,128]{1,0:T(8,128)(2,1)S(1)}, bf16[576,128]{1,0:T(8,128)(2,1)S(1)}, u32[]{:S(2)}, u32[]{:S(2)}) %collective-permute-start.11) | collective-permute-done | bytes 147488 | tf_op jit(solution)/shard_map/ppermute | solution.py:504
  42.1 1.5 %collective-permute-start.13 = (bf16[768,128]{1,0:T(8,128)(2,1)S(1)}, bf16[768,128]{1,0:T(8,128)(2,1)S(1)}, u32[]{:S(2)}, u32[]{:S(2)}) collective-permute-start(bf16[768,128]{1,0:T(8,128)(2,1)S(1)} %filtered_0.1.own), channel_id=1, source_target_pairs={{0,1},{1,0},{2,3},{3,2},{4,5},{5,4},{6,7},{7,6},{8,9},{9,8},{10,11... | collective-permute-start | bytes 589832 | tf_op jit(solution)/shard_map/ppermute | solution.py:659
  43.6 0.7 %filtered_1.1.own = bf16[768,128]{1,0:T(8,128)(2,1)S(1)} custom-call(f32[1536,128]{1,0:T(8,128)S(1)} %nonlocal_second.1.acc, bf16[768,128]{1,0:T(8,128)(2,1)S(1)} %collective-permute-done.10.refs_0_, bf16[576,128]{1,0:T(8,128)(2,1)S(1)} %collective-permute-done.11.refs_1_.refs_0_), custom_call_target="tpu_custom_call" | custom-call | flops 1000 | bytes 1000 | tf_op jit(solution)/shard_map/filtered_1/pallas_call | solution.py:486
  45.2 4.8 %collective-permute-done.13.other = bf16[768,128]{1,0:T(8,128)(2,1)S(1)} collective-permute-done((bf16[768,128]{1,0:T(8,128)(2,1)S(1)}, bf16[768,128]{1,0:T(8,128)(2,1)S(1)}, u32[]{:S(2)}, u32[]{:S(2)}) %collective-permute-start.13) | collective-permute-done | bytes 196640 | tf_op jit(solution)/shard_map/ppermute | solution.py:659
  50.0 1.0 %rotate_0.1.refs_0_ = f32[8,192,128]{2,1,0:T(8,128)} custom-call(bf16[768,128]{1,0:T(8,128)(2,1)S(1)} %filtered_0.1.own, bf16[768,128]{1,0:T(8,128)(2,1)S(1)} %collective-permute-done.13.other, bf16[128,256]{1,0:T(8,128)(2,1)S(1)} %panel.2.weights), custom_call_target="tpu_custom_call" | custom-call | flops 1000 | bytes 1000 | tf_op jit(solution)/shard_map/rotate_0/pallas_call | solution.py:486
  50.9 1.1 %collective-permute-done.12.other = bf16[768,128]{1,0:T(8,128)(2,1)S(1)} collective-permute-done((bf16[768,128]{1,0:T(8,128)(2,1)S(1)}, bf16[768,128]{1,0:T(8,128)(2,1)S(1)}, u32[]{:S(2)}, u32[]{:S(2)}) %collective-permute-start.12) | collective-permute-done | bytes 196640 | tf_op jit(solution)/shard_map/ppermute | solution.py:659
  52.1 1.0 %rotate_1.1 = f32[8,192,128]{2,1,0:T(8,128)} custom-call(bf16[768,128]{1,0:T(8,128)(2,1)S(1)} %filtered_1.1.own, bf16[768,128]{1,0:T(8,128)(2,1)S(1)} %collective-permute-done.12.other, bf16[128,256]{1,0:T(8,128)(2,1)S(1)} %panel.2.weights, f32[8,192,128]{2,1,0:T(8,128)} %rotate_0.1.refs_0_), custom_call_target="tpu_custom_call", output_to_operand_aliasing={{}: (3, {})} | custom-call | flops 1000 | bytes 1000 | tf_op jit(solution)/shard_map/rotate_1/pallas_call | solution.py:486
  (38 shorter events, 4.1 us)
Async XLA Ops:
  0.0 6.0 %copy-start.1 = (f32[64,4]{0,1:T(4,128)S(1)}, f32[64,4]{0,1:T(4,128)}, u32[]{:S(2)}) copy-start(f32[64,4]{0,1:T(4,128)} %param.12) | copy-start | bytes 3076
  2.9 4.7 %collective-permute-start = (f32[16,128]{1,0:T(8,128)S(1)}, f32[16,128]{1,0:T(8,128)S(1)}, u32[]{:S(2)}, u32[]{:S(2)}) collective-permute-start(f32[16,128]{1,0:T(8,128)S(1)} %get-tuple-element.26.a), channel_id=1, source_target_pairs={{0,8},{2,10},{4,12},{6,14},{8,0},{10,2},{12,4},{14,6},{16,24},{18,... | collective-permute-start | bytes 24584 | tf_op jit(solution)/shard_map/ppermute | solution.py:546
  7.6 4.7 %collective-permute-start.1 = (f32[16,128]{1,0:T(8,128)S(1)}, f32[16,128]{1,0:T(8,128)S(1)}, u32[]{:S(2)}, u32[]{:S(2)}) collective-permute-start(f32[16,128]{1,0:T(8,128)S(1)} %pair_first.1.refs_0_), channel_id=1, source_target_pairs={{0,16},{2,18},{4,20},{6,22},{8,24},{10,26},{12,28},{14,30},{16,0},... | collective-permute-start | bytes 24584 | tf_op jit(solution)/shard_map/ppermute | solution.py:546
  10.7 11.5 %collective-permute-start.4 = (bf16[768,128]{1,0:T(8,128)(2,1)S(1)}, bf16[768,128]{1,0:T(8,128)(2,1)S(1)}, u32[]{:S(2)}, u32[]{:S(2)}) collective-permute-start(bf16[768,128]{1,0:T(8,128)(2,1)S(1)} %pack_x_first.1), channel_id=1, source_target_pairs={{0,16},{2,18},{4,20},{6,22},{8,24},{10,26},{12,28},{14,30},{16,0},... | collective-permute-start | bytes 589832 | tf_op jit(solution)/shard_map/ppermute | solution.py:504
  12.6 9.6 %collective-permute-start.5 = (bf16[576,128]{1,0:T(8,128)(2,1)S(1)}, bf16[576,128]{1,0:T(8,128)(2,1)S(1)}, u32[]{:S(2)}, u32[]{:S(2)}) collective-permute-start(bf16[576,128]{1,0:T(8,128)(2,1)S(1)} %get-tuple-element.32), channel_id=1, source_target_pairs={{0,8},{2,10},{4,12},{6,14},{8,0},{10,2},{12,4},{14,6},{16,24},{18,... | collective-permute-start | bytes 442376 | tf_op jit(solution)/shard_map/ppermute | solution.py:504
  14.7 4.0 %collective-permute-start.2 = (f32[8,1536]{1,0:T(8,128)S(1)}, f32[8,1536]{1,0:T(8,128)S(1)}, u32[]{:S(2)}, u32[]{:S(2)}) collective-permute-start(f32[8,1536]{1,0:T(8,128)S(1)} %get-tuple-element.28), channel_id=1, source_target_pairs={{0,6},{2,4},{4,2},{6,0},{8,14},{10,12},{12,10},{14,8},{16,22},{18,... | collective-permute-start | bytes 147464 | tf_op jit(solution)/shard_map/ppermute | solution.py:550
  18.6 1.3 %collective-permute-start.3 = (f32[8,1536]{1,0:T(8,128)S(1)}, f32[8,1536]{1,0:T(8,128)S(1)}, u32[]{:S(2)}, u32[]{:S(2)}) collective-permute-start(f32[8,1536]{1,0:T(8,128)S(1)} %get-tuple-element.30), channel_id=1, source_target_pairs={{0,2},{2,0},{4,6},{6,4},{8,10},{10,8},{12,14},{14,12},{16,18},{18,... | collective-permute-start | bytes 147464 | tf_op jit(solution)/shard_map/ppermute | solution.py:546
  24.1 3.7 %collective-permute-start.6 = (f32[16,128]{1,0:T(8,128)S(1)}, f32[16,128]{1,0:T(8,128)S(1)}, u32[]{:S(2)}, u32[]{:S(2)}) collective-permute-start(f32[16,128]{1,0:T(8,128)S(1)} %get-tuple-element.34.a), channel_id=1, source_target_pairs={{0,8},{2,10},{4,12},{6,14},{8,0},{10,2},{12,4},{14,6},{16,24},{18,... | collective-permute-start | bytes 24584 | tf_op jit(solution)/shard_map/ppermute | solution.py:546
  27.9 4.5 %collective-permute-start.7 = (f32[16,128]{1,0:T(8,128)S(1)}, f32[16,128]{1,0:T(8,128)S(1)}, u32[]{:S(2)}, u32[]{:S(2)}) collective-permute-start(f32[16,128]{1,0:T(8,128)S(1)} %pair_second.1.refs_0_), channel_id=1, source_target_pairs={{0,16},{2,18},{4,20},{6,22},{8,24},{10,26},{12,28},{14,30},{16,0},... | collective-permute-start | bytes 24584 | tf_op jit(solution)/shard_map/ppermute | solution.py:546
  30.7 12.9 %collective-permute-start.10 = (bf16[768,128]{1,0:T(8,128)(2,1)S(1)}, bf16[768,128]{1,0:T(8,128)(2,1)S(1)}, u32[]{:S(2)}, u32[]{:S(2)}) collective-permute-start(bf16[768,128]{1,0:T(8,128)(2,1)S(1)} %pack_x_second.1), channel_id=1, source_target_pairs={{0,16},{2,18},{4,20},{6,22},{8,24},{10,26},{12,28},{14,30},{16,0},... | collective-permute-start | bytes 589832 | tf_op jit(solution)/shard_map/ppermute | solution.py:504
  32.7 8.9 %collective-permute-start.11 = (bf16[576,128]{1,0:T(8,128)(2,1)S(1)}, bf16[576,128]{1,0:T(8,128)(2,1)S(1)}, u32[]{:S(2)}, u32[]{:S(2)}) collective-permute-start(bf16[576,128]{1,0:T(8,128)(2,1)S(1)} %get-tuple-element.40), channel_id=1, source_target_pairs={{0,8},{2,10},{4,12},{6,14},{8,0},{10,2},{12,4},{14,6},{16,24},{18,... | collective-permute-start | bytes 442376 | tf_op jit(solution)/shard_map/ppermute | solution.py:504
  33.0 3.7 %collective-permute-start.8 = (f32[8,1536]{1,0:T(8,128)S(1)}, f32[8,1536]{1,0:T(8,128)S(1)}, u32[]{:S(2)}, u32[]{:S(2)}) collective-permute-start(f32[8,1536]{1,0:T(8,128)S(1)} %get-tuple-element.36), channel_id=1, source_target_pairs={{0,6},{2,4},{4,2},{6,0},{8,14},{10,12},{12,10},{14,8},{16,22},{18,... | collective-permute-start | bytes 147464 | tf_op jit(solution)/shard_map/ppermute | solution.py:550
  36.8 1.3 %collective-permute-start.9 = (f32[8,1536]{1,0:T(8,128)S(1)}, f32[8,1536]{1,0:T(8,128)S(1)}, u32[]{:S(2)}, u32[]{:S(2)}) collective-permute-start(f32[8,1536]{1,0:T(8,128)S(1)} %get-tuple-element.38), channel_id=1, source_target_pairs={{0,2},{2,0},{4,6},{6,4},{8,10},{10,8},{12,14},{14,12},{16,18},{18,... | collective-permute-start | bytes 147464 | tf_op jit(solution)/shard_map/ppermute | solution.py:546
  42.1 2.8 %copy-start = (bf16[16,16]{1,0:T(8,128)(2,1)S(1)}, bf16[16,16]{1,0:T(8,128)(2,1)}, u32[]{:S(2)}) copy-start(bf16[16,16]{1,0:T(8,128)(2,1)} %panel.3) | copy-start | bytes 1540
  42.1 7.9 %collective-permute-start.13 = (bf16[768,128]{1,0:T(8,128)(2,1)S(1)}, bf16[768,128]{1,0:T(8,128)(2,1)S(1)}, u32[]{:S(2)}, u32[]{:S(2)}) collective-permute-start(bf16[768,128]{1,0:T(8,128)(2,1)S(1)} %filtered_0.1.own), channel_id=1, source_target_pairs={{0,1},{1,0},{2,3},{3,2},{4,5},{5,4},{6,7},{7,6},{8,9},{9,8},{10,11... | collective-permute-start | bytes 589832 | tf_op jit(solution)/shard_map/ppermute | solution.py:659
  44.3 7.8 %collective-permute-start.12 = (bf16[768,128]{1,0:T(8,128)(2,1)S(1)}, bf16[768,128]{1,0:T(8,128)(2,1)S(1)}, u32[]{:S(2)}, u32[]{:S(2)}) collective-permute-start(bf16[768,128]{1,0:T(8,128)(2,1)S(1)} %filtered_1.1.own), channel_id=1, source_target_pairs={{0,1},{1,0},{2,3},{3,2},{4,5},{5,4},{6,7},{7,6},{8,9},{9,8},{10,11... | collective-permute-start | bytes 589832 | tf_op jit(solution)/shard_map/ppermute | solution.py:659

commit v11 on v8

--- a/solution.py
+++ b/solution.py
@@ -241,23 +241,26 @@
     inner_tables(g, dom, v_ref, projf, blk, atom, lut, sums, table)
 
 
-def pack_kernel(g, v_ref, energy, *refs):
+def pack_kernel(g, v_ref, *refs):
     dom = lax.axis_index("dom")
     if g.butterfly:
         part, from_x, from_y, from_xy = refs[:4]
         group = refs[-1]
         group[...] = (part[...] + from_x[...]) + (from_y[...] + from_xy[...])
-        refs = refs[4:-1]
-    first, second = refs[:2]
-    pack_y(g, dom, v_ref, refs[2:])
+        refs = refs[:-1]
+    first, second = refs[-2:]
     pack_ends(g, dom, v_ref, first, second)
     if g.butterfly:
         put_table(g, first, group)
         put_table(g, second, group)
 
 
-def pack_x_kernel(g, nafter, v_ref, *refs):
-    pack_x(g, lax.axis_index("dom"), v_ref, refs[nafter:])
+def pack_faces_kernel(g, nafter, v_ref, *refs):
+    nx = len(g.face_rows(0))
+    dom = lax.axis_index("dom")
+    refs = refs[nafter:]
+    pack_x(g, dom, v_ref, refs[:nx])
+    pack_y(g, dom, v_ref, refs[nx:])
 
 
 def inside_kernel(g, scale, subtract, v_ref, pot, *refs):
@@ -311,25 +314,26 @@
         out[rows, :] = acc[rows, :] + lax.dot_general(halo, coefs, TN, preferred_element_type=F32)
 
 
-def add_x_faces(g, dom, scale, face_refs, out):
+def add_x_faces(g, dom, scale, face_refs, out, count):
     unit = 2 * g.no
     for (side, present), face in zip(g.faces(dom, 0), face_refs):
         for y in range(0, g.cy, 2):
             starts = [j * g.slab + y * g.no for j in range(RADIUS)]
             part = [flag(present) * face[at : at + unit, :].astype(F32) for at in starts]
             for i in range(RADIUS):
-                at = aligned(layer(side, g.cx, i) * g.slab + y * g.no, unit)
+                at = aligned(layer(side, count, i) * g.slab + y * g.no, unit)
                 total = out[pl.ds(at, unit), :]
                 for j in range(RADIUS - i):
                     total = total + (scale * WEIGHT[i + j + 1]) * part[j]
                 out[pl.ds(at, unit), :] = total
 
 
-def add_y_faces(g, dom, scale, face_refs, out):
+def add_y_faces(g, dom, scale, face_refs, out, start, count):
     size = RADIUS * g.no
     for (side, present), face in zip(g.faces(dom, 1), face_refs):
-        for x in range(g.cx):
-            part = flag(present) * face[x * size : (x + 1) * size, :].astype(F32)
+        for x in range(count):
+            part = face[pl.ds(aligned((start + x) * size, 16), size), :]
+            part = flag(present) * part.astype(F32)
             for i in range(RADIUS):
                 at = aligned(x * g.slab + layer(side, g.cy, i) * g.no, g.no)
                 total = out[pl.ds(at, g.no), :]
@@ -406,8 +410,8 @@
     fill_lut(g, dom, lut)
     clear(sums)
     u_ref[...] = acc[...]
-    add_x_faces(g, dom, 1.0, faces[:nx], u_ref)
-    add_y_faces(g, dom, 1.0, faces[nx:], u_ref)
+    add_x_faces(g, dom, 1.0, faces[:nx], u_ref, g.cx)
+    add_y_faces(g, dom, 1.0, faces[nx:], u_ref, 0, g.cx)
     for copy in copies:
         copy.wait()
     inner_tables(g, dom, u_ref, projf, blk, atom, lut, sums, table)
@@ -427,13 +431,12 @@
     dom = lax.axis_index("dom")
     parts = halves(g, dom)
     start, count = parts[number]
-    work[...] = acc[...]
+    work[...] = acc[pl.ds(aligned(start * g.slab, g.slab), count * g.slab), :]
     if number == len(parts) - 1:
-        add_x_faces(g, dom, 2.0, refs[:nx], work)
+        add_x_faces(g, dom, 2.0, refs[:nx], work, count)
         refs = refs[nx:]
-    add_y_faces(g, dom, 2.0, refs, work)
-    at = aligned(start * g.slab, g.slab)
-    filtered[...] = work[pl.ds(at, count * g.slab), :].astype(BF16)
+    add_y_faces(g, dom, 2.0, refs, work, start, count)
+    filtered[...] = work[...].astype(BF16)
 
 
 def panel_kernel(g, panel, weights):
@@ -552,26 +555,28 @@
             [values, pot, *prev],
             [VMEM] * (2 + len(prev)),
         )
-        inputs = [values, energy]
-        outputs = [ends, ends, *y_faces]
-        after = [acc]
+
+        inputs = [values]
+        outputs = [ends, ends]
+        after = []
         if g.butterfly:
             inputs += [part, swap(part, g.plane), swap(part, g.third), swap(part, g.plane, g.third)]
             outputs.append(table)
             after.append(inputs[-2])
-        sent_x = call(
-            functools.partial(pack_x_kernel, g, len(after)),
-            "pack_x_" + which,
-            x_faces,
+        faces = call(
+            functools.partial(pack_faces_kernel, g, len(after)),
+            "faces_" + which,
+            [*x_faces, *y_faces],
             [],
             [values, *after],
             [VMEM] * (1 + len(after)),
         )
-        from_x = swap_faces(g, sent_x, g.plane, g.first)
+        from_x = swap_faces(g, faces[:nx], g.plane, g.first)
+        from_y = swap_faces(g, faces[nx:], g.third, g.second)
+        inputs += [energy]
         first, second, *sent = call(
             functools.partial(pack_kernel, g), "pack_" + which, outputs, [], inputs, [VMEM] * len(inputs)
         )
-        from_y = swap_faces(g, sent[: len(y_faces)], g.third, g.second)
         first, second = swap(first, 1), reverse(second)
         tables = [sent[-1], swap(sent[-1], 2)] if g.butterfly else [lax.psum(part, "dom")]
         acc = call(
@@ -625,7 +630,7 @@
             functools.partial(last_kernel, g, number),
             "filtered_%d" % number,
             jax.ShapeDtypeStruct((count * g.slab, g.cz), BF16),
-            [pltpu.VMEM((g.flat, g.cz), F32)],
+            [pltpu.VMEM((count * g.slab, g.cz), F32)],
             inputs,
             [VMEM] * len(inputs),
         )

time: 52.4 us -> 51.3 us (0.979)
  waiting for transfers between devices: 17.7 us -> 14.4 us
  starting transfers between devices: 18.4 us -> 20.9 us
    ppermute x10, waiting for transfers between devices: 11.4 us -> 7.98 us  [swap(): return lax.ppermute(array, 'dom', pairs)]
    ppermute x4, starting transfers between devices: 1.78 us -> 4.31 us  [shift(): return lax.ppermute(array, 'dom', pairs)]
  transfers between devices with their start and end apart: 18 -> 18, of which waited for: 9 -> 7; matrix products, arithmetic and copies ran while one was open for 1% -> 1% of each run, Pallas kernels for 18% -> 18%
where the time goes in v11:
time: 51.3 us; the launch traced here: 51 us
  starting transfers between devices  20.9 us (41%)
  Pallas kernels  14.9 us (29%)
  waiting for transfers between devices  14.4 us (28%)
  local copies, waits for them, and re-layouts  0.61 us (1%)
    pallas_call x15, Pallas kernels, call(): pl.pallas_call(kernel, name=name, out_shape=out_shape, in_specs=specs, ou...  14.9 us
    ppermute x10, starting transfers between devices, swap(): return lax.ppermute(array, 'dom', pairs)  11.3 us
    ppermute x10, waiting for transfers between devices, swap(): return lax.ppermute(array, 'dom', pairs)  7.98 us
    ppermute x2, waiting for transfers between devices, shards(): lax.ppermute(filtered, 'band', [(0, 1), (1, 0)])  6.45 us
    ppermute x4, starting transfers between devices, shift(): return lax.ppermute(array, 'dom', pairs)  4.31 us
    ppermute x2, starting transfers between devices, reverse(): return lax.ppermute(array, 'dom', pairs)  3.11 us
    ppermute x2, starting transfers between devices, shards(): lax.ppermute(filtered, 'band', [(0, 1), (1, 0)])  2.16 us
  transfers between devices with their start and end apart: 18, of which 7 were waited for; matrix products, arithmetic and copies ran while one was open for 1% of the time, Pallas kernels for 18%

profile of v11, /device:TPU:0, one launch (start us, length us, event | category | flops | bytes accessed | tf_op | source)
XLA Modules:
  0.0 51.0 jit_solution(1663387955063928852)
XLA Ops:
  0.0 2.9 %tables_first.1 = (f32[1536,128]{1,0:T(8,128)S(1)}, f32[256,4,128]{2,1,0:T(4,128)S(1)}, f32[192,128]{1,0:T(8,128)S(1)}, f32[16,128]{1,0:T(8,128)S(1)}) custom-call(f32[1536,128]{1,0:T(8,128)} %bitcast.7, bf16[256,4,128]{2,1,0:T(4,128)(2,1)} %proj_hbm.1, f32[192,128]{1,0:T(8,128)} %bitcast.8, s32[256]{0:T(256)} %blk_hbm.7, s32[256]{0:T(256)} %atom_hbm.7), custom_call_target="tpu_custom_call" | custom-call | flops 1000 | bytes 1000 | tf_op jit(solution)/shard_map/tables_first/pallas_call | solution.py:481
  2.9 4.1 %collective-permute-start = (f32[16,128]{1,0:T(8,128)S(1)}, f32[16,128]{1,0:T(8,128)S(1)}, u32[]{:S(2)}, u32[]{:S(2)}) collective-permute-start(f32[16,128]{1,0:T(8,128)S(1)} %get-tuple-element.24.refs_0_), channel_id=1, source_target_pairs={{0,16},{2,18},{4,20},{6,22},{8,24},{10,26},{12,28},{14,30},{16,0},... | collective-permute-start | bytes 24584 | tf_op jit(solution)/shard_map/ppermute | solution.py:541
  7.0 1.6 %collective-permute-start.1 = (f32[16,128]{1,0:T(8,128)S(1)}, f32[16,128]{1,0:T(8,128)S(1)}, u32[]{:S(2)}, u32[]{:S(2)}) collective-permute-start(f32[16,128]{1,0:T(8,128)S(1)} %get-tuple-element.24.refs_0_), channel_id=1, source_target_pairs={{0,8},{2,10},{4,12},{6,14},{8,0},{10,2},{12,4},{14,6},{16,24},{18,... | collective-permute-start | bytes 24584 | tf_op jit(solution)/shard_map/ppermute | solution.py:541
  8.9 1.8 %collective-permute-done.1.refs_2_.refs_0_ = f32[16,128]{1,0:T(8,128)S(1)} collective-permute-done((f32[16,128]{1,0:T(8,128)S(1)}, f32[16,128]{1,0:T(8,128)S(1)}, u32[]{:S(2)}, u32[]{:S(2)}) %collective-permute-start.1) | collective-permute-done | bytes 8224 | tf_op jit(solution)/shard_map/ppermute | solution.py:541
  10.9 2.5 %collective-permute-start.7 = (bf16[576,128]{1,0:T(8,128)(2,1)S(1)}, bf16[576,128]{1,0:T(8,128)(2,1)S(1)}, u32[]{:S(2)}, u32[]{:S(2)}) collective-permute-start(bf16[576,128]{1,0:T(8,128)(2,1)S(1)} %get-tuple-element.29), channel_id=1, source_target_pairs={{0,8},{2,10},{4,12},{6,14},{8,0},{10,2},{12,4},{14,6},{16,24},{18,... | collective-permute-start | bytes 442376 | tf_op jit(solution)/shard_map/ppermute | solution.py:499
  13.4 0.8 %collective-permute-done.2.refs_3_ = f32[16,128]{1,0:T(8,128)S(1)} collective-permute-done((f32[16,128]{1,0:T(8,128)S(1)}, f32[16,128]{1,0:T(8,128)S(1)}, u32[]{:S(2)}, u32[]{:S(2)}) %collective-permute-start.2) | collective-permute-done | bytes 8224 | tf_op jit(solution)/shard_map/ppermute | solution.py:541
  14.6 1.6 %collective-permute-start.4 = (f32[8,1536]{1,0:T(8,128)S(1)}, f32[8,1536]{1,0:T(8,128)S(1)}, u32[]{:S(2)}, u32[]{:S(2)}) collective-permute-start(f32[8,1536]{1,0:T(8,128)S(1)} %get-tuple-element.26), channel_id=1, source_target_pairs={{0,6},{2,4},{4,2},{6,0},{8,14},{10,12},{12,10},{14,8},{16,22},{18,... | collective-permute-start | bytes 147464 | tf_op jit(solution)/shard_map/ppermute | solution.py:545
  16.7 0.9 %inside_first.1.acc = f32[1536,128]{1,0:T(8,128)S(1)} custom-call(f32[1536,128]{1,0:T(8,128)S(1)} %get-tuple-element.21.v_ref.refs_0_, f32[192,128]{1,0:T(8,128)S(1)} %get-tuple-element.22.pot), custom_call_target="tpu_custom_call" | custom-call | flops 1000 | bytes 1000 | tf_op jit(solution)/shard_map/inside_first/pallas_call | solution.py:481
  17.7 2.2 %collective-permute-done.5.refs_1_ = f32[16,128]{1,0:T(8,128)S(1)} collective-permute-done((f32[16,128]{1,0:T(8,128)S(1)}, f32[16,128]{1,0:T(8,128)S(1)}, u32[]{:S(2)}, u32[]{:S(2)}) %collective-permute-start.5) | collective-permute-done | bytes 8224 | tf_op jit(solution)/shard_map/ppermute | solution.py:541
  19.9 2.3 %nonlocal_first.1.acc = f32[1536,128]{1,0:T(8,128)S(1)} custom-call(f32[1536,128]{1,0:T(8,128)S(1)} %inside_first.1.acc, f32[256,4,128]{2,1,0:T(4,128)S(1)} %get-tuple-element.23.projf, f32[16,128]{1,0:T(8,128)S(1)} %copy.12.refs_4_.energy, s32[256]{0:T(256)} %blk_hbm.7, s32[256]{0:T(256)} %atom_hbm.7, f32[8,1536]{1,0:T(8,128)S(1)} %collective-permute-done.3.first, ...), custom_call_target="tpu_custom_call" | custom-call | flops 1000 | bytes 1000 | tf_op jit(solution)/shard_map/nonlocal_first/pallas_call | solution.py:481
  22.2 1.9 %tables_second.1 = (f32[1536,128]{1,0:T(8,128)S(1)}, f32[16,128]{1,0:T(8,128)S(1)}) custom-call(f32[1536,128]{1,0:T(8,128)S(1)} %nonlocal_first.1.acc, f32[256,4,128]{2,1,0:T(4,128)S(1)} %get-tuple-element.23.projf, s32[256]{0:T(256)} %blk_hbm.7, s32[256]{0:T(256)} %atom_hbm.7, bf16[768,128]{1,0:T(8,128)(2,1)S(1)} %collective-permute-done.6.refs_0_, ...), custom_call_target="tpu_custom_call" | custom-call | flops 1000 | bytes 1000 | tf_op jit(solution)/shard_map/tables_second/pallas_call | solution.py:481
  24.4 1.6 %collective-permute-start.8 = (f32[16,128]{1,0:T(8,128)S(1)}, f32[16,128]{1,0:T(8,128)S(1)}, u32[]{:S(2)}, u32[]{:S(2)}) collective-permute-start(f32[16,128]{1,0:T(8,128)S(1)} %get-tuple-element.31.refs_0_), channel_id=1, source_target_pairs={{0,16},{2,18},{4,20},{6,22},{8,24},{10,26},{12,28},{14,30},{16,0},... | collective-permute-start | bytes 24584 | tf_op jit(solution)/shard_map/ppermute | solution.py:541
  26.0 2.8 %collective-permute-start.10 = (f32[16,128]{1,0:T(8,128)S(1)}, f32[16,128]{1,0:T(8,128)S(1)}, u32[]{:S(2)}, u32[]{:S(2)}) collective-permute-start(f32[16,128]{1,0:T(8,128)S(1)} %get-tuple-element.31.refs_0_), channel_id=1, source_target_pairs={{0,24},{2,26},{4,28},{6,30},{8,16},{10,18},{12,20},{14,22},{16,8},... | collective-permute-start | bytes 24584 | tf_op jit(solution)/shard_map/ppermute | solution.py:541
  29.2 1.3 %collective-permute-start.15 = (bf16[576,128]{1,0:T(8,128)(2,1)S(1)}, bf16[576,128]{1,0:T(8,128)(2,1)S(1)}, u32[]{:S(2)}, u32[]{:S(2)}) collective-permute-start(bf16[576,128]{1,0:T(8,128)(2,1)S(1)} %get-tuple-element.36), channel_id=1, source_target_pairs={{0,8},{2,10},{4,12},{6,14},{8,0},{10,2},{12,4},{14,6},{16,24},{18,... | collective-permute-start | bytes 442376 | tf_op jit(solution)/shard_map/ppermute | solution.py:499
  30.6 1.1 %collective-permute-done.10.refs_3_ = f32[16,128]{1,0:T(8,128)S(1)} collective-permute-done((f32[16,128]{1,0:T(8,128)S(1)}, f32[16,128]{1,0:T(8,128)S(1)}, u32[]{:S(2)}, u32[]{:S(2)}) %collective-permute-start.10) | collective-permute-done | bytes 8224 | tf_op jit(solution)/shard_map/ppermute | solution.py:541
  32.0 1.5 %collective-permute-start.12 = (f32[8,1536]{1,0:T(8,128)S(1)}, f32[8,1536]{1,0:T(8,128)S(1)}, u32[]{:S(2)}, u32[]{:S(2)}) collective-permute-start(f32[8,1536]{1,0:T(8,128)S(1)} %get-tuple-element.33), channel_id=1, source_target_pairs={{0,6},{2,4},{4,2},{6,0},{8,14},{10,12},{12,10},{14,8},{16,22},{18,... | collective-permute-start | bytes 147464 | tf_op jit(solution)/shard_map/ppermute | solution.py:545
  34.2 1.0 %inside_second.1.acc = f32[1536,128]{1,0:T(8,128)S(1)} custom-call(f32[1536,128]{1,0:T(8,128)S(1)} %get-tuple-element.30.v_ref, f32[192,128]{1,0:T(8,128)S(1)} %get-tuple-element.22.pot, f32[1536,128]{1,0:T(8,128)S(1)} %get-tuple-element.21.v_ref.refs_0_), custom_call_target="tpu_custom_call" | custom-call | flops 1000 | bytes 1000 | tf_op jit(solution)/shard_map/inside_second/pallas_call | solution.py:481
  35.1 2.0 %collective-permute-done.13.refs_1_ = f32[16,128]{1,0:T(8,128)S(1)} collective-permute-done((f32[16,128]{1,0:T(8,128)S(1)}, f32[16,128]{1,0:T(8,128)S(1)}, u32[]{:S(2)}, u32[]{:S(2)}) %collective-permute-start.13) | collective-permute-done | bytes 8224 | tf_op jit(solution)/shard_map/ppermute | solution.py:541
  37.2 2.3 %nonlocal_second.1.acc = f32[1536,128]{1,0:T(8,128)S(1)} custom-call(f32[1536,128]{1,0:T(8,128)S(1)} %inside_second.1.acc, f32[256,4,128]{2,1,0:T(4,128)S(1)} %get-tuple-element.23.projf, f32[16,128]{1,0:T(8,128)S(1)} %copy.16.refs_4_.energy, s32[256]{0:T(256)} %blk_hbm.7, s32[256]{0:T(256)} %atom_hbm.7, f32[8,1536]{1,0:T(8,128)S(1)} %collective-permute-done.11.first, ...), custom_call_target="tpu_custom_call" | custom-call | flops 1000 | bytes 1000 | tf_op jit(solution)/shard_map/nonlocal_second/pallas_call | solution.py:481
  39.7 1.6 %collective-permute-start.17 = (bf16[768,128]{1,0:T(8,128)(2,1)S(1)}, bf16[768,128]{1,0:T(8,128)(2,1)S(1)}, u32[]{:S(2)}, u32[]{:S(2)}) collective-permute-start(bf16[768,128]{1,0:T(8,128)(2,1)S(1)} %filtered_0.1.own), channel_id=1, source_target_pairs={{0,1},{1,0},{2,3},{3,2},{4,5},{5,4},{6,7},{7,6},{8,9},{9,8},{10,11... | collective-permute-start | bytes 589832 | tf_op jit(solution)/shard_map/ppermute | solution.py:637
  42.6 5.0 %collective-permute-done.17.other = bf16[768,128]{1,0:T(8,128)(2,1)S(1)} collective-permute-done((bf16[768,128]{1,0:T(8,128)(2,1)S(1)}, bf16[768,128]{1,0:T(8,128)(2,1)S(1)}, u32[]{:S(2)}, u32[]{:S(2)}) %collective-permute-start.17) | collective-permute-done | bytes 196640 | tf_op jit(solution)/shard_map/ppermute | solution.py:637
  47.6 1.0 %rotate_0.1.refs_0_ = f32[8,192,128]{2,1,0:T(8,128)} custom-call(bf16[768,128]{1,0:T(8,128)(2,1)S(1)} %filtered_0.1.own, bf16[768,128]{1,0:T(8,128)(2,1)S(1)} %collective-permute-done.17.other, bf16[128,256]{1,0:T(8,128)(2,1)S(1)} %panel.2.weights), custom_call_target="tpu_custom_call" | custom-call | flops 1000 | bytes 1000 | tf_op jit(solution)/shard_map/rotate_0/pallas_call | solution.py:481
  48.6 1.4 %collective-permute-done.16.other = bf16[768,128]{1,0:T(8,128)(2,1)S(1)} collective-permute-done((bf16[768,128]{1,0:T(8,128)(2,1)S(1)}, bf16[768,128]{1,0:T(8,128)(2,1)S(1)}, u32[]{:S(2)}, u32[]{:S(2)}) %collective-permute-start.16) | collective-permute-done | bytes 196640 | tf_op jit(solution)/shard_map/ppermute | solution.py:637
  50.1 1.0 %rotate_1.1 = f32[8,192,128]{2,1,0:T(8,128)} custom-call(bf16[768,128]{1,0:T(8,128)(2,1)S(1)} %filtered_1.1.own, bf16[768,128]{1,0:T(8,128)(2,1)S(1)} %collective-permute-done.16.other, bf16[128,256]{1,0:T(8,128)(2,1)S(1)} %panel.2.weights, f32[8,192,128]{2,1,0:T(8,128)} %rotate_0.1.refs_0_), custom_call_target="tpu_custom_call", output_to_operand_aliasing={{}: (3, {})} | custom-call | flops 1000 | bytes 1000 | tf_op jit(solution)/shard_map/rotate_1/pallas_call | solution.py:481
  (42 shorter events, 4.7 us)
Async XLA Ops:
  0.0 8.6 %copy-start.1 = (f32[64,4]{0,1:T(4,128)S(1)}, f32[64,4]{0,1:T(4,128)}, u32[]{:S(2)}) copy-start(f32[64,4]{0,1:T(4,128)} %param.12) | copy-start | bytes 3076
  2.9 10.5 %collective-permute-start = (f32[16,128]{1,0:T(8,128)S(1)}, f32[16,128]{1,0:T(8,128)S(1)}, u32[]{:S(2)}, u32[]{:S(2)}) collective-permute-start(f32[16,128]{1,0:T(8,128)S(1)} %get-tuple-element.24.refs_0_), channel_id=1, source_target_pairs={{0,16},{2,18},{4,20},{6,22},{8,24},{10,26},{12,28},{14,30},{16,0},... | collective-permute-start | bytes 24584 | tf_op jit(solution)/shard_map/ppermute | solution.py:541
  7.0 3.7 %collective-permute-start.1 = (f32[16,128]{1,0:T(8,128)S(1)}, f32[16,128]{1,0:T(8,128)S(1)}, u32[]{:S(2)}, u32[]{:S(2)}) collective-permute-start(f32[16,128]{1,0:T(8,128)S(1)} %get-tuple-element.24.refs_0_), channel_id=1, source_target_pairs={{0,8},{2,10},{4,12},{6,14},{8,0},{10,2},{12,4},{14,6},{16,24},{18,... | collective-permute-start | bytes 24584 | tf_op jit(solution)/shard_map/ppermute | solution.py:541
  8.6 5.6 %collective-permute-start.2 = (f32[16,128]{1,0:T(8,128)S(1)}, f32[16,128]{1,0:T(8,128)S(1)}, u32[]{:S(2)}, u32[]{:S(2)}) collective-permute-start(f32[16,128]{1,0:T(8,128)S(1)} %get-tuple-element.24.refs_0_), channel_id=1, source_target_pairs={{0,24},{2,26},{4,28},{6,30},{8,16},{10,18},{12,20},{14,22},{16,8},... | collective-permute-start | bytes 24584 | tf_op jit(solution)/shard_map/ppermute | solution.py:541
  10.7 11.4 %collective-permute-start.6 = (bf16[768,128]{1,0:T(8,128)(2,1)S(1)}, bf16[768,128]{1,0:T(8,128)(2,1)S(1)}, u32[]{:S(2)}, u32[]{:S(2)}) collective-permute-start(bf16[768,128]{1,0:T(8,128)(2,1)S(1)} %get-tuple-element.28), channel_id=1, source_target_pairs={{0,16},{2,18},{4,20},{6,22},{8,24},{10,26},{12,28},{14,30},{16,0},... | collective-permute-start | bytes 589832 | tf_op jit(solution)/shard_map/ppermute | solution.py:499
  10.9 11.2 %collective-permute-start.7 = (bf16[576,128]{1,0:T(8,128)(2,1)S(1)}, bf16[576,128]{1,0:T(8,128)(2,1)S(1)}, u32[]{:S(2)}, u32[]{:S(2)}) collective-permute-start(bf16[576,128]{1,0:T(8,128)(2,1)S(1)} %get-tuple-element.29), channel_id=1, source_target_pairs={{0,8},{2,10},{4,12},{6,14},{8,0},{10,2},{12,4},{14,6},{16,24},{18,... | collective-permute-start | bytes 442376 | tf_op jit(solution)/shard_map/ppermute | solution.py:499
  14.5 5.3 %collective-permute-start.3 = (f32[8,1536]{1,0:T(8,128)S(1)}, f32[8,1536]{1,0:T(8,128)S(1)}, u32[]{:S(2)}, u32[]{:S(2)}) collective-permute-start(f32[8,1536]{1,0:T(8,128)S(1)} %get-tuple-element.25), channel_id=1, source_target_pairs={{0,2},{2,0},{4,6},{6,4},{8,10},{10,8},{12,14},{14,12},{16,18},{18,... | collective-permute-start | bytes 147464 | tf_op jit(solution)/shard_map/ppermute | solution.py:541
  14.6 5.3 %collective-permute-start.4 = (f32[8,1536]{1,0:T(8,128)S(1)}, f32[8,1536]{1,0:T(8,128)S(1)}, u32[]{:S(2)}, u32[]{:S(2)}) collective-permute-start(f32[8,1536]{1,0:T(8,128)S(1)} %get-tuple-element.26), channel_id=1, source_target_pairs={{0,6},{2,4},{4,2},{6,0},{8,14},{10,12},{12,10},{14,8},{16,22},{18,... | collective-permute-start | bytes 147464 | tf_op jit(solution)/shard_map/ppermute | solution.py:545
  16.2 3.7 %collective-permute-start.5 = (f32[16,128]{1,0:T(8,128)S(1)}, f32[16,128]{1,0:T(8,128)S(1)}, u32[]{:S(2)}, u32[]{:S(2)}) collective-permute-start(f32[16,128]{1,0:T(8,128)S(1)} %get-tuple-element.27.refs_0_), channel_id=1, source_target_pairs={{0,4},{2,6},{4,0},{6,2},{8,12},{10,14},{12,8},{14,10},{16,20},{18,... | collective-permute-start | bytes 24584 | tf_op jit(solution)/shard_map/ppermute | solution.py:541
  24.1 4.7 %collective-permute-start.9 = (f32[16,128]{1,0:T(8,128)S(1)}, f32[16,128]{1,0:T(8,128)S(1)}, u32[]{:S(2)}, u32[]{:S(2)}) collective-permute-start(f32[16,128]{1,0:T(8,128)S(1)} %get-tuple-element.31.refs_0_), channel_id=1, source_target_pairs={{0,8},{2,10},{4,12},{6,14},{8,0},{10,2},{12,4},{14,6},{16,24},{18,... | collective-permute-start | bytes 24584 | tf_op jit(solution)/shard_map/ppermute | solution.py:541
  24.4 6.2 %collective-permute-start.8 = (f32[16,128]{1,0:T(8,128)S(1)}, f32[16,128]{1,0:T(8,128)S(1)}, u32[]{:S(2)}, u32[]{:S(2)}) collective-permute-start(f32[16,128]{1,0:T(8,128)S(1)} %get-tuple-element.31.refs_0_), channel_id=1, source_target_pairs={{0,16},{2,18},{4,20},{6,22},{8,24},{10,26},{12,28},{14,30},{16,0},... | collective-permute-start | bytes 24584 | tf_op jit(solution)/shard_map/ppermute | solution.py:541
  26.0 5.7 %collective-permute-start.10 = (f32[16,128]{1,0:T(8,128)S(1)}, f32[16,128]{1,0:T(8,128)S(1)}, u32[]{:S(2)}, u32[]{:S(2)}) collective-permute-start(f32[16,128]{1,0:T(8,128)S(1)} %get-tuple-element.31.refs_0_), channel_id=1, source_target_pairs={{0,24},{2,26},{4,28},{6,30},{8,16},{10,18},{12,20},{14,22},{16,8},... | collective-permute-start | bytes 24584 | tf_op jit(solution)/shard_map/ppermute | solution.py:541
  28.8 12.4 %collective-permute-start.14 = (bf16[768,128]{1,0:T(8,128)(2,1)S(1)}, bf16[768,128]{1,0:T(8,128)(2,1)S(1)}, u32[]{:S(2)}, u32[]{:S(2)}) collective-permute-start(bf16[768,128]{1,0:T(8,128)(2,1)S(1)} %get-tuple-element.35), channel_id=1, source_target_pairs={{0,16},{2,18},{4,20},{6,22},{8,24},{10,26},{12,28},{14,30},{16,0},... | collective-permute-start | bytes 589832 | tf_op jit(solution)/shard_map/ppermute | solution.py:499
  29.2 10.3 %collective-permute-start.15 = (bf16[576,128]{1,0:T(8,128)(2,1)S(1)}, bf16[576,128]{1,0:T(8,128)(2,1)S(1)}, u32[]{:S(2)}, u32[]{:S(2)}) collective-permute-start(bf16[576,128]{1,0:T(8,128)(2,1)S(1)} %get-tuple-element.36), channel_id=1, source_target_pairs={{0,8},{2,10},{4,12},{6,14},{8,0},{10,2},{12,4},{14,6},{16,24},{18,... | collective-permute-start | bytes 442376 | tf_op jit(solution)/shard_map/ppermute | solution.py:499
  32.0 5.2 %collective-permute-start.11 = (f32[8,1536]{1,0:T(8,128)S(1)}, f32[8,1536]{1,0:T(8,128)S(1)}, u32[]{:S(2)}, u32[]{:S(2)}) collective-permute-start(f32[8,1536]{1,0:T(8,128)S(1)} %get-tuple-element.32), channel_id=1, source_target_pairs={{0,2},{2,0},{4,6},{6,4},{8,10},{10,8},{12,14},{14,12},{16,18},{18,... | collective-permute-start | bytes 147464 | tf_op jit(solution)/shard_map/ppermute | solution.py:541
  32.0 5.1 %collective-permute-start.12 = (f32[8,1536]{1,0:T(8,128)S(1)}, f32[8,1536]{1,0:T(8,128)S(1)}, u32[]{:S(2)}, u32[]{:S(2)}) collective-permute-start(f32[8,1536]{1,0:T(8,128)S(1)} %get-tuple-element.33), channel_id=1, source_target_pairs={{0,6},{2,4},{4,2},{6,0},{8,14},{10,12},{12,10},{14,8},{16,22},{18,... | collective-permute-start | bytes 147464 | tf_op jit(solution)/shard_map/ppermute | solution.py:545
  33.5 3.7 %collective-permute-start.13 = (f32[16,128]{1,0:T(8,128)S(1)}, f32[16,128]{1,0:T(8,128)S(1)}, u32[]{:S(2)}, u32[]{:S(2)}) collective-permute-start(f32[16,128]{1,0:T(8,128)S(1)} %get-tuple-element.34.refs_0_), channel_id=1, source_target_pairs={{0,4},{2,6},{4,0},{6,2},{8,12},{10,14},{12,8},{14,10},{16,20},{18,... | collective-permute-start | bytes 24584 | tf_op jit(solution)/shard_map/ppermute | solution.py:541
  39.7 2.6 %copy-start = (bf16[16,16]{1,0:T(8,128)(2,1)S(1)}, bf16[16,16]{1,0:T(8,128)(2,1)}, u32[]{:S(2)}) copy-start(bf16[16,16]{1,0:T(8,128)(2,1)} %panel.3) | copy-start | bytes 1540
  39.7 7.9 %collective-permute-start.17 = (bf16[768,128]{1,0:T(8,128)(2,1)S(1)}, bf16[768,128]{1,0:T(8,128)(2,1)S(1)}, u32[]{:S(2)}, u32[]{:S(2)}) collective-permute-start(bf16[768,128]{1,0:T(8,128)(2,1)S(1)} %filtered_0.1.own), channel_id=1, source_target_pairs={{0,1},{1,0},{2,3},{3,2},{4,5},{5,4},{6,7},{7,6},{8,9},{9,8},{10,11... | collective-permute-start | bytes 589832 | tf_op jit(solution)/shard_map/ppermute | solution.py:637
  41.8 8.3 %collective-permute-start.16 = (bf16[768,128]{1,0:T(8,128)(2,1)S(1)}, bf16[768,128]{1,0:T(8,128)(2,1)S(1)}, u32[]{:S(2)}, u32[]{:S(2)}) collective-permute-start(bf16[768,128]{1,0:T(8,128)(2,1)S(1)} %filtered_1.1.own), channel_id=1, source_target_pairs={{0,1},{1,0},{2,3},{3,2},{4,5},{5,4},{6,7},{7,6},{8,9},{9,8},{10,11... | collective-permute-start | bytes 589832 | tf_op jit(solution)/shard_map/ppermute | solution.py:637

commit v12 on v11

--- a/solution.py
+++ b/solution.py
@@ -175,7 +175,7 @@
 def inner_tables(g, dom, v_ref, projf, blk, atom, lut, sums, table):
     size = g.nproj * g.no
 
-    unroll = 16
+    unroll = 64
 
     def step(i, _):
         for u in range(unroll):
@@ -241,18 +241,13 @@
     inner_tables(g, dom, v_ref, projf, blk, atom, lut, sums, table)
 
 
-def pack_kernel(g, v_ref, *refs):
-    dom = lax.axis_index("dom")
-    if g.butterfly:
-        part, from_x, from_y, from_xy = refs[:4]
-        group = refs[-1]
-        group[...] = (part[...] + from_x[...]) + (from_y[...] + from_xy[...])
-        refs = refs[:-1]
-    first, second = refs[-2:]
-    pack_ends(g, dom, v_ref, first, second)
-    if g.butterfly:
-        put_table(g, first, group)
-        put_table(g, second, group)
+def pack_kernel(g, *refs):
+    part, from_x, from_y, from_xy = refs[:4]
+    ends, outs, group = refs[4:6], refs[-3:-1], refs[-1]
+    group[...] = (part[...] + from_x[...]) + (from_y[...] + from_xy[...])
+    for source, out in zip(ends, outs):
+        out[...] = source[...]
+        put_table(g, out, group)
 
 
 def pack_faces_kernel(g, nafter, v_ref, *refs):
@@ -260,7 +255,8 @@
     dom = lax.axis_index("dom")
     refs = refs[nafter:]
     pack_x(g, dom, v_ref, refs[:nx])
-    pack_y(g, dom, v_ref, refs[nx:])
+    pack_y(g, dom, v_ref, refs[nx:-2])
+    pack_ends(g, dom, v_ref, *refs[-2:])
 
 
 def inside_kernel(g, scale, subtract, v_ref, pot, *refs):
@@ -363,7 +359,7 @@
     out_all = lax.dot_general(parts, ones, TN, preferred_element_type=F32)
     for number in range(count):
         spread[number * lanes : (number + 1) * lanes, :] = out_all[:, number * g.cz : (number + 1) * g.cz]
-    unroll = 16
+    unroll = 64
 
     def step(i, _):
         additions = []
@@ -384,8 +380,13 @@
     lax.fori_loop(0, g.ent // unroll, step, 0)
 
 
-def nonlocal_kernel(g, scale, acc, projf, energy, blk_hbm, atom_hbm, first, second, *refs):
-    out, table, blk, atom, lut, sem, spread = refs[-7:]
+def nonlocal_kernel(g, scale, far, acc, projf, energy, blk_hbm, atom_hbm, first, second, *refs):
+    table, blk, atom, lut, sem, spread = refs[-6:]
+    out = refs[-7]
+    filtered = None
+    if far:
+        out, filtered = refs[-8:-6]
+        y_refs = refs[-8 - len(g.face_rows(1)) : -8]
     copies = entry_copies(blk_hbm, atom_hbm, blk, atom, sem)
     dom = lax.axis_index("dom")
     fill_lut(g, dom, lut)
@@ -398,6 +399,11 @@
     for copy in copies:
         copy.wait()
     add_nonlocal(g, dom, table, energy, projf, blk, atom, lut, spread, out)
+    if far:
+        start, count = halves(g, dom)[0]
+        rows = pl.ds(aligned(start * g.slab, g.slab), count * g.slab)
+        add_y_faces(g, dom, scale, y_refs, out.at[rows, :], start, count)
+        filtered[...] = out[rows, :].astype(BF16)
 
 
 def middle_kernel(g, acc, projf, blk_hbm, atom_hbm, *refs):
@@ -424,18 +430,14 @@
     return [((1 - side) * RADIUS, RADIUS), (side * RADIUS, RADIUS)]
 
 
-def last_kernel(g, number, acc, *refs):
+def last_kernel(g, acc, *refs):
     nx = len(g.face_rows(0))
     filtered, work = refs[-2:]
-    refs = refs[:-2]
     dom = lax.axis_index("dom")
-    parts = halves(g, dom)
-    start, count = parts[number]
+    start, count = halves(g, dom)[-1]
     work[...] = acc[pl.ds(aligned(start * g.slab, g.slab), count * g.slab), :]
-    if number == len(parts) - 1:
-        add_x_faces(g, dom, 2.0, refs[:nx], work, count)
-        refs = refs[nx:]
-    add_y_faces(g, dom, 2.0, refs, work, start, count)
+    add_x_faces(g, dom, 2.0, refs[:nx], work, count)
+    add_y_faces(g, dom, 2.0, refs[nx:-2], work, start, count)
     filtered[...] = work[...].astype(BF16)
 
 
@@ -556,38 +558,44 @@
             [VMEM] * (2 + len(prev)),
         )
 
-        inputs = [values]
-        outputs = [ends, ends]
         after = []
         if g.butterfly:
-            inputs += [part, swap(part, g.plane), swap(part, g.third), swap(part, g.plane, g.third)]
-            outputs.append(table)
-            after.append(inputs[-2])
-        faces = call(
+            tables = [part, swap(part, g.plane), swap(part, g.third), swap(part, g.plane, g.third)]
+            after.append(tables[2])
+        *faces, first, second = call(
             functools.partial(pack_faces_kernel, g, len(after)),
             "faces_" + which,
-            [*x_faces, *y_faces],
+            [*x_faces, *y_faces, ends, ends],
             [],
             [values, *after],
             [VMEM] * (1 + len(after)),
         )
         from_x = swap_faces(g, faces[:nx], g.plane, g.first)
         from_y = swap_faces(g, faces[nx:], g.third, g.second)
-        inputs += [energy]
-        first, second, *sent = call(
-            functools.partial(pack_kernel, g), "pack_" + which, outputs, [], inputs, [VMEM] * len(inputs)
-        )
+        if g.butterfly:
+            first, second, group = call(
+                functools.partial(pack_kernel, g),
+                "pack_" + which,
+                [ends, ends, table],
+                [],
+                [*tables, first, second, energy],
+                [VMEM] * 7,
+            )
         first, second = swap(first, 1), reverse(second)
-        tables = [sent[-1], swap(sent[-1], 2)] if g.butterfly else [lax.psum(part, "dom")]
-        acc = call(
-            functools.partial(nonlocal_kernel, g, scale),
+        tables = [group, swap(group, 2)] if g.butterfly else [lax.psum(part, "dom")]
+        far = []
+        if prev and len(halves(g, 0)) == 2:
+            far = [jax.ShapeDtypeStruct((halves(g, 0)[0][1] * g.slab, g.cz), BF16)]
+            tables += from_y
+        out = call(
+            functools.partial(nonlocal_kernel, g, scale, len(far) > 0),
             "nonlocal_" + which,
-            field,
+            [field, *far],
             [pltpu.VMEM(table.shape, F32), *entries, spread],
             [acc, projf, energy, blk, atom, first, second, *tables],
             [VMEM] * 3 + [HBM] * 2 + [VMEM] * (2 + len(tables)),
         )
-        return acc, from_x + from_y
+        return out, from_x + from_y
 
     v, projf, pot, part = call(
         functools.partial(first_kernel, g),
@@ -603,7 +611,7 @@
         [orb, proj, pot, blk, atom],
         [HBM] * 5,
     )
-    acc, received = local_and_ends(1.0, "first", v, [], part)
+    (acc,), received = local_and_ends(1.0, "first", v, [], part)
     u, part = call(
         functools.partial(middle_kernel, g),
         "tables_second",
@@ -612,7 +620,7 @@
         [acc, projf, blk, atom, *received],
         [VMEM] * 2 + [HBM] * 2 + [VMEM] * len(received),
     )
-    acc, received = local_and_ends(2.0, "second", u, [v], part)
+    (acc, *far), received = local_and_ends(2.0, "second", u, [v], part)
     weights = call(
         functools.partial(panel_kernel, g),
         "panel",
@@ -625,15 +633,18 @@
     pieces = []
     parts = halves(g, 0)
     for number, (_, count) in enumerate(parts):
-        inputs = [acc, *received[nx:]] if number < len(parts) - 1 else [acc, *received]
-        filtered = call(
-            functools.partial(last_kernel, g, number),
-            "filtered_%d" % number,
-            jax.ShapeDtypeStruct((count * g.slab, g.cz), BF16),
-            [pltpu.VMEM((count * g.slab, g.cz), F32)],
-            inputs,
-            [VMEM] * len(inputs),
-        )
+        if number < len(far):
+            filtered = far[number]
+        else:
+            inputs = [acc, *received]
+            filtered = call(
+                functools.partial(last_kernel, g),
+                "filtered",
+                jax.ShapeDtypeStruct((count * g.slab, g.cz), BF16),
+                [pltpu.VMEM((count * g.slab, g.cz), F32)],
+                inputs,
+                [VMEM] * len(inputs),
+            )
         pieces.append((filtered, lax.ppermute(filtered, "band", [(0, 1), (1, 0)]), count))
     for number, (filtered, other, count) in enumerate(pieces):
         inputs = [filtered, other, weights] + ([] if rotated is None else [rotated])

time: 51.3 us -> 49.2 us (0.959)
  waiting for transfers between devices: 14.4 us -> 10.7 us
  starting transfers between devices: 20.9 us -> 22.6 us
    ppermute x10, waiting for transfers between devices: 7.98 us -> 5.07 us  [swap(): return lax.ppermute(array, 'dom', pairs)]
    ppermute x4, starting transfers between devices: 4.31 us -> 5.99 us  [shift(): return lax.ppermute(array, 'dom', pairs)]
    ppermute x10, starting transfers between devices: 11.3 us -> 10.3 us  [swap(): return lax.ppermute(array, 'dom', pairs)]
    ppermute x2, waiting for transfers between devices: 6.45 us -> 5.66 us  [shards(): lax.ppermute(filtered, 'band', [(0, 1), (1, 0)])]
    ppermute x2, starting transfers between devices: 2.16 us -> 2.91 us  [shards(): lax.ppermute(filtered, 'band', [(0, 1), (1, 0)])]
    pallas_call x15 -> x14, Pallas kernels: 14.9 us -> 14.9 us  [call(): pl.pallas_call(kernel, name=name, out_shape=out_shape, in_specs=specs, ou...]
  transfers between devices with their start and end apart: 18 -> 18, of which waited for: 7 -> 7; matrix products, arithmetic and copies ran while one was open for 1% -> 1% of each run, Pallas kernels for 18% -> 19%
where the time goes in v12:
time: 49.2 us; the launch traced here: 48.9 us
  starting transfers between devices  22.6 us (46%)
  Pallas kernels  14.9 us (30%)
  waiting for transfers between devices  10.7 us (22%)
  local copies, waits for them, and re-layouts  0.61 us (1%)
    pallas_call x14, Pallas kernels, call(): pl.pallas_call(kernel, name=name, out_shape=out_shape, in_specs=specs, ou...  14.9 us
    ppermute x10, starting transfers between devices, swap(): return lax.ppermute(array, 'dom', pairs)  10.3 us
    ppermute x4, starting transfers between devices, shift(): return lax.ppermute(array, 'dom', pairs)  5.99 us
    ppermute x2, waiting for transfers between devices, shards(): lax.ppermute(filtered, 'band', [(0, 1), (1, 0)])  5.66 us
    ppermute x10, waiting for transfers between devices, swap(): return lax.ppermute(array, 'dom', pairs)  5.07 us
    ppermute x2, starting transfers between devices, reverse(): return lax.ppermute(array, 'dom', pairs)  3.3 us
    ppermute x2, starting transfers between devices, shards(): lax.ppermute(filtered, 'band', [(0, 1), (1, 0)])  2.91 us
  transfers between devices with their start and end apart: 18, of which 7 were waited for; matrix products, arithmetic and copies ran while one was open for 1% of the time, Pallas kernels for 19%

profile of v12, /device:TPU:0, one launch (start us, length us, event | category | flops | bytes accessed | tf_op | source)
XLA Modules:
  0.0 48.9 jit_solution(7460813052106587396)
XLA Ops:
  0.0 2.8 %tables_first.1 = (f32[1536,128]{1,0:T(8,128)S(1)}, f32[256,4,128]{2,1,0:T(4,128)S(1)}, f32[192,128]{1,0:T(8,128)S(1)}, f32[16,128]{1,0:T(8,128)S(1)}) custom-call(f32[1536,128]{1,0:T(8,128)} %bitcast.7, bf16[256,4,128]{2,1,0:T(4,128)(2,1)} %proj_hbm.1, f32[192,128]{1,0:T(8,128)} %bitcast.8, s32[256]{0:T(256)} %blk_hbm.7, s32[256]{0:T(256)} %atom_hbm.7), custom_call_target="tpu_custom_call" | custom-call | flops 1000 | bytes 1000 | tf_op jit(solution)/shard_map/tables_first/pallas_call | solution.py:483
  2.9 3.1 %collective-permute-start.1 = (f32[16,128]{1,0:T(8,128)S(1)}, f32[16,128]{1,0:T(8,128)S(1)}, u32[]{:S(2)}, u32[]{:S(2)}) collective-permute-start(f32[16,128]{1,0:T(8,128)S(1)} %get-tuple-element.30.refs_0_), channel_id=1, source_target_pairs={{0,8},{2,10},{4,12},{6,14},{8,0},{10,2},{12,4},{14,6},{16,24},{18,... | collective-permute-start | bytes 24584 | tf_op jit(solution)/shard_map/ppermute | solution.py:543
  5.9 2.6 %collective-permute-start = (f32[16,128]{1,0:T(8,128)S(1)}, f32[16,128]{1,0:T(8,128)S(1)}, u32[]{:S(2)}, u32[]{:S(2)}) collective-permute-start(f32[16,128]{1,0:T(8,128)S(1)} %get-tuple-element.30.refs_0_), channel_id=1, source_target_pairs={{0,16},{2,18},{4,20},{6,22},{8,24},{10,26},{12,28},{14,30},{16,0},... | collective-permute-start | bytes 24584 | tf_op jit(solution)/shard_map/ppermute | solution.py:543
  9.1 1.9 %collective-permute-start.6 = (bf16[768,128]{1,0:T(8,128)(2,1)S(1)}, bf16[768,128]{1,0:T(8,128)(2,1)S(1)}, u32[]{:S(2)}, u32[]{:S(2)}) collective-permute-start(bf16[768,128]{1,0:T(8,128)(2,1)S(1)} %get-tuple-element.36), channel_id=1, source_target_pairs={{0,16},{2,18},{4,20},{6,22},{8,24},{10,26},{12,28},{14,30},{16,0},... | collective-permute-start | bytes 589832 | tf_op jit(solution)/shard_map/ppermute | solution.py:501
  11.1 2.5 %collective-permute-start.7 = (bf16[576,128]{1,0:T(8,128)(2,1)S(1)}, bf16[576,128]{1,0:T(8,128)(2,1)S(1)}, u32[]{:S(2)}, u32[]{:S(2)}) collective-permute-start(bf16[576,128]{1,0:T(8,128)(2,1)S(1)} %get-tuple-element.37), channel_id=1, source_target_pairs={{0,8},{2,10},{4,12},{6,14},{8,0},{10,2},{12,4},{14,6},{16,24},{18,... | collective-permute-start | bytes 442376 | tf_op jit(solution)/shard_map/ppermute | solution.py:501
  14.2 1.6 %collective-permute-start.4 = (f32[8,1536]{1,0:T(8,128)S(1)}, f32[8,1536]{1,0:T(8,128)S(1)}, u32[]{:S(2)}, u32[]{:S(2)}) collective-permute-start(f32[8,1536]{1,0:T(8,128)S(1)} %get-tuple-element.34), channel_id=1, source_target_pairs={{0,6},{2,4},{4,2},{6,0},{8,14},{10,12},{12,10},{14,8},{16,22},{18,... | collective-permute-start | bytes 147464 | tf_op jit(solution)/shard_map/ppermute | solution.py:547
  16.3 0.9 %inside_first.1.acc = f32[1536,128]{1,0:T(8,128)S(1)} custom-call(f32[1536,128]{1,0:T(8,128)S(1)} %get-tuple-element.27.v_ref.refs_0_, f32[192,128]{1,0:T(8,128)S(1)} %get-tuple-element.28.pot), custom_call_target="tpu_custom_call" | custom-call | flops 1000 | bytes 1000 | tf_op jit(solution)/shard_map/inside_first/pallas_call | solution.py:483
  17.3 2.2 %collective-permute-done.5.refs_1_ = f32[16,128]{1,0:T(8,128)S(1)} collective-permute-done((f32[16,128]{1,0:T(8,128)S(1)}, f32[16,128]{1,0:T(8,128)S(1)}, u32[]{:S(2)}, u32[]{:S(2)}) %collective-permute-start.5) | collective-permute-done | bytes 8224 | tf_op jit(solution)/shard_map/ppermute | solution.py:543
  19.5 2.3 %nonlocal_first.1.acc = f32[1536,128]{1,0:T(8,128)S(1)} custom-call(f32[1536,128]{1,0:T(8,128)S(1)} %inside_first.1.acc, f32[256,4,128]{2,1,0:T(4,128)S(1)} %get-tuple-element.29.projf, f32[16,128]{1,0:T(8,128)S(1)} %copy.12.refs_6_.energy, s32[256]{0:T(256)} %blk_hbm.7, s32[256]{0:T(256)} %atom_hbm.7, f32[8,1536]{1,0:T(8,128)S(1)} %collective-permute-done.3.first, ...), custom_call_target="tpu_custom_call" | custom-call | flops 1000 | bytes 1000 | tf_op jit(solution)/shard_map/nonlocal_first/pallas_call | solution.py:483
  21.8 1.8 %tables_second.1 = (f32[1536,128]{1,0:T(8,128)S(1)}, f32[16,128]{1,0:T(8,128)S(1)}) custom-call(f32[1536,128]{1,0:T(8,128)S(1)} %nonlocal_first.1.acc, f32[256,4,128]{2,1,0:T(4,128)S(1)} %get-tuple-element.29.projf, s32[256]{0:T(256)} %blk_hbm.7, s32[256]{0:T(256)} %atom_hbm.7, bf16[768,128]{1,0:T(8,128)(2,1)S(1)} %collective-permute-done.6.refs_0_, ...), custom_call_target="tpu_custom_call" | custom-call | flops 1000 | bytes 1000 | tf_op jit(solution)/shard_map/tables_second/pallas_call | solution.py:483
  24.0 1.0 %collective-permute-start.10 = (f32[16,128]{1,0:T(8,128)S(1)}, f32[16,128]{1,0:T(8,128)S(1)}, u32[]{:S(2)}, u32[]{:S(2)}) collective-permute-start(f32[16,128]{1,0:T(8,128)S(1)} %get-tuple-element.39.refs_0_), channel_id=1, source_target_pairs={{0,24},{2,26},{4,28},{6,30},{8,16},{10,18},{12,20},{14,22},{16,8},... | collective-permute-start | bytes 24584 | tf_op jit(solution)/shard_map/ppermute | solution.py:543
  25.0 2.4 %collective-permute-start.8 = (f32[16,128]{1,0:T(8,128)S(1)}, f32[16,128]{1,0:T(8,128)S(1)}, u32[]{:S(2)}, u32[]{:S(2)}) collective-permute-start(f32[16,128]{1,0:T(8,128)S(1)} %get-tuple-element.39.refs_0_), channel_id=1, source_target_pairs={{0,16},{2,18},{4,20},{6,22},{8,24},{10,26},{12,28},{14,30},{16,0},... | collective-permute-start | bytes 24584 | tf_op jit(solution)/shard_map/ppermute | solution.py:543
  27.8 0.9 %collective-permute-start.14 = (bf16[576,128]{1,0:T(8,128)(2,1)S(1)}, bf16[576,128]{1,0:T(8,128)(2,1)S(1)}, u32[]{:S(2)}, u32[]{:S(2)}) collective-permute-start(bf16[576,128]{1,0:T(8,128)(2,1)S(1)} %get-tuple-element.45), channel_id=1, source_target_pairs={{0,8},{2,10},{4,12},{6,14},{8,0},{10,2},{12,4},{14,6},{16,24},{18,... | collective-permute-start | bytes 442376 | tf_op jit(solution)/shard_map/ppermute | solution.py:501
  28.8 0.7 %collective-permute-start.15 = (bf16[768,128]{1,0:T(8,128)(2,1)S(1)}, bf16[768,128]{1,0:T(8,128)(2,1)S(1)}, u32[]{:S(2)}, u32[]{:S(2)}) collective-permute-start(bf16[768,128]{1,0:T(8,128)(2,1)S(1)} %get-tuple-element.47), channel_id=1, source_target_pairs={{0,16},{2,18},{4,20},{6,22},{8,24},{10,26},{12,28},{14,30},{16,0},... | collective-permute-start | bytes 589832 | tf_op jit(solution)/shard_map/ppermute | solution.py:501
  29.8 1.7 %collective-permute-start.12 = (f32[8,1536]{1,0:T(8,128)S(1)}, f32[8,1536]{1,0:T(8,128)S(1)}, u32[]{:S(2)}, u32[]{:S(2)}) collective-permute-start(f32[8,1536]{1,0:T(8,128)S(1)} %get-tuple-element.43), channel_id=1, source_target_pairs={{0,6},{2,4},{4,2},{6,0},{8,14},{10,12},{12,10},{14,8},{16,22},{18,... | collective-permute-start | bytes 147464 | tf_op jit(solution)/shard_map/ppermute | solution.py:547
  31.9 1.0 %inside_second.1.acc = f32[1536,128]{1,0:T(8,128)S(1)} custom-call(f32[1536,128]{1,0:T(8,128)S(1)} %get-tuple-element.38.v_ref, f32[192,128]{1,0:T(8,128)S(1)} %get-tuple-element.28.pot, f32[1536,128]{1,0:T(8,128)S(1)} %get-tuple-element.27.v_ref.refs_0_), custom_call_target="tpu_custom_call" | custom-call | flops 1000 | bytes 1000 | tf_op jit(solution)/shard_map/inside_second/pallas_call | solution.py:483
  32.9 2.2 %collective-permute-done.13.refs_1_ = f32[16,128]{1,0:T(8,128)S(1)} collective-permute-done((f32[16,128]{1,0:T(8,128)S(1)}, f32[16,128]{1,0:T(8,128)S(1)}, u32[]{:S(2)}, u32[]{:S(2)}) %collective-permute-start.13) | collective-permute-done | bytes 8224 | tf_op jit(solution)/shard_map/ppermute | solution.py:543
  35.1 2.6 %nonlocal_second.1 = (f32[1536,128]{1,0:T(8,128)S(1)}, bf16[768,128]{1,0:T(8,128)(2,1)S(1)}) custom-call(f32[1536,128]{1,0:T(8,128)S(1)} %inside_second.1.acc, f32[256,4,128]{2,1,0:T(4,128)S(1)} %get-tuple-element.29.projf, f32[16,128]{1,0:T(8,128)S(1)} %copy.16.refs_6_.energy, s32[256]{0:T(256)} %blk_hbm.7, s32[256]{0:T(256)} %atom_hbm.7, ...), custom_call_target="tpu_custom_call" | custom-call | flops 1000 | bytes 1000 | tf_op jit(solution)/shard_map/nonlocal_second/pallas_call | solution.py:483
  37.7 1.6 %collective-permute-start.17 = (bf16[768,128]{1,0:T(8,128)(2,1)S(1)}, bf16[768,128]{1,0:T(8,128)(2,1)S(1)}, u32[]{:S(2)}, u32[]{:S(2)}) collective-permute-start(bf16[768,128]{1,0:T(8,128)(2,1)S(1)} %get-tuple-element.48.own), channel_id=1, source_target_pairs={{0,1},{1,0},{2,3},{3,2},{4,5},{5,4},{6,7},{7,6},{8,9},{9,8},{10,11... | collective-permute-start | bytes 589832 | tf_op jit(solution)/shard_map/ppermute | solution.py:648
  39.7 1.4 %collective-permute-start.16 = (bf16[768,128]{1,0:T(8,128)(2,1)S(1)}, bf16[768,128]{1,0:T(8,128)(2,1)S(1)}, u32[]{:S(2)}, u32[]{:S(2)}) collective-permute-start(bf16[768,128]{1,0:T(8,128)(2,1)S(1)} %filtered.1.own), channel_id=1, source_target_pairs={{0,1},{1,0},{2,3},{3,2},{4,5},{5,4},{6,7},{7,6},{8,9},{9,8},{10,11... | collective-permute-start | bytes 589832 | tf_op jit(solution)/shard_map/ppermute | solution.py:648
  41.3 4.2 %collective-permute-done.17.other = bf16[768,128]{1,0:T(8,128)(2,1)S(1)} collective-permute-done((bf16[768,128]{1,0:T(8,128)(2,1)S(1)}, bf16[768,128]{1,0:T(8,128)(2,1)S(1)}, u32[]{:S(2)}, u32[]{:S(2)}) %collective-permute-start.17) | collective-permute-done | bytes 196640 | tf_op jit(solution)/shard_map/ppermute | solution.py:648
  45.6 1.0 %rotate_0.1.refs_0_ = f32[8,192,128]{2,1,0:T(8,128)} custom-call(bf16[768,128]{1,0:T(8,128)(2,1)S(1)} %get-tuple-element.48.own, bf16[768,128]{1,0:T(8,128)(2,1)S(1)} %collective-permute-done.17.other, bf16[128,256]{1,0:T(8,128)(2,1)S(1)} %panel.2.weights), custom_call_target="tpu_custom_call" | custom-call | flops 1000 | bytes 1000 | tf_op jit(solution)/shard_map/rotate_0/pallas_call | solution.py:483
  46.6 1.4 %collective-permute-done.16.other = bf16[768,128]{1,0:T(8,128)(2,1)S(1)} collective-permute-done((bf16[768,128]{1,0:T(8,128)(2,1)S(1)}, bf16[768,128]{1,0:T(8,128)(2,1)S(1)}, u32[]{:S(2)}, u32[]{:S(2)}) %collective-permute-start.16) | collective-permute-done | bytes 196640 | tf_op jit(solution)/shard_map/ppermute | solution.py:648
  48.0 1.0 %rotate_1.1 = f32[8,192,128]{2,1,0:T(8,128)} custom-call(bf16[768,128]{1,0:T(8,128)(2,1)S(1)} %filtered.1.own, bf16[768,128]{1,0:T(8,128)(2,1)S(1)} %collective-permute-done.16.other, bf16[128,256]{1,0:T(8,128)(2,1)S(1)} %panel.2.weights, f32[8,192,128]{2,1,0:T(8,128)} %rotate_0.1.refs_0_), custom_call_target="tpu_custom_call", output_to_operand_aliasing={{}: (3, {})} | custom-call | flops 1000 | bytes 1000 | tf_op jit(solution)/shard_map/rotate_1/pallas_call | solution.py:483
  (41 shorter events, 3.9 us)
Async XLA Ops:
  0.0 8.5 %copy-start.1 = (f32[64,4]{0,1:T(4,128)S(1)}, f32[64,4]{0,1:T(4,128)}, u32[]{:S(2)}) copy-start(f32[64,4]{0,1:T(4,128)} %param.12) | copy-start | bytes 3076
  2.9 5.9 %collective-permute-start.1 = (f32[16,128]{1,0:T(8,128)S(1)}, f32[16,128]{1,0:T(8,128)S(1)}, u32[]{:S(2)}, u32[]{:S(2)}) collective-permute-start(f32[16,128]{1,0:T(8,128)S(1)} %get-tuple-element.30.refs_0_), channel_id=1, source_target_pairs={{0,8},{2,10},{4,12},{6,14},{8,0},{10,2},{12,4},{14,6},{16,24},{18,... | collective-permute-start | bytes 24584 | tf_op jit(solution)/shard_map/ppermute | solution.py:543
  5.9 7.7 %collective-permute-start = (f32[16,128]{1,0:T(8,128)S(1)}, f32[16,128]{1,0:T(8,128)S(1)}, u32[]{:S(2)}, u32[]{:S(2)}) collective-permute-start(f32[16,128]{1,0:T(8,128)S(1)} %get-tuple-element.30.refs_0_), channel_id=1, source_target_pairs={{0,16},{2,18},{4,20},{6,22},{8,24},{10,26},{12,28},{14,30},{16,0},... | collective-permute-start | bytes 24584 | tf_op jit(solution)/shard_map/ppermute | solution.py:543
  8.5 5.6 %collective-permute-start.2 = (f32[16,128]{1,0:T(8,128)S(1)}, f32[16,128]{1,0:T(8,128)S(1)}, u32[]{:S(2)}, u32[]{:S(2)}) collective-permute-start(f32[16,128]{1,0:T(8,128)S(1)} %get-tuple-element.30.refs_0_), channel_id=1, source_target_pairs={{0,24},{2,26},{4,28},{6,30},{8,16},{10,18},{12,20},{14,22},{16,8},... | collective-permute-start | bytes 24584 | tf_op jit(solution)/shard_map/ppermute | solution.py:543
  9.1 12.7 %collective-permute-start.6 = (bf16[768,128]{1,0:T(8,128)(2,1)S(1)}, bf16[768,128]{1,0:T(8,128)(2,1)S(1)}, u32[]{:S(2)}, u32[]{:S(2)}) collective-permute-start(bf16[768,128]{1,0:T(8,128)(2,1)S(1)} %get-tuple-element.36), channel_id=1, source_target_pairs={{0,16},{2,18},{4,20},{6,22},{8,24},{10,26},{12,28},{14,30},{16,0},... | collective-permute-start | bytes 589832 | tf_op jit(solution)/shard_map/ppermute | solution.py:501
  11.1 10.8 %collective-permute-start.7 = (bf16[576,128]{1,0:T(8,128)(2,1)S(1)}, bf16[576,128]{1,0:T(8,128)(2,1)S(1)}, u32[]{:S(2)}, u32[]{:S(2)}) collective-permute-start(bf16[576,128]{1,0:T(8,128)(2,1)S(1)} %get-tuple-element.37), channel_id=1, source_target_pairs={{0,8},{2,10},{4,12},{6,14},{8,0},{10,2},{12,4},{14,6},{16,24},{18,... | collective-permute-start | bytes 442376 | tf_op jit(solution)/shard_map/ppermute | solution.py:501
  14.1 5.4 %collective-permute-start.3 = (f32[8,1536]{1,0:T(8,128)S(1)}, f32[8,1536]{1,0:T(8,128)S(1)}, u32[]{:S(2)}, u32[]{:S(2)}) collective-permute-start(f32[8,1536]{1,0:T(8,128)S(1)} %get-tuple-element.33), channel_id=1, source_target_pairs={{0,2},{2,0},{4,6},{6,4},{8,10},{10,8},{12,14},{14,12},{16,18},{18,... | collective-permute-start | bytes 147464 | tf_op jit(solution)/shard_map/ppermute | solution.py:543
  14.2 5.3 %collective-permute-start.4 = (f32[8,1536]{1,0:T(8,128)S(1)}, f32[8,1536]{1,0:T(8,128)S(1)}, u32[]{:S(2)}, u32[]{:S(2)}) collective-permute-start(f32[8,1536]{1,0:T(8,128)S(1)} %get-tuple-element.34), channel_id=1, source_target_pairs={{0,6},{2,4},{4,2},{6,0},{8,14},{10,12},{12,10},{14,8},{16,22},{18,... | collective-permute-start | bytes 147464 | tf_op jit(solution)/shard_map/ppermute | solution.py:547
  15.8 3.7 %collective-permute-start.5 = (f32[16,128]{1,0:T(8,128)S(1)}, f32[16,128]{1,0:T(8,128)S(1)}, u32[]{:S(2)}, u32[]{:S(2)}) collective-permute-start(f32[16,128]{1,0:T(8,128)S(1)} %get-tuple-element.35.refs_0_), channel_id=1, source_target_pairs={{0,4},{2,6},{4,0},{6,2},{8,12},{10,14},{12,8},{14,10},{16,20},{18,... | collective-permute-start | bytes 24584 | tf_op jit(solution)/shard_map/ppermute | solution.py:543
  23.7 3.8 %collective-permute-start.9 = (f32[16,128]{1,0:T(8,128)S(1)}, f32[16,128]{1,0:T(8,128)S(1)}, u32[]{:S(2)}, u32[]{:S(2)}) collective-permute-start(f32[16,128]{1,0:T(8,128)S(1)} %get-tuple-element.39.refs_0_), channel_id=1, source_target_pairs={{0,8},{2,10},{4,12},{6,14},{8,0},{10,2},{12,4},{14,6},{16,24},{18,... | collective-permute-start | bytes 24584 | tf_op jit(solution)/shard_map/ppermute | solution.py:543
  24.0 5.6 %collective-permute-start.10 = (f32[16,128]{1,0:T(8,128)S(1)}, f32[16,128]{1,0:T(8,128)S(1)}, u32[]{:S(2)}, u32[]{:S(2)}) collective-permute-start(f32[16,128]{1,0:T(8,128)S(1)} %get-tuple-element.39.refs_0_), channel_id=1, source_target_pairs={{0,24},{2,26},{4,28},{6,30},{8,16},{10,18},{12,20},{14,22},{16,8},... | collective-permute-start | bytes 24584 | tf_op jit(solution)/shard_map/ppermute | solution.py:543
  25.0 4.6 %collective-permute-start.8 = (f32[16,128]{1,0:T(8,128)S(1)}, f32[16,128]{1,0:T(8,128)S(1)}, u32[]{:S(2)}, u32[]{:S(2)}) collective-permute-start(f32[16,128]{1,0:T(8,128)S(1)} %get-tuple-element.39.refs_0_), channel_id=1, source_target_pairs={{0,16},{2,18},{4,20},{6,22},{8,24},{10,26},{12,28},{14,30},{16,0},... | collective-permute-start | bytes 24584 | tf_op jit(solution)/shard_map/ppermute | solution.py:543
  27.8 7.3 %collective-permute-start.14 = (bf16[576,128]{1,0:T(8,128)(2,1)S(1)}, bf16[576,128]{1,0:T(8,128)(2,1)S(1)}, u32[]{:S(2)}, u32[]{:S(2)}) collective-permute-start(bf16[576,128]{1,0:T(8,128)(2,1)S(1)} %get-tuple-element.45), channel_id=1, source_target_pairs={{0,8},{2,10},{4,12},{6,14},{8,0},{10,2},{12,4},{14,6},{16,24},{18,... | collective-permute-start | bytes 442376 | tf_op jit(solution)/shard_map/ppermute | solution.py:501
  28.8 10.5 %collective-permute-start.15 = (bf16[768,128]{1,0:T(8,128)(2,1)S(1)}, bf16[768,128]{1,0:T(8,128)(2,1)S(1)}, u32[]{:S(2)}, u32[]{:S(2)}) collective-permute-start(bf16[768,128]{1,0:T(8,128)(2,1)S(1)} %get-tuple-element.47), channel_id=1, source_target_pairs={{0,16},{2,18},{4,20},{6,22},{8,24},{10,26},{12,28},{14,30},{16,0},... | collective-permute-start | bytes 589832 | tf_op jit(solution)/shard_map/ppermute | solution.py:501
  29.7 5.4 %collective-permute-start.11 = (f32[8,1536]{1,0:T(8,128)S(1)}, f32[8,1536]{1,0:T(8,128)S(1)}, u32[]{:S(2)}, u32[]{:S(2)}) collective-permute-start(f32[8,1536]{1,0:T(8,128)S(1)} %get-tuple-element.42), channel_id=1, source_target_pairs={{0,2},{2,0},{4,6},{6,4},{8,10},{10,8},{12,14},{14,12},{16,18},{18,... | collective-permute-start | bytes 147464 | tf_op jit(solution)/shard_map/ppermute | solution.py:543
  29.8 5.3 %collective-permute-start.12 = (f32[8,1536]{1,0:T(8,128)S(1)}, f32[8,1536]{1,0:T(8,128)S(1)}, u32[]{:S(2)}, u32[]{:S(2)}) collective-permute-start(f32[8,1536]{1,0:T(8,128)S(1)} %get-tuple-element.43), channel_id=1, source_target_pairs={{0,6},{2,4},{4,2},{6,0},{8,14},{10,12},{12,10},{14,8},{16,22},{18,... | collective-permute-start | bytes 147464 | tf_op jit(solution)/shard_map/ppermute | solution.py:547
  31.4 3.7 %collective-permute-start.13 = (f32[16,128]{1,0:T(8,128)S(1)}, f32[16,128]{1,0:T(8,128)S(1)}, u32[]{:S(2)}, u32[]{:S(2)}) collective-permute-start(f32[16,128]{1,0:T(8,128)S(1)} %get-tuple-element.44.refs_0_), channel_id=1, source_target_pairs={{0,4},{2,6},{4,0},{6,2},{8,12},{10,14},{12,8},{14,10},{16,20},{18,... | collective-permute-start | bytes 24584 | tf_op jit(solution)/shard_map/ppermute | solution.py:543
  37.7 7.9 %collective-permute-start.17 = (bf16[768,128]{1,0:T(8,128)(2,1)S(1)}, bf16[768,128]{1,0:T(8,128)(2,1)S(1)}, u32[]{:S(2)}, u32[]{:S(2)}) collective-permute-start(bf16[768,128]{1,0:T(8,128)(2,1)S(1)} %get-tuple-element.48.own), channel_id=1, source_target_pairs={{0,1},{1,0},{2,3},{3,2},{4,5},{5,4},{6,7},{7,6},{8,9},{9,8},{10,11... | collective-permute-start | bytes 589832 | tf_op jit(solution)/shard_map/ppermute | solution.py:648
  39.2 1.8 %copy-start = (bf16[16,16]{1,0:T(8,128)(2,1)S(1)}, bf16[16,16]{1,0:T(8,128)(2,1)}, u32[]{:S(2)}) copy-start(bf16[16,16]{1,0:T(8,128)(2,1)} %panel.3) | copy-start | bytes 1540
  39.7 8.3 %collective-permute-start.16 = (bf16[768,128]{1,0:T(8,128)(2,1)S(1)}, bf16[768,128]{1,0:T(8,128)(2,1)S(1)}, u32[]{:S(2)}, u32[]{:S(2)}) collective-permute-start(bf16[768,128]{1,0:T(8,128)(2,1)S(1)} %filtered.1.own), channel_id=1, source_target_pairs={{0,1},{1,0},{2,3},{3,2},{4,5},{5,4},{6,7},{7,6},{8,9},{9,8},{10,11... | collective-permute-start | bytes 589832 | tf_op jit(solution)/shard_map/ppermute | solution.py:648

commit v13 on v12

--- a/solution.py
+++ b/solution.py
@@ -8,6 +8,7 @@
 from jax.sharding import PartitionSpec as P
 
 RADIUS = 6
+PIECES = 3
 COEFFS = (
     -5369.0 / 1800.0,
     12.0 / 7.0,
@@ -175,7 +176,7 @@
 def inner_tables(g, dom, v_ref, projf, blk, atom, lut, sums, table):
     size = g.nproj * g.no
 
-    unroll = 64
+    unroll = 32
 
     def step(i, _):
         for u in range(unroll):
@@ -221,33 +222,45 @@
     orb, proj, sem, blk, atom, lut, entry_sem = scratch[:7]
     sums = scratch[7:]
     copies = [
-        pltpu.make_async_copy(orb_hbm, orb, sem.at[0]),
-        pltpu.make_async_copy(proj_hbm, proj, sem.at[1]),
-        pltpu.make_async_copy(pot_hbm, pot, sem.at[2]),
+        pltpu.make_async_copy(proj_hbm, proj, sem.at[0]),
+        pltpu.make_async_copy(pot_hbm, pot, sem.at[1]),
     ]
     for copy in copies:
         copy.start()
+    size = g.rows // PIECES
+    pieces = []
+    for n in range(PIECES):
+        for o in range(g.no):
+            at = pl.ds(o * g.rows + n * size, size)
+            pieces.append(pltpu.make_async_copy(orb_hbm.at[at, :], orb.at[at, :], sem.at[2 + len(pieces)]))
+            pieces[-1].start()
     copies += entry_copies(blk_hbm, atom_hbm, blk, atom, entry_sem)
     dom = lax.axis_index("dom")
     fill_lut(g, dom, lut)
     clear(sums)
-    copies[1].wait()
+    copies[0].wait()
     projf[...] = proj[...].astype(F32)
-    copies[0].wait()
     for r in range(g.rows):
+        if r % size == 0:
+            for piece in pieces[r // size * g.no : (r // size + 1) * g.no]:
+                piece.wait()
         v_ref[r * g.no : (r + 1) * g.no, :] = orb[pl.ds(r, g.no, stride=g.rows), :]
-    for copy in copies[2:]:
+    for copy in copies[1:]:
         copy.wait()
     inner_tables(g, dom, v_ref, projf, blk, atom, lut, sums, table)
 
 
-def pack_kernel(g, *refs):
-    part, from_x, from_y, from_xy = refs[:4]
-    ends, outs, group = refs[4:6], refs[-3:-1], refs[-1]
-    group[...] = (part[...] + from_x[...]) + (from_y[...] + from_xy[...])
-    for source, out in zip(ends, outs):
-        out[...] = source[...]
-        put_table(g, out, group)
+def pack_kernel(g, v_ref, energy, *refs):
+    if g.butterfly:
+        part, from_x, from_y, from_xy = refs[:4]
+        group = refs[-1]
+        group[...] = (part[...] + from_x[...]) + (from_y[...] + from_xy[...])
+        refs = refs[:-1]
+    first, second = refs[-2:]
+    pack_ends(g, lax.axis_index("dom"), v_ref, first, second)
+    if g.butterfly:
+        put_table(g, first, group)
+        put_table(g, second, group)
 
 
 def pack_faces_kernel(g, nafter, v_ref, *refs):
@@ -255,8 +268,7 @@
     dom = lax.axis_index("dom")
     refs = refs[nafter:]
     pack_x(g, dom, v_ref, refs[:nx])
-    pack_y(g, dom, v_ref, refs[nx:-2])
-    pack_ends(g, dom, v_ref, *refs[-2:])
+    pack_y(g, dom, v_ref, refs[nx:])
 
 
 def inside_kernel(g, scale, subtract, v_ref, pot, *refs):
@@ -296,7 +308,7 @@
     return 1.0 if present is None else jnp.where(present, 1.0, 0.0)
 
 
-def add_ends(g, dom, scale, acc, low, high, out):
+def add_ends(g, dom, scale, acc, low, high, others, out):
     inward, row = end_columns(g, dom)
     middle = (dom % g.third > 0) & (dom % g.third < g.third - 1)
     present = (row % 8 < RADIUS) & ((row < 8) | middle)
@@ -307,7 +319,10 @@
         rows = slice(x * g.slab, (x + 1) * g.slab)
         h_high, h_low = split2(jnp.concatenate([low[:, rows], high[:, rows]], axis=0))
         halo = jnp.concatenate([h_high, h_low, h_high, h_low], axis=0)
-        out[rows, :] = acc[rows, :] + lax.dot_general(halo, coefs, TN, preferred_element_type=F32)
+        total = acc[rows, :]
+        for other in others:
+            total = total + other[rows, :]
+        out[rows, :] = total + lax.dot_general(halo, coefs, TN, preferred_element_type=F32)
 
 
 def add_x_faces(g, dom, scale, face_refs, out, count):
@@ -338,8 +353,7 @@
                 out[pl.ds(at, g.no), :] = total
 
 
-def add_nonlocal(g, dom, table, energy, projf, blk, atom, lut, spread, out):
-    size = g.nproj * g.no
+def spread_rows(g, dom, table, energy, spread):
     lanes = g.table
     count = g.slots()
     rows = []
@@ -359,10 +373,12 @@
     out_all = lax.dot_general(parts, ones, TN, preferred_element_type=F32)
     for number in range(count):
         spread[number * lanes : (number + 1) * lanes, :] = out_all[:, number * g.cz : (number + 1) * g.cz]
-    unroll = 64
+
+def add_nonlocal(g, projf, blk, atom, lut, spread, outs):
+    size = g.nproj * g.no
+    unroll = 32
 
     def step(i, _):
-        additions = []
         for u in range(unroll):
             e = i * unroll + u
             col = column_of(g, lut, atom[e])
@@ -372,21 +388,19 @@
                 coef = jnp.broadcast_to(projf[e, p : p + 1, :], (g.no, g.cz))
                 term = spread[at, :] * coef
                 total = term if total is None else total + term
-            additions.append((pl.ds(pl.multiple_of(blk[e] * g.no, g.no), g.no), total))
-        for at, total in additions:
-            out[at, :] += total
+            at = pl.ds(pl.multiple_of(blk[e] * g.no, g.no), g.no)
+            outs[u % len(outs)][at, :] += total
         return 0
 
     lax.fori_loop(0, g.ent // unroll, step, 0)
 
 
 def nonlocal_kernel(g, scale, far, acc, projf, energy, blk_hbm, atom_hbm, first, second, *refs):
-    table, blk, atom, lut, sem, spread = refs[-6:]
-    out = refs[-7]
-    filtered = None
+    table, blk, atom, lut, sem, spread, *sums = refs[-8:]
+    out = refs[-9]
     if far:
-        out, filtered = refs[-8:-6]
-        y_refs = refs[-8 - len(g.face_rows(1)) : -8]
+        out, filtered = refs[-10:-8]
+        y_refs = refs[-10 - len(g.face_rows(1)) : -10]
     copies = entry_copies(blk_hbm, atom_hbm, blk, atom, sem)
     dom = lax.axis_index("dom")
     fill_lut(g, dom, lut)
@@ -395,10 +409,12 @@
         table[...] = (group[...] + get_table(g, first)) + (get_table(g, second) + opposite[...])
     else:
         table[...] = refs[0][...]
-    add_ends(g, dom, scale, acc, first, second, out)
+    spread_rows(g, dom, table, energy, spread)
+    clear(sums)
     for copy in copies:
         copy.wait()
-    add_nonlocal(g, dom, table, energy, projf, blk, atom, lut, spread, out)
+    add_nonlocal(g, projf, blk, atom, lut, spread, sums)
+    add_ends(g, dom, scale, acc, first, second, sums, out)
     if far:
         start, count = halves(g, dom)[0]
         rows = pl.ds(aligned(start * g.slab, g.slab), count * g.slab)
@@ -559,30 +575,30 @@
         )
 
         after = []
+        tables = []
         if g.butterfly:
             tables = [part, swap(part, g.plane), swap(part, g.third), swap(part, g.plane, g.third)]
             after.append(tables[2])
-        *faces, first, second = call(
+        faces = call(
             functools.partial(pack_faces_kernel, g, len(after)),
             "faces_" + which,
-            [*x_faces, *y_faces, ends, ends],
+            [*x_faces, *y_faces],
             [],
             [values, *after],
             [VMEM] * (1 + len(after)),
         )
         from_x = swap_faces(g, faces[:nx], g.plane, g.first)
         from_y = swap_faces(g, faces[nx:], g.third, g.second)
-        if g.butterfly:
-            first, second, group = call(
-                functools.partial(pack_kernel, g),
-                "pack_" + which,
-                [ends, ends, table],
-                [],
-                [*tables, first, second, energy],
-                [VMEM] * 7,
-            )
+        first, second, *group = call(
+            functools.partial(pack_kernel, g),
+            "pack_" + which,
+            [ends, ends, table] if g.butterfly else [ends, ends],
+            [],
+            [values, energy, *tables],
+            [VMEM] * (2 + len(tables)),
+        )
         first, second = swap(first, 1), reverse(second)
-        tables = [group, swap(group, 2)] if g.butterfly else [lax.psum(part, "dom")]
+        tables = [*group, swap(group[0], 2)] if g.butterfly else [lax.psum(part, "dom")]
         far = []
         if prev and len(halves(g, 0)) == 2:
             far = [jax.ShapeDtypeStruct((halves(g, 0)[0][1] * g.slab, g.cz), BF16)]
@@ -591,7 +607,7 @@
             functools.partial(nonlocal_kernel, g, scale, len(far) > 0),
             "nonlocal_" + which,
             [field, *far],
-            [pltpu.VMEM(table.shape, F32), *entries, spread],
+            [pltpu.VMEM(table.shape, F32), *entries, spread] + [pltpu.VMEM(field.shape, F32)] * 2,
             [acc, projf, energy, blk, atom, first, second, *tables],
             [VMEM] * 3 + [HBM] * 2 + [VMEM] * (2 + len(tables)),
         )
@@ -604,7 +620,7 @@
         [
             pltpu.VMEM(orb.shape, F32),
             pltpu.VMEM(proj.shape, BF16),
-            pltpu.SemaphoreType.DMA((3,)),
+            pltpu.SemaphoreType.DMA((2 + PIECES * g.no,)),
             *entries,
             *sums,
         ],

time: 49.2 us -> 50.7 us (1.030)
  waiting for transfers between devices: 10.7 us -> 14.4 us
  starting transfers between devices: 22.6 us -> 21.2 us
  Pallas kernels: 14.9 us -> 14.2 us
    ppermute x10, waiting for transfers between devices: 5.07 us -> 7.97 us  [swap(): return lax.ppermute(array, 'dom', pairs)]
    ppermute x4, starting transfers between devices: 5.99 us -> 4.6 us  [shift(): return lax.ppermute(array, 'dom', pairs)]
    ppermute x10, starting transfers between devices: 10.3 us -> 11.3 us  [swap(): return lax.ppermute(array, 'dom', pairs)]
    ppermute x2, waiting for transfers between devices: 5.66 us -> 6.43 us  [shards(): lax.ppermute(filtered, 'band', [(0, 1), (1, 0)])]
    ppermute x2, starting transfers between devices: 2.91 us -> 2.16 us  [shards(): lax.ppermute(filtered, 'band', [(0, 1), (1, 0)])]
    pallas_call x14, Pallas kernels: 14.9 us -> 14.2 us  [call(): pl.pallas_call(kernel, name=name, out_shape=out_shape, in_specs=specs, ou...]
  transfers between devices with their start and end apart: 18 -> 18, of which waited for: 7 -> 7; matrix products, arithmetic and copies ran while one was open for 1% -> 1% of each run, Pallas kernels for 19% -> 17%
where the time goes in v13:
time: 50.7 us; the launch traced here: 50.5 us
  starting transfers between devices  21.2 us (42%)
  waiting for transfers between devices  14.4 us (28%)
  Pallas kernels  14.2 us (28%)
  local copies, waits for them, and re-layouts  0.61 us (1%)
    pallas_call x14, Pallas kernels, call(): pl.pallas_call(kernel, name=name, out_shape=out_shape, in_specs=specs, ou...  14.2 us
    ppermute x10, starting transfers between devices, swap(): return lax.ppermute(array, 'dom', pairs)  11.3 us
    ppermute x10, waiting for transfers between devices, swap(): return lax.ppermute(array, 'dom', pairs)  7.97 us
    ppermute x2, waiting for transfers between devices, shards(): lax.ppermute(filtered, 'band', [(0, 1), (1, 0)])  6.43 us
    ppermute x4, starting transfers between devices, shift(): return lax.ppermute(array, 'dom', pairs)  4.6 us
    ppermute x2, starting transfers between devices, reverse(): return lax.ppermute(array, 'dom', pairs)  3.16 us
    ppermute x2, starting transfers between devices, shards(): lax.ppermute(filtered, 'band', [(0, 1), (1, 0)])  2.16 us
  transfers between devices with their start and end apart: 18, of which 7 were waited for; matrix products, arithmetic and copies ran while one was open for 1% of the time, Pallas kernels for 17%

profile of v13, /device:TPU:0, one launch (start us, length us, event | category | flops | bytes accessed | tf_op | source)
XLA Modules:
  0.0 50.5 jit_solution(13232169049900039337)
XLA Ops:
  0.0 2.9 %tables_first.1 = (f32[1536,128]{1,0:T(8,128)S(1)}, f32[256,4,128]{2,1,0:T(4,128)S(1)}, f32[192,128]{1,0:T(8,128)S(1)}, f32[16,128]{1,0:T(8,128)S(1)}) custom-call(f32[1536,128]{1,0:T(8,128)} %bitcast.7, bf16[256,4,128]{2,1,0:T(4,128)(2,1)} %proj_hbm.1, f32[192,128]{1,0:T(8,128)} %bitcast.8, s32[256]{0:T(256)} %blk_hbm.7, s32[256]{0:T(256)} %atom_hbm.7), custom_call_target="tpu_custom_call" | custom-call | flops 1000 | bytes 1000 | tf_op jit(solution)/shard_map/tables_first/pallas_call | solution.py:499
  2.9 4.1 %collective-permute-start = (f32[16,128]{1,0:T(8,128)S(1)}, f32[16,128]{1,0:T(8,128)S(1)}, u32[]{:S(2)}, u32[]{:S(2)}) collective-permute-start(f32[16,128]{1,0:T(8,128)S(1)} %get-tuple-element.26.refs_0_), channel_id=1, source_target_pairs={{0,16},{2,18},{4,20},{6,22},{8,24},{10,26},{12,28},{14,30},{16,0},... | collective-permute-start | bytes 24584 | tf_op jit(solution)/shard_map/ppermute | solution.py:559
  7.0 1.6 %collective-permute-start.1 = (f32[16,128]{1,0:T(8,128)S(1)}, f32[16,128]{1,0:T(8,128)S(1)}, u32[]{:S(2)}, u32[]{:S(2)}) collective-permute-start(f32[16,128]{1,0:T(8,128)S(1)} %get-tuple-element.26.refs_0_), channel_id=1, source_target_pairs={{0,8},{2,10},{4,12},{6,14},{8,0},{10,2},{12,4},{14,6},{16,24},{18,... | collective-permute-start | bytes 24584 | tf_op jit(solution)/shard_map/ppermute | solution.py:559
  8.8 1.8 %collective-permute-done.1.refs_2_.refs_0_ = f32[16,128]{1,0:T(8,128)S(1)} collective-permute-done((f32[16,128]{1,0:T(8,128)S(1)}, f32[16,128]{1,0:T(8,128)S(1)}, u32[]{:S(2)}, u32[]{:S(2)}) %collective-permute-start.1) | collective-permute-done | bytes 8224 | tf_op jit(solution)/shard_map/ppermute | solution.py:559
  10.9 2.5 %collective-permute-start.7 = (bf16[576,128]{1,0:T(8,128)(2,1)S(1)}, bf16[576,128]{1,0:T(8,128)(2,1)S(1)}, u32[]{:S(2)}, u32[]{:S(2)}) collective-permute-start(bf16[576,128]{1,0:T(8,128)(2,1)S(1)} %get-tuple-element.31), channel_id=1, source_target_pairs={{0,8},{2,10},{4,12},{6,14},{8,0},{10,2},{12,4},{14,6},{16,24},{18,... | collective-permute-start | bytes 442376 | tf_op jit(solution)/shard_map/ppermute | solution.py:517
  13.4 0.8 %collective-permute-done.2.refs_3_ = f32[16,128]{1,0:T(8,128)S(1)} collective-permute-done((f32[16,128]{1,0:T(8,128)S(1)}, f32[16,128]{1,0:T(8,128)S(1)}, u32[]{:S(2)}, u32[]{:S(2)}) %collective-permute-start.2) | collective-permute-done | bytes 8224 | tf_op jit(solution)/shard_map/ppermute | solution.py:559
  14.5 1.6 %collective-permute-start.4 = (f32[8,1536]{1,0:T(8,128)S(1)}, f32[8,1536]{1,0:T(8,128)S(1)}, u32[]{:S(2)}, u32[]{:S(2)}) collective-permute-start(f32[8,1536]{1,0:T(8,128)S(1)} %get-tuple-element.28), channel_id=1, source_target_pairs={{0,6},{2,4},{4,2},{6,0},{8,14},{10,12},{12,10},{14,8},{16,22},{18,... | collective-permute-start | bytes 147464 | tf_op jit(solution)/shard_map/ppermute | solution.py:563
  16.7 0.9 %inside_first.1.acc = f32[1536,128]{1,0:T(8,128)S(1)} custom-call(f32[1536,128]{1,0:T(8,128)S(1)} %get-tuple-element.23.v_ref.refs_0_, f32[192,128]{1,0:T(8,128)S(1)} %get-tuple-element.24.pot), custom_call_target="tpu_custom_call" | custom-call | flops 1000 | bytes 1000 | tf_op jit(solution)/shard_map/inside_first/pallas_call | solution.py:499
  17.6 2.2 %collective-permute-done.5.refs_1_ = f32[16,128]{1,0:T(8,128)S(1)} collective-permute-done((f32[16,128]{1,0:T(8,128)S(1)}, f32[16,128]{1,0:T(8,128)S(1)}, u32[]{:S(2)}, u32[]{:S(2)}) %collective-permute-start.5) | collective-permute-done | bytes 8224 | tf_op jit(solution)/shard_map/ppermute | solution.py:559
  19.8 2.0 %nonlocal_first.1.acc = f32[1536,128]{1,0:T(8,128)S(1)} custom-call(f32[1536,128]{1,0:T(8,128)S(1)} %inside_first.1.acc, f32[256,4,128]{2,1,0:T(4,128)S(1)} %get-tuple-element.25.projf, f32[16,128]{1,0:T(8,128)S(1)} %copy.12.energy, s32[256]{0:T(256)} %blk_hbm.7, s32[256]{0:T(256)} %atom_hbm.7, f32[8,1536]{1,0:T(8,128)S(1)} %collective-permute-done.3.first, ...), custom_call_target="tpu_custom_call" | custom-call | flops 1000 | bytes 1000 | tf_op jit(solution)/shard_map/nonlocal_first/pallas_call | solution.py:499
  21.8 1.9 %tables_second.1 = (f32[1536,128]{1,0:T(8,128)S(1)}, f32[16,128]{1,0:T(8,128)S(1)}) custom-call(f32[1536,128]{1,0:T(8,128)S(1)} %nonlocal_first.1.acc, f32[256,4,128]{2,1,0:T(4,128)S(1)} %get-tuple-element.25.projf, s32[256]{0:T(256)} %blk_hbm.7, s32[256]{0:T(256)} %atom_hbm.7, bf16[768,128]{1,0:T(8,128)(2,1)S(1)} %collective-permute-done.6.refs_0_, ...), custom_call_target="tpu_custom_call" | custom-call | flops 1000 | bytes 1000 | tf_op jit(solution)/shard_map/tables_second/pallas_call | solution.py:499
  24.0 1.9 %collective-permute-start.8 = (f32[16,128]{1,0:T(8,128)S(1)}, f32[16,128]{1,0:T(8,128)S(1)}, u32[]{:S(2)}, u32[]{:S(2)}) collective-permute-start(f32[16,128]{1,0:T(8,128)S(1)} %get-tuple-element.33.refs_0_), channel_id=1, source_target_pairs={{0,16},{2,18},{4,20},{6,22},{8,24},{10,26},{12,28},{14,30},{16,0},... | collective-permute-start | bytes 24584 | tf_op jit(solution)/shard_map/ppermute | solution.py:559
  25.9 2.5 %collective-permute-start.10 = (f32[16,128]{1,0:T(8,128)S(1)}, f32[16,128]{1,0:T(8,128)S(1)}, u32[]{:S(2)}, u32[]{:S(2)}) collective-permute-start(f32[16,128]{1,0:T(8,128)S(1)} %get-tuple-element.33.refs_0_), channel_id=1, source_target_pairs={{0,24},{2,26},{4,28},{6,30},{8,16},{10,18},{12,20},{14,22},{16,8},... | collective-permute-start | bytes 24584 | tf_op jit(solution)/shard_map/ppermute | solution.py:559
  28.5 1.9 %collective-permute-start.15 = (bf16[768,128]{1,0:T(8,128)(2,1)S(1)}, bf16[768,128]{1,0:T(8,128)(2,1)S(1)}, u32[]{:S(2)}, u32[]{:S(2)}) collective-permute-start(bf16[768,128]{1,0:T(8,128)(2,1)S(1)} %get-tuple-element.39), channel_id=1, source_target_pairs={{0,16},{2,18},{4,20},{6,22},{8,24},{10,26},{12,28},{14,30},{16,0},... | collective-permute-start | bytes 589832 | tf_op jit(solution)/shard_map/ppermute | solution.py:517
  30.5 1.1 %collective-permute-done.10.refs_3_ = f32[16,128]{1,0:T(8,128)S(1)} collective-permute-done((f32[16,128]{1,0:T(8,128)S(1)}, f32[16,128]{1,0:T(8,128)S(1)}, u32[]{:S(2)}, u32[]{:S(2)}) %collective-permute-start.10) | collective-permute-done | bytes 8224 | tf_op jit(solution)/shard_map/ppermute | solution.py:559
  31.9 1.5 %collective-permute-start.12 = (f32[8,1536]{1,0:T(8,128)S(1)}, f32[8,1536]{1,0:T(8,128)S(1)}, u32[]{:S(2)}, u32[]{:S(2)}) collective-permute-start(f32[8,1536]{1,0:T(8,128)S(1)} %get-tuple-element.35), channel_id=1, source_target_pairs={{0,6},{2,4},{4,2},{6,0},{8,14},{10,12},{12,10},{14,8},{16,22},{18,... | collective-permute-start | bytes 147464 | tf_op jit(solution)/shard_map/ppermute | solution.py:563
  34.0 1.0 %inside_second.1.acc = f32[1536,128]{1,0:T(8,128)S(1)} custom-call(f32[1536,128]{1,0:T(8,128)S(1)} %get-tuple-element.32.v_ref, f32[192,128]{1,0:T(8,128)S(1)} %get-tuple-element.24.pot, f32[1536,128]{1,0:T(8,128)S(1)} %get-tuple-element.23.v_ref.refs_0_), custom_call_target="tpu_custom_call" | custom-call | flops 1000 | bytes 1000 | tf_op jit(solution)/shard_map/inside_second/pallas_call | solution.py:499
  35.0 2.1 %collective-permute-done.13.refs_1_ = f32[16,128]{1,0:T(8,128)S(1)} collective-permute-done((f32[16,128]{1,0:T(8,128)S(1)}, f32[16,128]{1,0:T(8,128)S(1)}, u32[]{:S(2)}, u32[]{:S(2)}) %collective-permute-start.13) | collective-permute-done | bytes 8224 | tf_op jit(solution)/shard_map/ppermute | solution.py:559
  37.1 2.2 %nonlocal_second.1 = (f32[1536,128]{1,0:T(8,128)S(1)}, bf16[768,128]{1,0:T(8,128)(2,1)S(1)}) custom-call(f32[1536,128]{1,0:T(8,128)S(1)} %inside_second.1.acc, f32[256,4,128]{2,1,0:T(4,128)S(1)} %get-tuple-element.25.projf, f32[16,128]{1,0:T(8,128)S(1)} %copy.16.energy, s32[256]{0:T(256)} %blk_hbm.7, s32[256]{0:T(256)} %atom_hbm.7, ...), custom_call_target="tpu_custom_call" | custom-call | flops 1000 | bytes 1000 | tf_op jit(solution)/shard_map/nonlocal_second/pallas_call | solution.py:499
  39.3 1.6 %collective-permute-start.17 = (bf16[768,128]{1,0:T(8,128)(2,1)S(1)}, bf16[768,128]{1,0:T(8,128)(2,1)S(1)}, u32[]{:S(2)}, u32[]{:S(2)}) collective-permute-start(bf16[768,128]{1,0:T(8,128)(2,1)S(1)} %get-tuple-element.40.own), channel_id=1, source_target_pairs={{0,1},{1,0},{2,3},{3,2},{4,5},{5,4},{6,7},{7,6},{8,9},{9,8},{10,11... | collective-permute-start | bytes 589832 | tf_op jit(solution)/shard_map/ppermute | solution.py:664
  42.2 5.0 %collective-permute-done.17.other = bf16[768,128]{1,0:T(8,128)(2,1)S(1)} collective-permute-done((bf16[768,128]{1,0:T(8,128)(2,1)S(1)}, bf16[768,128]{1,0:T(8,128)(2,1)S(1)}, u32[]{:S(2)}, u32[]{:S(2)}) %collective-permute-start.17) | collective-permute-done | bytes 196640 | tf_op jit(solution)/shard_map/ppermute | solution.py:664
  47.2 1.0 %rotate_0.1.refs_0_ = f32[8,192,128]{2,1,0:T(8,128)} custom-call(bf16[768,128]{1,0:T(8,128)(2,1)S(1)} %get-tuple-element.40.own, bf16[768,128]{1,0:T(8,128)(2,1)S(1)} %collective-permute-done.17.other, bf16[128,256]{1,0:T(8,128)(2,1)S(1)} %panel.2.weights), custom_call_target="tpu_custom_call" | custom-call | flops 1000 | bytes 1000 | tf_op jit(solution)/shard_map/rotate_0/pallas_call | solution.py:499
  48.1 1.4 %collective-permute-done.16.other = bf16[768,128]{1,0:T(8,128)(2,1)S(1)} collective-permute-done((bf16[768,128]{1,0:T(8,128)(2,1)S(1)}, bf16[768,128]{1,0:T(8,128)(2,1)S(1)}, u32[]{:S(2)}, u32[]{:S(2)}) %collective-permute-start.16) | collective-permute-done | bytes 196640 | tf_op jit(solution)/shard_map/ppermute | solution.py:664
  49.6 1.0 %rotate_1.1 = f32[8,192,128]{2,1,0:T(8,128)} custom-call(bf16[768,128]{1,0:T(8,128)(2,1)S(1)} %filtered.1.own, bf16[768,128]{1,0:T(8,128)(2,1)S(1)} %collective-permute-done.16.other, bf16[128,256]{1,0:T(8,128)(2,1)S(1)} %panel.2.weights, f32[8,192,128]{2,1,0:T(8,128)} %rotate_0.1.refs_0_), custom_call_target="tpu_custom_call", output_to_operand_aliasing={{}: (3, {})} | custom-call | flops 1000 | bytes 1000 | tf_op jit(solution)/shard_map/rotate_1/pallas_call | solution.py:499
  (41 shorter events, 4.1 us)
Async XLA Ops:
  0.0 8.6 %copy-start.1 = (f32[64,4]{0,1:T(4,128)S(1)}, f32[64,4]{0,1:T(4,128)}, u32[]{:S(2)}) copy-start(f32[64,4]{0,1:T(4,128)} %param.12) | copy-start | bytes 3076
  2.9 10.5 %collective-permute-start = (f32[16,128]{1,0:T(8,128)S(1)}, f32[16,128]{1,0:T(8,128)S(1)}, u32[]{:S(2)}, u32[]{:S(2)}) collective-permute-start(f32[16,128]{1,0:T(8,128)S(1)} %get-tuple-element.26.refs_0_), channel_id=1, source_target_pairs={{0,16},{2,18},{4,20},{6,22},{8,24},{10,26},{12,28},{14,30},{16,0},... | collective-permute-start | bytes 24584 | tf_op jit(solution)/shard_map/ppermute | solution.py:559
  7.0 3.7 %collective-permute-start.1 = (f32[16,128]{1,0:T(8,128)S(1)}, f32[16,128]{1,0:T(8,128)S(1)}, u32[]{:S(2)}, u32[]{:S(2)}) collective-permute-start(f32[16,128]{1,0:T(8,128)S(1)} %get-tuple-element.26.refs_0_), channel_id=1, source_target_pairs={{0,8},{2,10},{4,12},{6,14},{8,0},{10,2},{12,4},{14,6},{16,24},{18,... | collective-permute-start | bytes 24584 | tf_op jit(solution)/shard_map/ppermute | solution.py:559
  8.6 5.6 %collective-permute-start.2 = (f32[16,128]{1,0:T(8,128)S(1)}, f32[16,128]{1,0:T(8,128)S(1)}, u32[]{:S(2)}, u32[]{:S(2)}) collective-permute-start(f32[16,128]{1,0:T(8,128)S(1)} %get-tuple-element.26.refs_0_), channel_id=1, source_target_pairs={{0,24},{2,26},{4,28},{6,30},{8,16},{10,18},{12,20},{14,22},{16,8},... | collective-permute-start | bytes 24584 | tf_op jit(solution)/shard_map/ppermute | solution.py:559
  10.7 11.1 %collective-permute-start.6 = (bf16[768,128]{1,0:T(8,128)(2,1)S(1)}, bf16[768,128]{1,0:T(8,128)(2,1)S(1)}, u32[]{:S(2)}, u32[]{:S(2)}) collective-permute-start(bf16[768,128]{1,0:T(8,128)(2,1)S(1)} %get-tuple-element.30), channel_id=1, source_target_pairs={{0,16},{2,18},{4,20},{6,22},{8,24},{10,26},{12,28},{14,30},{16,0},... | collective-permute-start | bytes 589832 | tf_op jit(solution)/shard_map/ppermute | solution.py:517
  10.9 10.9 %collective-permute-start.7 = (bf16[576,128]{1,0:T(8,128)(2,1)S(1)}, bf16[576,128]{1,0:T(8,128)(2,1)S(1)}, u32[]{:S(2)}, u32[]{:S(2)}) collective-permute-start(bf16[576,128]{1,0:T(8,128)(2,1)S(1)} %get-tuple-element.31), channel_id=1, source_target_pairs={{0,8},{2,10},{4,12},{6,14},{8,0},{10,2},{12,4},{14,6},{16,24},{18,... | collective-permute-start | bytes 442376 | tf_op jit(solution)/shard_map/ppermute | solution.py:517
  14.5 5.3 %collective-permute-start.3 = (f32[8,1536]{1,0:T(8,128)S(1)}, f32[8,1536]{1,0:T(8,128)S(1)}, u32[]{:S(2)}, u32[]{:S(2)}) collective-permute-start(f32[8,1536]{1,0:T(8,128)S(1)} %get-tuple-element.27), channel_id=1, source_target_pairs={{0,2},{2,0},{4,6},{6,4},{8,10},{10,8},{12,14},{14,12},{16,18},{18,... | collective-permute-start | bytes 147464 | tf_op jit(solution)/shard_map/ppermute | solution.py:559
  14.5 5.3 %collective-permute-start.4 = (f32[8,1536]{1,0:T(8,128)S(1)}, f32[8,1536]{1,0:T(8,128)S(1)}, u32[]{:S(2)}, u32[]{:S(2)}) collective-permute-start(f32[8,1536]{1,0:T(8,128)S(1)} %get-tuple-element.28), channel_id=1, source_target_pairs={{0,6},{2,4},{4,2},{6,0},{8,14},{10,12},{12,10},{14,8},{16,22},{18,... | collective-permute-start | bytes 147464 | tf_op jit(solution)/shard_map/ppermute | solution.py:563
  16.2 3.7 %collective-permute-start.5 = (f32[16,128]{1,0:T(8,128)S(1)}, f32[16,128]{1,0:T(8,128)S(1)}, u32[]{:S(2)}, u32[]{:S(2)}) collective-permute-start(f32[16,128]{1,0:T(8,128)S(1)} %get-tuple-element.29.refs_0_), channel_id=1, source_target_pairs={{0,4},{2,6},{4,0},{6,2},{8,12},{10,14},{12,8},{14,10},{16,20},{18,... | collective-permute-start | bytes 24584 | tf_op jit(solution)/shard_map/ppermute | solution.py:559
  23.7 4.7 %collective-permute-start.9 = (f32[16,128]{1,0:T(8,128)S(1)}, f32[16,128]{1,0:T(8,128)S(1)}, u32[]{:S(2)}, u32[]{:S(2)}) collective-permute-start(f32[16,128]{1,0:T(8,128)S(1)} %get-tuple-element.33.refs_0_), channel_id=1, source_target_pairs={{0,8},{2,10},{4,12},{6,14},{8,0},{10,2},{12,4},{14,6},{16,24},{18,... | collective-permute-start | bytes 24584 | tf_op jit(solution)/shard_map/ppermute | solution.py:559
  24.0 6.5 %collective-permute-start.8 = (f32[16,128]{1,0:T(8,128)S(1)}, f32[16,128]{1,0:T(8,128)S(1)}, u32[]{:S(2)}, u32[]{:S(2)}) collective-permute-start(f32[16,128]{1,0:T(8,128)S(1)} %get-tuple-element.33.refs_0_), channel_id=1, source_target_pairs={{0,16},{2,18},{4,20},{6,22},{8,24},{10,26},{12,28},{14,30},{16,0},... | collective-permute-start | bytes 24584 | tf_op jit(solution)/shard_map/ppermute | solution.py:559
  25.9 5.7 %collective-permute-start.10 = (f32[16,128]{1,0:T(8,128)S(1)}, f32[16,128]{1,0:T(8,128)S(1)}, u32[]{:S(2)}, u32[]{:S(2)}) collective-permute-start(f32[16,128]{1,0:T(8,128)S(1)} %get-tuple-element.33.refs_0_), channel_id=1, source_target_pairs={{0,24},{2,26},{4,28},{6,30},{8,16},{10,18},{12,20},{14,22},{16,8},... | collective-permute-start | bytes 24584 | tf_op jit(solution)/shard_map/ppermute | solution.py:559
  28.4 8.6 %collective-permute-start.14 = (bf16[576,128]{1,0:T(8,128)(2,1)S(1)}, bf16[576,128]{1,0:T(8,128)(2,1)S(1)}, u32[]{:S(2)}, u32[]{:S(2)}) collective-permute-start(bf16[576,128]{1,0:T(8,128)(2,1)S(1)} %get-tuple-element.37), channel_id=1, source_target_pairs={{0,8},{2,10},{4,12},{6,14},{8,0},{10,2},{12,4},{14,6},{16,24},{18,... | collective-permute-start | bytes 442376 | tf_op jit(solution)/shard_map/ppermute | solution.py:517
  28.5 12.3 %collective-permute-start.15 = (bf16[768,128]{1,0:T(8,128)(2,1)S(1)}, bf16[768,128]{1,0:T(8,128)(2,1)S(1)}, u32[]{:S(2)}, u32[]{:S(2)}) collective-permute-start(bf16[768,128]{1,0:T(8,128)(2,1)S(1)} %get-tuple-element.39), channel_id=1, source_target_pairs={{0,16},{2,18},{4,20},{6,22},{8,24},{10,26},{12,28},{14,30},{16,0},... | collective-permute-start | bytes 589832 | tf_op jit(solution)/shard_map/ppermute | solution.py:517
  31.8 5.2 %collective-permute-start.11 = (f32[8,1536]{1,0:T(8,128)S(1)}, f32[8,1536]{1,0:T(8,128)S(1)}, u32[]{:S(2)}, u32[]{:S(2)}) collective-permute-start(f32[8,1536]{1,0:T(8,128)S(1)} %get-tuple-element.34), channel_id=1, source_target_pairs={{0,2},{2,0},{4,6},{6,4},{8,10},{10,8},{12,14},{14,12},{16,18},{18,... | collective-permute-start | bytes 147464 | tf_op jit(solution)/shard_map/ppermute | solution.py:559
  31.9 5.2 %collective-permute-start.12 = (f32[8,1536]{1,0:T(8,128)S(1)}, f32[8,1536]{1,0:T(8,128)S(1)}, u32[]{:S(2)}, u32[]{:S(2)}) collective-permute-start(f32[8,1536]{1,0:T(8,128)S(1)} %get-tuple-element.35), channel_id=1, source_target_pairs={{0,6},{2,4},{4,2},{6,0},{8,14},{10,12},{12,10},{14,8},{16,22},{18,... | collective-permute-start | bytes 147464 | tf_op jit(solution)/shard_map/ppermute | solution.py:563
  33.4 3.7 %collective-permute-start.13 = (f32[16,128]{1,0:T(8,128)S(1)}, f32[16,128]{1,0:T(8,128)S(1)}, u32[]{:S(2)}, u32[]{:S(2)}) collective-permute-start(f32[16,128]{1,0:T(8,128)S(1)} %get-tuple-element.36.refs_0_), channel_id=1, source_target_pairs={{0,4},{2,6},{4,0},{6,2},{8,12},{10,14},{12,8},{14,10},{16,20},{18,... | collective-permute-start | bytes 24584 | tf_op jit(solution)/shard_map/ppermute | solution.py:559
  39.3 7.9 %collective-permute-start.17 = (bf16[768,128]{1,0:T(8,128)(2,1)S(1)}, bf16[768,128]{1,0:T(8,128)(2,1)S(1)}, u32[]{:S(2)}, u32[]{:S(2)}) collective-permute-start(bf16[768,128]{1,0:T(8,128)(2,1)S(1)} %get-tuple-element.40.own), channel_id=1, source_target_pairs={{0,1},{1,0},{2,3},{3,2},{4,5},{5,4},{6,7},{7,6},{8,9},{9,8},{10,11... | collective-permute-start | bytes 589832 | tf_op jit(solution)/shard_map/ppermute | solution.py:664
  40.8 1.1 %copy-start = (bf16[16,16]{1,0:T(8,128)(2,1)S(1)}, bf16[16,16]{1,0:T(8,128)(2,1)}, u32[]{:S(2)}) copy-start(bf16[16,16]{1,0:T(8,128)(2,1)} %panel.3) | copy-start | bytes 1540
  41.3 8.3 %collective-permute-start.16 = (bf16[768,128]{1,0:T(8,128)(2,1)S(1)}, bf16[768,128]{1,0:T(8,128)(2,1)S(1)}, u32[]{:S(2)}, u32[]{:S(2)}) collective-permute-start(bf16[768,128]{1,0:T(8,128)(2,1)S(1)} %filtered.1.own), channel_id=1, source_target_pairs={{0,1},{1,0},{2,3},{3,2},{4,5},{5,4},{6,7},{7,6},{8,9},{9,8},{10,11... | collective-permute-start | bytes 589832 | tf_op jit(solution)/shard_map/ppermute | solution.py:664

commit v14 on v13

--- a/solution.py
+++ b/solution.py
@@ -308,21 +308,22 @@
     return 1.0 if present is None else jnp.where(present, 1.0, 0.0)
 
 
-def add_ends(g, dom, scale, acc, low, high, others, out):
+def add_ends(g, dom, scale, acc, low, high, others, out, start, count):
     inward, row = end_columns(g, dom)
     middle = (dom % g.third > 0) & (dom % g.third < g.third - 1)
     present = (row % 8 < RADIUS) & ((row < 8) | middle)
     coef = jnp.where(present, weight_at(inward + row % 8 + 1, scale), 0.0)
     c_high, c_low = split2(coef)
     coefs = jnp.concatenate([c_high, c_high, c_low, c_low], axis=0)
-    for x in range(g.cx):
-        rows = slice(x * g.slab, (x + 1) * g.slab)
+    for x in range(count):
+        rows = pl.ds(aligned((start + x) * g.slab, g.slab), g.slab)
         h_high, h_low = split2(jnp.concatenate([low[:, rows], high[:, rows]], axis=0))
         halo = jnp.concatenate([h_high, h_low, h_high, h_low], axis=0)
         total = acc[rows, :]
         for other in others:
             total = total + other[rows, :]
-        out[rows, :] = total + lax.dot_general(halo, coefs, TN, preferred_element_type=F32)
+        total = total + lax.dot_general(halo, coefs, TN, preferred_element_type=F32)
+        out[x * g.slab : (x + 1) * g.slab, :] = total
 
 
 def add_x_faces(g, dom, scale, face_refs, out, count):
@@ -396,11 +397,11 @@
 
 
 def nonlocal_kernel(g, scale, far, acc, projf, energy, blk_hbm, atom_hbm, first, second, *refs):
-    table, blk, atom, lut, sem, spread, *sums = refs[-8:]
-    out = refs[-9]
     if far:
-        out, filtered = refs[-10:-8]
+        filtered, *sums, table, blk, atom, lut, sem, spread, out = refs[-10:]
         y_refs = refs[-10 - len(g.face_rows(1)) : -10]
+    else:
+        out, table, blk, atom, lut, sem, spread, *sums = refs[-9:]
     copies = entry_copies(blk_hbm, atom_hbm, blk, atom, sem)
     dom = lax.axis_index("dom")
     fill_lut(g, dom, lut)
@@ -414,12 +415,11 @@
     for copy in copies:
         copy.wait()
     add_nonlocal(g, projf, blk, atom, lut, spread, sums)
-    add_ends(g, dom, scale, acc, first, second, sums, out)
+    start, count = halves(g, dom)[0] if far else (0, g.cx)
+    add_ends(g, dom, scale, acc, first, second, sums, out, start, count)
     if far:
-        start, count = halves(g, dom)[0]
-        rows = pl.ds(aligned(start * g.slab, g.slab), count * g.slab)
-        add_y_faces(g, dom, scale, y_refs, out.at[rows, :], start, count)
-        filtered[...] = out[rows, :].astype(BF16)
+        add_y_faces(g, dom, scale, y_refs, out, start, count)
+        filtered[...] = out[...].astype(BF16)
 
 
 def middle_kernel(g, acc, projf, blk_hbm, atom_hbm, *refs):
@@ -446,12 +446,17 @@
     return [((1 - side) * RADIUS, RADIUS), (side * RADIUS, RADIUS)]
 
 
-def last_kernel(g, acc, *refs):
+def last_kernel(g, rest, acc, *refs):
     nx = len(g.face_rows(0))
     filtered, work = refs[-2:]
     dom = lax.axis_index("dom")
     start, count = halves(g, dom)[-1]
-    work[...] = acc[pl.ds(aligned(start * g.slab, g.slab), count * g.slab), :]
+    if rest:
+        first, second, *sums = refs[:4]
+        add_ends(g, dom, 2.0, acc, first, second, sums, work, start, count)
+        refs = refs[4:]
+    else:
+        work[...] = acc[pl.ds(aligned(start * g.slab, g.slab), count * g.slab), :]
     add_x_faces(g, dom, 2.0, refs[:nx], work, count)
     add_y_faces(g, dom, 2.0, refs[nx:-2], work, start, count)
     filtered[...] = work[...].astype(BF16)
@@ -577,8 +582,8 @@
         after = []
         tables = []
         if g.butterfly:
-            tables = [part, swap(part, g.plane), swap(part, g.third), swap(part, g.plane, g.third)]
-            after.append(tables[2])
+            tables = [part, swap(part, g.third), swap(part, g.plane), swap(part, g.plane, g.third)]
+            after.append(tables[1])
         faces = call(
             functools.partial(pack_faces_kernel, g, len(after)),
             "faces_" + which,
@@ -594,23 +599,31 @@
             "pack_" + which,
             [ends, ends, table] if g.butterfly else [ends, ends],
             [],
-            [values, energy, *tables],
-            [VMEM] * (2 + len(tables)),
+            [values, energy, *tables, *faces],
+            [VMEM] * (2 + len(tables) + len(faces)),
         )
         first, second = swap(first, 1), reverse(second)
         tables = [*group, swap(group[0], 2)] if g.butterfly else [lax.psum(part, "dom")]
-        far = []
-        if prev and len(halves(g, 0)) == 2:
-            far = [jax.ShapeDtypeStruct((halves(g, 0)[0][1] * g.slab, g.cz), BF16)]
+        far = prev and len(halves(g, 0)) == 2
+        scratch = [pltpu.VMEM(table.shape, F32), *entries, spread]
+        outputs = [field]
+        if far:
+            half = halves(g, 0)[0][1] * g.slab
+            outputs = [jax.ShapeDtypeStruct((half, g.cz), BF16), field, field]
+            scratch.append(pltpu.VMEM((half, g.cz), F32))
             tables += from_y
+        else:
+            scratch += [pltpu.VMEM(field.shape, F32)] * 2
         out = call(
-            functools.partial(nonlocal_kernel, g, scale, len(far) > 0),
+            functools.partial(nonlocal_kernel, g, scale, far),
             "nonlocal_" + which,
-            [field, *far],
-            [pltpu.VMEM(table.shape, F32), *entries, spread] + [pltpu.VMEM(field.shape, F32)] * 2,
+            outputs,
+            scratch,
             [acc, projf, energy, blk, atom, first, second, *tables],
             [VMEM] * 3 + [HBM] * 2 + [VMEM] * (2 + len(tables)),
         )
+        if far:
+            out = [acc, first, second, *out[1:], out[0]]
         return out, from_x + from_y
 
     v, projf, pot, part = call(
@@ -636,7 +649,8 @@
         [acc, projf, blk, atom, *received],
         [VMEM] * 2 + [HBM] * 2 + [VMEM] * len(received),
     )
-    (acc, *far), received = local_and_ends(2.0, "second", u, [v], part)
+    out, received = local_and_ends(2.0, "second", u, [v], part)
+    far = out[5:]
     weights = call(
         functools.partial(panel_kernel, g),
         "panel",
@@ -652,9 +666,9 @@
         if number < len(far):
             filtered = far[number]
         else:
-            inputs = [acc, *received]
+            inputs = [*out[:5], *received]
             filtered = call(
-                functools.partial(last_kernel, g),
+                functools.partial(last_kernel, g, len(far) > 0),
                 "filtered",
                 jax.ShapeDtypeStruct((count * g.slab, g.cz), BF16),
                 [pltpu.VMEM((count * g.slab, g.cz), F32)],

time: 50.7 us -> 50.3 us (level)
  waiting for transfers between devices: 14.4 us -> 12.4 us
  starting transfers between devices: 21.2 us -> 22.6 us
    ppermute x10, waiting for transfers between devices: 7.97 us -> 6.19 us  [swap(): return lax.ppermute(array, 'dom', pairs)]
    ppermute x4, starting transfers between devices: 4.6 us -> 6 us  [shift(): return lax.ppermute(array, 'dom', pairs)]
  transfers between devices with their start and end apart: 18 -> 18, of which waited for: 7 -> 6; matrix products, arithmetic and copies ran while one was open for 1% -> 1% of each run, Pallas kernels for 17% -> 17%
where the time goes in v14:
time: 50.3 us; the launch traced here: 50.1 us
  starting transfers between devices  22.6 us (45%)
  Pallas kernels  14.4 us (29%)
  waiting for transfers between devices  12.4 us (25%)
  local copies, waits for them, and re-layouts  0.61 us (1%)
    pallas_call x14, Pallas kernels, call(): pl.pallas_call(kernel, name=name, out_shape=out_shape, in_specs=specs, ou...  14.4 us
    ppermute x10, starting transfers between devices, swap(): return lax.ppermute(array, 'dom', pairs)  11.2 us
    ppermute x10, waiting for transfers between devices, swap(): return lax.ppermute(array, 'dom', pairs)  6.19 us
    ppermute x2, waiting for transfers between devices, shards(): lax.ppermute(filtered, 'band', [(0, 1), (1, 0)])  6.18 us
    ppermute x4, starting transfers between devices, shift(): return lax.ppermute(array, 'dom', pairs)  6 us
    ppermute x2, starting transfers between devices, reverse(): return lax.ppermute(array, 'dom', pairs)  3.26 us
    ppermute x2, starting transfers between devices, shards(): lax.ppermute(filtered, 'band', [(0, 1), (1, 0)])  2.16 us
  transfers between devices with their start and end apart: 18, of which 6 were waited for; matrix products, arithmetic and copies ran while one was open for 1% of the time, Pallas kernels for 17%

profile of v14, /device:TPU:0, one launch (start us, length us, event | category | flops | bytes accessed | tf_op | source)
XLA Modules:
  0.0 50.1 jit_solution(1072366759708824202)
XLA Ops:
  0.0 2.9 %tables_first.1 = (f32[1536,128]{1,0:T(8,128)S(1)}, f32[256,4,128]{2,1,0:T(4,128)S(1)}, f32[192,128]{1,0:T(8,128)S(1)}, f32[16,128]{1,0:T(8,128)S(1)}) custom-call(f32[1536,128]{1,0:T(8,128)} %bitcast.7, bf16[256,4,128]{2,1,0:T(4,128)(2,1)} %proj_hbm.1, f32[192,128]{1,0:T(8,128)} %bitcast.8, s32[256]{0:T(256)} %blk_hbm.7, s32[256]{0:T(256)} %atom_hbm.7), custom_call_target="tpu_custom_call" | custom-call | flops 1000 | bytes 1000 | tf_op jit(solution)/shard_map/tables_first/pallas_call | solution.py:504
  2.9 3.1 %collective-permute-start = (f32[16,128]{1,0:T(8,128)S(1)}, f32[16,128]{1,0:T(8,128)S(1)}, u32[]{:S(2)}, u32[]{:S(2)}) collective-permute-start(f32[16,128]{1,0:T(8,128)S(1)} %get-tuple-element.27.refs_0_), channel_id=1, source_target_pairs={{0,8},{2,10},{4,12},{6,14},{8,0},{10,2},{12,4},{14,6},{16,24},{18,... | collective-permute-start | bytes 24584 | tf_op jit(solution)/shard_map/ppermute | solution.py:564
  6.0 2.6 %collective-permute-start.1 = (f32[16,128]{1,0:T(8,128)S(1)}, f32[16,128]{1,0:T(8,128)S(1)}, u32[]{:S(2)}, u32[]{:S(2)}) collective-permute-start(f32[16,128]{1,0:T(8,128)S(1)} %get-tuple-element.27.refs_0_), channel_id=1, source_target_pairs={{0,16},{2,18},{4,20},{6,22},{8,24},{10,26},{12,28},{14,30},{16,0},... | collective-permute-start | bytes 24584 | tf_op jit(solution)/shard_map/ppermute | solution.py:564
  8.9 2.0 %collective-permute-start.6 = (bf16[768,128]{1,0:T(8,128)(2,1)S(1)}, bf16[768,128]{1,0:T(8,128)(2,1)S(1)}, u32[]{:S(2)}, u32[]{:S(2)}) collective-permute-start(bf16[768,128]{1,0:T(8,128)(2,1)S(1)} %get-tuple-element.28.refs_4_), channel_id=1, source_target_pairs={{0,16},{2,18},{4,20},{6,22},{8,24},{10,26},{12,28},{14,30},{16,0},... | collective-permute-start | bytes 589832 | tf_op jit(solution)/shard_map/ppermute | solution.py:522
  10.9 2.5 %collective-permute-start.7 = (bf16[576,128]{1,0:T(8,128)(2,1)S(1)}, bf16[576,128]{1,0:T(8,128)(2,1)S(1)}, u32[]{:S(2)}, u32[]{:S(2)}) collective-permute-start(bf16[576,128]{1,0:T(8,128)(2,1)S(1)} %get-tuple-element.29.refs_5_), channel_id=1, source_target_pairs={{0,8},{2,10},{4,12},{6,14},{8,0},{10,2},{12,4},{14,6},{16,24},{18,... | collective-permute-start | bytes 442376 | tf_op jit(solution)/shard_map/ppermute | solution.py:522
  13.4 0.7 %collective-permute-done.2.refs_3_ = f32[16,128]{1,0:T(8,128)S(1)} collective-permute-done((f32[16,128]{1,0:T(8,128)S(1)}, f32[16,128]{1,0:T(8,128)S(1)}, u32[]{:S(2)}, u32[]{:S(2)}) %collective-permute-start.2) | collective-permute-done | bytes 8224 | tf_op jit(solution)/shard_map/ppermute | solution.py:564
  14.5 1.6 %collective-permute-start.4 = (f32[8,1536]{1,0:T(8,128)S(1)}, f32[8,1536]{1,0:T(8,128)S(1)}, u32[]{:S(2)}, u32[]{:S(2)}) collective-permute-start(f32[8,1536]{1,0:T(8,128)S(1)} %get-tuple-element.31), channel_id=1, source_target_pairs={{0,6},{2,4},{4,2},{6,0},{8,14},{10,12},{12,10},{14,8},{16,22},{18,... | collective-permute-start | bytes 147464 | tf_op jit(solution)/shard_map/ppermute | solution.py:568
  16.6 0.9 %inside_first.1.acc = f32[1536,128]{1,0:T(8,128)S(1)} custom-call(f32[1536,128]{1,0:T(8,128)S(1)} %get-tuple-element.24.v_ref.refs_0_, f32[192,128]{1,0:T(8,128)S(1)} %get-tuple-element.25.pot), custom_call_target="tpu_custom_call" | custom-call | flops 1000 | bytes 1000 | tf_op jit(solution)/shard_map/inside_first/pallas_call | solution.py:504
  17.6 2.2 %collective-permute-done.5.refs_1_ = f32[16,128]{1,0:T(8,128)S(1)} collective-permute-done((f32[16,128]{1,0:T(8,128)S(1)}, f32[16,128]{1,0:T(8,128)S(1)}, u32[]{:S(2)}, u32[]{:S(2)}) %collective-permute-start.5) | collective-permute-done | bytes 8224 | tf_op jit(solution)/shard_map/ppermute | solution.py:564
  19.8 1.9 %nonlocal_first.1.acc = f32[1536,128]{1,0:T(8,128)S(1)} custom-call(f32[1536,128]{1,0:T(8,128)S(1)} %inside_first.1.acc, f32[256,4,128]{2,1,0:T(4,128)S(1)} %get-tuple-element.26.projf, f32[16,128]{1,0:T(8,128)S(1)} %copy.12.energy, s32[256]{0:T(256)} %blk_hbm.7, s32[256]{0:T(256)} %atom_hbm.7, f32[8,1536]{1,0:T(8,128)S(1)} %collective-permute-done.3.first, ...), custom_call_target="tpu_custom_call" | custom-call | flops 1000 | bytes 1000 | tf_op jit(solution)/shard_map/nonlocal_first/pallas_call | solution.py:504
  21.7 1.9 %tables_second.1 = (f32[1536,128]{1,0:T(8,128)S(1)}, f32[16,128]{1,0:T(8,128)S(1)}) custom-call(f32[1536,128]{1,0:T(8,128)S(1)} %nonlocal_first.1.acc, f32[256,4,128]{2,1,0:T(4,128)S(1)} %get-tuple-element.26.projf, s32[256]{0:T(256)} %blk_hbm.7, s32[256]{0:T(256)} %atom_hbm.7, bf16[768,128]{1,0:T(8,128)(2,1)S(1)} %collective-permute-done.6.refs_0_, ...), custom_call_target="tpu_custom_call" | custom-call | flops 1000 | bytes 1000 | tf_op jit(solution)/shard_map/tables_second/pallas_call | solution.py:504
  23.9 1.5 %collective-permute-start.9 = (f32[16,128]{1,0:T(8,128)S(1)}, f32[16,128]{1,0:T(8,128)S(1)}, u32[]{:S(2)}, u32[]{:S(2)}) collective-permute-start(f32[16,128]{1,0:T(8,128)S(1)} %get-tuple-element.34.refs_0_), channel_id=1, source_target_pairs={{0,16},{2,18},{4,20},{6,22},{8,24},{10,26},{12,28},{14,30},{16,0},... | collective-permute-start | bytes 24584 | tf_op jit(solution)/shard_map/ppermute | solution.py:564
  25.4 2.9 %collective-permute-start.10 = (f32[16,128]{1,0:T(8,128)S(1)}, f32[16,128]{1,0:T(8,128)S(1)}, u32[]{:S(2)}, u32[]{:S(2)}) collective-permute-start(f32[16,128]{1,0:T(8,128)S(1)} %get-tuple-element.34.refs_0_), channel_id=1, source_target_pairs={{0,24},{2,26},{4,28},{6,30},{8,16},{10,18},{12,20},{14,22},{16,8},... | collective-permute-start | bytes 24584 | tf_op jit(solution)/shard_map/ppermute | solution.py:564
  28.4 1.5 %collective-permute-start.15 = (bf16[768,128]{1,0:T(8,128)(2,1)S(1)}, bf16[768,128]{1,0:T(8,128)(2,1)S(1)}, u32[]{:S(2)}, u32[]{:S(2)}) collective-permute-start(bf16[768,128]{1,0:T(8,128)(2,1)S(1)} %get-tuple-element.35.refs_4_), channel_id=1, source_target_pairs={{0,16},{2,18},{4,20},{6,22},{8,24},{10,26},{12,28},{14,30},{16,0},... | collective-permute-start | bytes 589832 | tf_op jit(solution)/shard_map/ppermute | solution.py:522
  30.0 1.1 %collective-permute-done.10.refs_3_ = f32[16,128]{1,0:T(8,128)S(1)} collective-permute-done((f32[16,128]{1,0:T(8,128)S(1)}, f32[16,128]{1,0:T(8,128)S(1)}, u32[]{:S(2)}, u32[]{:S(2)}) %collective-permute-start.10) | collective-permute-done | bytes 8224 | tf_op jit(solution)/shard_map/ppermute | solution.py:564
  31.4 1.6 %collective-permute-start.12 = (f32[8,1536]{1,0:T(8,128)S(1)}, f32[8,1536]{1,0:T(8,128)S(1)}, u32[]{:S(2)}, u32[]{:S(2)}) collective-permute-start(f32[8,1536]{1,0:T(8,128)S(1)} %get-tuple-element.38), channel_id=1, source_target_pairs={{0,6},{2,4},{4,2},{6,0},{8,14},{10,12},{12,10},{14,8},{16,22},{18,... | collective-permute-start | bytes 147464 | tf_op jit(solution)/shard_map/ppermute | solution.py:568
  33.5 1.0 %inside_second.1.acc = f32[1536,128]{1,0:T(8,128)S(1)} custom-call(f32[1536,128]{1,0:T(8,128)S(1)} %get-tuple-element.33.v_ref, f32[192,128]{1,0:T(8,128)S(1)} %get-tuple-element.25.pot, f32[1536,128]{1,0:T(8,128)S(1)} %get-tuple-element.24.v_ref.refs_0_), custom_call_target="tpu_custom_call" | custom-call | flops 1000 | bytes 1000 | tf_op jit(solution)/shard_map/inside_second/pallas_call | solution.py:504
  34.5 2.2 %collective-permute-done.13.refs_1_ = f32[16,128]{1,0:T(8,128)S(1)} collective-permute-done((f32[16,128]{1,0:T(8,128)S(1)}, f32[16,128]{1,0:T(8,128)S(1)}, u32[]{:S(2)}, u32[]{:S(2)}) %collective-permute-start.13) | collective-permute-done | bytes 8224 | tf_op jit(solution)/shard_map/ppermute | solution.py:564
  36.7 2.2 %nonlocal_second.1 = (bf16[768,128]{1,0:T(8,128)(2,1)S(1)}, f32[1536,128]{1,0:T(8,128)S(1)}, f32[1536,128]{1,0:T(8,128)S(1)}) custom-call(f32[1536,128]{1,0:T(8,128)S(1)} %inside_second.1.acc, f32[256,4,128]{2,1,0:T(4,128)S(1)} %get-tuple-element.26.projf, f32[16,128]{1,0:T(8,128)S(1)} %copy.15.energy, s32[256]{0:T(256)} %blk_hbm.7, s32[256]{0:T(256)} %atom_hbm.7, ...), custom_call_target="tpu_custom_call" | custom-call | flops 1000 | bytes 1000 | tf_op jit(solution)/shard_map/nonlocal_second/pallas_call | solution.py:504
  38.9 1.6 %collective-permute-start.17 = (bf16[768,128]{1,0:T(8,128)(2,1)S(1)}, bf16[768,128]{1,0:T(8,128)(2,1)S(1)}, u32[]{:S(2)}, u32[]{:S(2)}) collective-permute-start(bf16[768,128]{1,0:T(8,128)(2,1)S(1)} %get-tuple-element.42.own), channel_id=1, source_target_pairs={{0,1},{1,0},{2,3},{3,2},{4,5},{5,4},{6,7},{7,6},{8,9},{9,8},{10,11... | collective-permute-start | bytes 589832 | tf_op jit(solution)/shard_map/ppermute | solution.py:678
  42.0 4.8 %collective-permute-done.17.other = bf16[768,128]{1,0:T(8,128)(2,1)S(1)} collective-permute-done((bf16[768,128]{1,0:T(8,128)(2,1)S(1)}, bf16[768,128]{1,0:T(8,128)(2,1)S(1)}, u32[]{:S(2)}, u32[]{:S(2)}) %collective-permute-start.17) | collective-permute-done | bytes 196640 | tf_op jit(solution)/shard_map/ppermute | solution.py:678
  46.8 1.0 %rotate_0.1.refs_0_ = f32[8,192,128]{2,1,0:T(8,128)} custom-call(bf16[768,128]{1,0:T(8,128)(2,1)S(1)} %get-tuple-element.42.own, bf16[768,128]{1,0:T(8,128)(2,1)S(1)} %collective-permute-done.17.other, bf16[128,256]{1,0:T(8,128)(2,1)S(1)} %panel.2.weights), custom_call_target="tpu_custom_call" | custom-call | flops 1000 | bytes 1000 | tf_op jit(solution)/shard_map/rotate_0/pallas_call | solution.py:504
  47.7 1.4 %collective-permute-done.16.other = bf16[768,128]{1,0:T(8,128)(2,1)S(1)} collective-permute-done((bf16[768,128]{1,0:T(8,128)(2,1)S(1)}, bf16[768,128]{1,0:T(8,128)(2,1)S(1)}, u32[]{:S(2)}, u32[]{:S(2)}) %collective-permute-start.16) | collective-permute-done | bytes 196640 | tf_op jit(solution)/shard_map/ppermute | solution.py:678
  49.2 1.0 %rotate_1.1 = f32[8,192,128]{2,1,0:T(8,128)} custom-call(bf16[768,128]{1,0:T(8,128)(2,1)S(1)} %filtered.1.own, bf16[768,128]{1,0:T(8,128)(2,1)S(1)} %collective-permute-done.16.other, bf16[128,256]{1,0:T(8,128)(2,1)S(1)} %panel.2.weights, f32[8,192,128]{2,1,0:T(8,128)} %rotate_0.1.refs_0_), custom_call_target="tpu_custom_call", output_to_operand_aliasing={{}: (3, {})} | custom-call | flops 1000 | bytes 1000 | tf_op jit(solution)/shard_map/rotate_1/pallas_call | solution.py:504
  (41 shorter events, 4.1 us)
Async XLA Ops:
  0.0 8.6 %copy-start.1 = (f32[64,4]{0,1:T(4,128)S(1)}, f32[64,4]{0,1:T(4,128)}, u32[]{:S(2)}) copy-start(f32[64,4]{0,1:T(4,128)} %param.12) | copy-start | bytes 3076
  2.9 5.9 %collective-permute-start = (f32[16,128]{1,0:T(8,128)S(1)}, f32[16,128]{1,0:T(8,128)S(1)}, u32[]{:S(2)}, u32[]{:S(2)}) collective-permute-start(f32[16,128]{1,0:T(8,128)S(1)} %get-tuple-element.27.refs_0_), channel_id=1, source_target_pairs={{0,8},{2,10},{4,12},{6,14},{8,0},{10,2},{12,4},{14,6},{16,24},{18,... | collective-permute-start | bytes 24584 | tf_op jit(solution)/shard_map/ppermute | solution.py:564
  6.0 7.4 %collective-permute-start.1 = (f32[16,128]{1,0:T(8,128)S(1)}, f32[16,128]{1,0:T(8,128)S(1)}, u32[]{:S(2)}, u32[]{:S(2)}) collective-permute-start(f32[16,128]{1,0:T(8,128)S(1)} %get-tuple-element.27.refs_0_), channel_id=1, source_target_pairs={{0,16},{2,18},{4,20},{6,22},{8,24},{10,26},{12,28},{14,30},{16,0},... | collective-permute-start | bytes 24584 | tf_op jit(solution)/shard_map/ppermute | solution.py:564
  8.6 5.6 %collective-permute-start.2 = (f32[16,128]{1,0:T(8,128)S(1)}, f32[16,128]{1,0:T(8,128)S(1)}, u32[]{:S(2)}, u32[]{:S(2)}) collective-permute-start(f32[16,128]{1,0:T(8,128)S(1)} %get-tuple-element.27.refs_0_), channel_id=1, source_target_pairs={{0,24},{2,26},{4,28},{6,30},{8,16},{10,18},{12,20},{14,22},{16,8},... | collective-permute-start | bytes 24584 | tf_op jit(solution)/shard_map/ppermute | solution.py:564
  8.9 12.8 %collective-permute-start.6 = (bf16[768,128]{1,0:T(8,128)(2,1)S(1)}, bf16[768,128]{1,0:T(8,128)(2,1)S(1)}, u32[]{:S(2)}, u32[]{:S(2)}) collective-permute-start(bf16[768,128]{1,0:T(8,128)(2,1)S(1)} %get-tuple-element.28.refs_4_), channel_id=1, source_target_pairs={{0,16},{2,18},{4,20},{6,22},{8,24},{10,26},{12,28},{14,30},{16,0},... | collective-permute-start | bytes 589832 | tf_op jit(solution)/shard_map/ppermute | solution.py:522
  10.9 10.9 %collective-permute-start.7 = (bf16[576,128]{1,0:T(8,128)(2,1)S(1)}, bf16[576,128]{1,0:T(8,128)(2,1)S(1)}, u32[]{:S(2)}, u32[]{:S(2)}) collective-permute-start(bf16[576,128]{1,0:T(8,128)(2,1)S(1)} %get-tuple-element.29.refs_5_), channel_id=1, source_target_pairs={{0,8},{2,10},{4,12},{6,14},{8,0},{10,2},{12,4},{14,6},{16,24},{18,... | collective-permute-start | bytes 442376 | tf_op jit(solution)/shard_map/ppermute | solution.py:522
  14.5 5.3 %collective-permute-start.3 = (f32[8,1536]{1,0:T(8,128)S(1)}, f32[8,1536]{1,0:T(8,128)S(1)}, u32[]{:S(2)}, u32[]{:S(2)}) collective-permute-start(f32[8,1536]{1,0:T(8,128)S(1)} %get-tuple-element.30), channel_id=1, source_target_pairs={{0,2},{2,0},{4,6},{6,4},{8,10},{10,8},{12,14},{14,12},{16,18},{18,... | collective-permute-start | bytes 147464 | tf_op jit(solution)/shard_map/ppermute | solution.py:564
  14.5 5.3 %collective-permute-start.4 = (f32[8,1536]{1,0:T(8,128)S(1)}, f32[8,1536]{1,0:T(8,128)S(1)}, u32[]{:S(2)}, u32[]{:S(2)}) collective-permute-start(f32[8,1536]{1,0:T(8,128)S(1)} %get-tuple-element.31), channel_id=1, source_target_pairs={{0,6},{2,4},{4,2},{6,0},{8,14},{10,12},{12,10},{14,8},{16,22},{18,... | collective-permute-start | bytes 147464 | tf_op jit(solution)/shard_map/ppermute | solution.py:568
  16.1 3.7 %collective-permute-start.5 = (f32[16,128]{1,0:T(8,128)S(1)}, f32[16,128]{1,0:T(8,128)S(1)}, u32[]{:S(2)}, u32[]{:S(2)}) collective-permute-start(f32[16,128]{1,0:T(8,128)S(1)} %get-tuple-element.32.refs_0_), channel_id=1, source_target_pairs={{0,4},{2,6},{4,0},{6,2},{8,12},{10,14},{12,8},{14,10},{16,20},{18,... | collective-permute-start | bytes 24584 | tf_op jit(solution)/shard_map/ppermute | solution.py:564
  23.6 4.7 %collective-permute-start.8 = (f32[16,128]{1,0:T(8,128)S(1)}, f32[16,128]{1,0:T(8,128)S(1)}, u32[]{:S(2)}, u32[]{:S(2)}) collective-permute-start(f32[16,128]{1,0:T(8,128)S(1)} %get-tuple-element.34.refs_0_), channel_id=1, source_target_pairs={{0,8},{2,10},{4,12},{6,14},{8,0},{10,2},{12,4},{14,6},{16,24},{18,... | collective-permute-start | bytes 24584 | tf_op jit(solution)/shard_map/ppermute | solution.py:564
  23.9 6.1 %collective-permute-start.9 = (f32[16,128]{1,0:T(8,128)S(1)}, f32[16,128]{1,0:T(8,128)S(1)}, u32[]{:S(2)}, u32[]{:S(2)}) collective-permute-start(f32[16,128]{1,0:T(8,128)S(1)} %get-tuple-element.34.refs_0_), channel_id=1, source_target_pairs={{0,16},{2,18},{4,20},{6,22},{8,24},{10,26},{12,28},{14,30},{16,0},... | collective-permute-start | bytes 24584 | tf_op jit(solution)/shard_map/ppermute | solution.py:564
  25.4 5.7 %collective-permute-start.10 = (f32[16,128]{1,0:T(8,128)S(1)}, f32[16,128]{1,0:T(8,128)S(1)}, u32[]{:S(2)}, u32[]{:S(2)}) collective-permute-start(f32[16,128]{1,0:T(8,128)S(1)} %get-tuple-element.34.refs_0_), channel_id=1, source_target_pairs={{0,24},{2,26},{4,28},{6,30},{8,16},{10,18},{12,20},{14,22},{16,8},... | collective-permute-start | bytes 24584 | tf_op jit(solution)/shard_map/ppermute | solution.py:564
  28.4 8.3 %collective-permute-start.14 = (bf16[576,128]{1,0:T(8,128)(2,1)S(1)}, bf16[576,128]{1,0:T(8,128)(2,1)S(1)}, u32[]{:S(2)}, u32[]{:S(2)}) collective-permute-start(bf16[576,128]{1,0:T(8,128)(2,1)S(1)} %get-tuple-element.36.refs_5_), channel_id=1, source_target_pairs={{0,8},{2,10},{4,12},{6,14},{8,0},{10,2},{12,4},{14,6},{16,24},{18,... | collective-permute-start | bytes 442376 | tf_op jit(solution)/shard_map/ppermute | solution.py:522
  28.4 12.0 %collective-permute-start.15 = (bf16[768,128]{1,0:T(8,128)(2,1)S(1)}, bf16[768,128]{1,0:T(8,128)(2,1)S(1)}, u32[]{:S(2)}, u32[]{:S(2)}) collective-permute-start(bf16[768,128]{1,0:T(8,128)(2,1)S(1)} %get-tuple-element.35.refs_4_), channel_id=1, source_target_pairs={{0,16},{2,18},{4,20},{6,22},{8,24},{10,26},{12,28},{14,30},{16,0},... | collective-permute-start | bytes 589832 | tf_op jit(solution)/shard_map/ppermute | solution.py:522
  31.4 5.3 %collective-permute-start.11 = (f32[8,1536]{1,0:T(8,128)S(1)}, f32[8,1536]{1,0:T(8,128)S(1)}, u32[]{:S(2)}, u32[]{:S(2)}) collective-permute-start(f32[8,1536]{1,0:T(8,128)S(1)} %get-tuple-element.37), channel_id=1, source_target_pairs={{0,2},{2,0},{4,6},{6,4},{8,10},{10,8},{12,14},{14,12},{16,18},{18,... | collective-permute-start | bytes 147464 | tf_op jit(solution)/shard_map/ppermute | solution.py:564
  31.4 5.3 %collective-permute-start.12 = (f32[8,1536]{1,0:T(8,128)S(1)}, f32[8,1536]{1,0:T(8,128)S(1)}, u32[]{:S(2)}, u32[]{:S(2)}) collective-permute-start(f32[8,1536]{1,0:T(8,128)S(1)} %get-tuple-element.38), channel_id=1, source_target_pairs={{0,6},{2,4},{4,2},{6,0},{8,14},{10,12},{12,10},{14,8},{16,22},{18,... | collective-permute-start | bytes 147464 | tf_op jit(solution)/shard_map/ppermute | solution.py:568
  33.0 3.7 %collective-permute-start.13 = (f32[16,128]{1,0:T(8,128)S(1)}, f32[16,128]{1,0:T(8,128)S(1)}, u32[]{:S(2)}, u32[]{:S(2)}) collective-permute-start(f32[16,128]{1,0:T(8,128)S(1)} %get-tuple-element.39.refs_0_), channel_id=1, source_target_pairs={{0,4},{2,6},{4,0},{6,2},{8,12},{10,14},{12,8},{14,10},{16,20},{18,... | collective-permute-start | bytes 24584 | tf_op jit(solution)/shard_map/ppermute | solution.py:564
  38.9 7.9 %collective-permute-start.17 = (bf16[768,128]{1,0:T(8,128)(2,1)S(1)}, bf16[768,128]{1,0:T(8,128)(2,1)S(1)}, u32[]{:S(2)}, u32[]{:S(2)}) collective-permute-start(bf16[768,128]{1,0:T(8,128)(2,1)S(1)} %get-tuple-element.42.own), channel_id=1, source_target_pairs={{0,1},{1,0},{2,3},{3,2},{4,5},{5,4},{6,7},{7,6},{8,9},{9,8},{10,11... | collective-permute-start | bytes 589832 | tf_op jit(solution)/shard_map/ppermute | solution.py:678
  40.4 1.3 %copy-start = (bf16[16,16]{1,0:T(8,128)(2,1)S(1)}, bf16[16,16]{1,0:T(8,128)(2,1)}, u32[]{:S(2)}) copy-start(bf16[16,16]{1,0:T(8,128)(2,1)} %panel.3) | copy-start | bytes 1540
  41.1 8.0 %collective-permute-start.16 = (bf16[768,128]{1,0:T(8,128)(2,1)S(1)}, bf16[768,128]{1,0:T(8,128)(2,1)S(1)}, u32[]{:S(2)}, u32[]{:S(2)}) collective-permute-start(bf16[768,128]{1,0:T(8,128)(2,1)S(1)} %filtered.1.own), channel_id=1, source_target_pairs={{0,1},{1,0},{2,3},{3,2},{4,5},{5,4},{6,7},{7,6},{8,9},{9,8},{10,11... | collective-permute-start | bytes 589832 | tf_op jit(solution)/shard_map/ppermute | solution.py:678

commit v15 on v14

--- a/solution.py
+++ b/solution.py
@@ -250,17 +250,17 @@
     inner_tables(g, dom, v_ref, projf, blk, atom, lut, sums, table)
 
 
-def pack_kernel(g, v_ref, energy, *refs):
-    if g.butterfly:
-        part, from_x, from_y, from_xy = refs[:4]
-        group = refs[-1]
-        group[...] = (part[...] + from_x[...]) + (from_y[...] + from_xy[...])
-        refs = refs[:-1]
-    first, second = refs[-2:]
-    pack_ends(g, lax.axis_index("dom"), v_ref, first, second)
-    if g.butterfly:
-        put_table(g, first, group)
-        put_table(g, second, group)
+def pack_kernel(g, count, *refs):
+    source, refs = refs[:count], refs[count:]
+    part, from_x, from_y, from_xy = refs[:4]
+    outs, group = refs[-3:-1], refs[-1]
+    group[...] = (part[...] + from_x[...]) + (from_y[...] + from_xy[...])
+    if len(source) == 1:
+        pack_ends(g, lax.axis_index("dom"), *source, *outs)
+    for n, out in enumerate(outs):
+        if len(source) == 2:
+            out[...] = source[n][...]
+        put_table(g, out, group)
 
 
 def pack_faces_kernel(g, nafter, v_ref, *refs):
@@ -268,7 +268,10 @@
     dom = lax.axis_index("dom")
     refs = refs[nafter:]
     pack_x(g, dom, v_ref, refs[:nx])
-    pack_y(g, dom, v_ref, refs[nx:])
+    ny = len(g.face_rows(1))
+    pack_y(g, dom, v_ref, refs[nx : nx + ny])
+    if len(refs) > nx + ny:
+        pack_ends(g, dom, v_ref, *refs[nx + ny :])
 
 
 def inside_kernel(g, scale, subtract, v_ref, pot, *refs):
@@ -582,28 +585,37 @@
         after = []
         tables = []
         if g.butterfly:
-            tables = [part, swap(part, g.third), swap(part, g.plane), swap(part, g.plane, g.third)]
+            routes = [(g.third,), (g.plane, g.third), (g.plane,)]
+            if not prev:
+                routes = [(g.third,), (g.plane,), (g.plane, g.third)]
+            tables = [part] + [swap(part, *route) for route in routes]
             after.append(tables[1])
+        packed = [ends, ends] if prev or not g.butterfly else []
         faces = call(
             functools.partial(pack_faces_kernel, g, len(after)),
             "faces_" + which,
-            [*x_faces, *y_faces],
+            [*x_faces, *y_faces, *packed],
             [],
             [values, *after],
             [VMEM] * (1 + len(after)),
         )
+        both = nx + len(y_faces)
         from_x = swap_faces(g, faces[:nx], g.plane, g.first)
-        from_y = swap_faces(g, faces[nx:], g.third, g.second)
-        first, second, *group = call(
-            functools.partial(pack_kernel, g),
-            "pack_" + which,
-            [ends, ends, table] if g.butterfly else [ends, ends],
-            [],
-            [values, energy, *tables, *faces],
-            [VMEM] * (2 + len(tables) + len(faces)),
-        )
+        from_y = swap_faces(g, faces[nx:both], g.third, g.second)
+        source = faces[both:] or [values]
+        if g.butterfly:
+            first, second, group = call(
+                functools.partial(pack_kernel, g, len(source)),
+                "pack_" + which,
+                [ends, ends, table],
+                [],
+                [*source, *tables, energy],
+                [VMEM] * (len(source) + 5),
+            )
+        else:
+            first, second = source
         first, second = swap(first, 1), reverse(second)
-        tables = [*group, swap(group[0], 2)] if g.butterfly else [lax.psum(part, "dom")]
+        tables = [group, swap(group, 2)] if g.butterfly else [lax.psum(part, "dom")]
         far = prev and len(halves(g, 0)) == 2
         scratch = [pltpu.VMEM(table.shape, F32), *entries, spread]
         outputs = [field]

time: 50.3 us -> 48.6 us (0.966)
  waiting for transfers between devices: 12.4 us -> 10.5 us
    ppermute x2, waiting for transfers between devices: 6.18 us -> 4.9 us  [shards(): lax.ppermute(filtered, 'band', [(0, 1), (1, 0)])]
    ppermute x2, starting transfers between devices: 2.16 us -> 3.11 us  [shards(): lax.ppermute(filtered, 'band', [(0, 1), (1, 0)])]
    ppermute x10, waiting for transfers between devices: 6.19 us -> 5.3 us  [swap(): return lax.ppermute(array, 'dom', pairs)]
    ppermute x10, starting transfers between devices: 11.2 us -> 10.4 us  [swap(): return lax.ppermute(array, 'dom', pairs)]
  transfers between devices with their start and end apart: 18 -> 18, of which waited for: 6 -> 7; matrix products, arithmetic and copies ran while one was open for 1% -> 1% of each run, Pallas kernels for 17% -> 18%
where the time goes in v15:
time: 48.6 us; the launch traced here: 48.4 us
  starting transfers between devices  22.7 us (47%)
  Pallas kernels  14.4 us (30%)
  waiting for transfers between devices  10.5 us (22%)
  local copies, waits for them, and re-layouts  0.61 us (1%)
    pallas_call x14, Pallas kernels, call(): pl.pallas_call(kernel, name=name, out_shape=out_shape, in_specs=specs, ou...  14.4 us
    ppermute x10, starting transfers between devices, swap(): return lax.ppermute(array, 'dom', pairs)  10.4 us
    ppermute x4, starting transfers between devices, shift(): return lax.ppermute(array, 'dom', pairs)  5.95 us
    ppermute x10, waiting for transfers between devices, swap(): return lax.ppermute(array, 'dom', pairs)  5.3 us
    ppermute x2, waiting for transfers between devices, shards(): lax.ppermute(filtered, 'band', [(0, 1), (1, 0)])  4.9 us
    ppermute x2, starting transfers between devices, reverse(): return lax.ppermute(array, 'dom', pairs)  3.19 us
    ppermute x2, starting transfers between devices, shards(): lax.ppermute(filtered, 'band', [(0, 1), (1, 0)])  3.11 us
  transfers between devices with their start and end apart: 18, of which 7 were waited for; matrix products, arithmetic and copies ran while one was open for 1% of the time, Pallas kernels for 18%

profile of v15, /device:TPU:0, one launch (start us, length us, event | category | flops | bytes accessed | tf_op | source)
XLA Modules:
  0.0 48.4 jit_solution(902079233254373208)
XLA Ops:
  0.0 2.9 %tables_first.1 = (f32[1536,128]{1,0:T(8,128)S(1)}, f32[256,4,128]{2,1,0:T(4,128)S(1)}, f32[192,128]{1,0:T(8,128)S(1)}, f32[16,128]{1,0:T(8,128)S(1)}) custom-call(f32[1536,128]{1,0:T(8,128)} %bitcast.7, bf16[256,4,128]{2,1,0:T(4,128)(2,1)} %proj_hbm.1, f32[192,128]{1,0:T(8,128)} %bitcast.8, s32[256]{0:T(256)} %blk_hbm.7, s32[256]{0:T(256)} %atom_hbm.7), custom_call_target="tpu_custom_call" | custom-call | flops 1000 | bytes 1000 | tf_op jit(solution)/shard_map/tables_first/pallas_call | solution.py:507
  2.9 3.1 %collective-permute-start = (f32[16,128]{1,0:T(8,128)S(1)}, f32[16,128]{1,0:T(8,128)S(1)}, u32[]{:S(2)}, u32[]{:S(2)}) collective-permute-start(f32[16,128]{1,0:T(8,128)S(1)} %get-tuple-element.29.refs_1_), channel_id=1, source_target_pairs={{0,8},{2,10},{4,12},{6,14},{8,0},{10,2},{12,4},{14,6},{16,24},{18,... | collective-permute-start | bytes 24584 | tf_op jit(solution)/shard_map/ppermute | solution.py:567
  6.0 2.6 %collective-permute-start.1 = (f32[16,128]{1,0:T(8,128)S(1)}, f32[16,128]{1,0:T(8,128)S(1)}, u32[]{:S(2)}, u32[]{:S(2)}) collective-permute-start(f32[16,128]{1,0:T(8,128)S(1)} %get-tuple-element.29.refs_1_), channel_id=1, source_target_pairs={{0,16},{2,18},{4,20},{6,22},{8,24},{10,26},{12,28},{14,30},{16,0},... | collective-permute-start | bytes 24584 | tf_op jit(solution)/shard_map/ppermute | solution.py:567
  8.9 2.0 %collective-permute-start.6 = (bf16[768,128]{1,0:T(8,128)(2,1)S(1)}, bf16[768,128]{1,0:T(8,128)(2,1)S(1)}, u32[]{:S(2)}, u32[]{:S(2)}) collective-permute-start(bf16[768,128]{1,0:T(8,128)(2,1)S(1)} %get-tuple-element.33), channel_id=1, source_target_pairs={{0,16},{2,18},{4,20},{6,22},{8,24},{10,26},{12,28},{14,30},{16,0},... | collective-permute-start | bytes 589832 | tf_op jit(solution)/shard_map/ppermute | solution.py:525
  10.9 2.5 %collective-permute-start.7 = (bf16[576,128]{1,0:T(8,128)(2,1)S(1)}, bf16[576,128]{1,0:T(8,128)(2,1)S(1)}, u32[]{:S(2)}, u32[]{:S(2)}) collective-permute-start(bf16[576,128]{1,0:T(8,128)(2,1)S(1)} %get-tuple-element.34), channel_id=1, source_target_pairs={{0,8},{2,10},{4,12},{6,14},{8,0},{10,2},{12,4},{14,6},{16,24},{18,... | collective-permute-start | bytes 442376 | tf_op jit(solution)/shard_map/ppermute | solution.py:525
  13.4 0.7 %collective-permute-done.2.refs_4_ = f32[16,128]{1,0:T(8,128)S(1)} collective-permute-done((f32[16,128]{1,0:T(8,128)S(1)}, f32[16,128]{1,0:T(8,128)S(1)}, u32[]{:S(2)}, u32[]{:S(2)}) %collective-permute-start.2) | collective-permute-done | bytes 8224 | tf_op jit(solution)/shard_map/ppermute | solution.py:567
  14.5 1.6 %collective-permute-start.4 = (f32[8,1536]{1,0:T(8,128)S(1)}, f32[8,1536]{1,0:T(8,128)S(1)}, u32[]{:S(2)}, u32[]{:S(2)}) collective-permute-start(f32[8,1536]{1,0:T(8,128)S(1)} %get-tuple-element.31), channel_id=1, source_target_pairs={{0,6},{2,4},{4,2},{6,0},{8,14},{10,12},{12,10},{14,8},{16,22},{18,... | collective-permute-start | bytes 147464 | tf_op jit(solution)/shard_map/ppermute | solution.py:571
  16.6 0.9 %inside_first.1.acc = f32[1536,128]{1,0:T(8,128)S(1)} custom-call(f32[1536,128]{1,0:T(8,128)S(1)} %get-tuple-element.26.v_ref.refs_0_, f32[192,128]{1,0:T(8,128)S(1)} %get-tuple-element.27.pot), custom_call_target="tpu_custom_call" | custom-call | flops 1000 | bytes 1000 | tf_op jit(solution)/shard_map/inside_first/pallas_call | solution.py:507
  17.6 2.2 %collective-permute-done.5.refs_1_ = f32[16,128]{1,0:T(8,128)S(1)} collective-permute-done((f32[16,128]{1,0:T(8,128)S(1)}, f32[16,128]{1,0:T(8,128)S(1)}, u32[]{:S(2)}, u32[]{:S(2)}) %collective-permute-start.5) | collective-permute-done | bytes 8224 | tf_op jit(solution)/shard_map/ppermute | solution.py:567
  19.8 1.9 %nonlocal_first.1.acc = f32[1536,128]{1,0:T(8,128)S(1)} custom-call(f32[1536,128]{1,0:T(8,128)S(1)} %inside_first.1.acc, f32[256,4,128]{2,1,0:T(4,128)S(1)} %get-tuple-element.28.projf, f32[16,128]{1,0:T(8,128)S(1)} %copy.12.refs_5_.energy, s32[256]{0:T(256)} %blk_hbm.7, s32[256]{0:T(256)} %atom_hbm.7, f32[8,1536]{1,0:T(8,128)S(1)} %collective-permute-done.3.first, ...), custom_call_target="tpu_custom_call" | custom-call | flops 1000 | bytes 1000 | tf_op jit(solution)/shard_map/nonlocal_first/pallas_call | solution.py:507
  21.7 1.9 %tables_second.1 = (f32[1536,128]{1,0:T(8,128)S(1)}, f32[16,128]{1,0:T(8,128)S(1)}) custom-call(f32[1536,128]{1,0:T(8,128)S(1)} %nonlocal_first.1.acc, f32[256,4,128]{2,1,0:T(4,128)S(1)} %get-tuple-element.28.projf, s32[256]{0:T(256)} %blk_hbm.7, s32[256]{0:T(256)} %atom_hbm.7, bf16[768,128]{1,0:T(8,128)(2,1)S(1)} %collective-permute-done.6.refs_0_, ...), custom_call_target="tpu_custom_call" | custom-call | flops 1000 | bytes 1000 | tf_op jit(solution)/shard_map/tables_second/pallas_call | solution.py:507
  23.9 0.9 %collective-permute-start.9 = (f32[16,128]{1,0:T(8,128)S(1)}, f32[16,128]{1,0:T(8,128)S(1)}, u32[]{:S(2)}, u32[]{:S(2)}) collective-permute-start(f32[16,128]{1,0:T(8,128)S(1)} %get-tuple-element.36.refs_2_), channel_id=1, source_target_pairs={{0,24},{2,26},{4,28},{6,30},{8,16},{10,18},{12,20},{14,22},{16,8},... | collective-permute-start | bytes 24584 | tf_op jit(solution)/shard_map/ppermute | solution.py:567
  24.9 2.6 %collective-permute-start.10 = (f32[16,128]{1,0:T(8,128)S(1)}, f32[16,128]{1,0:T(8,128)S(1)}, u32[]{:S(2)}, u32[]{:S(2)}) collective-permute-start(f32[16,128]{1,0:T(8,128)S(1)} %get-tuple-element.36.refs_2_), channel_id=1, source_target_pairs={{0,16},{2,18},{4,20},{6,22},{8,24},{10,26},{12,28},{14,30},{16,0},... | collective-permute-start | bytes 24584 | tf_op jit(solution)/shard_map/ppermute | solution.py:567
  27.8 0.9 %collective-permute-start.14 = (bf16[576,128]{1,0:T(8,128)(2,1)S(1)}, bf16[576,128]{1,0:T(8,128)(2,1)S(1)}, u32[]{:S(2)}, u32[]{:S(2)}) collective-permute-start(bf16[576,128]{1,0:T(8,128)(2,1)S(1)} %get-tuple-element.42), channel_id=1, source_target_pairs={{0,8},{2,10},{4,12},{6,14},{8,0},{10,2},{12,4},{14,6},{16,24},{18,... | collective-permute-start | bytes 442376 | tf_op jit(solution)/shard_map/ppermute | solution.py:525
  29.7 1.6 %collective-permute-start.12 = (f32[8,1536]{1,0:T(8,128)S(1)}, f32[8,1536]{1,0:T(8,128)S(1)}, u32[]{:S(2)}, u32[]{:S(2)}) collective-permute-start(f32[8,1536]{1,0:T(8,128)S(1)} %get-tuple-element.40), channel_id=1, source_target_pairs={{0,6},{2,4},{4,2},{6,0},{8,14},{10,12},{12,10},{14,8},{16,22},{18,... | collective-permute-start | bytes 147464 | tf_op jit(solution)/shard_map/ppermute | solution.py:571
  31.8 1.0 %inside_second.1.acc = f32[1536,128]{1,0:T(8,128)S(1)} custom-call(f32[1536,128]{1,0:T(8,128)S(1)} %get-tuple-element.35.v_ref, f32[192,128]{1,0:T(8,128)S(1)} %get-tuple-element.27.pot, f32[1536,128]{1,0:T(8,128)S(1)} %get-tuple-element.26.v_ref.refs_0_), custom_call_target="tpu_custom_call" | custom-call | flops 1000 | bytes 1000 | tf_op jit(solution)/shard_map/inside_second/pallas_call | solution.py:507
  32.8 2.1 %collective-permute-done.13.refs_1_ = f32[16,128]{1,0:T(8,128)S(1)} collective-permute-done((f32[16,128]{1,0:T(8,128)S(1)}, f32[16,128]{1,0:T(8,128)S(1)}, u32[]{:S(2)}, u32[]{:S(2)}) %collective-permute-start.13) | collective-permute-done | bytes 8224 | tf_op jit(solution)/shard_map/ppermute | solution.py:567
  34.9 2.2 %nonlocal_second.1 = (bf16[768,128]{1,0:T(8,128)(2,1)S(1)}, f32[1536,128]{1,0:T(8,128)S(1)}, f32[1536,128]{1,0:T(8,128)S(1)}) custom-call(f32[1536,128]{1,0:T(8,128)S(1)} %inside_second.1.acc, f32[256,4,128]{2,1,0:T(4,128)S(1)} %get-tuple-element.28.projf, f32[16,128]{1,0:T(8,128)S(1)} %copy.15.refs_6_.energy, s32[256]{0:T(256)} %blk_hbm.7, s32[256]{0:T(256)} %atom_hbm.7, ...), custom_call_target="tpu_custom_call" | custom-call | flops 1000 | bytes 1000 | tf_op jit(solution)/shard_map/nonlocal_second/pallas_call | solution.py:507
  37.1 1.6 %collective-permute-start.17 = (bf16[768,128]{1,0:T(8,128)(2,1)S(1)}, bf16[768,128]{1,0:T(8,128)(2,1)S(1)}, u32[]{:S(2)}, u32[]{:S(2)}) collective-permute-start(bf16[768,128]{1,0:T(8,128)(2,1)S(1)} %get-tuple-element.46.own), channel_id=1, source_target_pairs={{0,1},{1,0},{2,3},{3,2},{4,5},{5,4},{6,7},{7,6},{8,9},{9,8},{10,11... | collective-permute-start | bytes 589832 | tf_op jit(solution)/shard_map/ppermute | solution.py:690
  39.7 1.6 %collective-permute-start.16 = (bf16[768,128]{1,0:T(8,128)(2,1)S(1)}, bf16[768,128]{1,0:T(8,128)(2,1)S(1)}, u32[]{:S(2)}, u32[]{:S(2)}) collective-permute-start(bf16[768,128]{1,0:T(8,128)(2,1)S(1)} %filtered.1.own), channel_id=1, source_target_pairs={{0,1},{1,0},{2,3},{3,2},{4,5},{5,4},{6,7},{7,6},{8,9},{9,8},{10,11... | collective-permute-start | bytes 589832 | tf_op jit(solution)/shard_map/ppermute | solution.py:690
  41.5 3.5 %collective-permute-done.17.other = bf16[768,128]{1,0:T(8,128)(2,1)S(1)} collective-permute-done((bf16[768,128]{1,0:T(8,128)(2,1)S(1)}, bf16[768,128]{1,0:T(8,128)(2,1)S(1)}, u32[]{:S(2)}, u32[]{:S(2)}) %collective-permute-start.17) | collective-permute-done | bytes 196640 | tf_op jit(solution)/shard_map/ppermute | solution.py:690
  45.0 1.0 %rotate_0.1.refs_0_ = f32[8,192,128]{2,1,0:T(8,128)} custom-call(bf16[768,128]{1,0:T(8,128)(2,1)S(1)} %get-tuple-element.46.own, bf16[768,128]{1,0:T(8,128)(2,1)S(1)} %collective-permute-done.17.other, bf16[128,256]{1,0:T(8,128)(2,1)S(1)} %panel.2.weights), custom_call_target="tpu_custom_call" | custom-call | flops 1000 | bytes 1000 | tf_op jit(solution)/shard_map/rotate_0/pallas_call | solution.py:507
  46.0 1.4 %collective-permute-done.16.other = bf16[768,128]{1,0:T(8,128)(2,1)S(1)} collective-permute-done((bf16[768,128]{1,0:T(8,128)(2,1)S(1)}, bf16[768,128]{1,0:T(8,128)(2,1)S(1)}, u32[]{:S(2)}, u32[]{:S(2)}) %collective-permute-start.16) | collective-permute-done | bytes 196640 | tf_op jit(solution)/shard_map/ppermute | solution.py:690
  47.4 1.0 %rotate_1.1 = f32[8,192,128]{2,1,0:T(8,128)} custom-call(bf16[768,128]{1,0:T(8,128)(2,1)S(1)} %filtered.1.own, bf16[768,128]{1,0:T(8,128)(2,1)S(1)} %collective-permute-done.16.other, bf16[128,256]{1,0:T(8,128)(2,1)S(1)} %panel.2.weights, f32[8,192,128]{2,1,0:T(8,128)} %rotate_0.1.refs_0_), custom_call_target="tpu_custom_call", output_to_operand_aliasing={{}: (3, {})} | custom-call | flops 1000 | bytes 1000 | tf_op jit(solution)/shard_map/rotate_1/pallas_call | solution.py:507
  (41 shorter events, 4.8 us)
Async XLA Ops:
  0.0 8.6 %copy-start.1 = (f32[64,4]{0,1:T(4,128)S(1)}, f32[64,4]{0,1:T(4,128)}, u32[]{:S(2)}) copy-start(f32[64,4]{0,1:T(4,128)} %param.12) | copy-start | bytes 3076
  2.9 5.9 %collective-permute-start = (f32[16,128]{1,0:T(8,128)S(1)}, f32[16,128]{1,0:T(8,128)S(1)}, u32[]{:S(2)}, u32[]{:S(2)}) collective-permute-start(f32[16,128]{1,0:T(8,128)S(1)} %get-tuple-element.29.refs_1_), channel_id=1, source_target_pairs={{0,8},{2,10},{4,12},{6,14},{8,0},{10,2},{12,4},{14,6},{16,24},{18,... | collective-permute-start | bytes 24584 | tf_op jit(solution)/shard_map/ppermute | solution.py:567
  6.0 7.4 %collective-permute-start.1 = (f32[16,128]{1,0:T(8,128)S(1)}, f32[16,128]{1,0:T(8,128)S(1)}, u32[]{:S(2)}, u32[]{:S(2)}) collective-permute-start(f32[16,128]{1,0:T(8,128)S(1)} %get-tuple-element.29.refs_1_), channel_id=1, source_target_pairs={{0,16},{2,18},{4,20},{6,22},{8,24},{10,26},{12,28},{14,30},{16,0},... | collective-permute-start | bytes 24584 | tf_op jit(solution)/shard_map/ppermute | solution.py:567
  8.6 5.6 %collective-permute-start.2 = (f32[16,128]{1,0:T(8,128)S(1)}, f32[16,128]{1,0:T(8,128)S(1)}, u32[]{:S(2)}, u32[]{:S(2)}) collective-permute-start(f32[16,128]{1,0:T(8,128)S(1)} %get-tuple-element.29.refs_1_), channel_id=1, source_target_pairs={{0,24},{2,26},{4,28},{6,30},{8,16},{10,18},{12,20},{14,22},{16,8},... | collective-permute-start | bytes 24584 | tf_op jit(solution)/shard_map/ppermute | solution.py:567
  8.9 12.8 %collective-permute-start.6 = (bf16[768,128]{1,0:T(8,128)(2,1)S(1)}, bf16[768,128]{1,0:T(8,128)(2,1)S(1)}, u32[]{:S(2)}, u32[]{:S(2)}) collective-permute-start(bf16[768,128]{1,0:T(8,128)(2,1)S(1)} %get-tuple-element.33), channel_id=1, source_target_pairs={{0,16},{2,18},{4,20},{6,22},{8,24},{10,26},{12,28},{14,30},{16,0},... | collective-permute-start | bytes 589832 | tf_op jit(solution)/shard_map/ppermute | solution.py:525
  10.9 10.9 %collective-permute-start.7 = (bf16[576,128]{1,0:T(8,128)(2,1)S(1)}, bf16[576,128]{1,0:T(8,128)(2,1)S(1)}, u32[]{:S(2)}, u32[]{:S(2)}) collective-permute-start(bf16[576,128]{1,0:T(8,128)(2,1)S(1)} %get-tuple-element.34), channel_id=1, source_target_pairs={{0,8},{2,10},{4,12},{6,14},{8,0},{10,2},{12,4},{14,6},{16,24},{18,... | collective-permute-start | bytes 442376 | tf_op jit(solution)/shard_map/ppermute | solution.py:525
  14.5 5.3 %collective-permute-start.3 = (f32[8,1536]{1,0:T(8,128)S(1)}, f32[8,1536]{1,0:T(8,128)S(1)}, u32[]{:S(2)}, u32[]{:S(2)}) collective-permute-start(f32[8,1536]{1,0:T(8,128)S(1)} %get-tuple-element.30), channel_id=1, source_target_pairs={{0,2},{2,0},{4,6},{6,4},{8,10},{10,8},{12,14},{14,12},{16,18},{18,... | collective-permute-start | bytes 147464 | tf_op jit(solution)/shard_map/ppermute | solution.py:567
  14.5 5.3 %collective-permute-start.4 = (f32[8,1536]{1,0:T(8,128)S(1)}, f32[8,1536]{1,0:T(8,128)S(1)}, u32[]{:S(2)}, u32[]{:S(2)}) collective-permute-start(f32[8,1536]{1,0:T(8,128)S(1)} %get-tuple-element.31), channel_id=1, source_target_pairs={{0,6},{2,4},{4,2},{6,0},{8,14},{10,12},{12,10},{14,8},{16,22},{18,... | collective-permute-start | bytes 147464 | tf_op jit(solution)/shard_map/ppermute | solution.py:571
  16.1 3.7 %collective-permute-start.5 = (f32[16,128]{1,0:T(8,128)S(1)}, f32[16,128]{1,0:T(8,128)S(1)}, u32[]{:S(2)}, u32[]{:S(2)}) collective-permute-start(f32[16,128]{1,0:T(8,128)S(1)} %get-tuple-element.32.refs_0_), channel_id=1, source_target_pairs={{0,4},{2,6},{4,0},{6,2},{8,12},{10,14},{12,8},{14,10},{16,20},{18,... | collective-permute-start | bytes 24584 | tf_op jit(solution)/shard_map/ppermute | solution.py:567
  23.6 3.8 %collective-permute-start.8 = (f32[16,128]{1,0:T(8,128)S(1)}, f32[16,128]{1,0:T(8,128)S(1)}, u32[]{:S(2)}, u32[]{:S(2)}) collective-permute-start(f32[16,128]{1,0:T(8,128)S(1)} %get-tuple-element.36.refs_2_), channel_id=1, source_target_pairs={{0,8},{2,10},{4,12},{6,14},{8,0},{10,2},{12,4},{14,6},{16,24},{18,... | collective-permute-start | bytes 24584 | tf_op jit(solution)/shard_map/ppermute | solution.py:567
  23.9 5.6 %collective-permute-start.9 = (f32[16,128]{1,0:T(8,128)S(1)}, f32[16,128]{1,0:T(8,128)S(1)}, u32[]{:S(2)}, u32[]{:S(2)}) collective-permute-start(f32[16,128]{1,0:T(8,128)S(1)} %get-tuple-element.36.refs_2_), channel_id=1, source_target_pairs={{0,24},{2,26},{4,28},{6,30},{8,16},{10,18},{12,20},{14,22},{16,8},... | collective-permute-start | bytes 24584 | tf_op jit(solution)/shard_map/ppermute | solution.py:567
  24.9 4.7 %collective-permute-start.10 = (f32[16,128]{1,0:T(8,128)S(1)}, f32[16,128]{1,0:T(8,128)S(1)}, u32[]{:S(2)}, u32[]{:S(2)}) collective-permute-start(f32[16,128]{1,0:T(8,128)S(1)} %get-tuple-element.36.refs_2_), channel_id=1, source_target_pairs={{0,16},{2,18},{4,20},{6,22},{8,24},{10,26},{12,28},{14,30},{16,0},... | collective-permute-start | bytes 24584 | tf_op jit(solution)/shard_map/ppermute | solution.py:567
  27.8 7.1 %collective-permute-start.14 = (bf16[576,128]{1,0:T(8,128)(2,1)S(1)}, bf16[576,128]{1,0:T(8,128)(2,1)S(1)}, u32[]{:S(2)}, u32[]{:S(2)}) collective-permute-start(bf16[576,128]{1,0:T(8,128)(2,1)S(1)} %get-tuple-element.42), channel_id=1, source_target_pairs={{0,8},{2,10},{4,12},{6,14},{8,0},{10,2},{12,4},{14,6},{16,24},{18,... | collective-permute-start | bytes 442376 | tf_op jit(solution)/shard_map/ppermute | solution.py:525
  28.7 10.3 %collective-permute-start.15 = (bf16[768,128]{1,0:T(8,128)(2,1)S(1)}, bf16[768,128]{1,0:T(8,128)(2,1)S(1)}, u32[]{:S(2)}, u32[]{:S(2)}) collective-permute-start(bf16[768,128]{1,0:T(8,128)(2,1)S(1)} %get-tuple-element.45), channel_id=1, source_target_pairs={{0,16},{2,18},{4,20},{6,22},{8,24},{10,26},{12,28},{14,30},{16,0},... | collective-permute-start | bytes 589832 | tf_op jit(solution)/shard_map/ppermute | solution.py:525
  29.6 5.3 %collective-permute-start.11 = (f32[8,1536]{1,0:T(8,128)S(1)}, f32[8,1536]{1,0:T(8,128)S(1)}, u32[]{:S(2)}, u32[]{:S(2)}) collective-permute-start(f32[8,1536]{1,0:T(8,128)S(1)} %get-tuple-element.39), channel_id=1, source_target_pairs={{0,2},{2,0},{4,6},{6,4},{8,10},{10,8},{12,14},{14,12},{16,18},{18,... | collective-permute-start | bytes 147464 | tf_op jit(solution)/shard_map/ppermute | solution.py:567
  29.7 5.2 %collective-permute-start.12 = (f32[8,1536]{1,0:T(8,128)S(1)}, f32[8,1536]{1,0:T(8,128)S(1)}, u32[]{:S(2)}, u32[]{:S(2)}) collective-permute-start(f32[8,1536]{1,0:T(8,128)S(1)} %get-tuple-element.40), channel_id=1, source_target_pairs={{0,6},{2,4},{4,2},{6,0},{8,14},{10,12},{12,10},{14,8},{16,22},{18,... | collective-permute-start | bytes 147464 | tf_op jit(solution)/shard_map/ppermute | solution.py:571
  31.3 3.7 %collective-permute-start.13 = (f32[16,128]{1,0:T(8,128)S(1)}, f32[16,128]{1,0:T(8,128)S(1)}, u32[]{:S(2)}, u32[]{:S(2)}) collective-permute-start(f32[16,128]{1,0:T(8,128)S(1)} %get-tuple-element.41.refs_0_), channel_id=1, source_target_pairs={{0,4},{2,6},{4,0},{6,2},{8,12},{10,14},{12,8},{14,10},{16,20},{18,... | collective-permute-start | bytes 24584 | tf_op jit(solution)/shard_map/ppermute | solution.py:567
  37.1 7.9 %collective-permute-start.17 = (bf16[768,128]{1,0:T(8,128)(2,1)S(1)}, bf16[768,128]{1,0:T(8,128)(2,1)S(1)}, u32[]{:S(2)}, u32[]{:S(2)}) collective-permute-start(bf16[768,128]{1,0:T(8,128)(2,1)S(1)} %get-tuple-element.46.own), channel_id=1, source_target_pairs={{0,1},{1,0},{2,3},{3,2},{4,5},{5,4},{6,7},{7,6},{8,9},{9,8},{10,11... | collective-permute-start | bytes 589832 | tf_op jit(solution)/shard_map/ppermute | solution.py:690
  39.0 2.3 %copy-start = (bf16[16,16]{1,0:T(8,128)(2,1)S(1)}, bf16[16,16]{1,0:T(8,128)(2,1)}, u32[]{:S(2)}) copy-start(bf16[16,16]{1,0:T(8,128)(2,1)} %panel.3) | copy-start | bytes 1540
  39.7 7.7 %collective-permute-start.16 = (bf16[768,128]{1,0:T(8,128)(2,1)S(1)}, bf16[768,128]{1,0:T(8,128)(2,1)S(1)}, u32[]{:S(2)}, u32[]{:S(2)}) collective-permute-start(bf16[768,128]{1,0:T(8,128)(2,1)S(1)} %filtered.1.own), channel_id=1, source_target_pairs={{0,1},{1,0},{2,3},{3,2},{4,5},{5,4},{6,7},{7,6},{8,9},{9,8},{10,11... | collective-permute-start | bytes 589832 | tf_op jit(solution)/shard_map/ppermute | solution.py:690

commit v16 on v15

--- a/solution.py
+++ b/solution.py
@@ -399,12 +399,14 @@
     lax.fori_loop(0, g.ent // unroll, step, 0)
 
 
-def nonlocal_kernel(g, scale, far, acc, projf, energy, blk_hbm, atom_hbm, first, second, *refs):
+def nonlocal_kernel(g, scale, far, with_y, acc, projf, energy, blk_hbm, atom_hbm, first, second, *refs):
     if far:
         filtered, *sums, table, blk, atom, lut, sem, spread, out = refs[-10:]
-        y_refs = refs[-10 - len(g.face_rows(1)) : -10]
+        rest = refs[:-10]
     else:
         out, table, blk, atom, lut, sem, spread, *sums = refs[-9:]
+        rest = refs[:-9]
+    y_refs = rest[len(rest) - len(g.face_rows(1)) :]
     copies = entry_copies(blk_hbm, atom_hbm, blk, atom, sem)
     dom = lax.axis_index("dom")
     fill_lut(g, dom, lut)
@@ -420,8 +422,9 @@
     add_nonlocal(g, projf, blk, atom, lut, spread, sums)
     start, count = halves(g, dom)[0] if far else (0, g.cx)
     add_ends(g, dom, scale, acc, first, second, sums, out, start, count)
+    if with_y:
+        add_y_faces(g, dom, scale, y_refs, out, start, count)
     if far:
-        add_y_faces(g, dom, scale, y_refs, out, start, count)
         filtered[...] = out[...].astype(BF16)
 
 
@@ -449,20 +452,34 @@
     return [((1 - side) * RADIUS, RADIUS), (side * RADIUS, RADIUS)]
 
 
+def strips(g, dom):
+    parts = halves(g, dom)
+    if len(parts) == 1:
+        return parts
+    start, count = parts[1]
+    return [parts[0], (start, count - 2), (start + count - 2, 2)]
+
+
 def last_kernel(g, rest, acc, *refs):
     nx = len(g.face_rows(0))
-    filtered, work = refs[-2:]
+    work = refs[-1]
     dom = lax.axis_index("dom")
     start, count = halves(g, dom)[-1]
     if rest:
         first, second, *sums = refs[:4]
+        refs = refs[4:]
         add_ends(g, dom, 2.0, acc, first, second, sums, work, start, count)
-        refs = refs[4:]
+        add_y_faces(g, dom, 2.0, refs[nx : nx + len(g.face_rows(1))], work, start, count)
+        parts = strips(g, 0)[1:]
     else:
-        work[...] = acc[pl.ds(aligned(start * g.slab, g.slab), count * g.slab), :]
+        work[...] = acc[...]
+        parts = strips(g, 0)
     add_x_faces(g, dom, 2.0, refs[:nx], work, count)
-    add_y_faces(g, dom, 2.0, refs[nx:-2], work, start, count)
-    filtered[...] = work[...].astype(BF16)
+    at = 0
+    for out, (_, layers) in zip(refs[-1 - len(parts) : -1], parts):
+        size = layers * g.slab
+        out[...] = work[at : at + size, :].astype(BF16)
+        at += size
 
 
 def panel_kernel(g, panel, weights):
@@ -484,7 +501,7 @@
 
 def rotate_kernel(g, number, own, other, weights, *refs):
     out_hbm, out, sem = refs[-3:]
-    start, count = halves(g, lax.axis_index("dom"))[number]
+    start, count = strips(g, lax.axis_index("dom"))[number]
     group = 16
     span = group * g.no
     copies = []
@@ -623,11 +640,11 @@
             half = halves(g, 0)[0][1] * g.slab
             outputs = [jax.ShapeDtypeStruct((half, g.cz), BF16), field, field]
             scratch.append(pltpu.VMEM((half, g.cz), F32))
-            tables += from_y
         else:
             scratch += [pltpu.VMEM(field.shape, F32)] * 2
+        tables += from_y if prev else []
         out = call(
-            functools.partial(nonlocal_kernel, g, scale, far),
+            functools.partial(nonlocal_kernel, g, scale, far, len(prev) > 0),
             "nonlocal_" + which,
             outputs,
             scratch,
@@ -636,7 +653,7 @@
         )
         if far:
             out = [acc, first, second, *out[1:], out[0]]
-        return out, from_x + from_y
+        return out, from_x, from_y
 
     v, projf, pot, part = call(
         functools.partial(first_kernel, g),
@@ -652,7 +669,8 @@
         [orb, proj, pot, blk, atom],
         [HBM] * 5,
     )
-    (acc,), received = local_and_ends(1.0, "first", v, [], part)
+    (acc,), from_x, from_y = local_and_ends(1.0, "first", v, [], part)
+    received = [*from_x, *from_y]
     u, part = call(
         functools.partial(middle_kernel, g),
         "tables_second",
@@ -661,7 +679,7 @@
         [acc, projf, blk, atom, *received],
         [VMEM] * 2 + [HBM] * 2 + [VMEM] * len(received),
     )
-    out, received = local_and_ends(2.0, "second", u, [v], part)
+    out, from_x, from_y = local_and_ends(2.0, "second", u, [v], part)
     far = out[5:]
     weights = call(
         functools.partial(panel_kernel, g),
@@ -672,21 +690,18 @@
         [VMEM],
     )
     rotated = None
+    parts = strips(g, 0)
+    inputs = [*out[:5], *from_x, *from_y] if far else [*out, *from_x]
+    near = call(
+        functools.partial(last_kernel, g, len(far) > 0),
+        "filtered",
+        [jax.ShapeDtypeStruct((count * g.slab, g.cz), BF16) for _, count in parts[len(far) :]],
+        [pltpu.VMEM((halves(g, 0)[-1][1] * g.slab, g.cz), F32)],
+        inputs,
+        [VMEM] * len(inputs),
+    )
     pieces = []
-    parts = halves(g, 0)
-    for number, (_, count) in enumerate(parts):
-        if number < len(far):
-            filtered = far[number]
-        else:
-            inputs = [*out[:5], *received]
-            filtered = call(
-                functools.partial(last_kernel, g, len(far) > 0),
-                "filtered",
-                jax.ShapeDtypeStruct((count * g.slab, g.cz), BF16),
-                [pltpu.VMEM((count * g.slab, g.cz), F32)],
-                inputs,
-                [VMEM] * len(inputs),
-            )
+    for filtered, (_, count) in zip([*far, *near], parts):
         pieces.append((filtered, lax.ppermute(filtered, "band", [(0, 1), (1, 0)]), count))
     for number, (filtered, other, count) in enumerate(pieces):
         inputs = [filtered, other, weights] + ([] if rotated is None else [rotated])

time: 48.6 us -> 48.7 us (level)
  waiting for transfers between devices: 10.5 us -> 9.32 us
  Pallas kernels: 14.4 us -> 15.1 us
  starting transfers between devices: 22.7 us -> 23.2 us
    ppermute x2 -> x3, waiting for transfers between devices: 4.9 us -> 3.68 us  [shards(): lax.ppermute(filtered, 'band', [(0, 1), (1, 0)])]
    pallas_call x14 -> x15, Pallas kernels: 14.4 us -> 15.1 us  [call(): pl.pallas_call(kernel, name=name, out_shape=out_shape, in_specs=specs, ou...]
    ppermute x2 -> x3, starting transfers between devices: 3.11 us -> 3.64 us  [shards(): lax.ppermute(filtered, 'band', [(0, 1), (1, 0)])]
  transfers between devices with their start and end apart: 18 -> 19, of which waited for: 7 -> 7; matrix products, arithmetic and copies ran while one was open for 1% -> 1% of each run, Pallas kernels for 18% -> 20%
where the time goes in v16:
time: 48.7 us; the launch traced here: 48.4 us
  starting transfers between devices  23.2 us (48%)
  Pallas kernels  15.1 us (31%)
  waiting for transfers between devices  9.32 us (19%)
  local copies, waits for them, and re-layouts  0.61 us (1%)
    pallas_call x15, Pallas kernels, call(): pl.pallas_call(kernel, name=name, out_shape=out_shape, in_specs=specs, ou...  15.1 us
    ppermute x10, starting transfers between devices, swap(): return lax.ppermute(array, 'dom', pairs)  10.4 us
    ppermute x4, starting transfers between devices, shift(): return lax.ppermute(array, 'dom', pairs)  5.96 us
    ppermute x10, waiting for transfers between devices, swap(): return lax.ppermute(array, 'dom', pairs)  5.3 us
    ppermute x3, waiting for transfers between devices, shards(): lax.ppermute(filtered, 'band', [(0, 1), (1, 0)])  3.68 us
    ppermute x3, starting transfers between devices, shards(): lax.ppermute(filtered, 'band', [(0, 1), (1, 0)])  3.64 us
    ppermute x2, starting transfers between devices, reverse(): return lax.ppermute(array, 'dom', pairs)  3.2 us
  transfers between devices with their start and end apart: 19, of which 7 were waited for; matrix products, arithmetic and copies ran while one was open for 1% of the time, Pallas kernels for 20%

profile of v16, /device:TPU:0, one launch (start us, length us, event | category | flops | bytes accessed | tf_op | source)
XLA Modules:
  0.0 48.4 jit_solution(1002004711113557083)
XLA Ops:
  0.0 2.9 %tables_first.1 = (f32[1536,128]{1,0:T(8,128)S(1)}, f32[256,4,128]{2,1,0:T(4,128)S(1)}, f32[192,128]{1,0:T(8,128)S(1)}, f32[16,128]{1,0:T(8,128)S(1)}) custom-call(f32[1536,128]{1,0:T(8,128)} %bitcast.7, bf16[256,4,128]{2,1,0:T(4,128)(2,1)} %proj_hbm.1, f32[192,128]{1,0:T(8,128)} %bitcast.8, s32[256]{0:T(256)} %blk_hbm.7, s32[256]{0:T(256)} %atom_hbm.7), custom_call_target="tpu_custom_call" | custom-call | flops 1000 | bytes 1000 | tf_op jit(solution)/shard_map/tables_first/pallas_call | solution.py:524
  2.9 3.1 %collective-permute-start = (f32[16,128]{1,0:T(8,128)S(1)}, f32[16,128]{1,0:T(8,128)S(1)}, u32[]{:S(2)}, u32[]{:S(2)}) collective-permute-start(f32[16,128]{1,0:T(8,128)S(1)} %get-tuple-element.31.refs_1_), channel_id=1, source_target_pairs={{0,8},{2,10},{4,12},{6,14},{8,0},{10,2},{12,4},{14,6},{16,24},{18,... | collective-permute-start | bytes 24584 | tf_op jit(solution)/shard_map/ppermute | solution.py:584
  6.0 2.6 %collective-permute-start.1 = (f32[16,128]{1,0:T(8,128)S(1)}, f32[16,128]{1,0:T(8,128)S(1)}, u32[]{:S(2)}, u32[]{:S(2)}) collective-permute-start(f32[16,128]{1,0:T(8,128)S(1)} %get-tuple-element.31.refs_1_), channel_id=1, source_target_pairs={{0,16},{2,18},{4,20},{6,22},{8,24},{10,26},{12,28},{14,30},{16,0},... | collective-permute-start | bytes 24584 | tf_op jit(solution)/shard_map/ppermute | solution.py:584
  8.9 2.0 %collective-permute-start.6 = (bf16[768,128]{1,0:T(8,128)(2,1)S(1)}, bf16[768,128]{1,0:T(8,128)(2,1)S(1)}, u32[]{:S(2)}, u32[]{:S(2)}) collective-permute-start(bf16[768,128]{1,0:T(8,128)(2,1)S(1)} %get-tuple-element.35), channel_id=1, source_target_pairs={{0,16},{2,18},{4,20},{6,22},{8,24},{10,26},{12,28},{14,30},{16,0},... | collective-permute-start | bytes 589832 | tf_op jit(solution)/shard_map/ppermute | solution.py:542
  10.9 2.5 %collective-permute-start.7 = (bf16[576,128]{1,0:T(8,128)(2,1)S(1)}, bf16[576,128]{1,0:T(8,128)(2,1)S(1)}, u32[]{:S(2)}, u32[]{:S(2)}) collective-permute-start(bf16[576,128]{1,0:T(8,128)(2,1)S(1)} %get-tuple-element.36), channel_id=1, source_target_pairs={{0,8},{2,10},{4,12},{6,14},{8,0},{10,2},{12,4},{14,6},{16,24},{18,... | collective-permute-start | bytes 442376 | tf_op jit(solution)/shard_map/ppermute | solution.py:542
  13.4 0.7 %collective-permute-done.2.refs_4_ = f32[16,128]{1,0:T(8,128)S(1)} collective-permute-done((f32[16,128]{1,0:T(8,128)S(1)}, f32[16,128]{1,0:T(8,128)S(1)}, u32[]{:S(2)}, u32[]{:S(2)}) %collective-permute-start.2) | collective-permute-done | bytes 8224 | tf_op jit(solution)/shard_map/ppermute | solution.py:584
  14.5 1.6 %collective-permute-start.4 = (f32[8,1536]{1,0:T(8,128)S(1)}, f32[8,1536]{1,0:T(8,128)S(1)}, u32[]{:S(2)}, u32[]{:S(2)}) collective-permute-start(f32[8,1536]{1,0:T(8,128)S(1)} %get-tuple-element.33), channel_id=1, source_target_pairs={{0,6},{2,4},{4,2},{6,0},{8,14},{10,12},{12,10},{14,8},{16,22},{18,... | collective-permute-start | bytes 147464 | tf_op jit(solution)/shard_map/ppermute | solution.py:588
  16.6 0.9 %inside_first.1.acc = f32[1536,128]{1,0:T(8,128)S(1)} custom-call(f32[1536,128]{1,0:T(8,128)S(1)} %get-tuple-element.28.v_ref.refs_0_, f32[192,128]{1,0:T(8,128)S(1)} %get-tuple-element.29.pot), custom_call_target="tpu_custom_call" | custom-call | flops 1000 | bytes 1000 | tf_op jit(solution)/shard_map/inside_first/pallas_call | solution.py:524
  17.6 2.2 %collective-permute-done.5.refs_1_ = f32[16,128]{1,0:T(8,128)S(1)} collective-permute-done((f32[16,128]{1,0:T(8,128)S(1)}, f32[16,128]{1,0:T(8,128)S(1)}, u32[]{:S(2)}, u32[]{:S(2)}) %collective-permute-start.5) | collective-permute-done | bytes 8224 | tf_op jit(solution)/shard_map/ppermute | solution.py:584
  19.8 1.9 %nonlocal_first.1.acc = f32[1536,128]{1,0:T(8,128)S(1)} custom-call(f32[1536,128]{1,0:T(8,128)S(1)} %inside_first.1.acc, f32[256,4,128]{2,1,0:T(4,128)S(1)} %get-tuple-element.30.projf, f32[16,128]{1,0:T(8,128)S(1)} %copy.13.refs_5_.energy, s32[256]{0:T(256)} %blk_hbm.7, s32[256]{0:T(256)} %atom_hbm.7, f32[8,1536]{1,0:T(8,128)S(1)} %collective-permute-done.3.first, ...), custom_call_target="tpu_custom_call" | custom-call | flops 1000 | bytes 1000 | tf_op jit(solution)/shard_map/nonlocal_first/pallas_call | solution.py:524
  21.7 1.9 %tables_second.1 = (f32[1536,128]{1,0:T(8,128)S(1)}, f32[16,128]{1,0:T(8,128)S(1)}) custom-call(f32[1536,128]{1,0:T(8,128)S(1)} %nonlocal_first.1.acc, f32[256,4,128]{2,1,0:T(4,128)S(1)} %get-tuple-element.30.projf, s32[256]{0:T(256)} %blk_hbm.7, s32[256]{0:T(256)} %atom_hbm.7, bf16[768,128]{1,0:T(8,128)(2,1)S(1)} %collective-permute-done.6.refs_0_, ...), custom_call_target="tpu_custom_call" | custom-call | flops 1000 | bytes 1000 | tf_op jit(solution)/shard_map/tables_second/pallas_call | solution.py:524
  23.9 0.9 %collective-permute-start.9 = (f32[16,128]{1,0:T(8,128)S(1)}, f32[16,128]{1,0:T(8,128)S(1)}, u32[]{:S(2)}, u32[]{:S(2)}) collective-permute-start(f32[16,128]{1,0:T(8,128)S(1)} %get-tuple-element.38.refs_2_), channel_id=1, source_target_pairs={{0,24},{2,26},{4,28},{6,30},{8,16},{10,18},{12,20},{14,22},{16,8},... | collective-permute-start | bytes 24584 | tf_op jit(solution)/shard_map/ppermute | solution.py:584
  24.9 2.6 %collective-permute-start.10 = (f32[16,128]{1,0:T(8,128)S(1)}, f32[16,128]{1,0:T(8,128)S(1)}, u32[]{:S(2)}, u32[]{:S(2)}) collective-permute-start(f32[16,128]{1,0:T(8,128)S(1)} %get-tuple-element.38.refs_2_), channel_id=1, source_target_pairs={{0,16},{2,18},{4,20},{6,22},{8,24},{10,26},{12,28},{14,30},{16,0},... | collective-permute-start | bytes 24584 | tf_op jit(solution)/shard_map/ppermute | solution.py:584
  27.8 0.9 %collective-permute-start.14 = (bf16[576,128]{1,0:T(8,128)(2,1)S(1)}, bf16[576,128]{1,0:T(8,128)(2,1)S(1)}, u32[]{:S(2)}, u32[]{:S(2)}) collective-permute-start(bf16[576,128]{1,0:T(8,128)(2,1)S(1)} %get-tuple-element.44), channel_id=1, source_target_pairs={{0,8},{2,10},{4,12},{6,14},{8,0},{10,2},{12,4},{14,6},{16,24},{18,... | collective-permute-start | bytes 442376 | tf_op jit(solution)/shard_map/ppermute | solution.py:542
  29.7 1.6 %collective-permute-start.12 = (f32[8,1536]{1,0:T(8,128)S(1)}, f32[8,1536]{1,0:T(8,128)S(1)}, u32[]{:S(2)}, u32[]{:S(2)}) collective-permute-start(f32[8,1536]{1,0:T(8,128)S(1)} %get-tuple-element.42), channel_id=1, source_target_pairs={{0,6},{2,4},{4,2},{6,0},{8,14},{10,12},{12,10},{14,8},{16,22},{18,... | collective-permute-start | bytes 147464 | tf_op jit(solution)/shard_map/ppermute | solution.py:588
  31.8 1.0 %inside_second.1.acc = f32[1536,128]{1,0:T(8,128)S(1)} custom-call(f32[1536,128]{1,0:T(8,128)S(1)} %get-tuple-element.37.v_ref, f32[192,128]{1,0:T(8,128)S(1)} %get-tuple-element.29.pot, f32[1536,128]{1,0:T(8,128)S(1)} %get-tuple-element.28.v_ref.refs_0_), custom_call_target="tpu_custom_call" | custom-call | flops 1000 | bytes 1000 | tf_op jit(solution)/shard_map/inside_second/pallas_call | solution.py:524
  32.8 2.1 %collective-permute-done.13.refs_1_ = f32[16,128]{1,0:T(8,128)S(1)} collective-permute-done((f32[16,128]{1,0:T(8,128)S(1)}, f32[16,128]{1,0:T(8,128)S(1)}, u32[]{:S(2)}, u32[]{:S(2)}) %collective-permute-start.13) | collective-permute-done | bytes 8224 | tf_op jit(solution)/shard_map/ppermute | solution.py:584
  34.9 2.2 %nonlocal_second.1 = (bf16[768,128]{1,0:T(8,128)(2,1)S(1)}, f32[1536,128]{1,0:T(8,128)S(1)}, f32[1536,128]{1,0:T(8,128)S(1)}) custom-call(f32[1536,128]{1,0:T(8,128)S(1)} %inside_second.1.acc, f32[256,4,128]{2,1,0:T(4,128)S(1)} %get-tuple-element.30.projf, f32[16,128]{1,0:T(8,128)S(1)} %copy.16.refs_6_.energy, s32[256]{0:T(256)} %blk_hbm.7, s32[256]{0:T(256)} %atom_hbm.7, ...), custom_call_target="tpu_custom_call" | custom-call | flops 1000 | bytes 1000 | tf_op jit(solution)/shard_map/nonlocal_second/pallas_call | solution.py:524
  37.1 1.6 %collective-permute-start.18 = (bf16[768,128]{1,0:T(8,128)(2,1)S(1)}, bf16[768,128]{1,0:T(8,128)(2,1)S(1)}, u32[]{:S(2)}, u32[]{:S(2)}) collective-permute-start(bf16[768,128]{1,0:T(8,128)(2,1)S(1)} %get-tuple-element.50.own), channel_id=1, source_target_pairs={{0,1},{1,0},{2,3},{3,2},{4,5},{5,4},{6,7},{7,6},{8,9},{9,8},{10,11... | collective-permute-start | bytes 589832 | tf_op jit(solution)/shard_map/ppermute | solution.py:705
  39.7 1.6 %collective-permute-start.17 = (bf16[512,128]{1,0:T(8,128)(2,1)S(1)}, bf16[512,128]{1,0:T(8,128)(2,1)S(1)}, u32[]{:S(2)}, u32[]{:S(2)}) collective-permute-start(bf16[512,128]{1,0:T(8,128)(2,1)S(1)} %get-tuple-element.49.own), channel_id=1, source_target_pairs={{0,1},{1,0},{2,3},{3,2},{4,5},{5,4},{6,7},{7,6},{8,9},{9,8},{10,11... | collective-permute-start | bytes 393224 | tf_op jit(solution)/shard_map/ppermute | solution.py:705
  42.0 3.0 %collective-permute-done.18.other = bf16[768,128]{1,0:T(8,128)(2,1)S(1)} collective-permute-done((bf16[768,128]{1,0:T(8,128)(2,1)S(1)}, bf16[768,128]{1,0:T(8,128)(2,1)S(1)}, u32[]{:S(2)}, u32[]{:S(2)}) %collective-permute-start.18) | collective-permute-done | bytes 196640 | tf_op jit(solution)/shard_map/ppermute | solution.py:705
  45.0 1.0 %rotate_0.1.refs_0_ = f32[8,192,128]{2,1,0:T(8,128)} custom-call(bf16[768,128]{1,0:T(8,128)(2,1)S(1)} %get-tuple-element.50.own, bf16[768,128]{1,0:T(8,128)(2,1)S(1)} %collective-permute-done.18.other, bf16[128,256]{1,0:T(8,128)(2,1)S(1)} %panel.2.weights), custom_call_target="tpu_custom_call" | custom-call | flops 1000 | bytes 1000 | tf_op jit(solution)/shard_map/rotate_0/pallas_call | solution.py:524
  46.7 0.9 %rotate_1.1.refs_0_ = f32[8,192,128]{2,1,0:T(8,128)} custom-call(bf16[512,128]{1,0:T(8,128)(2,1)S(1)} %get-tuple-element.49.own, bf16[512,128]{1,0:T(8,128)(2,1)S(1)} %collective-permute-done.17.other, bf16[128,256]{1,0:T(8,128)(2,1)S(1)} %panel.2.weights, f32[8,192,128]{2,1,0:T(8,128)} %rotate_0.1.refs_0_), custom_call_target="tpu_custom_call", output_to_operand_aliasing={{}: (3, {})} | custom-call | flops 1000 | bytes 1000 | tf_op jit(solution)/shard_map/rotate_1/pallas_call | solution.py:524
  47.6 0.8 %rotate_2.1 = f32[8,192,128]{2,1,0:T(8,128)} custom-call(bf16[256,128]{1,0:T(8,128)(2,1)S(1)} %get-tuple-element.48.own, bf16[256,128]{1,0:T(8,128)(2,1)S(1)} %collective-permute-done.16.other, bf16[128,256]{1,0:T(8,128)(2,1)S(1)} %panel.2.weights, f32[8,192,128]{2,1,0:T(8,128)} %rotate_1.1.refs_0_), custom_call_target="tpu_custom_call", output_to_operand_aliasing={{}: (3, {})} | custom-call | flops 1000 | bytes 1000 | tf_op jit(solution)/shard_map/rotate_2/pallas_call | solution.py:524
  (44 shorter events, 6.0 us)
Async XLA Ops:
  0.0 8.6 %copy-start.1 = (f32[64,4]{0,1:T(4,128)S(1)}, f32[64,4]{0,1:T(4,128)}, u32[]{:S(2)}) copy-start(f32[64,4]{0,1:T(4,128)} %param.12) | copy-start | bytes 3076
  2.9 5.9 %collective-permute-start = (f32[16,128]{1,0:T(8,128)S(1)}, f32[16,128]{1,0:T(8,128)S(1)}, u32[]{:S(2)}, u32[]{:S(2)}) collective-permute-start(f32[16,128]{1,0:T(8,128)S(1)} %get-tuple-element.31.refs_1_), channel_id=1, source_target_pairs={{0,8},{2,10},{4,12},{6,14},{8,0},{10,2},{12,4},{14,6},{16,24},{18,... | collective-permute-start | bytes 24584 | tf_op jit(solution)/shard_map/ppermute | solution.py:584
  6.0 7.4 %collective-permute-start.1 = (f32[16,128]{1,0:T(8,128)S(1)}, f32[16,128]{1,0:T(8,128)S(1)}, u32[]{:S(2)}, u32[]{:S(2)}) collective-permute-start(f32[16,128]{1,0:T(8,128)S(1)} %get-tuple-element.31.refs_1_), channel_id=1, source_target_pairs={{0,16},{2,18},{4,20},{6,22},{8,24},{10,26},{12,28},{14,30},{16,0},... | collective-permute-start | bytes 24584 | tf_op jit(solution)/shard_map/ppermute | solution.py:584
  8.6 5.6 %collective-permute-start.2 = (f32[16,128]{1,0:T(8,128)S(1)}, f32[16,128]{1,0:T(8,128)S(1)}, u32[]{:S(2)}, u32[]{:S(2)}) collective-permute-start(f32[16,128]{1,0:T(8,128)S(1)} %get-tuple-element.31.refs_1_), channel_id=1, source_target_pairs={{0,24},{2,26},{4,28},{6,30},{8,16},{10,18},{12,20},{14,22},{16,8},... | collective-permute-start | bytes 24584 | tf_op jit(solution)/shard_map/ppermute | solution.py:584
  8.9 12.8 %collective-permute-start.6 = (bf16[768,128]{1,0:T(8,128)(2,1)S(1)}, bf16[768,128]{1,0:T(8,128)(2,1)S(1)}, u32[]{:S(2)}, u32[]{:S(2)}) collective-permute-start(bf16[768,128]{1,0:T(8,128)(2,1)S(1)} %get-tuple-element.35), channel_id=1, source_target_pairs={{0,16},{2,18},{4,20},{6,22},{8,24},{10,26},{12,28},{14,30},{16,0},... | collective-permute-start | bytes 589832 | tf_op jit(solution)/shard_map/ppermute | solution.py:542
  10.9 10.9 %collective-permute-start.7 = (bf16[576,128]{1,0:T(8,128)(2,1)S(1)}, bf16[576,128]{1,0:T(8,128)(2,1)S(1)}, u32[]{:S(2)}, u32[]{:S(2)}) collective-permute-start(bf16[576,128]{1,0:T(8,128)(2,1)S(1)} %get-tuple-element.36), channel_id=1, source_target_pairs={{0,8},{2,10},{4,12},{6,14},{8,0},{10,2},{12,4},{14,6},{16,24},{18,... | collective-permute-start | bytes 442376 | tf_op jit(solution)/shard_map/ppermute | solution.py:542
  14.5 5.3 %collective-permute-start.3 = (f32[8,1536]{1,0:T(8,128)S(1)}, f32[8,1536]{1,0:T(8,128)S(1)}, u32[]{:S(2)}, u32[]{:S(2)}) collective-permute-start(f32[8,1536]{1,0:T(8,128)S(1)} %get-tuple-element.32), channel_id=1, source_target_pairs={{0,2},{2,0},{4,6},{6,4},{8,10},{10,8},{12,14},{14,12},{16,18},{18,... | collective-permute-start | bytes 147464 | tf_op jit(solution)/shard_map/ppermute | solution.py:584
  14.5 5.3 %collective-permute-start.4 = (f32[8,1536]{1,0:T(8,128)S(1)}, f32[8,1536]{1,0:T(8,128)S(1)}, u32[]{:S(2)}, u32[]{:S(2)}) collective-permute-start(f32[8,1536]{1,0:T(8,128)S(1)} %get-tuple-element.33), channel_id=1, source_target_pairs={{0,6},{2,4},{4,2},{6,0},{8,14},{10,12},{12,10},{14,8},{16,22},{18,... | collective-permute-start | bytes 147464 | tf_op jit(solution)/shard_map/ppermute | solution.py:588
  16.1 3.7 %collective-permute-start.5 = (f32[16,128]{1,0:T(8,128)S(1)}, f32[16,128]{1,0:T(8,128)S(1)}, u32[]{:S(2)}, u32[]{:S(2)}) collective-permute-start(f32[16,128]{1,0:T(8,128)S(1)} %get-tuple-element.34.refs_0_), channel_id=1, source_target_pairs={{0,4},{2,6},{4,0},{6,2},{8,12},{10,14},{12,8},{14,10},{16,20},{18,... | collective-permute-start | bytes 24584 | tf_op jit(solution)/shard_map/ppermute | solution.py:584
  23.6 3.8 %collective-permute-start.8 = (f32[16,128]{1,0:T(8,128)S(1)}, f32[16,128]{1,0:T(8,128)S(1)}, u32[]{:S(2)}, u32[]{:S(2)}) collective-permute-start(f32[16,128]{1,0:T(8,128)S(1)} %get-tuple-element.38.refs_2_), channel_id=1, source_target_pairs={{0,8},{2,10},{4,12},{6,14},{8,0},{10,2},{12,4},{14,6},{16,24},{18,... | collective-permute-start | bytes 24584 | tf_op jit(solution)/shard_map/ppermute | solution.py:584
  23.9 5.6 %collective-permute-start.9 = (f32[16,128]{1,0:T(8,128)S(1)}, f32[16,128]{1,0:T(8,128)S(1)}, u32[]{:S(2)}, u32[]{:S(2)}) collective-permute-start(f32[16,128]{1,0:T(8,128)S(1)} %get-tuple-element.38.refs_2_), channel_id=1, source_target_pairs={{0,24},{2,26},{4,28},{6,30},{8,16},{10,18},{12,20},{14,22},{16,8},... | collective-permute-start | bytes 24584 | tf_op jit(solution)/shard_map/ppermute | solution.py:584
  24.9 4.7 %collective-permute-start.10 = (f32[16,128]{1,0:T(8,128)S(1)}, f32[16,128]{1,0:T(8,128)S(1)}, u32[]{:S(2)}, u32[]{:S(2)}) collective-permute-start(f32[16,128]{1,0:T(8,128)S(1)} %get-tuple-element.38.refs_2_), channel_id=1, source_target_pairs={{0,16},{2,18},{4,20},{6,22},{8,24},{10,26},{12,28},{14,30},{16,0},... | collective-permute-start | bytes 24584 | tf_op jit(solution)/shard_map/ppermute | solution.py:584
  27.8 7.2 %collective-permute-start.14 = (bf16[576,128]{1,0:T(8,128)(2,1)S(1)}, bf16[576,128]{1,0:T(8,128)(2,1)S(1)}, u32[]{:S(2)}, u32[]{:S(2)}) collective-permute-start(bf16[576,128]{1,0:T(8,128)(2,1)S(1)} %get-tuple-element.44), channel_id=1, source_target_pairs={{0,8},{2,10},{4,12},{6,14},{8,0},{10,2},{12,4},{14,6},{16,24},{18,... | collective-permute-start | bytes 442376 | tf_op jit(solution)/shard_map/ppermute | solution.py:542
  28.7 10.3 %collective-permute-start.15 = (bf16[768,128]{1,0:T(8,128)(2,1)S(1)}, bf16[768,128]{1,0:T(8,128)(2,1)S(1)}, u32[]{:S(2)}, u32[]{:S(2)}) collective-permute-start(bf16[768,128]{1,0:T(8,128)(2,1)S(1)} %get-tuple-element.47), channel_id=1, source_target_pairs={{0,16},{2,18},{4,20},{6,22},{8,24},{10,26},{12,28},{14,30},{16,0},... | collective-permute-start | bytes 589832 | tf_op jit(solution)/shard_map/ppermute | solution.py:542
  29.6 5.3 %collective-permute-start.11 = (f32[8,1536]{1,0:T(8,128)S(1)}, f32[8,1536]{1,0:T(8,128)S(1)}, u32[]{:S(2)}, u32[]{:S(2)}) collective-permute-start(f32[8,1536]{1,0:T(8,128)S(1)} %get-tuple-element.41), channel_id=1, source_target_pairs={{0,2},{2,0},{4,6},{6,4},{8,10},{10,8},{12,14},{14,12},{16,18},{18,... | collective-permute-start | bytes 147464 | tf_op jit(solution)/shard_map/ppermute | solution.py:584
  29.7 5.2 %collective-permute-start.12 = (f32[8,1536]{1,0:T(8,128)S(1)}, f32[8,1536]{1,0:T(8,128)S(1)}, u32[]{:S(2)}, u32[]{:S(2)}) collective-permute-start(f32[8,1536]{1,0:T(8,128)S(1)} %get-tuple-element.42), channel_id=1, source_target_pairs={{0,6},{2,4},{4,2},{6,0},{8,14},{10,12},{12,10},{14,8},{16,22},{18,... | collective-permute-start | bytes 147464 | tf_op jit(solution)/shard_map/ppermute | solution.py:588
  31.3 3.7 %collective-permute-start.13 = (f32[16,128]{1,0:T(8,128)S(1)}, f32[16,128]{1,0:T(8,128)S(1)}, u32[]{:S(2)}, u32[]{:S(2)}) collective-permute-start(f32[16,128]{1,0:T(8,128)S(1)} %get-tuple-element.43.refs_0_), channel_id=1, source_target_pairs={{0,4},{2,6},{4,0},{6,2},{8,12},{10,14},{12,8},{14,10},{16,20},{18,... | collective-permute-start | bytes 24584 | tf_op jit(solution)/shard_map/ppermute | solution.py:584
  37.1 7.9 %collective-permute-start.18 = (bf16[768,128]{1,0:T(8,128)(2,1)S(1)}, bf16[768,128]{1,0:T(8,128)(2,1)S(1)}, u32[]{:S(2)}, u32[]{:S(2)}) collective-permute-start(bf16[768,128]{1,0:T(8,128)(2,1)S(1)} %get-tuple-element.50.own), channel_id=1, source_target_pairs={{0,1},{1,0},{2,3},{3,2},{4,5},{5,4},{6,7},{7,6},{8,9},{9,8},{10,11... | collective-permute-start | bytes 589832 | tf_op jit(solution)/shard_map/ppermute | solution.py:705
  39.0 2.8 %copy-start = (bf16[16,16]{1,0:T(8,128)(2,1)S(1)}, bf16[16,16]{1,0:T(8,128)(2,1)}, u32[]{:S(2)}) copy-start(bf16[16,16]{1,0:T(8,128)(2,1)} %panel.3) | copy-start | bytes 1540
  39.7 7.0 %collective-permute-start.17 = (bf16[512,128]{1,0:T(8,128)(2,1)S(1)}, bf16[512,128]{1,0:T(8,128)(2,1)S(1)}, u32[]{:S(2)}, u32[]{:S(2)}) collective-permute-start(bf16[512,128]{1,0:T(8,128)(2,1)S(1)} %get-tuple-element.49.own), channel_id=1, source_target_pairs={{0,1},{1,0},{2,3},{3,2},{4,5},{5,4},{6,7},{7,6},{8,9},{9,8},{10,11... | collective-permute-start | bytes 393224 | tf_op jit(solution)/shard_map/ppermute | solution.py:705
  41.2 6.4 %collective-permute-start.16 = (bf16[256,128]{1,0:T(8,128)(2,1)S(1)}, bf16[256,128]{1,0:T(8,128)(2,1)S(1)}, u32[]{:S(2)}, u32[]{:S(2)}) collective-permute-start(bf16[256,128]{1,0:T(8,128)(2,1)S(1)} %get-tuple-element.48.own), channel_id=1, source_target_pairs={{0,1},{1,0},{2,3},{3,2},{4,5},{5,4},{6,7},{7,6},{8,9},{9,8},{10,11... | collective-permute-start | bytes 196616 | tf_op jit(solution)/shard_map/ppermute | solution.py:705

commit v17 on v16

--- a/solution.py
+++ b/solution.py
@@ -357,13 +357,26 @@
                 out[pl.ds(at, g.no), :] = total
 
 
-def spread_rows(g, dom, table, energy, spread):
+def spread_rows(g, dom, table, energy, wide, spread):
     lanes = g.table
     count = g.slots()
+    row, col = iota((g.nproj, lanes), 0), iota((g.nproj, lanes), 1)
+    pick = jnp.where(row == col // g.no % g.nproj, 1.0, 0.0)
+    if energy.shape[0] == g.nproj:
+        wide[...] = lax.dot_general(
+            energy[...], pick, TN, precision=lax.Precision.HIGHEST, preferred_element_type=F32
+        )
+    place = iota((1, lanes), 1) // (g.nproj * g.no)
     rows = []
     for step in g.steps(dom):
-        owner = pl.ds(jnp.clip(dom + step, 0, g.dom_count - 1), 1)
-        rows.append(table[owner, :] * energy[owner, :])
+        owner = jnp.clip(dom + step, 0, g.dom_count - 1)
+        if energy.shape[0] == g.nproj:
+            factor = jnp.zeros((1, lanes), F32)
+            for a in range(g.owned):
+                factor = jnp.where(place == a, wide[pl.ds(owner * g.owned + a, 1), :], factor)
+        else:
+            factor = energy[pl.ds(owner, 1), :]
+        rows.append(table[pl.ds(owner, 1), :] * factor)
     rows.append(jnp.zeros((8 - count, lanes), F32))
     scaled = jnp.concatenate(rows, axis=0)
     high = scaled.astype(BF16)
@@ -371,8 +384,7 @@
     mid = rest.astype(BF16)
     low = (rest - mid.astype(F32)).astype(BF16)
     parts = jnp.concatenate([high, mid, low], axis=0)
-    wide = count * g.cz
-    row, col = iota((24, wide), 0), iota((24, wide), 1)
+    row, col = iota((24, count * g.cz), 0), iota((24, count * g.cz), 1)
     ones = jnp.where(row % 8 == col // g.cz, 1.0, 0.0).astype(BF16)
     out_all = lax.dot_general(parts, ones, TN, preferred_element_type=F32)
     for number in range(count):
@@ -401,11 +413,11 @@
 
 def nonlocal_kernel(g, scale, far, with_y, acc, projf, energy, blk_hbm, atom_hbm, first, second, *refs):
     if far:
-        filtered, *sums, table, blk, atom, lut, sem, spread, out = refs[-10:]
+        filtered, *sums, table, wide, blk, atom, lut, sem, spread, out = refs[-11:]
+        rest = refs[:-11]
+    else:
+        out, table, wide, blk, atom, lut, sem, spread, *sums = refs[-10:]
         rest = refs[:-10]
-    else:
-        out, table, blk, atom, lut, sem, spread, *sums = refs[-9:]
-        rest = refs[:-9]
     y_refs = rest[len(rest) - len(g.face_rows(1)) :]
     copies = entry_copies(blk_hbm, atom_hbm, blk, atom, sem)
     dom = lax.axis_index("dom")
@@ -415,7 +427,7 @@
         table[...] = (group[...] + get_table(g, first)) + (get_table(g, second) + opposite[...])
     else:
         table[...] = refs[0][...]
-    spread_rows(g, dom, table, energy, spread)
+    spread_rows(g, dom, table, energy, wide, spread)
     clear(sums)
     for copy in copies:
         copy.wait()
@@ -589,7 +601,10 @@
 
     def local_and_ends(scale, which, values, prev, part):
         energy = (scale / HALF_WIDTH) * kb_energy
-        energy = jnp.repeat(energy.reshape(g.dom_count, g.owned * g.nproj), g.no, axis=1)
+        if prev:
+            energy = jnp.repeat(energy.reshape(g.dom_count, g.owned * g.nproj), g.no, axis=1)
+        else:
+            energy = energy.T
         acc = call(
             functools.partial(inside_kernel, g, scale, len(prev) > 0),
             "inside_" + which,
@@ -634,7 +649,8 @@
         first, second = swap(first, 1), reverse(second)
         tables = [group, swap(group, 2)] if g.butterfly else [lax.psum(part, "dom")]
         far = prev and len(halves(g, 0)) == 2
-        scratch = [pltpu.VMEM(table.shape, F32), *entries, spread]
+        wide = pltpu.VMEM((kb_energy.shape[0], g.table), F32)
+        scratch = [pltpu.VMEM(table.shape, F32), wide, *entries, spread]
         outputs = [field]
         if far:
             half = halves(g, 0)[0][1] * g.slab

time: 48.7 us -> 48.7 us (level)
  no operation moved by 1% of the time
where the time goes in v17:
time: 48.7 us; the launch traced here: 48.5 us
  starting transfers between devices  23.2 us (48%)
  Pallas kernels  15.2 us (31%)
  waiting for transfers between devices  9.53 us (20%)
    pallas_call x15, Pallas kernels, call(): pl.pallas_call(kernel, name=name, out_shape=out_shape, in_specs=specs, ou...  15.2 us
    ppermute x10, starting transfers between devices, swap(): return lax.ppermute(array, 'dom', pairs)  10.6 us
    ppermute x4, starting transfers between devices, shift(): return lax.ppermute(array, 'dom', pairs)  5.98 us
    ppermute x10, waiting for transfers between devices, swap(): return lax.ppermute(array, 'dom', pairs)  5.34 us
    ppermute x3, starting transfers between devices, shards(): lax.ppermute(filtered, 'band', [(0, 1), (1, 0)])  3.65 us
    ppermute x3, waiting for transfers between devices, shards(): lax.ppermute(filtered, 'band', [(0, 1), (1, 0)])  3.55 us
    ppermute x2, starting transfers between devices, reverse(): return lax.ppermute(array, 'dom', pairs)  2.99 us
  transfers between devices with their start and end apart: 19, of which 7 were waited for; matrix products, arithmetic and copies ran while one was open for 1% of the time, Pallas kernels for 20%

profile of v17, /device:TPU:0, one launch (start us, length us, event | category | flops | bytes accessed | tf_op | source)
XLA Modules:
  0.0 48.5 jit_solution(4115345517358172346)
XLA Ops:
  0.0 2.9 %tables_first.1 = (f32[1536,128]{1,0:T(8,128)S(1)}, f32[256,4,128]{2,1,0:T(4,128)S(1)}, f32[192,128]{1,0:T(8,128)S(1)}, f32[16,128]{1,0:T(8,128)S(1)}) custom-call(f32[1536,128]{1,0:T(8,128)} %bitcast.7, bf16[256,4,128]{2,1,0:T(4,128)(2,1)} %proj_hbm.1, f32[192,128]{1,0:T(8,128)} %bitcast.8, s32[256]{0:T(256)} %blk_hbm.7, s32[256]{0:T(256)} %atom_hbm.7), custom_call_target="tpu_custom_call" | custom-call | flops 1000 | bytes 1000 | tf_op jit(solution)/shard_map/tables_first/pallas_call | solution.py:536
  2.9 3.1 %collective-permute-start = (f32[16,128]{1,0:T(8,128)S(1)}, f32[16,128]{1,0:T(8,128)S(1)}, u32[]{:S(2)}, u32[]{:S(2)}) collective-permute-start(f32[16,128]{1,0:T(8,128)S(1)} %get-tuple-element.31.refs_1_), channel_id=1, source_target_pairs={{0,8},{2,10},{4,12},{6,14},{8,0},{10,2},{12,4},{14,6},{16,24},{18,... | collective-permute-start | bytes 24584 | tf_op jit(solution)/shard_map/ppermute | solution.py:596
  6.0 2.6 %collective-permute-start.1 = (f32[16,128]{1,0:T(8,128)S(1)}, f32[16,128]{1,0:T(8,128)S(1)}, u32[]{:S(2)}, u32[]{:S(2)}) collective-permute-start(f32[16,128]{1,0:T(8,128)S(1)} %get-tuple-element.31.refs_1_), channel_id=1, source_target_pairs={{0,16},{2,18},{4,20},{6,22},{8,24},{10,26},{12,28},{14,30},{16,0},... | collective-permute-start | bytes 24584 | tf_op jit(solution)/shard_map/ppermute | solution.py:596
  8.6 2.1 %collective-permute-start.6 = (bf16[768,128]{1,0:T(8,128)(2,1)S(1)}, bf16[768,128]{1,0:T(8,128)(2,1)S(1)}, u32[]{:S(2)}, u32[]{:S(2)}) collective-permute-start(bf16[768,128]{1,0:T(8,128)(2,1)S(1)} %get-tuple-element.35), channel_id=1, source_target_pairs={{0,16},{2,18},{4,20},{6,22},{8,24},{10,26},{12,28},{14,30},{16,0},... | collective-permute-start | bytes 589832 | tf_op jit(solution)/shard_map/ppermute | solution.py:554
  10.8 2.3 %collective-permute-start.7 = (bf16[576,128]{1,0:T(8,128)(2,1)S(1)}, bf16[576,128]{1,0:T(8,128)(2,1)S(1)}, u32[]{:S(2)}, u32[]{:S(2)}) collective-permute-start(bf16[576,128]{1,0:T(8,128)(2,1)S(1)} %get-tuple-element.36), channel_id=1, source_target_pairs={{0,8},{2,10},{4,12},{6,14},{8,0},{10,2},{12,4},{14,6},{16,24},{18,... | collective-permute-start | bytes 442376 | tf_op jit(solution)/shard_map/ppermute | solution.py:554
  13.1 1.1 %collective-permute-done.2.refs_4_ = f32[16,128]{1,0:T(8,128)S(1)} collective-permute-done((f32[16,128]{1,0:T(8,128)S(1)}, f32[16,128]{1,0:T(8,128)S(1)}, u32[]{:S(2)}, u32[]{:S(2)}) %collective-permute-start.2) | collective-permute-done | bytes 8224 | tf_op jit(solution)/shard_map/ppermute | solution.py:596
  14.5 1.6 %collective-permute-start.4 = (f32[8,1536]{1,0:T(8,128)S(1)}, f32[8,1536]{1,0:T(8,128)S(1)}, u32[]{:S(2)}, u32[]{:S(2)}) collective-permute-start(f32[8,1536]{1,0:T(8,128)S(1)} %get-tuple-element.33), channel_id=1, source_target_pairs={{0,6},{2,4},{4,2},{6,0},{8,14},{10,12},{12,10},{14,8},{16,22},{18,... | collective-permute-start | bytes 147464 | tf_op jit(solution)/shard_map/ppermute | solution.py:600
  16.7 0.9 %inside_first.1.acc = f32[1536,128]{1,0:T(8,128)S(1)} custom-call(f32[1536,128]{1,0:T(8,128)S(1)} %get-tuple-element.28.v_ref.refs_0_, f32[192,128]{1,0:T(8,128)S(1)} %get-tuple-element.29.pot), custom_call_target="tpu_custom_call" | custom-call | flops 1000 | bytes 1000 | tf_op jit(solution)/shard_map/inside_first/pallas_call | solution.py:536
  17.6 2.2 %collective-permute-done.5.refs_1_ = f32[16,128]{1,0:T(8,128)S(1)} collective-permute-done((f32[16,128]{1,0:T(8,128)S(1)}, f32[16,128]{1,0:T(8,128)S(1)}, u32[]{:S(2)}, u32[]{:S(2)}) %collective-permute-start.5) | collective-permute-done | bytes 8224 | tf_op jit(solution)/shard_map/ppermute | solution.py:596
  19.8 2.0 %nonlocal_first.1.acc = f32[1536,128]{1,0:T(8,128)S(1)} custom-call(f32[1536,128]{1,0:T(8,128)S(1)} %inside_first.1.acc, f32[256,4,128]{2,1,0:T(4,128)S(1)} %get-tuple-element.30.projf, f32[4,64]{1,0:T(4,128)S(1)} %get-tuple-element.52.refs_5_.energy, s32[256]{0:T(256)} %blk_hbm.7, s32[256]{0:T(256)} %atom_hbm.7, ...), custom_call_target="tpu_custom_call" | custom-call | flops 1000 | bytes 1000 | tf_op jit(solution)/shard_map/nonlocal_first/pallas_call | solution.py:536
  21.9 1.9 %tables_second.1 = (f32[1536,128]{1,0:T(8,128)S(1)}, f32[16,128]{1,0:T(8,128)S(1)}) custom-call(f32[1536,128]{1,0:T(8,128)S(1)} %nonlocal_first.1.acc, f32[256,4,128]{2,1,0:T(4,128)S(1)} %get-tuple-element.30.projf, s32[256]{0:T(256)} %blk_hbm.7, s32[256]{0:T(256)} %atom_hbm.7, bf16[768,128]{1,0:T(8,128)(2,1)S(1)} %collective-permute-done.6.refs_0_, ...), custom_call_target="tpu_custom_call" | custom-call | flops 1000 | bytes 1000 | tf_op jit(solution)/shard_map/tables_second/pallas_call | solution.py:536
  24.7 2.9 %collective-permute-start.10 = (f32[16,128]{1,0:T(8,128)S(1)}, f32[16,128]{1,0:T(8,128)S(1)}, u32[]{:S(2)}, u32[]{:S(2)}) collective-permute-start(f32[16,128]{1,0:T(8,128)S(1)} %get-tuple-element.38.refs_2_), channel_id=1, source_target_pairs={{0,16},{2,18},{4,20},{6,22},{8,24},{10,26},{12,28},{14,30},{16,0},... | collective-permute-start | bytes 24584 | tf_op jit(solution)/shard_map/ppermute | solution.py:596
  27.9 0.9 %collective-permute-start.14 = (bf16[576,128]{1,0:T(8,128)(2,1)S(1)}, bf16[576,128]{1,0:T(8,128)(2,1)S(1)}, u32[]{:S(2)}, u32[]{:S(2)}) collective-permute-start(bf16[576,128]{1,0:T(8,128)(2,1)S(1)} %get-tuple-element.44), channel_id=1, source_target_pairs={{0,8},{2,10},{4,12},{6,14},{8,0},{10,2},{12,4},{14,6},{16,24},{18,... | collective-permute-start | bytes 442376 | tf_op jit(solution)/shard_map/ppermute | solution.py:554
  29.7 1.4 %collective-permute-start.12 = (f32[8,1536]{1,0:T(8,128)S(1)}, f32[8,1536]{1,0:T(8,128)S(1)}, u32[]{:S(2)}, u32[]{:S(2)}) collective-permute-start(f32[8,1536]{1,0:T(8,128)S(1)} %get-tuple-element.42), channel_id=1, source_target_pairs={{0,6},{2,4},{4,2},{6,0},{8,14},{10,12},{12,10},{14,8},{16,22},{18,... | collective-permute-start | bytes 147464 | tf_op jit(solution)/shard_map/ppermute | solution.py:600
  31.9 1.0 %inside_second.1.acc = f32[1536,128]{1,0:T(8,128)S(1)} custom-call(f32[1536,128]{1,0:T(8,128)S(1)} %get-tuple-element.37.v_ref, f32[192,128]{1,0:T(8,128)S(1)} %get-tuple-element.29.pot, f32[1536,128]{1,0:T(8,128)S(1)} %get-tuple-element.28.v_ref.refs_0_), custom_call_target="tpu_custom_call" | custom-call | flops 1000 | bytes 1000 | tf_op jit(solution)/shard_map/inside_second/pallas_call | solution.py:536
  32.8 1.9 %collective-permute-done.13.refs_1_ = f32[16,128]{1,0:T(8,128)S(1)} collective-permute-done((f32[16,128]{1,0:T(8,128)S(1)}, f32[16,128]{1,0:T(8,128)S(1)}, u32[]{:S(2)}, u32[]{:S(2)}) %collective-permute-start.13) | collective-permute-done | bytes 8224 | tf_op jit(solution)/shard_map/ppermute | solution.py:596
  34.8 2.2 %nonlocal_second.1 = (bf16[768,128]{1,0:T(8,128)(2,1)S(1)}, f32[1536,128]{1,0:T(8,128)S(1)}, f32[1536,128]{1,0:T(8,128)S(1)}) custom-call(f32[1536,128]{1,0:T(8,128)S(1)} %inside_second.1.acc, f32[256,4,128]{2,1,0:T(4,128)S(1)} %get-tuple-element.30.projf, f32[16,128]{1,0:T(8,128)S(1)} %copy.12.refs_6_.energy, s32[256]{0:T(256)} %blk_hbm.7, s32[256]{0:T(256)} %atom_hbm.7, ...), custom_call_target="tpu_custom_call" | custom-call | flops 1000 | bytes 1000 | tf_op jit(solution)/shard_map/nonlocal_second/pallas_call | solution.py:536
  36.9 1.6 %collective-permute-start.18 = (bf16[768,128]{1,0:T(8,128)(2,1)S(1)}, bf16[768,128]{1,0:T(8,128)(2,1)S(1)}, u32[]{:S(2)}, u32[]{:S(2)}) collective-permute-start(bf16[768,128]{1,0:T(8,128)(2,1)S(1)} %get-tuple-element.50.own), channel_id=1, source_target_pairs={{0,1},{1,0},{2,3},{3,2},{4,5},{5,4},{6,7},{7,6},{8,9},{9,8},{10,11... | collective-permute-start | bytes 589832 | tf_op jit(solution)/shard_map/ppermute | solution.py:721
  39.8 1.6 %collective-permute-start.17 = (bf16[512,128]{1,0:T(8,128)(2,1)S(1)}, bf16[512,128]{1,0:T(8,128)(2,1)S(1)}, u32[]{:S(2)}, u32[]{:S(2)}) collective-permute-start(bf16[512,128]{1,0:T(8,128)(2,1)S(1)} %get-tuple-element.49.own), channel_id=1, source_target_pairs={{0,1},{1,0},{2,3},{3,2},{4,5},{5,4},{6,7},{7,6},{8,9},{9,8},{10,11... | collective-permute-start | bytes 393224 | tf_op jit(solution)/shard_map/ppermute | solution.py:721
  42.2 2.7 %collective-permute-done.18.other = bf16[768,128]{1,0:T(8,128)(2,1)S(1)} collective-permute-done((bf16[768,128]{1,0:T(8,128)(2,1)S(1)}, bf16[768,128]{1,0:T(8,128)(2,1)S(1)}, u32[]{:S(2)}, u32[]{:S(2)}) %collective-permute-start.18) | collective-permute-done | bytes 196640 | tf_op jit(solution)/shard_map/ppermute | solution.py:721
  44.8 1.0 %rotate_0.1.refs_0_ = f32[8,192,128]{2,1,0:T(8,128)} custom-call(bf16[768,128]{1,0:T(8,128)(2,1)S(1)} %get-tuple-element.50.own, bf16[768,128]{1,0:T(8,128)(2,1)S(1)} %collective-permute-done.18.other, bf16[128,256]{1,0:T(8,128)(2,1)S(1)} %panel.2.weights), custom_call_target="tpu_custom_call" | custom-call | flops 1000 | bytes 1000 | tf_op jit(solution)/shard_map/rotate_0/pallas_call | solution.py:536
  45.8 0.9 %collective-permute-done.17.other = bf16[512,128]{1,0:T(8,128)(2,1)S(1)} collective-permute-done((bf16[512,128]{1,0:T(8,128)(2,1)S(1)}, bf16[512,128]{1,0:T(8,128)(2,1)S(1)}, u32[]{:S(2)}, u32[]{:S(2)}) %collective-permute-start.17) | collective-permute-done | bytes 131104 | tf_op jit(solution)/shard_map/ppermute | solution.py:721
  46.7 0.9 %rotate_1.1.refs_0_ = f32[8,192,128]{2,1,0:T(8,128)} custom-call(bf16[512,128]{1,0:T(8,128)(2,1)S(1)} %get-tuple-element.49.own, bf16[512,128]{1,0:T(8,128)(2,1)S(1)} %collective-permute-done.17.other, bf16[128,256]{1,0:T(8,128)(2,1)S(1)} %panel.2.weights, f32[8,192,128]{2,1,0:T(8,128)} %rotate_0.1.refs_0_), custom_call_target="tpu_custom_call", output_to_operand_aliasing={{}: (3, {})} | custom-call | flops 1000 | bytes 1000 | tf_op jit(solution)/shard_map/rotate_1/pallas_call | solution.py:536
  47.6 0.8 %rotate_2.1 = f32[8,192,128]{2,1,0:T(8,128)} custom-call(bf16[256,128]{1,0:T(8,128)(2,1)S(1)} %get-tuple-element.48.own, bf16[256,128]{1,0:T(8,128)(2,1)S(1)} %collective-permute-done.16.other, bf16[128,256]{1,0:T(8,128)(2,1)S(1)} %panel.2.weights, f32[8,192,128]{2,1,0:T(8,128)} %rotate_1.1.refs_0_), custom_call_target="tpu_custom_call", output_to_operand_aliasing={{}: (3, {})} | custom-call | flops 1000 | bytes 1000 | tf_op jit(solution)/shard_map/rotate_2/pallas_call | solution.py:536
  (39 shorter events, 6.0 us)
Async XLA Ops:
  2.9 5.7 %collective-permute-start = (f32[16,128]{1,0:T(8,128)S(1)}, f32[16,128]{1,0:T(8,128)S(1)}, u32[]{:S(2)}, u32[]{:S(2)}) collective-permute-start(f32[16,128]{1,0:T(8,128)S(1)} %get-tuple-element.31.refs_1_), channel_id=1, source_target_pairs={{0,8},{2,10},{4,12},{6,14},{8,0},{10,2},{12,4},{14,6},{16,24},{18,... | collective-permute-start | bytes 24584 | tf_op jit(solution)/shard_map/ppermute | solution.py:596
  6.0 7.1 %collective-permute-start.1 = (f32[16,128]{1,0:T(8,128)S(1)}, f32[16,128]{1,0:T(8,128)S(1)}, u32[]{:S(2)}, u32[]{:S(2)}) collective-permute-start(f32[16,128]{1,0:T(8,128)S(1)} %get-tuple-element.31.refs_1_), channel_id=1, source_target_pairs={{0,16},{2,18},{4,20},{6,22},{8,24},{10,26},{12,28},{14,30},{16,0},... | collective-permute-start | bytes 24584 | tf_op jit(solution)/shard_map/ppermute | solution.py:596
  8.5 5.6 %collective-permute-start.2 = (f32[16,128]{1,0:T(8,128)S(1)}, f32[16,128]{1,0:T(8,128)S(1)}, u32[]{:S(2)}, u32[]{:S(2)}) collective-permute-start(f32[16,128]{1,0:T(8,128)S(1)} %get-tuple-element.31.refs_1_), channel_id=1, source_target_pairs={{0,24},{2,26},{4,28},{6,30},{8,16},{10,18},{12,20},{14,22},{16,8},... | collective-permute-start | bytes 24584 | tf_op jit(solution)/shard_map/ppermute | solution.py:596
  8.6 4.5 %copy-start.1 = (f32[64,4]{0,1:T(4,128)S(1)}, f32[64,4]{0,1:T(4,128)}, u32[]{:S(2)}) copy-start(f32[64,4]{0,1:T(4,128)} %param.12) | copy-start | bytes 3076
  8.6 13.3 %collective-permute-start.6 = (bf16[768,128]{1,0:T(8,128)(2,1)S(1)}, bf16[768,128]{1,0:T(8,128)(2,1)S(1)}, u32[]{:S(2)}, u32[]{:S(2)}) collective-permute-start(bf16[768,128]{1,0:T(8,128)(2,1)S(1)} %get-tuple-element.35), channel_id=1, source_target_pairs={{0,16},{2,18},{4,20},{6,22},{8,24},{10,26},{12,28},{14,30},{16,0},... | collective-permute-start | bytes 589832 | tf_op jit(solution)/shard_map/ppermute | solution.py:554
  10.8 11.1 %collective-permute-start.7 = (bf16[576,128]{1,0:T(8,128)(2,1)S(1)}, bf16[576,128]{1,0:T(8,128)(2,1)S(1)}, u32[]{:S(2)}, u32[]{:S(2)}) collective-permute-start(bf16[576,128]{1,0:T(8,128)(2,1)S(1)} %get-tuple-element.36), channel_id=1, source_target_pairs={{0,8},{2,10},{4,12},{6,14},{8,0},{10,2},{12,4},{14,6},{16,24},{18,... | collective-permute-start | bytes 442376 | tf_op jit(solution)/shard_map/ppermute | solution.py:554
  14.5 5.3 %collective-permute-start.3 = (f32[8,1536]{1,0:T(8,128)S(1)}, f32[8,1536]{1,0:T(8,128)S(1)}, u32[]{:S(2)}, u32[]{:S(2)}) collective-permute-start(f32[8,1536]{1,0:T(8,128)S(1)} %get-tuple-element.32), channel_id=1, source_target_pairs={{0,2},{2,0},{4,6},{6,4},{8,10},{10,8},{12,14},{14,12},{16,18},{18,... | collective-permute-start | bytes 147464 | tf_op jit(solution)/shard_map/ppermute | solution.py:596
  14.5 5.3 %collective-permute-start.4 = (f32[8,1536]{1,0:T(8,128)S(1)}, f32[8,1536]{1,0:T(8,128)S(1)}, u32[]{:S(2)}, u32[]{:S(2)}) collective-permute-start(f32[8,1536]{1,0:T(8,128)S(1)} %get-tuple-element.33), channel_id=1, source_target_pairs={{0,6},{2,4},{4,2},{6,0},{8,14},{10,12},{12,10},{14,8},{16,22},{18,... | collective-permute-start | bytes 147464 | tf_op jit(solution)/shard_map/ppermute | solution.py:600
  16.2 3.7 %collective-permute-start.5 = (f32[16,128]{1,0:T(8,128)S(1)}, f32[16,128]{1,0:T(8,128)S(1)}, u32[]{:S(2)}, u32[]{:S(2)}) collective-permute-start(f32[16,128]{1,0:T(8,128)S(1)} %get-tuple-element.34.refs_0_), channel_id=1, source_target_pairs={{0,4},{2,6},{4,0},{6,2},{8,12},{10,14},{12,8},{14,10},{16,20},{18,... | collective-permute-start | bytes 24584 | tf_op jit(solution)/shard_map/ppermute | solution.py:596
  23.8 3.8 %collective-permute-start.8 = (f32[16,128]{1,0:T(8,128)S(1)}, f32[16,128]{1,0:T(8,128)S(1)}, u32[]{:S(2)}, u32[]{:S(2)}) collective-permute-start(f32[16,128]{1,0:T(8,128)S(1)} %get-tuple-element.38.refs_2_), channel_id=1, source_target_pairs={{0,8},{2,10},{4,12},{6,14},{8,0},{10,2},{12,4},{14,6},{16,24},{18,... | collective-permute-start | bytes 24584 | tf_op jit(solution)/shard_map/ppermute | solution.py:596
  24.1 5.5 %collective-permute-start.9 = (f32[16,128]{1,0:T(8,128)S(1)}, f32[16,128]{1,0:T(8,128)S(1)}, u32[]{:S(2)}, u32[]{:S(2)}) collective-permute-start(f32[16,128]{1,0:T(8,128)S(1)} %get-tuple-element.38.refs_2_), channel_id=1, source_target_pairs={{0,24},{2,26},{4,28},{6,30},{8,16},{10,18},{12,20},{14,22},{16,8},... | collective-permute-start | bytes 24584 | tf_op jit(solution)/shard_map/ppermute | solution.py:596
  24.7 4.9 %collective-permute-start.10 = (f32[16,128]{1,0:T(8,128)S(1)}, f32[16,128]{1,0:T(8,128)S(1)}, u32[]{:S(2)}, u32[]{:S(2)}) collective-permute-start(f32[16,128]{1,0:T(8,128)S(1)} %get-tuple-element.38.refs_2_), channel_id=1, source_target_pairs={{0,16},{2,18},{4,20},{6,22},{8,24},{10,26},{12,28},{14,30},{16,0},... | collective-permute-start | bytes 24584 | tf_op jit(solution)/shard_map/ppermute | solution.py:596
  27.9 6.9 %collective-permute-start.14 = (bf16[576,128]{1,0:T(8,128)(2,1)S(1)}, bf16[576,128]{1,0:T(8,128)(2,1)S(1)}, u32[]{:S(2)}, u32[]{:S(2)}) collective-permute-start(bf16[576,128]{1,0:T(8,128)(2,1)S(1)} %get-tuple-element.44), channel_id=1, source_target_pairs={{0,8},{2,10},{4,12},{6,14},{8,0},{10,2},{12,4},{14,6},{16,24},{18,... | collective-permute-start | bytes 442376 | tf_op jit(solution)/shard_map/ppermute | solution.py:554
  28.8 10.3 %collective-permute-start.15 = (bf16[768,128]{1,0:T(8,128)(2,1)S(1)}, bf16[768,128]{1,0:T(8,128)(2,1)S(1)}, u32[]{:S(2)}, u32[]{:S(2)}) collective-permute-start(bf16[768,128]{1,0:T(8,128)(2,1)S(1)} %get-tuple-element.47), channel_id=1, source_target_pairs={{0,16},{2,18},{4,20},{6,22},{8,24},{10,26},{12,28},{14,30},{16,0},... | collective-permute-start | bytes 589832 | tf_op jit(solution)/shard_map/ppermute | solution.py:554
  29.6 5.1 %collective-permute-start.11 = (f32[8,1536]{1,0:T(8,128)S(1)}, f32[8,1536]{1,0:T(8,128)S(1)}, u32[]{:S(2)}, u32[]{:S(2)}) collective-permute-start(f32[8,1536]{1,0:T(8,128)S(1)} %get-tuple-element.41), channel_id=1, source_target_pairs={{0,2},{2,0},{4,6},{6,4},{8,10},{10,8},{12,14},{14,12},{16,18},{18,... | collective-permute-start | bytes 147464 | tf_op jit(solution)/shard_map/ppermute | solution.py:596
  29.7 5.0 %collective-permute-start.12 = (f32[8,1536]{1,0:T(8,128)S(1)}, f32[8,1536]{1,0:T(8,128)S(1)}, u32[]{:S(2)}, u32[]{:S(2)}) collective-permute-start(f32[8,1536]{1,0:T(8,128)S(1)} %get-tuple-element.42), channel_id=1, source_target_pairs={{0,6},{2,4},{4,2},{6,0},{8,14},{10,12},{12,10},{14,8},{16,22},{18,... | collective-permute-start | bytes 147464 | tf_op jit(solution)/shard_map/ppermute | solution.py:600
  31.1 3.7 %collective-permute-start.13 = (f32[16,128]{1,0:T(8,128)S(1)}, f32[16,128]{1,0:T(8,128)S(1)}, u32[]{:S(2)}, u32[]{:S(2)}) collective-permute-start(f32[16,128]{1,0:T(8,128)S(1)} %get-tuple-element.43.refs_0_), channel_id=1, source_target_pairs={{0,4},{2,6},{4,0},{6,2},{8,12},{10,14},{12,8},{14,10},{16,20},{18,... | collective-permute-start | bytes 24584 | tf_op jit(solution)/shard_map/ppermute | solution.py:596
  36.9 7.9 %collective-permute-start.18 = (bf16[768,128]{1,0:T(8,128)(2,1)S(1)}, bf16[768,128]{1,0:T(8,128)(2,1)S(1)}, u32[]{:S(2)}, u32[]{:S(2)}) collective-permute-start(bf16[768,128]{1,0:T(8,128)(2,1)S(1)} %get-tuple-element.50.own), channel_id=1, source_target_pairs={{0,1},{1,0},{2,3},{3,2},{4,5},{5,4},{6,7},{7,6},{8,9},{9,8},{10,11... | collective-permute-start | bytes 589832 | tf_op jit(solution)/shard_map/ppermute | solution.py:721
  39.1 2.8 %copy-start = (bf16[16,16]{1,0:T(8,128)(2,1)S(1)}, bf16[16,16]{1,0:T(8,128)(2,1)}, u32[]{:S(2)}) copy-start(bf16[16,16]{1,0:T(8,128)(2,1)} %panel.3) | copy-start | bytes 1540
  39.8 6.9 %collective-permute-start.17 = (bf16[512,128]{1,0:T(8,128)(2,1)S(1)}, bf16[512,128]{1,0:T(8,128)(2,1)S(1)}, u32[]{:S(2)}, u32[]{:S(2)}) collective-permute-start(bf16[512,128]{1,0:T(8,128)(2,1)S(1)} %get-tuple-element.49.own), channel_id=1, source_target_pairs={{0,1},{1,0},{2,3},{3,2},{4,5},{5,4},{6,7},{7,6},{8,9},{9,8},{10,11... | collective-permute-start | bytes 393224 | tf_op jit(solution)/shard_map/ppermute | solution.py:721
  41.4 6.2 %collective-permute-start.16 = (bf16[256,128]{1,0:T(8,128)(2,1)S(1)}, bf16[256,128]{1,0:T(8,128)(2,1)S(1)}, u32[]{:S(2)}, u32[]{:S(2)}) collective-permute-start(bf16[256,128]{1,0:T(8,128)(2,1)S(1)} %get-tuple-element.48.own), channel_id=1, source_target_pairs={{0,1},{1,0},{2,3},{3,2},{4,5},{5,4},{6,7},{7,6},{8,9},{9,8},{10,11... | collective-permute-start | bytes 196616 | tf_op jit(solution)/shard_map/ppermute | solution.py:721
